TPU v7x, 256 devices: a whole 4x4x8 slice. The times are simulated.
256 devices in a mesh: cam: 8 (over x, y_lo), tm: 32 (over z, y_hi, core).
Axes of the slice: x: 4, y: 4 (y_hi: 2, y_lo: 2; y = y_hi * 2 + y_lo), z: 8, core: 2. Of those that a mesh axis runs over, the one named last changes fastest.
Arguments:
- queries: bfloat16 [8, 512, 8, 1536], P('cam', 'tm'), may hold values from -6 to 6
- keys: bfloat16 [8, 512, 8, 1536], P('cam', 'tm'), may hold values from -6 to 6
- values: bfloat16 [8, 512, 8, 1536], P('cam', 'tm'), may hold values from -6 to 6
- cam_valid: int32 [8, 512], P('cam', 'tm'), may hold values 0 or 1
- windows: int32 [12], replicated, may hold values from 1 to 64, as said below
- actions: int32 [512, 7], P('tm'), may hold values from 0 to 255
- act_table: bfloat16 [7, 256, 1536], replicated, may hold values from -1.796875 to 1.796875
- w_out: bfloat16 [1536, 1536], P('tm'), may hold values from -0.15625 to 0.15625
- cotangent: bfloat16 [8, 512, 8, 1536], P('cam', 'tm'), may hold values from -6 to 6
Outputs:
- predicted: bfloat16 [8, 512, 8, 1536], P('cam', 'tm')
- grad_queries: bfloat16 [8, 512, 8, 1536], P('cam', 'tm')
- grad_keys: bfloat16 [8, 512, 8, 1536], P('cam', 'tm')
- grad_values: bfloat16 [8, 512, 8, 1536], P('cam', 'tm')
- grad_out_weight: float32 [1536, 1536], P(('cam', 'tm'))
Inputs may be any that keep to these rules, and one draw needn't show every extreme that they name: `windows`: some entry equals 64.
All inputs are finite; a program needn't handle non-finite values. No bound on the sum of `cam_valid` on one device may be relied on, other than what follows from the above.
Results may differ from a plain program's by a relative error of at most 0.009.
Values may be sent and summed in bfloat16 or wider, within the bound.
No kernel may reach another device: no remote copies, remote signals or barrier semaphores. Data moves between devices by JAX's collectives and lax.ppermute only.
A program may use at most 128 MiB of HBM per device.

v0:
```python
import math

import jax
import jax.numpy as jnp
from jax import lax
from jax.sharding import PartitionSpec as P

HC = 12
HT = 12
HD = 64
WIN = 64


def from_behind(value, axis, steps):
    count = lax.axis_size(axis)
    first, last = (max(0, -steps), min(count, count - steps))
    return lax.ppermute(value, axis, [(source, source + steps) for source in range(first, last)])


def softmax_rows(scores, axes):
    largest = jnp.max(scores, axis=axes, keepdims=True)
    exponent = jnp.exp(scores - largest)
    return exponent / jnp.sum(exponent, axis=axes, keepdims=True)


def view_block(query_heads, key_heads, value_heads, grad_heads, allowed, score_scale):
    view_scores = (
        jnp.einsum(
            "cmphd,emrhd->cmhper", query_heads, key_heads, preferred_element_type=jnp.float32
        )
        * score_scale
    )
    view_scores = jnp.where(allowed, view_scores, -jnp.inf)
    view_prob = softmax_rows(view_scores, (4, 5))
    view_weights = view_prob.astype(jnp.bfloat16)
    attended = jnp.einsum(
        "cmhper,emrhd->cmphd", view_weights, value_heads, preferred_element_type=jnp.float32
    )
    grad_weights = jnp.einsum(
        "cmphd,emrhd->cmhper", grad_heads, value_heads, preferred_element_type=jnp.float32
    )
    grad_scores = (
        view_prob * (grad_weights - jnp.sum(view_prob * grad_weights, axis=(4, 5), keepdims=True))
    ).astype(jnp.bfloat16)
    grad_query = (
        jnp.einsum(
            "cmhper,emrhd->cmphd", grad_scores, key_heads, preferred_element_type=jnp.float32
        )
        * score_scale
    )
    key_terms = (
        jnp.einsum(
            "cmhper,cmphd->cemrhd", grad_scores, query_heads, preferred_element_type=jnp.float32
        )
        * score_scale
    ).astype(jnp.bfloat16)
    value_terms = jnp.einsum(
        "cmhper,cmphd->cemrhd", view_weights, grad_heads, preferred_element_type=jnp.float32
    ).astype(jnp.bfloat16)
    return (attended, grad_query, key_terms, value_terms)


def shards(queries, keys, values, cam_valid, windows, actions, act_table, w_out, cotangent):
    frames = queries.shape[1]
    tokens = queries.shape[2]
    model_width = queries.shape[3]
    cross_width = HC * HD
    time_width = model_width - cross_width
    score_scale = HD ** (-0.5)
    row_count = frames * tokens
    view_count = lax.axis_size("cam")
    query_local = queries[0]
    key_local = keys[0]
    value_local = values[0]
    flat_grad = cotangent[0].reshape(row_count, model_width)
    w_full = lax.all_gather(w_out, "tm", axis=0, tiled=True)
    grad_attn = jnp.einsum(
        "rk,ck->rc", flat_grad, w_full, preferred_element_type=jnp.float32
    ).astype(jnp.bfloat16)
    grad_attn = grad_attn.reshape(frames, tokens, model_width)
    grad_view = grad_attn[:, :, :cross_width]
    query_view = query_local[:, :, :cross_width]
    valid_row = cam_valid.astype(jnp.bfloat16)
    own_view = lax.axis_index("cam")
    key_views, value_views, valid_views = (
        lax.all_gather(key_local[None, :, :, :cross_width], "cam", axis=0, tiled=True),
        lax.all_gather(value_local[None, :, :, :cross_width], "cam", axis=0, tiled=True),
        lax.all_gather(valid_row, "cam", axis=0, tiled=True),
    )
    key_heads = key_views.reshape(view_count, frames, tokens, HC, HD)
    value_heads = value_views.reshape(view_count, frames, tokens, HC, HD)
    allowed = (valid_views > 0.5) | (jnp.arange(view_count)[:, None] == own_view)
    allowed = jnp.transpose(allowed)[None, :, None, None, :, None]
    attended, grad_query, key_terms, value_terms = view_block(
        query_view.reshape(1, frames, tokens, HC, HD),
        key_heads,
        value_heads,
        grad_view.reshape(1, frames, tokens, HC, HD),
        allowed,
        score_scale,
    )
    key_summed, value_summed = (
        lax.psum_scatter(
            key_terms.astype(jnp.float32)
            .reshape(view_count, frames, tokens, cross_width)
            .astype(jnp.bfloat16),
            "cam",
            scatter_dimension=0,
            tiled=True,
        ).astype(jnp.float32),
        lax.psum_scatter(
            value_terms.astype(jnp.float32)
            .reshape(view_count, frames, tokens, cross_width)
            .astype(jnp.bfloat16),
            "cam",
            scatter_dimension=0,
            tiled=True,
        ).astype(jnp.float32),
    )
    view_attended = attended.reshape(frames, tokens, cross_width)
    view_dq = grad_query.reshape(frames, tokens, cross_width)
    view_dk = key_summed[0]
    view_dv = value_summed[0]
    key_time = key_local[:, :, cross_width:]
    value_time = value_local[:, :, cross_width:]
    edge_send = jnp.stack([key_time, value_time])
    reach_count = (WIN + frames - 2) // frames
    tail_frames = WIN - 1 - (reach_count - 1) * frames
    received = []
    for distance in range(1, reach_count + 1):
        sent_frames = frames if distance < reach_count else tail_frames
        received.append(from_behind(edge_send[:, frames - sent_frames :], "tm", distance))
    extended = jnp.concatenate(received[::-1] + [edge_send], axis=1)
    span_frames = frames + WIN - 1
    key_ext = extended[0].reshape(span_frames, tokens, HT, HD)
    value_ext = extended[1].reshape(span_frames, tokens, HT, HD)
    query_time = query_local[:, :, cross_width:].reshape(frames, tokens, HT, HD)
    grad_time = grad_attn[:, :, cross_width:].reshape(frames, tokens, HT, HD)
    first_frame = lax.axis_index("tm") * frames
    query_frame = first_frame + jnp.arange(frames, dtype=jnp.int32)
    key_frame = first_frame - (WIN - 1) + jnp.arange(span_frames, dtype=jnp.int32)
    frame_gap = query_frame[:, None] - key_frame[None, :]
    usable = (
        (frame_gap[None, :, :] >= 0)
        & (frame_gap[None, :, :] < windows[:, None, None])
        & (key_frame[None, None, :] >= 0)
    )
    time_scores = (
        jnp.einsum("fphd,gphd->phfg", query_time, key_ext, preferred_element_type=jnp.float32)
        * score_scale
    )
    time_scores = jnp.where(usable[None], time_scores, -jnp.inf)
    time_prob = softmax_rows(time_scores, (3,))
    time_weights = time_prob.astype(jnp.bfloat16)
    time_attended = jnp.einsum(
        "phfg,gphd->fphd", time_weights, value_ext, preferred_element_type=jnp.float32
    )
    attn = jnp.concatenate(
        [view_attended, time_attended.reshape(frames, tokens, time_width)], axis=-1
    ).astype(jnp.bfloat16)
    flat_attn = attn.reshape(row_count, model_width)
    codes = jnp.arange(act_table.shape[1])
    one_hot = (actions[:, :, None] == codes[None, None, :]).astype(jnp.bfloat16).reshape(frames, -1)
    action_sum = jnp.dot(
        one_hot, act_table.reshape(-1, model_width), preferred_element_type=jnp.float32
    )
    mixed = jnp.dot(flat_attn, w_full, preferred_element_type=jnp.float32)
    predicted = (mixed.reshape(frames, tokens, model_width) + action_sum[:, None, :]).astype(
        jnp.bfloat16
    )[None]
    total_tokens = view_count * lax.axis_size("tm") * row_count
    grad_norm = 1.0 / math.sqrt(total_tokens)
    grad_out_weight = lax.psum_scatter(
        jnp.einsum("rc,rd->cd", flat_attn, flat_grad, preferred_element_type=jnp.float32)
        * grad_norm,
        ("cam", "tm"),
        scatter_dimension=0,
        tiled=True,
    )
    time_grad_weights = jnp.einsum(
        "fphd,gphd->phfg", grad_time, value_ext, preferred_element_type=jnp.float32
    )
    time_grad_scores = (
        time_prob
        * (time_grad_weights - jnp.sum(time_prob * time_grad_weights, axis=3, keepdims=True))
    ).astype(jnp.bfloat16)
    time_dq = (
        jnp.einsum("phfg,gphd->fphd", time_grad_scores, key_ext, preferred_element_type=jnp.float32)
        * score_scale
    )
    key_ext_grad = (
        jnp.einsum(
            "phfg,fphd->gphd", time_grad_scores, query_time, preferred_element_type=jnp.float32
        )
        * score_scale
    )
    value_ext_grad = jnp.einsum(
        "phfg,fphd->gphd", time_weights, grad_time, preferred_element_type=jnp.float32
    )
    ext_grads = jnp.stack(
        [
            key_ext_grad.reshape(span_frames, tokens, time_width),
            value_ext_grad.reshape(span_frames, tokens, time_width),
        ]
    )
    time_grads = ext_grads[:, WIN - 1 :]
    position = 0
    for distance in range(reach_count, 0, -1):
        sent_frames = frames if distance < reach_count else tail_frames
        returned = from_behind(
            ext_grads[:, position : position + sent_frames].astype(jnp.bfloat16), "tm", -distance
        ).astype(jnp.float32)
        time_grads = time_grads + jnp.pad(
            returned, ((0, 0), (frames - sent_frames, 0), (0, 0), (0, 0))
        )
        position = position + sent_frames
    grad_queries = jnp.concatenate(
        [view_dq, time_dq.reshape(frames, tokens, time_width)], axis=-1
    ).astype(jnp.bfloat16)[None]
    grad_keys = jnp.concatenate([view_dk, time_grads[0]], axis=-1).astype(jnp.bfloat16)[None]
    grad_values = jnp.concatenate([view_dv, time_grads[1]], axis=-1).astype(jnp.bfloat16)[None]
    return (predicted, grad_queries, grad_keys, grad_values, grad_out_weight)


def solution(mesh):
    in_specs = (
        P("cam", "tm", None, None),
        P("cam", "tm", None, None),
        P("cam", "tm", None, None),
        P("cam", "tm"),
        P(),
        P("tm", None),
        P(),
        P("tm", None),
        P("cam", "tm", None, None),
    )
    out_specs = (
        P("cam", "tm", None, None),
        P("cam", "tm", None, None),
        P("cam", "tm", None, None),
        P("cam", "tm", None, None),
        P(("cam", "tm"), None),
    )
    return jax.shard_map(shards, mesh=mesh, in_specs=in_specs, out_specs=out_specs, check_vma=False)
```

profile of v0, /device:TPU:1, one launch (start us, length us, event | category | flops | bytes accessed | tf_op | source)
XLA Modules:
  0.0 1697.7 jit_solution(2782669456004123868)
XLA Ops:
  10.9 15.1 collective-permute-start.2
  26.0 13.1 collective-permute-start.1
  39.1 13.1 collective-permute-start.3
  59.2 22.9 %all-gather.2 = bf16[8,1,16]{2,1,0:T(2,128)(2,1)S(1)} all-gather(bf16[1,1,16]{2,1,0:T(2,128)(2,1)S(1)} %convert_bitcast_fusion), channel_id=1, replica_groups=mesh['cam'=8,'tm'=32] {'cam'}, dimensions={0}, use_global_device_ids=true | all-gather | bytes 288 | tf_op jit(solution)/shard_map/all_gather | solution.py:88
  104.7 20.8 %all-gather.9.cloned.1.call-done = bf16[128,8,768]{2,1,0:T(8,128)(2,1)} async-done(((bf16[16,8,768]{2,1,0:T(8,128)(2,1)}), bf16[128,8,768]{2,1,0:T(8,128)(2,1)}) %all-gather.9.cloned.1.call-update) | async-done | bytes 1572880 | tf_op jit(solution)/shard_map/all_gather | solution.py:86
  151.1 68.7 %all-gather.7.cloned.1.call-done = bf16[1536,1536]{1,0:T(8,128)(2,1)} async-done(((bf16[48,1536]{1,0:T(8,128)(2,1)}), bf16[1536,1536]{1,0:T(8,128)(2,1)}) %all-gather.7.cloned.1.call-update) | async-done | bytes 4718608 | tf_op jit(solution)/shard_map/all_gather | solution.py:76
  225.0 6.9 fusion.2
  243.4 6.3 convert_element_type.109
  249.7 731.5 %fusion = f32[8,1536]{1,0:T(8,128)S(1)} fusion(f32[1536,1536]{1,0:T(8,128)} %convolution_multiply_fusion), kind=kCustom, calls=%all-reduce-scatter | all-reduce-scatter fusion | flops 3145729 | bytes 9486336
  1002.3 31.4 %collective-permute-start.55 = (f32[8,1536]{1,0:T(8,128)S(1)}, f32[8,1536]{1,0:T(8,128)S(1)}, u32[]{:S(2)}, u32[]{:S(2)}) collective-permute-start(f32[8,1536]{1,0:T(8,128)S(1)} %fusion), channel_id=1, source_target_pairs={{0,48},{1,49},{2,50},{3,51},{4,52},{5,53},{6,54},{7,55},{8,56},{9,... | collective-permute-start | bytes 147464
  1056.3 6.6 collective-permute-start.45
  1062.9 6.1 collective-permute-start.44
  1088.1 13.1 collective-permute-start.37
  1101.3 13.1 collective-permute-start.36
  1114.4 13.1 collective-permute-start.35
  1127.6 13.1 collective-permute-start.34
  1140.7 13.1 collective-permute-start.33
  1153.9 13.1 collective-permute-start.32
  1167.0 13.1 collective-permute-start.31
  1180.2 13.7 collective-permute-start.30
  1193.9 13.1 collective-permute-start.29
  1207.1 13.2 collective-permute-start.28
  1220.2 13.1 collective-permute-start.27
  1233.4 13.1 collective-permute-start.26
  1246.5 13.1 collective-permute-start.25
  1259.7 13.1 collective-permute-start.24
  1272.8 13.1 collective-permute-start.23
  1286.0 13.1 collective-permute-start.22
  1299.1 13.1 collective-permute-start.21
  1312.2 13.1 collective-permute-start.20
  1325.4 13.1 collective-permute-start.19
  1338.5 13.1 collective-permute-start.18
  1351.7 13.1 collective-permute-start.17
  1364.8 13.1 collective-permute-start.16
  1377.9 13.1 collective-permute-start.15
  1391.1 13.2 collective-permute-start.14
  1404.2 13.1 collective-permute-start.13
  1417.4 13.1 collective-permute-start.12
  1430.5 13.1 collective-permute-start.11
  1443.7 13.1 collective-permute-start.10
  1456.8 13.1 collective-permute-start.9
  1470.3 12.6 collective-permute-start.8
  1490.1 98.6 %concatenate.69 = f32[518,1536]{1,0:T(8,128)} concatenate(f32[6,1536]{1,0:T(8,128)} %copy-done.23, f32[8,1536]{1,0:T(8,128)S(1)} %collective-permute-done.70, f32[8,1536]{1,0:T(8,128)S(1)} %collective-permute-done.69, f32[8,1536]{1,0:T(8,128)} %copy-done.22, f32[8,1536]{1,0:T(8,128)} %copy-done.24, f32[8,1536]{1,0:T(8,128)} %copy-done.25, f32[8,1536]{1,0:T(8,128)} %copy-done.26, ...), dimensions={0} | concatenate | bytes 6365184
  1601.7 6.3 convert_element_type.116
  1632.9 13.6 collective-permute-start.5
  1646.5 13.8 collective-permute-start.7
  1660.3 12.6 collective-permute-start.6
  1679.1 6.8 collective-permute-done.6
  (318 shorter events, 193.8 us)
Async XLA Ops:
  7.2 91.6 %all-gather.11.cloned.1.call-start = ((), (), s32[]{:S(2)}) async-start(), calls=%async_computation.6 | async-start | bytes 1769472 | tf_op jit(solution)/shard_map/all_gather | solution.py:87
  9.3 116.2 %all-gather.9.cloned.1.call-start = ((), (), s32[]{:S(2)}) async-start(), calls=%async_computation.5 | async-start | bytes 1769472 | tf_op jit(solution)/shard_map/all_gather | solution.py:86
  10.1 209.8 %all-gather.7.cloned.1.call-start = ((), (), s32[]{:S(2)}) async-start(), calls=%async_computation.2 | async-start | bytes 4866048 | tf_op jit(solution)/shard_map/all_gather | solution.py:76
  10.8 1676.8 %reduce-scatter.5.cloned.1.call-start = ((), (), s32[]{:S(2)}) async-start(), calls=%async_computation.3 | async-start | bytes 1769472 | tf_op jit(solution)/shard_map/reduce_scatter | solution.py:103
  10.9 74.1 %collective-permute-start.2 = (bf16[2,16,8,768]{3,2,1,0:T(8,128)(2,1)S(1)}, bf16[2,16,8,768]{3,2,1,0:T(8,128)(2,1)S(1)}, u32[]{:S(2)}, u32[]{:S(2)}) collective-permute-start(bf16[2,16,8,768]{3,2,1,0:T(8,128)(2,1)S(1)} %pad_maximum_fusion.1), channel_id=1, source_target_pairs={{0,2},{1,3},{2,4},{3,5},{4,6},{5,7},{6,8},{7,9},{8,10},{9,11},{10,... | collective-permute-start | bytes 1179656 | tf_op jit(solution)/shard_map/ppermute | solution.py:17
  26.0 59.0 %collective-permute-start.1 = (bf16[2,16,8,768]{3,2,1,0:T(8,128)(2,1)S(1)}, bf16[2,16,8,768]{3,2,1,0:T(8,128)(2,1)S(1)}, u32[]{:S(2)}, u32[]{:S(2)}) collective-permute-start(bf16[2,16,8,768]{3,2,1,0:T(8,128)(2,1)S(1)} %pad_maximum_fusion.1), channel_id=1, source_target_pairs={{0,3},{1,4},{2,5},{3,6},{4,7},{5,8},{6,9},{7,10},{8,11},{9,12},{10... | collective-permute-start | bytes 1179656 | tf_op jit(solution)/shard_map/ppermute | solution.py:17
  39.1 45.9 %collective-permute-start.3 = (bf16[2,16,8,768]{3,2,1,0:T(8,128)(2,1)S(1)}, bf16[2,16,8,768]{3,2,1,0:T(8,128)(2,1)S(1)}, u32[]{:S(2)}, u32[]{:S(2)}) collective-permute-start(bf16[2,16,8,768]{3,2,1,0:T(8,128)(2,1)S(1)} %pad_maximum_fusion.1), channel_id=1, source_target_pairs={{0,1},{1,2},{2,3},{3,4},{4,5},{5,6},{6,7},{7,8},{8,9},{9,10},{10,1... | collective-permute-start | bytes 1179656 | tf_op jit(solution)/shard_map/ppermute | solution.py:17
  249.7 1439.6 %reduce-scatter.7.cloned.1.call-start = ((), (), s32[]{:S(2)}) async-start(), calls=%async_computation.4 | async-start | bytes 1769472 | tf_op jit(solution)/shard_map/reduce_scatter | solution.py:111
  997.0 36.6 %collective-permute-start.59 = (f32[8,1536]{1,0:T(8,128)S(1)}, f32[8,1536]{1,0:T(8,128)S(1)}, u32[]{:S(2)}, u32[]{:S(2)}) collective-permute-start(f32[8,1536]{1,0:T(8,128)S(1)} %fusion), channel_id=1, source_target_pairs={{0,52},{1,53},{2,54},{3,55},{4,56},{5,57},{6,58},{7,59},{8,60},{9,... | collective-permute-start | bytes 147464
  998.3 36.9 %collective-permute-start.58 = (f32[8,1536]{1,0:T(8,128)S(1)}, f32[8,1536]{1,0:T(8,128)S(1)}, u32[]{:S(2)}, u32[]{:S(2)}) collective-permute-start(f32[8,1536]{1,0:T(8,128)S(1)} %fusion), channel_id=1, source_target_pairs={{0,51},{1,52},{2,53},{3,54},{4,55},{5,56},{6,57},{7,58},{8,59},{9,... | collective-permute-start | bytes 147464
  999.6 37.3 %collective-permute-start.57 = (f32[8,1536]{1,0:T(8,128)S(1)}, f32[8,1536]{1,0:T(8,128)S(1)}, u32[]{:S(2)}, u32[]{:S(2)}) collective-permute-start(f32[8,1536]{1,0:T(8,128)S(1)} %fusion), channel_id=1, source_target_pairs={{0,50},{1,51},{2,52},{3,53},{4,54},{5,55},{6,56},{7,57},{8,58},{9,... | collective-permute-start | bytes 147464
  1000.9 39.2 %collective-permute-start.56 = (f32[8,1536]{1,0:T(8,128)S(1)}, f32[8,1536]{1,0:T(8,128)S(1)}, u32[]{:S(2)}, u32[]{:S(2)}) collective-permute-start(f32[8,1536]{1,0:T(8,128)S(1)} %fusion), channel_id=1, source_target_pairs={{0,49},{1,50},{2,51},{3,52},{4,53},{5,54},{6,55},{7,56},{8,57},{9,... | collective-permute-start | bytes 147464
  1002.3 40.2 %collective-permute-start.55 = (f32[8,1536]{1,0:T(8,128)S(1)}, f32[8,1536]{1,0:T(8,128)S(1)}, u32[]{:S(2)}, u32[]{:S(2)}) collective-permute-start(f32[8,1536]{1,0:T(8,128)S(1)} %fusion), channel_id=1, source_target_pairs={{0,48},{1,49},{2,50},{3,51},{4,52},{5,53},{6,54},{7,55},{8,56},{9,... | collective-permute-start | bytes 147464
  1077.5 36.9 %collective-permute-start.40 = (f32[8,1536]{1,0:T(8,128)S(1)}, f32[8,1536]{1,0:T(8,128)S(1)}, u32[]{:S(2)}, u32[]{:S(2)}) collective-permute-start(f32[8,1536]{1,0:T(8,128)S(1)} %fusion), channel_id=1, source_target_pairs={{0,33},{1,34},{2,35},{3,36},{4,37},{5,38},{6,39},{7,40},{8,41},{9,... | collective-permute-start | bytes 147464
  1082.6 45.0 %collective-permute-start.39 = (f32[8,1536]{1,0:T(8,128)S(1)}, f32[8,1536]{1,0:T(8,128)S(1)}, u32[]{:S(2)}, u32[]{:S(2)}) collective-permute-start(f32[8,1536]{1,0:T(8,128)S(1)} %fusion), channel_id=1, source_target_pairs={{0,32},{1,33},{2,34},{3,35},{4,36},{5,37},{6,38},{7,39},{8,40},{9,... | collective-permute-start | bytes 147464
  1083.9 56.8 %collective-permute-start.38 = (f32[8,1536]{1,0:T(8,128)S(1)}, f32[8,1536]{1,0:T(8,128)S(1)}, u32[]{:S(2)}, u32[]{:S(2)}) collective-permute-start(f32[8,1536]{1,0:T(8,128)S(1)} %fusion), channel_id=1, source_target_pairs={{0,31},{1,32},{2,33},{3,34},{4,35},{5,36},{6,37},{7,38},{8,39},{9,... | collective-permute-start | bytes 147464
  1088.1 65.7 %collective-permute-start.37 = (f32[8,1536]{1,0:T(8,128)S(1)}, f32[8,1536]{1,0:T(8,128)S(1)}, u32[]{:S(2)}, u32[]{:S(2)}) collective-permute-start(f32[8,1536]{1,0:T(8,128)S(1)} %fusion), channel_id=1, source_target_pairs={{0,30},{1,31},{2,32},{3,33},{4,34},{5,35},{6,36},{7,37},{8,38},{9,... | collective-permute-start | bytes 147464
  1101.3 65.7 %collective-permute-start.36 = (f32[8,1536]{1,0:T(8,128)S(1)}, f32[8,1536]{1,0:T(8,128)S(1)}, u32[]{:S(2)}, u32[]{:S(2)}) collective-permute-start(f32[8,1536]{1,0:T(8,128)S(1)} %fusion), channel_id=1, source_target_pairs={{0,29},{1,30},{2,31},{3,32},{4,33},{5,34},{6,35},{7,36},{8,37},{9,... | collective-permute-start | bytes 147464
  1114.4 65.7 %collective-permute-start.35 = (f32[8,1536]{1,0:T(8,128)S(1)}, f32[8,1536]{1,0:T(8,128)S(1)}, u32[]{:S(2)}, u32[]{:S(2)}) collective-permute-start(f32[8,1536]{1,0:T(8,128)S(1)} %fusion), channel_id=1, source_target_pairs={{0,28},{1,29},{2,30},{3,31},{4,32},{5,33},{6,34},{7,35},{8,36},{9,... | collective-permute-start | bytes 147464
  1127.6 66.3 %collective-permute-start.34 = (f32[8,1536]{1,0:T(8,128)S(1)}, f32[8,1536]{1,0:T(8,128)S(1)}, u32[]{:S(2)}, u32[]{:S(2)}) collective-permute-start(f32[8,1536]{1,0:T(8,128)S(1)} %fusion), channel_id=1, source_target_pairs={{0,27},{1,28},{2,29},{3,30},{4,31},{5,32},{6,33},{7,34},{8,35},{9,... | collective-permute-start | bytes 147464
  1140.7 66.3 %collective-permute-start.33 = (f32[8,1536]{1,0:T(8,128)S(1)}, f32[8,1536]{1,0:T(8,128)S(1)}, u32[]{:S(2)}, u32[]{:S(2)}) collective-permute-start(f32[8,1536]{1,0:T(8,128)S(1)} %fusion), channel_id=1, source_target_pairs={{0,26},{1,27},{2,28},{3,29},{4,30},{5,31},{6,32},{7,33},{8,34},{9,... | collective-permute-start | bytes 147464
  1153.9 66.3 %collective-permute-start.32 = (f32[8,1536]{1,0:T(8,128)S(1)}, f32[8,1536]{1,0:T(8,128)S(1)}, u32[]{:S(2)}, u32[]{:S(2)}) collective-permute-start(f32[8,1536]{1,0:T(8,128)S(1)} %fusion), channel_id=1, source_target_pairs={{0,25},{1,26},{2,27},{3,28},{4,29},{5,30},{6,31},{7,32},{8,33},{9,... | collective-permute-start | bytes 147464
  1167.0 66.3 %collective-permute-start.31 = (f32[8,1536]{1,0:T(8,128)S(1)}, f32[8,1536]{1,0:T(8,128)S(1)}, u32[]{:S(2)}, u32[]{:S(2)}) collective-permute-start(f32[8,1536]{1,0:T(8,128)S(1)} %fusion), channel_id=1, source_target_pairs={{0,24},{1,25},{2,26},{3,27},{4,28},{5,29},{6,30},{7,31},{8,32},{9,... | collective-permute-start | bytes 147464
  1180.2 66.3 %collective-permute-start.30 = (f32[8,1536]{1,0:T(8,128)S(1)}, f32[8,1536]{1,0:T(8,128)}, u32[]{:S(2)}, u32[]{:S(2)}) collective-permute-start(f32[8,1536]{1,0:T(8,128)S(1)} %fusion), channel_id=1, source_target_pairs={{0,23},{1,24},{2,25},{3,26},{4,27},{5,28},{6,29},{7,30},{8,31},{9,... | collective-permute-start | bytes 147464
  1193.9 65.7 %collective-permute-start.29 = (f32[8,1536]{1,0:T(8,128)S(1)}, f32[8,1536]{1,0:T(8,128)}, u32[]{:S(2)}, u32[]{:S(2)}) collective-permute-start(f32[8,1536]{1,0:T(8,128)S(1)} %fusion), channel_id=1, source_target_pairs={{0,22},{1,23},{2,24},{3,25},{4,26},{5,27},{6,28},{7,29},{8,30},{9,... | collective-permute-start | bytes 147464
  1207.1 65.7 %collective-permute-start.28 = (f32[8,1536]{1,0:T(8,128)S(1)}, f32[8,1536]{1,0:T(8,128)}, u32[]{:S(2)}, u32[]{:S(2)}) collective-permute-start(f32[8,1536]{1,0:T(8,128)S(1)} %fusion), channel_id=1, source_target_pairs={{0,21},{1,22},{2,23},{3,24},{4,25},{5,26},{6,27},{7,28},{8,29},{9,... | collective-permute-start | bytes 147464
  1220.2 65.7 %collective-permute-start.27 = (f32[8,1536]{1,0:T(8,128)S(1)}, f32[8,1536]{1,0:T(8,128)}, u32[]{:S(2)}, u32[]{:S(2)}) collective-permute-start(f32[8,1536]{1,0:T(8,128)S(1)} %fusion), channel_id=1, source_target_pairs={{0,20},{1,21},{2,22},{3,23},{4,24},{5,25},{6,26},{7,27},{8,28},{9,... | collective-permute-start | bytes 147464
  1233.4 65.7 %collective-permute-start.26 = (f32[8,1536]{1,0:T(8,128)S(1)}, f32[8,1536]{1,0:T(8,128)}, u32[]{:S(2)}, u32[]{:S(2)}) collective-permute-start(f32[8,1536]{1,0:T(8,128)S(1)} %fusion), channel_id=1, source_target_pairs={{0,19},{1,20},{2,21},{3,22},{4,23},{5,24},{6,25},{7,26},{8,27},{9,... | collective-permute-start | bytes 147464
  1246.5 65.7 %collective-permute-start.25 = (f32[8,1536]{1,0:T(8,128)S(1)}, f32[8,1536]{1,0:T(8,128)}, u32[]{:S(2)}, u32[]{:S(2)}) collective-permute-start(f32[8,1536]{1,0:T(8,128)S(1)} %fusion), channel_id=1, source_target_pairs={{0,18},{1,19},{2,20},{3,21},{4,22},{5,23},{6,24},{7,25},{8,26},{9,... | collective-permute-start | bytes 147464
  1259.7 65.7 %collective-permute-start.24 = (f32[8,1536]{1,0:T(8,128)S(1)}, f32[8,1536]{1,0:T(8,128)}, u32[]{:S(2)}, u32[]{:S(2)}) collective-permute-start(f32[8,1536]{1,0:T(8,128)S(1)} %fusion), channel_id=1, source_target_pairs={{0,17},{1,18},{2,19},{3,20},{4,21},{5,22},{6,23},{7,24},{8,25},{9,... | collective-permute-start | bytes 147464
  1272.8 65.7 %collective-permute-start.23 = (f32[8,1536]{1,0:T(8,128)S(1)}, f32[8,1536]{1,0:T(8,128)}, u32[]{:S(2)}, u32[]{:S(2)}) collective-permute-start(f32[8,1536]{1,0:T(8,128)S(1)} %fusion), channel_id=1, source_target_pairs={{0,16},{1,17},{2,18},{3,19},{4,20},{5,21},{6,22},{7,23},{8,24},{9,... | collective-permute-start | bytes 147464
  1286.0 65.7 %collective-permute-start.22 = (f32[8,1536]{1,0:T(8,128)S(1)}, f32[8,1536]{1,0:T(8,128)}, u32[]{:S(2)}, u32[]{:S(2)}) collective-permute-start(f32[8,1536]{1,0:T(8,128)S(1)} %fusion), channel_id=1, source_target_pairs={{0,15},{1,16},{2,17},{3,18},{4,19},{5,20},{6,21},{7,22},{8,23},{9,... | collective-permute-start | bytes 147464
  1299.1 65.7 %collective-permute-start.21 = (f32[8,1536]{1,0:T(8,128)S(1)}, f32[8,1536]{1,0:T(8,128)}, u32[]{:S(2)}, u32[]{:S(2)}) collective-permute-start(f32[8,1536]{1,0:T(8,128)S(1)} %fusion), channel_id=1, source_target_pairs={{0,14},{1,15},{2,16},{3,17},{4,18},{5,19},{6,20},{7,21},{8,22},{9,... | collective-permute-start | bytes 147464
  1312.2 65.7 %collective-permute-start.20 = (f32[8,1536]{1,0:T(8,128)S(1)}, f32[8,1536]{1,0:T(8,128)}, u32[]{:S(2)}, u32[]{:S(2)}) collective-permute-start(f32[8,1536]{1,0:T(8,128)S(1)} %fusion), channel_id=1, source_target_pairs={{0,13},{1,14},{2,15},{3,16},{4,17},{5,18},{6,19},{7,20},{8,21},{9,... | collective-permute-start | bytes 147464
  1325.4 65.7 %collective-permute-start.19 = (f32[8,1536]{1,0:T(8,128)S(1)}, f32[8,1536]{1,0:T(8,128)}, u32[]{:S(2)}, u32[]{:S(2)}) collective-permute-start(f32[8,1536]{1,0:T(8,128)S(1)} %fusion), channel_id=1, source_target_pairs={{0,12},{1,13},{2,14},{3,15},{4,16},{5,17},{6,18},{7,19},{8,20},{9,... | collective-permute-start | bytes 147464
  1338.5 65.7 %collective-permute-start.18 = (f32[8,1536]{1,0:T(8,128)S(1)}, f32[8,1536]{1,0:T(8,128)}, u32[]{:S(2)}, u32[]{:S(2)}) collective-permute-start(f32[8,1536]{1,0:T(8,128)S(1)} %fusion), channel_id=1, source_target_pairs={{0,11},{1,12},{2,13},{3,14},{4,15},{5,16},{6,17},{7,18},{8,19},{9,... | collective-permute-start | bytes 147464
  1351.7 65.7 %collective-permute-start.17 = (f32[8,1536]{1,0:T(8,128)S(1)}, f32[8,1536]{1,0:T(8,128)}, u32[]{:S(2)}, u32[]{:S(2)}) collective-permute-start(f32[8,1536]{1,0:T(8,128)S(1)} %fusion), channel_id=1, source_target_pairs={{0,10},{1,11},{2,12},{3,13},{4,14},{5,15},{6,16},{7,17},{8,18},{9,... | collective-permute-start | bytes 147464
  1364.8 65.7 %collective-permute-start.16 = (f32[8,1536]{1,0:T(8,128)S(1)}, f32[8,1536]{1,0:T(8,128)}, u32[]{:S(2)}, u32[]{:S(2)}) collective-permute-start(f32[8,1536]{1,0:T(8,128)S(1)} %fusion), channel_id=1, source_target_pairs={{0,9},{1,10},{2,11},{3,12},{4,13},{5,14},{6,15},{7,16},{8,17},{9,1... | collective-permute-start | bytes 147464
  1377.9 65.7 %collective-permute-start.15 = (f32[8,1536]{1,0:T(8,128)S(1)}, f32[8,1536]{1,0:T(8,128)}, u32[]{:S(2)}, u32[]{:S(2)}) collective-permute-start(f32[8,1536]{1,0:T(8,128)S(1)} %fusion), channel_id=1, source_target_pairs={{0,8},{1,9},{2,10},{3,11},{4,12},{5,13},{6,14},{7,15},{8,16},{9,17... | collective-permute-start | bytes 147464
  1391.1 65.7 %collective-permute-start.14 = (f32[8,1536]{1,0:T(8,128)S(1)}, f32[8,1536]{1,0:T(8,128)}, u32[]{:S(2)}, u32[]{:S(2)}) collective-permute-start(f32[8,1536]{1,0:T(8,128)S(1)} %fusion), channel_id=1, source_target_pairs={{0,7},{1,8},{2,9},{3,10},{4,11},{5,12},{6,13},{7,14},{8,15},{9,16}... | collective-permute-start | bytes 147464
  1404.2 65.7 %collective-permute-start.13 = (f32[8,1536]{1,0:T(8,128)S(1)}, f32[8,1536]{1,0:T(8,128)}, u32[]{:S(2)}, u32[]{:S(2)}) collective-permute-start(f32[8,1536]{1,0:T(8,128)S(1)} %fusion), channel_id=1, source_target_pairs={{0,6},{1,7},{2,8},{3,9},{4,10},{5,11},{6,12},{7,13},{8,14},{9,15},... | collective-permute-start | bytes 147464
  1417.4 72.7 %collective-permute-start.12 = (f32[8,1536]{1,0:T(8,128)S(1)}, f32[8,1536]{1,0:T(8,128)}, u32[]{:S(2)}, u32[]{:S(2)}) collective-permute-start(f32[8,1536]{1,0:T(8,128)S(1)} %fusion), channel_id=1, source_target_pairs={{0,5},{1,6},{2,7},{3,8},{4,9},{5,10},{6,11},{7,12},{8,13},{9,14},{... | collective-permute-start | bytes 147464
  1430.5 59.5 %collective-permute-start.11 = (f32[8,1536]{1,0:T(8,128)S(1)}, f32[8,1536]{1,0:T(8,128)}, u32[]{:S(2)}, u32[]{:S(2)}) collective-permute-start(f32[8,1536]{1,0:T(8,128)S(1)} %fusion), channel_id=1, source_target_pairs={{0,4},{1,5},{2,6},{3,7},{4,8},{5,9},{6,10},{7,11},{8,12},{9,13},{1... | collective-permute-start | bytes 147464
  1443.7 46.4 %collective-permute-start.10 = (f32[8,1536]{1,0:T(8,128)S(1)}, f32[8,1536]{1,0:T(8,128)}, u32[]{:S(2)}, u32[]{:S(2)}) collective-permute-start(f32[8,1536]{1,0:T(8,128)S(1)} %fusion), channel_id=1, source_target_pairs={{0,3},{1,4},{2,5},{3,6},{4,7},{5,8},{6,9},{7,10},{8,11},{9,12},{10... | collective-permute-start | bytes 147464
  1456.8 33.2 %collective-permute-start.9 = (f32[8,1536]{1,0:T(8,128)S(1)}, f32[8,1536]{1,0:T(8,128)}, u32[]{:S(2)}, u32[]{:S(2)}) collective-permute-start(f32[8,1536]{1,0:T(8,128)S(1)} %fusion), channel_id=1, source_target_pairs={{0,2},{1,3},{2,4},{3,5},{4,6},{5,7},{6,8},{7,9},{8,10},{9,11},{10,... | collective-permute-start | bytes 147464
  1630.4 48.7 %collective-permute-start.4 = (bf16[2,15,8,768]{3,2,1,0:T(8,128)(2,1)}, bf16[2,15,8,768]{3,2,1,0:T(8,128)(2,1)}, u32[]{:S(2)}, u32[]{:S(2)}) collective-permute-start(bf16[2,15,8,768]{3,2,1,0:T(8,128)(2,1)} %slice.92), channel_id=1, source_target_pairs={{4,0},{5,1},{6,2},{7,3},{8,4},{9,5},{10,6},{11,7},{12,8},{13,9},{1... | collective-permute-start | bytes 1105928 | tf_op jit(solution)/shard_map/ppermute | solution.py:17
  1632.9 46.2 %collective-permute-start.5 = (bf16[2,16,8,768]{3,2,1,0:T(8,128)(2,1)}, bf16[2,16,8,768]{3,2,1,0:T(8,128)(2,1)}, u32[]{:S(2)}, u32[]{:S(2)}) collective-permute-start(bf16[2,16,8,768]{3,2,1,0:T(8,128)(2,1)} %get-tuple-element.5), channel_id=1, source_target_pairs={{3,0},{4,1},{5,2},{6,3},{7,4},{8,5},{9,6},{10,7},{11,8},{12,9},{13... | collective-permute-start | bytes 1179656 | tf_op jit(solution)/shard_map/ppermute | solution.py:17
  1646.5 32.6 %collective-permute-start.7 = (bf16[2,16,8,768]{3,2,1,0:T(8,128)(2,1)}, bf16[2,16,8,768]{3,2,1,0:T(8,128)(2,1)}, u32[]{:S(2)}, u32[]{:S(2)}) collective-permute-start(bf16[2,16,8,768]{3,2,1,0:T(8,128)(2,1)} %get-tuple-element.6), channel_id=1, source_target_pairs={{1,0},{2,1},{3,2},{4,3},{5,4},{6,5},{7,6},{8,7},{9,8},{10,9},{11,1... | collective-permute-start | bytes 1179656 | tf_op jit(solution)/shard_map/ppermute | solution.py:17
  (93 other events, 17758.8 us)
Sparse Core Ops, SparseCore 0:
  10.4 60.6 all-gather.10
  73.4 52.0 all-gather.8
  128.3 91.4 all-gather.6
  249.8 44.2 reduce-scatter.4
  1611.8 50.0 reduce-scatter.6
where the time goes:
time: 1710 us; the launch traced here: 1700 us
  blocking collectives  754 us (44%)
  starting transfers between devices  587 us (34%)
  local copies, waits for them, and re-layouts  171 us (10%)
  waiting for transfers between devices  98 us (6%)
  matrix products  54.8 us (3%)
    unnamed x1, blocking collectives  731 us
    unnamed x64, starting transfers between devices  500 us
    unnamed x135, local copies, waits for them, and re-layouts  107 us
    ppermute x8, starting transfers between devices, from_behind(): lax.ppermute(value, axis, [(source, source + steps) for source in range(f...  86.8 us
    all_gather x1, waiting for transfers between devices, shards(): w_full = lax.all_gather(w_out, 'tm', axis=0, tiled=True)  68.7 us
  transfers between devices with their start and end apart: 77, of which 3 were waited for; matrix products, arithmetic and copies ran while one was open for 55% of the time, Pallas kernels for 0%

commit v1 on v0

v1 whole, which is shorter than its diff:
```python
import math

import jax
import jax.numpy as jnp
from jax import lax
from jax.experimental import pallas as pl
from jax.experimental.pallas import tpu as pltpu
from jax.sharding import PartitionSpec as P

HC = 12
HT = 12
HD = 64
WIN = 64
CW = HC * HD
GROUP = 4
SCALE = HD ** (-0.5)
BF = jnp.bfloat16
F32 = jnp.float32
PAIRS = HC // 2
VM = pl.BlockSpec(memory_space=pltpu.VMEM)
SM = pl.BlockSpec(memory_space=pltpu.SMEM)


def params():
    return pltpu.CompilerParams(vmem_limit_bytes=48 * 1024 * 1024)


def iota(shape, dim):
    return lax.broadcasted_iota(jnp.int32, shape, dim)


def dot_nt(a, b):
    return lax.dot_general(a, b, (((1,), (1,)), ((), ())), preferred_element_type=F32)


def dot_tn(a, b):
    return lax.dot_general(a, b, (((0,), (0,)), ((), ())), preferred_element_type=F32)


def dot_nn(a, b):
    return jnp.dot(a, b, preferred_element_type=F32)


def split_pair(rows):
    low = iota(rows.shape, 1) < HD
    zero = jnp.zeros_like(rows)
    return jnp.concatenate([jnp.where(low, rows, zero), jnp.where(low, zero, rows)], axis=0)


def join_pair(rows):
    count = rows.shape[0] // 2
    low = iota((count, rows.shape[1]), 1) < HD
    return jnp.where(low, rows[:count], rows[count:])


def softmax_pair(q, k, mask):
    scores = dot_nt(split_pair(q), k) * SCALE
    scores = jnp.where(mask, scores, -jnp.inf)
    largest = jnp.max(scores, axis=1, keepdims=True)
    e = jnp.exp(scores - largest)
    return e / jnp.sum(e, axis=1, keepdims=True)


def pack_kernel(valid, q, k, v, ct, view_ref, time_ref):
    rows = q.shape[0]
    per_cam = rows // 16
    row = iota((rows, rows), 0)
    col = iota((rows, rows), 1)
    frames = rows // 8
    source = ((row // 2) % frames) * 8 + 2 * (row // (2 * frames)) + row % 2
    perm = jnp.where(col == source, 1.0, 0.0).astype(BF)
    for i, ref in enumerate((q, k, v)):
        view_ref[:, i * CW : (i + 1) * CW] = ref[:, :CW]
        time_ref[:, i * CW : (i + 1) * CW] = dot_nn(perm, ref[:, CW:]).astype(BF)
    view_ref[:, 3 * CW : 5 * CW] = ct[...]
    time_ref[:, 3 * CW : 5 * CW] = dot_nn(perm, ct[...]).astype(BF)
    frame = iota((rows, 128), 0) // 8
    flags = jnp.zeros((rows, 128), F32)
    for f in range(frames):
        flags = jnp.where(frame == f, valid[0, f].astype(F32), flags)
    view_ref[:, 5 * CW :] = jnp.where(flags > 0.5, 1.0, 0.0).astype(BF)


def view_mask(flags):
    rows = flags.shape[0]
    pick = jnp.where(iota((8, 128), 1) == 0, 1.0, 0.0).astype(BF)
    valid_row = dot_nt(pick, flags)[:1]
    r = iota((2 * rows, rows), 0) % rows
    c = iota((2 * rows, rows), 1)
    same_frame = ((r // 8) % 2) == ((c // 8) % 2)
    return same_frame & ((valid_row > 0.5) | (r // 16 == c // 16))


def view_forward_kernel(x, attn_ref, prob_ref):
    mask = view_mask(x[:, 5 * CW :])
    for j in range(PAIRS):
        lanes = slice(128 * j, 128 * (j + 1))
        q = x[:, 128 * j : 128 * (j + 1)]
        k = x[:, CW + 128 * j : CW + 128 * (j + 1)]
        v = x[:, 2 * CW + 128 * j : 2 * CW + 128 * (j + 1)]
        prob = softmax_pair(q, k, mask)
        prob_ref[j] = prob
        attn_ref[:, lanes] = join_pair(dot_nn(prob.astype(BF), v)).astype(BF)


def time_forward_kernel(windows, block, x, prev, attn_ref, prob_ref):
    rows = x.shape[0]
    r = iota((2 * rows, 2 * rows), 0)
    c = iota((2 * rows, 2 * rows), 1)
    second = r >= rows
    r = r % rows
    key_frame = c // 2 - rows // 2
    gap = r // 2 - key_frame
    base = (r % 2 == c % 2) & (gap >= 0) & ((key_frame >= 0) | (block[0] > 0))
    for j in range(PAIRS):
        lanes = slice(128 * j, 128 * (j + 1))
        q = x[:, 128 * j : 128 * (j + 1)]
        k = jnp.concatenate([prev[:, lanes], x[:, CW + 128 * j : CW + 128 * (j + 1)]], axis=0)
        v = jnp.concatenate(
            [prev[:, CW + 128 * j : CW + 128 * (j + 1)], x[:, 2 * CW + 128 * j : 2 * CW + 128 * (j + 1)]],
            axis=0,
        )
        limit = jnp.where(second, windows[2 * j + 1], windows[2 * j])
        prob = softmax_pair(q, k, base & (gap < limit))
        prob_ref[j] = prob
        attn_ref[:, lanes] = join_pair(dot_nn(prob.astype(BF), v)).astype(BF)


def backward_pair(q, k, v, g, prob):
    g2 = split_pair(g)
    grad_prob = dot_nt(g2, v)
    total = jnp.sum(prob * grad_prob, axis=1, keepdims=True)
    grad_scores = (prob * (grad_prob - total)).astype(BF)
    dq = join_pair(dot_nn(grad_scores, k)) * SCALE
    dk = dot_tn(grad_scores, split_pair(q)) * SCALE
    dv = dot_tn(prob.astype(BF), g2)
    return dq, dk, dv


def view_backward_kernel(x, attn, prob_ref, w, out_ref):
    grad = dot_nt(x[:, 3 * CW : 5 * CW], w[...]).astype(BF)
    out_ref[:, :CW] = attn[...]
    for j in range(PAIRS):
        at = [slice(i * CW + 128 * j, i * CW + 128 * (j + 1)) for i in range(4)]
        dq, dk, dv = backward_pair(x[:, at[0]], x[:, at[1]], x[:, at[2]], grad[:, at[0]], prob_ref[j])
        out_ref[:, at[1]] = dq.astype(BF)
        out_ref[:, at[2]] = dk.astype(BF)
        out_ref[:, at[3]] = dv.astype(BF)


def time_backward_kernel(x, prev, prob_ref, w, dq_ref, own_ref, back_ref):
    rows = x.shape[0]
    grad = dot_nt(x[:, 3 * CW : 5 * CW], w[...]).astype(BF)
    for j in range(PAIRS):
        at = [slice(i * CW + 128 * j, i * CW + 128 * (j + 1)) for i in range(3)]
        k = jnp.concatenate([prev[:, at[0]], x[:, at[1]]], axis=0)
        v = jnp.concatenate([prev[:, at[1]], x[:, at[2]]], axis=0)
        dq, dk, dv = backward_pair(x[:, at[0]], k, v, grad[:, at[0]], prob_ref[j])
        dq_ref[:, at[0]] = dq.astype(BF)
        back_ref[:, at[0]] = dk[:rows].astype(BF)
        own_ref[:, at[0]] = dk[rows:]
        back_ref[:, at[1]] = dv[:rows].astype(BF)
        own_ref[:, at[1]] = dv[rows:]


def time_sum_kernel(attn, dq, own, back, out_ref):
    out_ref[:, :CW] = attn[...]
    out_ref[:, CW : 2 * CW] = dq[...]
    out_ref[:, 2 * CW :] = (own[...] + back[...].astype(F32)).astype(BF)


def finish_kernel(view, time, w, action, pred_ref, dq_ref, dk_ref, dv_ref):
    rows = view.shape[0]
    row = iota((rows, rows), 0)
    col = iota((rows, rows), 1)
    frames = rows // 8
    source = ((row // 2) % GROUP) * 2 * frames + (row // 8) * 2 + row % 2
    perm = jnp.where(col == source, 1.0, 0.0).astype(BF)
    for i, ref in enumerate((dq_ref, dk_ref, dv_ref), 1):
        part = slice(i * CW, (i + 1) * CW)
        ref[:, :CW] = view[:, part]
        ref[:, CW:] = dot_nn(perm, time[:, part]).astype(BF)
    attn_time = dot_nn(perm, time[:, :CW]).astype(BF)
    mixed = dot_nn(view[:, :CW], w[:CW]) + dot_nn(attn_time, w[CW:])
    total = mixed.reshape(frames, 8, 2 * CW) + action[...][:, None, :]
    pred_ref[...] = total.reshape(rows, 2 * CW).astype(BF)


def call(kernel, outs, specs, *args):
    return pl.pallas_call(
        kernel,
        out_shape=[jax.ShapeDtypeStruct(shape, kind) for shape, kind in outs],
        in_specs=specs,
        out_specs=[VM] * len(outs),
        compiler_params=params(),
    )(*args)


def shards(queries, keys, values, cam_valid, windows, actions, act_table, w_out, cotangent):
    _, frames, tokens, width = queries.shape
    rows = frames * tokens
    cams = lax.axis_size("cam")
    tm = lax.axis_size("tm")
    at_tm = lax.axis_index("tm")
    core = at_tm % 2
    fours = [[GROUP * i + j for j in range(GROUP)] for i in range(tm // GROUP)]
    same_core = [[2 * i + j for i in range(tm // 2)] for j in range(2)]
    swap = [(i, i ^ 1) for i in range(tm)]

    w_full = lax.all_gather(w_out, "tm", axis=0, tiled=True)
    q, k, v, ct = (a.reshape(rows, width) for a in (queries, keys, values, cotangent))
    view_send, time_send = call(
        pack_kernel,
        [((rows, 5 * CW + 128), BF), ((rows, 5 * CW), BF)],
        [SM] + [VM] * 4,
        cam_valid, q, k, v, ct,
    )
    view_x = lax.all_to_all(view_send, "cam", 0, 0, tiled=True)
    time_x = lax.all_to_all(time_send, "tm", 0, 0, tiled=True, axis_index_groups=fours)
    prev = lax.ppermute(
        time_x[:, CW : 3 * CW], "tm", [(i, i + GROUP) for i in range(tm - GROUP)]
    )

    attn_view, prob_view = call(
        view_forward_kernel, [((rows, CW), BF), ((PAIRS, 2 * rows, rows), F32)], [VM], view_x
    )
    attn_time, prob_time = call(
        time_forward_kernel,
        [((rows, CW), BF), ((PAIRS, 2 * rows, 2 * rows), F32)],
        [SM, SM, VM, VM],
        windows, (at_tm // GROUP).reshape(1), time_x, prev,
    )

    def half(which):
        return jnp.concatenate(
            [lax.dynamic_slice_in_dim(a[:, 3 * CW : 5 * CW], which * CW, CW, 1) for a in (view_x, time_x)],
            axis=1,
        )

    other_ct = lax.ppermute(half(1 - core), "tm", swap)
    own_ct = half(core)
    attn_both = jnp.concatenate([attn_view, attn_time], axis=1)
    other_attn = lax.ppermute(attn_both, "tm", swap)
    grad_norm = 1.0 / math.sqrt(cams * tm * rows)
    left = jnp.concatenate([attn_both, other_attn], axis=0)
    right = jnp.concatenate([own_ct, other_ct], axis=0)
    part = jnp.concatenate(
        [dot_tn(left[:, :CW], right[:, :CW]), dot_tn(left[:, CW:], right[:, CW:])], axis=0
    )
    part = (part * grad_norm).astype(BF)
    part = lax.all_to_all(part.reshape(cams, width // cams, CW), "cam", 0, 0, tiled=True)
    part = jnp.sum(part.astype(F32), axis=0).astype(BF)
    chips = tm // 2
    part = lax.all_to_all(
        part.reshape(chips, width // cams // chips, CW), "tm", 0, 0, tiled=True, axis_index_groups=same_core
    )
    part = jnp.sum(part.astype(F32), axis=0)
    final = width // cams // tm
    mine = lax.dynamic_slice_in_dim(part, core * final, final, 0)
    theirs = lax.ppermute(lax.dynamic_slice_in_dim(part, (1 - core) * final, final, 0), "tm", swap)
    grad_out_weight = jnp.concatenate(
        [jnp.where(core == 0, mine, theirs), jnp.where(core == 0, theirs, mine)], axis=1
    )

    codes = jnp.arange(act_table.shape[1])
    one_hot = (actions[:, :, None] == codes[None, None, :]).astype(BF).reshape(frames, -1)
    action_sum = jnp.dot(one_hot, act_table.reshape(-1, width), preferred_element_type=F32)

    (view_back,) = call(
        view_backward_kernel, [((rows, 4 * CW), BF)], [VM] * 4, view_x, attn_view, prob_view, w_full[:CW]
    )
    dq_time, own, back = call(
        time_backward_kernel,
        [((rows, CW), BF), ((rows, 2 * CW), F32), ((rows, 2 * CW), BF)],
        [VM] * 4,
        time_x, prev, prob_time, w_full[CW:],
    )
    returned = lax.ppermute(back, "tm", [(i + GROUP, i) for i in range(tm - GROUP)])
    view_back = lax.all_to_all(view_back, "cam", 0, 0, tiled=True)
    (time_back,) = call(time_sum_kernel, [((rows, 4 * CW), BF)], [VM] * 4, attn_time, dq_time, own, returned)
    time_back = lax.all_to_all(time_back, "tm", 0, 0, tiled=True, axis_index_groups=fours)
    outs = call(
        finish_kernel, [((rows, width), BF)] * 4, [VM] * 4, view_back, time_back, w_full, action_sum
    )
    return tuple(a.reshape(1, frames, tokens, width) for a in outs) + (grad_out_weight,)


def solution(mesh):
    in_specs = (
        P("cam", "tm", None, None),
        P("cam", "tm", None, None),
        P("cam", "tm", None, None),
        P("cam", "tm"),
        P(),
        P("tm", None),
        P(),
        P("tm", None),
        P("cam", "tm", None, None),
    )
    out_specs = (
        P("cam", "tm", None, None),
        P("cam", "tm", None, None),
        P("cam", "tm", None, None),
        P("cam", "tm", None, None),
        P(("cam", "tm"), None),
    )
    return jax.shard_map(shards, mesh=mesh, in_specs=in_specs, out_specs=out_specs, check_vma=False)
```

time: 1710 us -> 198 us (0.12)
  blocking collectives: 754 us -> 59.3 us
  starting transfers between devices: 587 us -> 29.6 us
  local copies, waits for them, and re-layouts: 171 us -> 16.6 us
  matrix products: 54.8 us -> 4.44 us
  waiting for transfers between devices: 98 us -> 48 us
  Pallas kernels: 0 us -> 18.5 us
    unnamed x1 -> x0, blocking collectives: 731 us -> none
    unnamed x64 -> x0, starting transfers between devices: 500 us -> none
    unnamed x135 -> x37, local copies, waits for them, and re-layouts: 107 us -> 9.32 us
    ppermute x8 -> x5, starting transfers between devices: 86.8 us -> 7.47 us  [the longest x1 3.68 us: shards(): lax.ppermute(time_x[:, CW:3 * CW], 'tm', [(i, i + GROUP) for i in range(t...]
    all_to_all x0 -> x2, blocking collectives: none -> 59.3 us  [the longest x1 37.5 us: shards(): lax.all_to_all(part.reshape(cams, width // cams, CW), 'cam', 0, 0, tiled=...]
    all_gather x1, waiting for transfers between devices: 68.7 us -> 20.4 us  [shards(): w_full = lax.all_gather(w_out, 'tm', axis=0, tiled=True)]
    dot_general x15 -> x3, matrix products: 50.2 us -> 4.44 us  [the longest x1 3.42 us: shards(): jnp.dot(one_hot, act_table.reshape(-1, width), preferred_element_type=F32)]
    convert_element_type x4 -> x0, local copies, waits for them, and re-layouts: 24.2 us -> none  [the longest x2 12.6 us: shards(): key_summed, value_summed = (lax.psum_scatter(key_terms.astype(jnp.float32...]
  transfers between devices with their start and end apart: 77 -> 10, of which waited for: 3 -> 5; matrix products, arithmetic and copies ran while one was open for 55% -> 9% of each run, Pallas kernels for 0% -> 7%
where the time goes in v1:
time: 198 us; the launch traced here: 197 us
  blocking collectives  59.3 us (30%)
  waiting for transfers between devices  48 us (24%)
  starting transfers between devices  29.6 us (15%)
  Pallas kernels  18.5 us (9%)
  local copies, waits for them, and re-layouts  16.6 us (8%)
  between operations  14.3 us (7%)
  other arithmetic  6.66 us (3%)
  matrix products  4.44 us (2%)
    all_to_all x1, blocking collectives, shards(): lax.all_to_all(part.reshape(cams, width // cams, CW), 'cam', 0, 0, tiled=...  37.5 us
    all_to_all x1, blocking collectives, shards(): lax.all_to_all(time_send, 'tm', 0, 0, tiled=True, axis_index_groups=fours)  21.9 us
    all_gather x1, waiting for transfers between devices, shards(): w_full = lax.all_gather(w_out, 'tm', axis=0, tiled=True)  20.4 us
    pallas_call x7, Pallas kernels, call(): pl.pallas_call(kernel, out_shape=[jax.ShapeDtypeStruct(shape, kind) for s...  18.5 us
    all_to_all x1, waiting for transfers between devices, shards(): view_x = lax.all_to_all(view_send, 'cam', 0, 0, tiled=True)  9.37 us
    unnamed x37, local copies, waits for them, and re-layouts  9.32 us
    ppermute x1, waiting for transfers between devices, shards(): lax.ppermute(back, 'tm', [(i + GROUP, i) for i in range(tm - GROUP)])  9.23 us
    all_to_all x1, starting transfers between devices, shards(): lax.all_to_all(part.reshape(chips, width // cams // chips, CW), 'tm', 0,...  8.53 us
  transfers between devices with their start and end apart: 10, of which 5 were waited for; matrix products, arithmetic and copies ran while one was open for 9% of the time, Pallas kernels for 7%

profile of v1, /device:TPU:1, one launch (start us, length us, event | category | flops | bytes accessed | tf_op | source)
XLA Modules:
  0.0 197.4 jit_solution(1926262275965966692)
XLA Ops:
  7.2 0.7 all-gather.2.cloned.1.call-update
  7.9 1.0 copy-done.8
  8.9 1.0 copy-done.9
  9.9 1.0 copy-done.10
  10.9 1.0 copy-done.11
  11.9 0.7 copy-done.14
  12.5 1.9 shard_map.128
  14.5 21.9 %all_to_all.54 = bf16[4,32,3840]{2,1,0:T(8,128)(2,1)S(1)} all-to-all(bf16[4,32,3840]{2,1,0:T(8,128)(2,1)S(1)} %bitcast.29), channel_id=1, replica_groups={{0,1,2,3},{4,5,6,7},{8,9,10,11},{12,13,14,15},{16,17,18,19},{20,21,22,2..., dimensions={0} | all-to-all | bytes 1966080 | tf_op jit(solution)/shard_map/all_to_all | solution.py:219
  36.3 4.1 %all-to-all-start = ((bf16[8,16,3968]{2,1,0:T(8,128)(2,1)}), bf16[8,16,3968]{2,1,0:T(8,128)(2,1)S(1)}, u32[]{:S(2)}, u32[]{:S(2)}) async-start(bf16[8,16,3968]{2,1,0:T(8,128)(2,1)} %bitcast.4), calls=%async_computation | async-start | bytes 2031616 | tf_op jit(solution)/shard_map/all_to_all | solution.py:218
  40.5 0.8 fusion.12
  41.3 3.7 %collective-permute-start = (bf16[128,1536]{1,0:T(8,128)(2,1)}, bf16[128,1536]{1,0:T(8,128)(2,1)S(1)}, u32[]{:S(2)}, u32[]{:S(2)}) collective-permute-start(bf16[128,1536]{1,0:T(8,128)(2,1)} %get-tuple-element.34), channel_id=1, source_target_pairs={{0,4},{1,5},{2,6},{3,7},{4,8},{5,9},{6,10},{7,11},{8,12},{9,13},{1... | collective-permute-start | bytes 1179656 | tf_op jit(solution)/shard_map/ppermute | solution.py:220
  45.0 0.7 constant_dynamic-slice_fusion.3
  45.7 9.4 %all-to-all-done = bf16[8,16,3968]{2,1,0:T(8,128)(2,1)S(1)} async-done(((bf16[8,16,3968]{2,1,0:T(8,128)(2,1)}), bf16[8,16,3968]{2,1,0:T(8,128)(2,1)S(1)}, u32[]{:S(2)}, u32[]{:S(2)}) %all-to-all-start) | async-done | bytes 1015840 | tf_op jit(solution)/shard_map/all_to_all | solution.py:218
  55.1 0.7 constant_dynamic-slice_fusion.4
  55.8 0.8 pad_maximum_fusion.3
  56.6 1.7 collective-permute-start.3
  58.2 0.8 shard_map.129
  59.1 1.9 shard_map.131
  61.0 0.1 collective-permute-start.2
  61.1 1.6 pad_maximum_fusion
  62.7 0.1 collective-permute-done.2
  62.8 0.5 fusion.4
  63.4 0.5 fusion.2
  63.9 0.5 fusion
  64.4 37.5 %all_to_all.55 = bf16[8,192,768]{2,1,0:T(8,128)(2,1)} all-to-all(bf16[8,192,768]{2,1,0:T(8,128)(2,1)S(1)} %bitcast.34), channel_id=1, replica_groups=mesh['cam'=8,'tm'=32] {'cam'}, dimensions={0} | all-to-all | bytes 4718592 | tf_op jit(solution)/shard_map/all_to_all | solution.py:251
  101.9 2.1 %reduce_sum.21 = bf16[192,768]{1,0:T(8,128)(2,1)S(1)} reduce(bf16[8,192,768]{2,1,0:T(8,128)(2,1)} %all_to_all.55, bf16[]{:T(256)} %constant.42.clone.1), dimensions={0}, to_apply=%region_0.1 | reduce | flops 1032192 | bytes 2654210 | tf_op jit(solution)/shard_map/reduce_sum | solution.py:252
  104.0 0.8 reshape.65
  104.8 8.5 %all-to-all-start.5 = ((bf16[16,12,768]{2,1,0:T(8,128)(2,1)}), bf16[16,12,768]{2,1,0:T(8,128)(2,1)}, u32[]{:S(2)}, u32[]{:S(2)}) async-start(bf16[16,12,768]{2,1,0:T(8,128)(2,1)} %reshape.65), calls=%async_computation.5 | async-start | bytes 786432 | tf_op jit(solution)/shard_map/all_to_all | solution.py:254
  113.3 20.4 %all-gather.2.cloned.1.call-done.w = bf16[1536,1536]{1,0:T(8,128)(2,1)} async-done(((bf16[48,1536]{1,0:T(8,128)(2,1)}), bf16[1536,1536]{1,0:T(8,128)(2,1)}) %all-gather.2.cloned.1.call-update) | async-done | bytes 4718608 | tf_op jit(solution)/shard_map/all_gather | solution.py:210
  133.7 4.1 %fusion.11 = (bf16[768,1536]{1,0:T(8,128)(2,1)}, bf16[768,1536]{1,0:T(8,128)(2,1)S(1)}) fusion(bf16[1536,1536]{1,0:T(8,128)(2,1)} %all-gather.2.cloned.1.call-done.w), kind=kLoop, calls=%fused_computation.29 | loop fusion | bytes 9437184 | tf_op jit(solution)/shard_map/slice | solution.py:276
  137.9 3.0 %shard_map.130 = bf16[128,3072]{1,0:T(8,128)(2,1)} custom-call(bf16[128,3968]{1,0:T(8,128)(2,1)S(1)} %bitcast.26, bf16[128,768]{1,0:T(8,128)(2,1)S(1)} %get-tuple-element.19.attn, f32[6,256,128]{2,1,0:T(8,128)S(1)} %get-tuple-element.20.prob_ref, bf16[768,1536]{1,0:T(8,128)(2,1)S(1)} %get-tuple-element.32.w), custom_call_target="tpu_custom_call" | custom-call | tf_op jit(solution)/shard_map/pallas_call | solution.py:190
  140.9 4.3 %all-to-all-start.1 = ((bf16[8,16,3072]{2,1,0:T(8,128)(2,1)}), bf16[8,16,3072]{2,1,0:T(8,128)(2,1)S(1)}, u32[]{:S(2)}, u32[]{:S(2)}) async-start(bf16[8,16,3072]{2,1,0:T(8,128)(2,1)} %bitcast.6), calls=%async_computation.1 | async-start | bytes 1572864 | tf_op jit(solution)/shard_map/all_to_all | solution.py:279
  145.2 1.0 copy-done.3
  146.2 5.5 %shard_map.132 = (bf16[128,768]{1,0:T(8,128)(2,1)S(1)}, f32[128,1536]{1,0:T(8,128)S(1)}, bf16[128,1536]{1,0:T(8,128)(2,1)}) custom-call(bf16[128,3840]{1,0:T(8,128)(2,1)S(1)} %bitcast.23, bf16[128,1536]{1,0:T(8,128)(2,1)S(1)} %copy-done.3, f32[6,256,256]{2,1,0:T(8,128)S(1)} %copy-done.1, bf16[768,1536]{1,0:T(8,128)(2,1)} %get-tuple-element.31.w), custom_call_target="tpu_custom_call" | custom-call | tf_op jit(solution)/shard_map/pallas_call | solution.py:190
  151.7 0.9 copy-done.6
  152.6 0.7 copy-done.12
  153.3 1.4 collective-permute-start.1
  154.7 1.1 convert_reduce_fusion
  155.8 0.6 collective-permute-start.4
  156.4 9.2 %collective-permute-done.1.back = bf16[128,1536]{1,0:T(8,128)(2,1)S(1)} collective-permute-done((bf16[128,1536]{1,0:T(8,128)(2,1)}, bf16[128,1536]{1,0:T(8,128)(2,1)S(1)}, u32[]{:S(2)}, u32[]{:S(2)}) %collective-permute-start.1) | collective-permute-done | bytes 393248 | tf_op jit(solution)/shard_map/ppermute | solution.py:278
  165.7 1.1 copy-done.7
  166.8 0.9 copy-done.13
  167.7 1.0 shard_map.133
  168.7 5.1 %all-to-all-start.3 = ((bf16[4,32,3072]{2,1,0:T(8,128)(2,1)}), bf16[4,32,3072]{2,1,0:T(8,128)(2,1)S(1)}, u32[]{:S(2)}, u32[]{:S(2)}) async-start(bf16[4,32,3072]{2,1,0:T(8,128)(2,1)} %bitcast.11), calls=%async_computation.3 | async-start | bytes 1572864 | tf_op jit(solution)/shard_map/all_to_all | solution.py:281
  173.8 3.4 %convolution_bitcast_fusion.action = f32[16,1536]{1,0:T(8,128)S(1)} fusion(bf16[7,256,1536]{2,1,0:T(8,128)(2,1)} %param.15, s32[16,7]{0,1:T(8,128)S(1)} %copy-done.17), kind=kOutput, calls=%fused_computation.2 | convolution fusion | flops 88109056 | bytes 5603776 | tf_op jit(solution)/shard_map/dot_general | solution.py:267
  177.3 0.6 pad_maximum_fusion.4
  177.9 8.2 %all-to-all-done.3 = bf16[4,32,3072]{2,1,0:T(8,128)(2,1)S(1)} async-done(((bf16[4,32,3072]{2,1,0:T(8,128)(2,1)}), bf16[4,32,3072]{2,1,0:T(8,128)(2,1)S(1)}, u32[]{:S(2)}, u32[]{:S(2)}) %all-to-all-start.3) | async-done | bytes 786464 | tf_op jit(solution)/shard_map/all_to_all | solution.py:281
  186.1 4.4 %shard_map.134 = (bf16[128,1536]{1,0:T(8,128)(2,1)}, bf16[128,1536]{1,0:T(8,128)(2,1)}, bf16[128,1536]{1,0:T(8,128)(2,1)}, bf16[128,1536]{1,0:T(8,128)(2,1)}) custom-call(bf16[128,3072]{1,0:T(8,128)(2,1)S(1)} %bitcast.27, bf16[128,3072]{1,0:T(8,128)(2,1)S(1)} %bitcast.28, bf16[1536,1536]{1,0:T(8,128)(2,1)} %all-gather.2.cloned.1.call-done.w, ...), custom_call_target="tpu_custom_call" | custom-call | tf_op jit(solution)/shard_map/pallas_call | solution.py:190
  (37 shorter events, 0.2 us)
Async XLA Ops:
  7.2 126.6 %all-gather.2.cloned.1.call-start = ((), (), s32[]{:S(2)}) async-start(), calls=%async_computation.6 | async-start | bytes 4866048 | tf_op jit(solution)/shard_map/all_gather | solution.py:210
  7.9 1.0 copy-start.8
  8.9 1.0 copy-start.9
  9.9 1.0 copy-start.10
  10.9 1.0 copy-start.11
  11.9 0.7 copy-start.14
  36.3 18.7 %all-to-all-start = ((bf16[8,16,3968]{2,1,0:T(8,128)(2,1)}), bf16[8,16,3968]{2,1,0:T(8,128)(2,1)S(1)}, u32[]{:S(2)}, u32[]{:S(2)}) async-start(bf16[8,16,3968]{2,1,0:T(8,128)(2,1)} %bitcast.4), calls=%async_computation | async-start | bytes 2031616 | tf_op jit(solution)/shard_map/all_to_all | solution.py:218
  41.3 17.8 %copy-start.15 = (s32[12]{0:T(128)S(1)}, s32[12]{0:T(128)}, u32[]{:S(2)}) copy-start(s32[12]{0:T(128)} %windows.1) | copy-start | bytes 148
  41.3 17.8 %collective-permute-start = (bf16[128,1536]{1,0:T(8,128)(2,1)}, bf16[128,1536]{1,0:T(8,128)(2,1)S(1)}, u32[]{:S(2)}, u32[]{:S(2)}) collective-permute-start(bf16[128,1536]{1,0:T(8,128)(2,1)} %get-tuple-element.34), channel_id=1, source_target_pairs={{0,4},{1,5},{2,6},{3,7},{4,8},{5,9},{6,10},{7,11},{8,12},{9,13},{1... | collective-permute-start | bytes 1179656 | tf_op jit(solution)/shard_map/ppermute | solution.py:220
  56.6 4.6 %collective-permute-start.3 = (bf16[128,1536]{1,0:T(8,128)(2,1)}, bf16[128,1536]{1,0:T(8,128)(2,1)}, u32[]{:S(2)}, u32[]{:S(2)}) collective-permute-start(bf16[128,1536]{1,0:T(8,128)(2,1)} %pad_maximum_fusion.3), channel_id=1, source_target_pairs={{0,1},{1,0},{2,3},{3,2},{4,5},{5,4},{6,7},{7,6},{8,9},{9,8},{10,11... | collective-permute-start | bytes 1179656 | tf_op jit(solution)/shard_map/ppermute | solution.py:240
  58.2 2.9 %copy-start.16 = (bf16[128,768]{1,0:T(8,128)(2,1)S(1)}, bf16[128,768]{1,0:T(8,128)(2,1)}, u32[]{:S(2)}) copy-start(bf16[128,768]{1,0:T(8,128)(2,1)} %get-tuple-element.35) | copy-start | bytes 589828
  59.1 4.3 %copy-start.2 = (bf16[128,1536]{1,0:T(8,128)(2,1)}, bf16[128,1536]{1,0:T(8,128)(2,1)S(1)}, u32[]{:S(2)}) copy-start(bf16[128,1536]{1,0:T(8,128)(2,1)S(1)} %collective-permute-done.prev) | copy-start | bytes 1179652
  61.0 2.4 %copy-start = (f32[6,256,256]{2,1,0:T(8,128)}, f32[6,256,256]{2,1,0:T(8,128)S(1)}, u32[]{:S(2)}) copy-start(f32[6,256,256]{2,1,0:T(8,128)S(1)} %get-tuple-element.23.prob_ref) | copy-start | bytes 4718596
  61.0 2.4 %copy-start.4 = (bf16[128,768]{1,0:T(8,128)(2,1)}, bf16[128,768]{1,0:T(8,128)(2,1)S(1)}, u32[]{:S(2)}) copy-start(bf16[128,768]{1,0:T(8,128)(2,1)S(1)} %get-tuple-element.22.attn) | copy-start | bytes 589828
  61.0 1.8 collective-permute-start.2
  104.8 36.1 %all-to-all-start.5 = ((bf16[16,12,768]{2,1,0:T(8,128)(2,1)}), bf16[16,12,768]{2,1,0:T(8,128)(2,1)}, u32[]{:S(2)}, u32[]{:S(2)}) async-start(bf16[16,12,768]{2,1,0:T(8,128)(2,1)} %reshape.65), calls=%async_computation.5 | async-start | bytes 786432 | tf_op jit(solution)/shard_map/all_to_all | solution.py:254
  140.9 4.3 %copy-start.1 = (f32[6,256,256]{2,1,0:T(8,128)S(1)}, f32[6,256,256]{2,1,0:T(8,128)}, u32[]{:S(2)}) copy-start(f32[6,256,256]{2,1,0:T(8,128)} %copy-done) | copy-start | bytes 4718596
  140.9 27.9 %all-to-all-start.1 = ((bf16[8,16,3072]{2,1,0:T(8,128)(2,1)}), bf16[8,16,3072]{2,1,0:T(8,128)(2,1)S(1)}, u32[]{:S(2)}, u32[]{:S(2)}) async-start(bf16[8,16,3072]{2,1,0:T(8,128)(2,1)} %bitcast.6), calls=%async_computation.1 | async-start | bytes 1572864 | tf_op jit(solution)/shard_map/all_to_all | solution.py:279
  145.2 1.0 copy-start.3
  146.2 19.5 %copy-start.5 = (bf16[128,768]{1,0:T(8,128)(2,1)S(1)}, bf16[128,768]{1,0:T(8,128)(2,1)}, u32[]{:S(2)}) copy-start(bf16[128,768]{1,0:T(8,128)(2,1)} %copy-done.4) | copy-start | bytes 589828
  151.7 0.9 copy-start.6
  152.6 0.7 copy-start.12
  153.3 20.6 %copy-start.17 = (s32[16,7]{0,1:T(8,128)S(1)}, s32[16,7]{0,1:T(8,128)}, u32[]{:S(2)}) copy-start(s32[16,7]{0,1:T(8,128)} %param.14) | copy-start | bytes 1348
  153.3 12.4 %collective-permute-start.1 = (bf16[128,1536]{1,0:T(8,128)(2,1)}, bf16[128,1536]{1,0:T(8,128)(2,1)S(1)}, u32[]{:S(2)}, u32[]{:S(2)}) collective-permute-start(bf16[128,1536]{1,0:T(8,128)(2,1)} %get-tuple-element.26), channel_id=1, source_target_pairs={{4,0},{5,1},{6,2},{7,3},{8,4},{9,5},{10,6},{11,7},{12,8},{13,9},{1... | collective-permute-start | bytes 1179656 | tf_op jit(solution)/shard_map/ppermute | solution.py:278
  155.8 21.5 %collective-permute-start.4 = (f32[6,768]{1,0:T(8,128)S(1)}, f32[6,768]{1,0:T(8,128)S(1)}, u32[]{:S(2)}, u32[]{:S(2)}) collective-permute-start(f32[6,768]{1,0:T(8,128)S(1)} %constant_dynamic-slice_fusion), channel_id=1, source_target_pairs={{0,1},{1,0},{2,3},{3,2},{4,5},{5,4},{6,7},{7,6},{8,9},{9,8},{10,11... | collective-permute-start | bytes 55304 | tf_op jit(solution)/shard_map/ppermute | solution.py:260
  165.6 1.1 copy-start.7
  166.8 0.9 copy-start.13
  168.7 17.4 %all-to-all-start.3 = ((bf16[4,32,3072]{2,1,0:T(8,128)(2,1)}), bf16[4,32,3072]{2,1,0:T(8,128)(2,1)S(1)}, u32[]{:S(2)}, u32[]{:S(2)}) async-start(bf16[4,32,3072]{2,1,0:T(8,128)(2,1)} %bitcast.11), calls=%async_computation.3 | async-start | bytes 1572864 | tf_op jit(solution)/shard_map/all_to_all | solution.py:281
Sparse Core Ops, SparseCore 0:
  10.8 122.9 all-gather.1

commit v2 on v1

v2 whole, which is shorter than its diff:
```python
import functools
import math

import jax
import jax.numpy as jnp
from jax import lax
from jax.experimental import pallas as pl
from jax.experimental.pallas import tpu as pltpu
from jax.sharding import PartitionSpec as P

HC = 12
HT = 12
HD = 64
WIN = 64
CW = HC * HD
GROUP = 4
SCALE = HD ** (-0.5)
BF = jnp.bfloat16
F32 = jnp.float32
PAIRS = HC // 2
VM = pl.BlockSpec(memory_space=pltpu.VMEM)
ANY = pl.BlockSpec(memory_space=pl.ANY)
SM = pl.BlockSpec(memory_space=pltpu.SMEM)


def params():
    return pltpu.CompilerParams(vmem_limit_bytes=56 * 1024 * 1024)


def iota(shape, dim):
    return lax.broadcasted_iota(jnp.int32, shape, dim)


def dot_nt(a, b):
    return lax.dot_general(a, b, (((1,), (1,)), ((), ())), preferred_element_type=F32)


def dot_tn(a, b):
    return lax.dot_general(a, b, (((0,), (0,)), ((), ())), preferred_element_type=F32)


def dot_nn(a, b):
    return jnp.dot(a, b, preferred_element_type=F32)


def split_pair(rows):
    low = iota(rows.shape, 1) < HD
    zero = jnp.zeros_like(rows)
    return jnp.concatenate([jnp.where(low, rows, zero), jnp.where(low, zero, rows)], axis=0)


def join_pair(rows):
    count = rows.shape[0] // 2
    low = iota((count, rows.shape[1]), 1) < HD
    return jnp.where(low, rows[:count], rows[count:])


def softmax_pair(q, k, mask):
    scores = dot_nt(split_pair(q), k) * SCALE
    scores = jnp.where(mask, scores, -jnp.inf)
    largest = jnp.max(scores, axis=1, keepdims=True)
    e = jnp.exp(scores - largest)
    return e / jnp.sum(e, axis=1, keepdims=True)


def pack_kernel(me, valid, q, k, v, ct, view_ref, *rest):
    own_refs, kv_refs, (held, sems) = rest[:GROUP], rest[GROUP : 2 * GROUP], rest[2 * GROUP :]
    copies = [pltpu.make_async_copy(ref, held.at[i], sems.at[i]) for i, ref in enumerate((q, k, v, ct))]
    for copy in copies:
        copy.start()
    rows = q.shape[0]
    frames = rows // 8
    block = 2 * frames
    row = iota((rows, rows), 0)
    col = iota((rows, rows), 1)
    member = (row // block) ^ me[0]
    source = ((row // 2) % frames) * 8 + 2 * member + row % 2
    perm = jnp.where(col == source, 1.0, 0.0).astype(BF)
    frame = iota((rows, 128), 0) // 8
    flags = jnp.zeros((rows, 128), F32)
    for f in range(frames):
        flags = jnp.where(frame == f, valid[0, f].astype(F32), flags)
    view_ref[:, 5 * CW :] = jnp.where(flags > 0.5, 1.0, 0.0).astype(BF)
    for i in range(4):
        copies[i].wait()
        if i < 3:
            part = slice(i * CW, (i + 1) * CW)
            view_ref[:, part] = held[i, :, :CW]
            moved = dot_nn(perm, held[i, :, CW:]).astype(BF)
        else:
            part = slice(3 * CW, 5 * CW)
            view_ref[:, part] = held[i]
            moved = dot_nn(perm, held[i]).astype(BF)
        for d in range(GROUP):
            own_refs[d][:, part] = moved[d * block : (d + 1) * block]
            if i in (1, 2):
                kv_refs[d][:, (i - 1) * CW : i * CW] = moved[d * block : (d + 1) * block]


def view_mask(flags):
    rows = flags.shape[0]
    pick = jnp.where(iota((8, 128), 1) == 0, 1.0, 0.0).astype(BF)
    valid_row = dot_nt(pick, flags)[:1]
    r = iota((2 * rows, rows), 0) % rows
    c = iota((2 * rows, rows), 1)
    same_frame = ((r // 8) % 2) == ((c // 8) % 2)
    return same_frame & ((valid_row > 0.5) | (r // 16 == c // 16))


def keep_for_weight(attn, ct, core, own_ref, send_ref):
    own_ref[:, :CW] = attn
    send_ref[:, :CW] = attn
    own_ref[:, CW:] = jnp.where(core == 0, ct[:, :CW], ct[:, CW:])
    send_ref[:, CW:] = jnp.where(core == 0, ct[:, CW:], ct[:, :CW])


def view_forward_kernel(me, x, own_ref, send_ref, prob_ref):
    mask = view_mask(x[:, 5 * CW :])
    attn = []
    for j in range(PAIRS):
        q = x[:, 128 * j : 128 * (j + 1)]
        k = x[:, CW + 128 * j : CW + 128 * (j + 1)]
        v = x[:, 2 * CW + 128 * j : 2 * CW + 128 * (j + 1)]
        prob = softmax_pair(q, k, mask)
        prob_ref[j] = prob
        attn.append(join_pair(dot_nn(prob.astype(BF), v)).astype(BF))
    keep_for_weight(jnp.concatenate(attn, axis=1), x[:, 3 * CW : 5 * CW], me[0] % 2, own_ref, send_ref)


def rows_of(refs, columns):
    return jnp.concatenate([ref[:, columns] for ref in refs], axis=0)


def time_forward_kernel(windows, me, block, *refs):
    x, prev, (own_ref, send_ref, prob_ref) = refs[:GROUP], refs[GROUP : 2 * GROUP], refs[2 * GROUP :]
    size = x[0].shape[0]
    rows = GROUP * size
    r = iota((2 * rows, 2 * rows), 0)
    c = iota((2 * rows, 2 * rows), 1)
    second = r >= rows

    def frame_of(row):
        return ((row // size) ^ me[0]) * (size // 2) + (row % size) // 2

    key_frame = frame_of(c % rows) - jnp.where(c < rows, rows // 2, 0)
    gap = frame_of(r % rows) - key_frame
    base = (r % 2 == c % 2) & (gap >= 0) & ((key_frame >= 0) | (block[0] > 0))
    attn = []
    for j in range(PAIRS):
        at = [slice(i * CW + 128 * j, i * CW + 128 * (j + 1)) for i in range(3)]
        k = jnp.concatenate([rows_of(prev, at[0]), rows_of(x, at[1])], axis=0)
        v = jnp.concatenate([rows_of(prev, at[1]), rows_of(x, at[2])], axis=0)
        limit = jnp.where(second, windows[2 * j + 1], windows[2 * j])
        prob = softmax_pair(rows_of(x, at[0]), k, base & (gap < limit))
        prob_ref[j] = prob
        attn.append(join_pair(dot_nn(prob.astype(BF), v)).astype(BF))
    keep_for_weight(
        jnp.concatenate(attn, axis=1), rows_of(x, slice(3 * CW, 5 * CW)), me[0] % 2, own_ref, send_ref
    )


def weight_kernel(scale, own_view, other_view, own_time, other_time, out_ref):
    for i, (own, other) in enumerate(((own_view, other_view), (own_time, other_time))):
        left = jnp.concatenate([own[:, :CW], other[:, :CW]], axis=0)
        right = jnp.concatenate([own[:, CW:], other[:, CW:]], axis=0)
        out_ref[i * CW : (i + 1) * CW, :] = (dot_tn(left, right) * scale).astype(BF)


def fetch_weight(me, own, other, held, sem, first, count):
    size = held.shape[0] // count
    core = me[0] % 2
    copies = []
    for i in range(count // 2):
        for which_at, (which, ref) in enumerate(((core, own), (1 - core, other))):
            start = pl.multiple_of((2 * i + which) * size, 16)
            copies.append(
                pltpu.make_async_copy(
                    ref.at[pl.ds((first // 2 + i) * size, size)], held.at[pl.ds(start, size)], sem.at[2 * i + which_at]
                )
            )
    for copy in copies:
        copy.start()
    return copies


def backward_pair(q, k, v, g, prob):
    g2 = split_pair(g)
    grad_prob = dot_nt(g2, v)
    total = jnp.sum(prob * grad_prob, axis=1, keepdims=True)
    grad_scores = (prob * (grad_prob - total)).astype(BF)
    dq = join_pair(dot_nn(grad_scores, k)) * SCALE
    dk = dot_tn(grad_scores, split_pair(q)) * SCALE
    dv = dot_tn(prob.astype(BF), g2)
    return dq, dk, dv


def view_backward_kernel(blocks, me, x, kept, prob_ref, w_own, w_other, out_ref, w, sem):
    copies = fetch_weight(me, w_own, w_other, w, sem, 0, blocks // 2)
    out_ref[:, :CW] = kept[:, :CW]
    for copy in copies:
        copy.wait()
    grad = dot_nt(x[:, 3 * CW : 5 * CW], w[...]).astype(BF)
    for j in range(PAIRS):
        at = [slice(i * CW + 128 * j, i * CW + 128 * (j + 1)) for i in range(4)]
        dq, dk, dv = backward_pair(x[:, at[0]], x[:, at[1]], x[:, at[2]], grad[:, at[0]], prob_ref[j])
        out_ref[:, at[1]] = dq.astype(BF)
        out_ref[:, at[2]] = dk.astype(BF)
        out_ref[:, at[3]] = dv.astype(BF)


def time_backward_kernel(blocks, me, *refs):
    x, prev = refs[:GROUP], refs[GROUP : 2 * GROUP]
    kept, prob_ref, w_own, w_other = refs[2 * GROUP : 2 * GROUP + 4]
    out_refs = refs[2 * GROUP + 4 : 3 * GROUP + 4]
    back_refs = refs[3 * GROUP + 4 : 4 * GROUP + 4]
    w, sem = refs[4 * GROUP + 4 :]
    copies = fetch_weight(me, w_own, w_other, w, sem, blocks // 2, blocks // 2)
    size = x[0].shape[0]
    rows = GROUP * size

    def store(out, columns, value):
        value = value.astype(BF)
        for d in range(GROUP):
            out[d][:, columns] = value[d * size : (d + 1) * size]

    store(out_refs, slice(0, CW), kept[:, :CW])
    for copy in copies:
        copy.wait()
    grad = dot_nt(rows_of(x, slice(3 * CW, 5 * CW)), w[...]).astype(BF)
    for j in range(PAIRS):
        at = [slice(i * CW + 128 * j, i * CW + 128 * (j + 1)) for i in range(4)]
        k = jnp.concatenate([rows_of(prev, at[0]), rows_of(x, at[1])], axis=0)
        v = jnp.concatenate([rows_of(prev, at[1]), rows_of(x, at[2])], axis=0)
        dq, dk, dv = backward_pair(rows_of(x, at[0]), k, v, grad[:, at[0]], prob_ref[j])
        store(out_refs, at[1], dq)
        store(back_refs, at[0], dk[:rows])
        store(out_refs, at[2], dk[rows:])
        store(back_refs, at[1], dv[:rows])
        store(out_refs, at[3], dv[rows:])


def finish_kernel(blocks, me, view, w_own, w_other, action, *refs):
    time, back = refs[:GROUP], refs[GROUP : 2 * GROUP]
    pred_ref, dq_ref, dk_ref, dv_ref, w, sem = refs[2 * GROUP :]
    copies = fetch_weight(me, w_own, w_other, w, sem, 0, blocks)
    rows = view.shape[0]
    frames = rows // 8
    row = iota((rows, rows), 0)
    col = iota((rows, rows), 1)
    source = (((row // 2) % GROUP) ^ me[0]) * 2 * frames + (row // 8) * 2 + row % 2
    perm = jnp.where(col == source, 1.0, 0.0).astype(BF)
    for i, ref in enumerate((dq_ref, dk_ref, dv_ref), 1):
        part = slice(i * CW, (i + 1) * CW)
        rows_time = rows_of(time, part)
        if i > 1:
            returned = rows_of(back, slice((i - 2) * CW, (i - 1) * CW))
            rows_time = (rows_time.astype(F32) + returned.astype(F32)).astype(BF)
        ref[:, :CW] = view[:, part]
        ref[:, CW:] = dot_nn(perm, rows_time).astype(BF)
    attn_time = dot_nn(perm, rows_of(time, slice(0, CW))).astype(BF)
    for copy in copies:
        copy.wait()
    mixed = dot_nn(view[:, :CW], w[:CW]) + dot_nn(attn_time, w[CW:])
    total = mixed.reshape(frames, 8, 2 * CW) + action[...][:, None, :]
    pred_ref[...] = total.reshape(rows, 2 * CW).astype(BF)


def whole(shape):
    return pl.BlockSpec(shape, lambda *at: (0,) * len(shape))


def call(kernel, outs, specs, *args, scratch=()):
    specs = [whole(arg.shape) if spec is VM else spec for spec, arg in zip(specs, args)]
    return pl.pallas_call(
        kernel,
        out_shape=[jax.ShapeDtypeStruct(shape, kind) for shape, kind in outs],
        in_specs=specs,
        out_specs=[whole(shape) for shape, _ in outs],
        grid=(1,),
        scratch_shapes=list(scratch),
        compiler_params=params(),
    )(*args)


def shards(queries, keys, values, cam_valid, windows, actions, act_table, w_out, cotangent):
    _, frames, tokens, width = queries.shape
    rows = frames * tokens
    block = rows // GROUP
    cams = lax.axis_size("cam")
    tm = lax.axis_size("tm")
    at_tm = lax.axis_index("tm")
    core = at_tm % 2
    me = (at_tm % GROUP).reshape(1)
    group = (at_tm // GROUP).reshape(1)
    same_core = [[2 * i + j for i in range(tm // 2)] for j in range(2)]
    swap = [(i, i ^ 1) for i in range(tm)]
    onward = [[(i, (i + GROUP) ^ d) for i in range(tm - GROUP)] for d in range(GROUP)]
    inward = [[((i + GROUP) ^ d, i) for i in range(tm - GROUP)] for d in range(GROUP)]
    within = [[(i, i ^ d) for i in range(tm)] for d in range(GROUP)]

    w_own = lax.all_gather(w_out, "tm", axis=0, tiled=True, axis_index_groups=same_core)
    w_other = lax.ppermute(w_own, "tm", swap)
    q, k, v, ct = (a.reshape(rows, width) for a in (queries, keys, values, cotangent))
    packed = call(
        pack_kernel,
        [((rows, 5 * CW + 128), BF)] + [((block, 5 * CW), BF)] * GROUP + [((block, 2 * CW), BF)] * GROUP,
        [SM, SM] + [ANY] * 4,
        me, cam_valid, q, k, v, ct,
        scratch=[pltpu.VMEM((4, rows, width), BF), pltpu.SemaphoreType.DMA((4,))],
    )
    view_send, time_send, kv_send = packed[0], packed[1 : GROUP + 1], packed[GROUP + 1 :]
    view_x = lax.all_to_all(view_send, "cam", 0, 0, tiled=True)
    time_x = [time_send[0]] + [lax.ppermute(time_send[d], "tm", within[d]) for d in range(1, GROUP)]
    prev = [lax.ppermute(kv_send[d], "tm", onward[d]) for d in range(GROUP)]

    kept_view, view_swap, prob_view = call(
        view_forward_kernel,
        [((rows, 2 * CW), BF)] * 2 + [((PAIRS, 2 * rows, rows), F32)],
        [SM, VM],
        me, view_x,
    )
    kept_time, time_swap, prob_time = call(
        time_forward_kernel,
        [((rows, 2 * CW), BF)] * 2 + [((PAIRS, 2 * rows, 2 * rows), F32)],
        [SM] * 3 + [VM] * (2 * GROUP),
        windows, me, group, *time_x, *prev,
    )

    view_swap = lax.ppermute(view_swap, "tm", swap)
    time_swap = lax.ppermute(time_swap, "tm", swap)
    grad_norm = 1.0 / math.sqrt(cams * tm * rows)
    (part,) = call(
        functools.partial(weight_kernel, grad_norm),
        [((width, CW), BF)],
        [VM] * 4,
        kept_view, view_swap, kept_time, time_swap,
    )
    part = lax.all_to_all(part.reshape(cams, width // cams, CW), "cam", 0, 0, tiled=True)
    part = jnp.sum(part.astype(F32), axis=0).astype(BF)
    chips = tm // 2
    part = lax.all_to_all(
        part.reshape(chips, width // cams // chips, CW), "tm", 0, 0, tiled=True, axis_index_groups=same_core
    )
    part = jnp.sum(part.astype(F32), axis=0)
    final = width // cams // tm
    mine = lax.dynamic_slice_in_dim(part, core * final, final, 0)
    theirs = lax.ppermute(lax.dynamic_slice_in_dim(part, (1 - core) * final, final, 0), "tm", swap)
    grad_out_weight = jnp.concatenate(
        [jnp.where(core == 0, mine, theirs), jnp.where(core == 0, theirs, mine)], axis=1
    )

    codes = jnp.arange(act_table.shape[1])
    one_hot = (actions[:, :, None] == codes[None, None, :]).astype(BF).reshape(frames, -1)
    action_sum = jnp.dot(one_hot, act_table.reshape(-1, width), preferred_element_type=F32)

    half_weight = [pltpu.VMEM((CW, width), BF), pltpu.SemaphoreType.DMA((tm // 2,))]
    (view_back,) = call(
        functools.partial(view_backward_kernel, tm),
        [((rows, 4 * CW), BF)],
        [SM] + [VM] * 3 + [ANY] * 2,
        me, view_x, kept_view, prob_view, w_own, w_other,
        scratch=half_weight,
    )
    returned = call(
        functools.partial(time_backward_kernel, tm),
        [((block, 4 * CW), BF)] * GROUP + [((block, 2 * CW), BF)] * GROUP,
        [SM] + [VM] * (2 * GROUP + 2) + [ANY] * 2,
        me, *time_x, *prev, kept_time, prob_time, w_own, w_other,
        scratch=half_weight,
    )
    view_back = lax.all_to_all(view_back, "cam", 0, 0, tiled=True)
    time_back = [returned[0]] + [lax.ppermute(returned[d], "tm", within[d]) for d in range(1, GROUP)]
    back = [lax.ppermute(returned[GROUP + d], "tm", inward[d]) for d in range(GROUP)]
    outs = call(
        functools.partial(finish_kernel, tm),
        [((rows, width), BF)] * 4,
        [SM, VM] + [ANY] * 2 + [VM] * (2 * GROUP + 1),
        me, view_back, w_own, w_other, action_sum, *time_back, *back,
        scratch=[pltpu.VMEM((width, width), BF), pltpu.SemaphoreType.DMA((tm,))],
    )
    return tuple(a.reshape(1, frames, tokens, width) for a in outs) + (grad_out_weight,)


def solution(mesh):
    in_specs = (
        P("cam", "tm", None, None),
        P("cam", "tm", None, None),
        P("cam", "tm", None, None),
        P("cam", "tm"),
        P(),
        P("tm", None),
        P(),
        P("tm", None),
        P("cam", "tm", None, None),
    )
    out_specs = (
        P("cam", "tm", None, None),
        P("cam", "tm", None, None),
        P("cam", "tm", None, None),
        P("cam", "tm", None, None),
        P(("cam", "tm"), None),
    )
    return jax.shard_map(shards, mesh=mesh, in_specs=in_specs, out_specs=out_specs, check_vma=False)
```

time: 198 us -> 216 us (1.091)
  blocking collectives: 59.3 us -> 0 us
  waiting for transfers between devices: 48 us -> 93.5 us
  starting transfers between devices: 29.6 us -> 58.7 us
  Pallas kernels: 18.5 us -> 35.1 us
  local copies, waits for them, and re-layouts: 16.6 us -> 5.59 us
  other arithmetic: 6.66 us -> 2.79 us
    all_to_all x2 -> x0, blocking collectives: 59.3 us -> none  [the longest x1 37.5 us: shards(): lax.all_to_all(part.reshape(cams, width // cams, CW), 'cam', 0, 0, tiled=...]
    all_gather x1, waiting for transfers between devices: 20.4 us -> 61.5 us  [shards(): lax.all_gather(w_out, 'tm', axis=0, tiled=True, axis_index_groups=same_core)]
    ppermute x4 -> x17, starting transfers between devices: 6.85 us -> 36.2 us  [the longest x4 18.3 us: shards(): prev = [lax.ppermute(kv_send[d], 'tm', onward[d]) for d in range(GROUP)]]
    pallas_call x7, Pallas kernels: 18.5 us -> 35.1 us  [call(): pl.pallas_call(kernel, out_shape=[jax.ShapeDtypeStruct(shape, kind) for s...]
    all_to_all x1, waiting for transfers between devices: 0.01 us -> 15.4 us  [shards(): lax.all_to_all(part.reshape(chips, width // cams // chips, CW), 'tm', 0,...]
    all_to_all x1, waiting for transfers between devices: 9.37 us -> 0.01 us  [shards(): view_x = lax.all_to_all(view_send, 'cam', 0, 0, tiled=True)]
    all_to_all x1, waiting for transfers between devices: 8.21 us -> 0.01 us  [shards(): lax.all_to_all(part.reshape(cams, width // cams, CW), 'cam', 0, 0, tiled=...]
    ppermute x4 -> x17, waiting for transfers between devices: 9.35 us -> 15.9 us  [the longest x4 8.42 us: shards(): lax.ppermute(returned[GROUP + d], 'tm', inward[d])]
  transfers between devices with their start and end apart: 10 -> 23, of which waited for: 5 -> 9; matrix products, arithmetic and copies ran while one was open for 9% -> 4% of each run, Pallas kernels for 7% -> 14%
where the time goes in v2:
time: 216 us; the launch traced here: 214 us
  waiting for transfers between devices  93.5 us (43%)
  starting transfers between devices  58.7 us (27%)
  Pallas kernels  35.1 us (16%)
  between operations  14.4 us (7%)
  local copies, waits for them, and re-layouts  5.59 us (3%)
  matrix products  4.06 us (2%)
  other arithmetic  2.79 us (1%)
    all_gather x1, waiting for transfers between devices, shards(): lax.all_gather(w_out, 'tm', axis=0, tiled=True, axis_index_groups=same_core)  61.5 us
    pallas_call x7, Pallas kernels, call(): pl.pallas_call(kernel, out_shape=[jax.ShapeDtypeStruct(shape, kind) for s...  35.1 us
    ppermute x4, starting transfers between devices, shards(): prev = [lax.ppermute(kv_send[d], 'tm', onward[d]) for d in range(GROUP)]  18.3 us
    all_to_all x1, waiting for transfers between devices, shards(): lax.all_to_all(part.reshape(chips, width // cams // chips, CW), 'tm', 0,...  15.4 us
    ppermute x4, waiting for transfers between devices, shards(): lax.ppermute(returned[GROUP + d], 'tm', inward[d])  8.42 us
    all_to_all x1, starting transfers between devices, shards(): view_x = lax.all_to_all(view_send, 'cam', 0, 0, tiled=True)  5.88 us
    all_to_all x1, starting transfers between devices, shards(): lax.all_to_all(part.reshape(cams, width // cams, CW), 'cam', 0, 0, tiled=...  5.31 us
    ppermute x4, starting transfers between devices, shards(): lax.ppermute(returned[GROUP + d], 'tm', inward[d])  5.15 us
  transfers between devices with their start and end apart: 23, of which 9 were waited for; matrix products, arithmetic and copies ran while one was open for 4% of the time, Pallas kernels for 14%

profile of v2, /device:TPU:1, one launch (start us, length us, event | category | flops | bytes accessed | tf_op | source)
XLA Modules:
  0.0 214.1 jit_solution(4960406701277670917)
XLA Ops:
  7.2 0.7 all-gather.2.cloned.1.call-update
  7.9 3.8 %shard_map.128 = (bf16[128,3968]{1,0:T(8,128)(2,1)}, bf16[32,3840]{1,0:T(8,128)(2,1)}, bf16[32,3840]{1,0:T(8,128)(2,1)}, bf16[32,3840]{1,0:T(8,128)(2,1)}, bf16[...) custom-call(s32[1]{0:T(128)} %bitcast.me, ...), custom_call_target="tpu_custom_call" | custom-call | tf_op jit(solution)/shard_map/pallas_call | solution.py:274
  11.7 5.9 %all-to-all-start = ((bf16[8,16,3968]{2,1,0:T(8,128)(2,1)}), bf16[8,16,3968]{2,1,0:T(8,128)(2,1)S(1)}, u32[]{:S(2)}, u32[]{:S(2)}) async-start(bf16[8,16,3968]{2,1,0:T(8,128)(2,1)} %bitcast.23), calls=%async_computation | async-start | bytes 2031616 | tf_op jit(solution)/shard_map/all_to_all | solution.py:312
  17.6 1.0 collective-permute-start.1
  18.7 2.6 %collective-permute-start.2 = (bf16[32,3840]{1,0:T(8,128)(2,1)}, bf16[32,3840]{1,0:T(8,128)(2,1)S(1)}, u32[]{:S(2)}, u32[]{:S(2)}) collective-permute-start(bf16[32,3840]{1,0:T(8,128)(2,1)} %get-tuple-element.37), channel_id=1, source_target_pairs={{0,2},{1,3},{2,0},{3,1},{4,6},{5,7},{6,4},{7,5},{8,10},{9,11},{10,... | collective-permute-start | bytes 737288 | tf_op jit(solution)/shard_map/ppermute | solution.py:313
  21.2 0.7 collective-permute-start.3
  21.9 3.5 %collective-permute-start.4 = (bf16[32,1536]{1,0:T(8,128)(2,1)}, bf16[32,1536]{1,0:T(8,128)(2,1)S(1)}, u32[]{:S(2)}, u32[]{:S(2)}) collective-permute-start(bf16[32,1536]{1,0:T(8,128)(2,1)} %get-tuple-element.39), channel_id=1, source_target_pairs={{0,4},{1,5},{2,6},{3,7},{4,8},{5,9},{6,10},{7,11},{8,12},{9,13},{1... | collective-permute-start | bytes 294920 | tf_op jit(solution)/shard_map/ppermute | solution.py:314
  25.4 3.9 %collective-permute-start.5 = (bf16[32,1536]{1,0:T(8,128)(2,1)}, bf16[32,1536]{1,0:T(8,128)(2,1)S(1)}, u32[]{:S(2)}, u32[]{:S(2)}) collective-permute-start(bf16[32,1536]{1,0:T(8,128)(2,1)} %get-tuple-element.40), channel_id=1, source_target_pairs={{0,5},{1,4},{2,7},{3,6},{4,9},{5,8},{6,11},{7,10},{8,13},{9,12},{1... | collective-permute-start | bytes 294920 | tf_op jit(solution)/shard_map/ppermute | solution.py:314
  29.3 5.9 %collective-permute-start.6 = (bf16[32,1536]{1,0:T(8,128)(2,1)}, bf16[32,1536]{1,0:T(8,128)(2,1)S(1)}, u32[]{:S(2)}, u32[]{:S(2)}) collective-permute-start(bf16[32,1536]{1,0:T(8,128)(2,1)} %get-tuple-element.41), channel_id=1, source_target_pairs={{0,6},{1,7},{2,4},{3,5},{4,10},{5,11},{6,8},{7,9},{8,14},{9,15},{1... | collective-permute-start | bytes 294920 | tf_op jit(solution)/shard_map/ppermute | solution.py:314
  35.2 5.1 %collective-permute-start.7 = (bf16[32,1536]{1,0:T(8,128)(2,1)}, bf16[32,1536]{1,0:T(8,128)(2,1)S(1)}, u32[]{:S(2)}, u32[]{:S(2)}) collective-permute-start(bf16[32,1536]{1,0:T(8,128)(2,1)} %get-tuple-element.42), channel_id=1, source_target_pairs={{0,7},{1,6},{2,5},{3,4},{4,11},{5,10},{6,9},{7,8},{8,15},{9,14},{1... | collective-permute-start | bytes 294920 | tf_op jit(solution)/shard_map/ppermute | solution.py:314
  40.3 2.6 %collective-permute-done.7.refs_7_ = bf16[32,1536]{1,0:T(8,128)(2,1)S(1)} collective-permute-done((bf16[32,1536]{1,0:T(8,128)(2,1)}, bf16[32,1536]{1,0:T(8,128)(2,1)S(1)}, u32[]{:S(2)}, u32[]{:S(2)}) %collective-permute-start.7) | collective-permute-done | bytes 98336 | tf_op jit(solution)/shard_map/ppermute | solution.py:314
  42.9 1.5 collective-permute-done.3.refs_3_
  44.4 0.7 copy-done.5
  45.1 4.2 %shard_map.131 = (bf16[128,1536]{1,0:T(8,128)(2,1)}, bf16[128,1536]{1,0:T(8,128)(2,1)}, f32[6,256,256]{2,1,0:T(8,128)}) custom-call(s32[12]{0:T(128)} %windows.1, s32[1]{0:T(128)} %bitcast.me, s32[1]{0:T(128)} %bitcast.10.block, bf16[32,3840]{1,0:T(8,128)(2,1)} %get-tuple-element.35.refs_0_, bf16[32,3840]{1,0:T(8,128)(2,1)} %copy-done.3, ...), custom_call_target="tpu_custom_call" | custom-call | tf_op jit(solution)/shard_map/pallas_call | solution.py:274
  49.4 1.0 copy-done.1
  50.3 3.1 %shard_map.129 = (bf16[128,1536]{1,0:T(8,128)(2,1)}, bf16[128,1536]{1,0:T(8,128)(2,1)}, f32[6,256,128]{2,1,0:T(8,128)}) custom-call(s32[1]{0:T(128)} %bitcast.me, bf16[128,3968]{1,0:T(8,128)(2,1)} %bitcast.19), custom_call_target="tpu_custom_call" | custom-call | tf_op jit(solution)/shard_map/pallas_call | solution.py:274
  53.5 0.5 collective-permute-start.15
  54.0 1.6 collective-permute-done.15.other_view
  55.5 0.7 copy-done.11
  56.3 3.6 %shard_map.134 = bf16[1536,768]{1,0:T(8,128)(2,1)} custom-call(bf16[128,1536]{1,0:T(8,128)(2,1)} %get-tuple-element.33.kept.own_view, bf16[128,1536]{1,0:T(8,128)(2,1)} %copy-done.11, bf16[128,1536]{1,0:T(8,128)(2,1)} %get-tuple-element.43.refs_8_.own_time, bf16[128,1536]{1,0:T(8,128)(2,1)} %copy-done.10), custom_call_target="tpu_custom_call" | custom-call | tf_op jit(solution)/shard_map/pallas_call | solution.py:274
  59.8 5.3 %all-to-all-start.2 = ((bf16[8,192,768]{2,1,0:T(8,128)(2,1)}), bf16[8,192,768]{2,1,0:T(8,128)(2,1)}, u32[]{:S(2)}, u32[]{:S(2)}) async-start(bf16[8,192,768]{2,1,0:T(8,128)(2,1)} %bitcast.18), calls=%async_computation.2 | async-start | bytes 4718592 | tf_op jit(solution)/shard_map/all_to_all | solution.py:338
  65.2 61.5 %all-gather.2.cloned.1.call-done.w_own.refs_10_ = bf16[768,1536]{1,0:T(8,128)(2,1)} async-done(((bf16[48,1536]{1,0:T(8,128)(2,1)}), bf16[768,1536]{1,0:T(8,128)(2,1)}) %all-gather.2.cloned.1.call-update) | async-done | bytes 2359312 | tf_op jit(solution)/shard_map/all_gather | solution.py:301
  126.7 4.3 %collective-permute-start = (bf16[768,1536]{1,0:T(8,128)(2,1)}, bf16[768,1536]{1,0:T(8,128)(2,1)S(1)}, u32[]{:S(2)}, u32[]{:S(2)}) collective-permute-start(bf16[768,1536]{1,0:T(8,128)(2,1)} %all-gather.2.cloned.1.call-done.w_own.refs_10_), channel_id=1, source_target_pairs={{0,1},{1,0},{2,3},{3,2},{4,5},{5,4},{6,7},{7,6},{8,9},{9,8},{10,11... | collective-permute-start | bytes 7077896 | tf_op jit(solution)/shard_map/ppermute | solution.py:302
  131.0 2.1 reduce_sum.21
  133.1 0.8 reshape.64
  133.9 4.2 %all-to-all-start.3 = ((bf16[16,12,768]{2,1,0:T(8,128)(2,1)}), bf16[16,12,768]{2,1,0:T(8,128)(2,1)S(1)}, u32[]{:S(2)}, u32[]{:S(2)}) async-start(bf16[16,12,768]{2,1,0:T(8,128)(2,1)} %reshape.64), calls=%async_computation.3 | async-start | bytes 786432 | tf_op jit(solution)/shard_map/all_to_all | solution.py:341
  138.1 15.4 %all-to-all-done.3 = bf16[16,12,768]{2,1,0:T(8,128)(2,1)S(1)} async-done(((bf16[16,12,768]{2,1,0:T(8,128)(2,1)}), bf16[16,12,768]{2,1,0:T(8,128)(2,1)S(1)}, u32[]{:S(2)}, u32[]{:S(2)}) %all-to-all-start.3) | async-done | bytes 294944 | tf_op jit(solution)/shard_map/all_to_all | solution.py:341
  153.6 2.2 %collective-permute-start.17 = (f32[6,768]{1,0:T(8,128)S(1)}, f32[6,768]{1,0:T(8,128)S(1)}, u32[]{:S(2)}, u32[]{:S(2)}) collective-permute-start(f32[6,768]{1,0:T(8,128)S(1)} %constant_dynamic-slice_fusion), channel_id=1, source_target_pairs={{0,1},{1,0},{2,3},{3,2},{4,5},{5,4},{6,7},{7,6},{8,9},{9,8},{10,11... | collective-permute-start | bytes 55304 | tf_op jit(solution)/shard_map/ppermute | solution.py:347
  155.8 1.4 copy-done
  157.2 6.4 %shard_map.130 = bf16[128,3072]{1,0:T(8,128)(2,1)} custom-call(s32[1]{0:T(128)} %bitcast.me, bf16[128,3968]{1,0:T(8,128)(2,1)} %bitcast.20, bf16[128,1536]{1,0:T(8,128)(2,1)} %get-tuple-element.33.kept.own_view, f32[6,256,128]{2,1,0:T(8,128)} %get-tuple-element.34.prob_ref, bf16[768,1536]{1,0:T(8,128)(2,1)} %all-gather.2.cloned.1.call-done.w_own.refs_10_, ...), custom_call_target="tpu_custom_call" | custom-call | tf_op jit(solution)/shard_map/pallas_call | solution.py:274
  163.7 4.9 %all-to-all-start.1 = ((bf16[8,16,3072]{2,1,0:T(8,128)(2,1)}), bf16[8,16,3072]{2,1,0:T(8,128)(2,1)S(1)}, u32[]{:S(2)}, u32[]{:S(2)}) async-start(bf16[8,16,3072]{2,1,0:T(8,128)(2,1)} %bitcast.21), calls=%async_computation.1 | async-start | bytes 1572864 | tf_op jit(solution)/shard_map/all_to_all | solution.py:371
  168.5 4.1 %convolution_bitcast_fusion.action = f32[16,1536]{1,0:T(8,128)} fusion(bf16[7,256,1536]{2,1,0:T(8,128)(2,1)} %param.15, s32[16,7]{0,1:T(8,128)S(1)} %copy-done.19), kind=kOutput, calls=%fused_computation | convolution fusion | flops 88109056 | bytes 5603776 | tf_op jit(solution)/shard_map/dot_general | solution.py:354
  172.6 8.0 %shard_map.132 = (bf16[32,3072]{1,0:T(8,128)(2,1)}, bf16[32,3072]{1,0:T(8,128)(2,1)}, bf16[32,3072]{1,0:T(8,128)(2,1)}, bf16[32,3072]{1,0:T(8,128)(2,1)}, bf16[3...) custom-call(s32[1]{0:T(128)} %bitcast.me, ...), custom_call_target="tpu_custom_call" | custom-call | tf_op jit(solution)/shard_map/pallas_call | solution.py:274
  180.6 1.3 collective-permute-start.11
  181.9 1.3 collective-permute-start.12
  183.2 0.4 collective-permute-start.8
  183.6 0.9 collective-permute-start.9
  184.5 2.4 %collective-permute-start.10 = (bf16[32,3072]{1,0:T(8,128)(2,1)}, bf16[32,3072]{1,0:T(8,128)(2,1)S(1)}, u32[]{:S(2)}, u32[]{:S(2)}) collective-permute-start(bf16[32,3072]{1,0:T(8,128)(2,1)} %get-tuple-element.48), channel_id=1, source_target_pairs={{0,3},{1,2},{2,1},{3,0},{4,7},{5,6},{6,5},{7,4},{8,11},{9,10},{10,... | collective-permute-start | bytes 589832 | tf_op jit(solution)/shard_map/ppermute | solution.py:372
  186.9 1.3 collective-permute-start.13
  188.2 1.4 collective-permute-done.12.refs_5_
  189.6 1.3 collective-permute-start.14
  190.9 0.6 pad_maximum_fusion
  191.5 3.5 %collective-permute-done.13.refs_6_ = bf16[32,1536]{1,0:T(8,128)(2,1)S(1)} collective-permute-done((bf16[32,1536]{1,0:T(8,128)(2,1)}, bf16[32,1536]{1,0:T(8,128)(2,1)S(1)}, u32[]{:S(2)}, u32[]{:S(2)}) %collective-permute-start.13) | collective-permute-done | bytes 98336 | tf_op jit(solution)/shard_map/ppermute | solution.py:373
  195.0 3.6 %collective-permute-done.14.refs_7_ = bf16[32,1536]{1,0:T(8,128)(2,1)S(1)} collective-permute-done((bf16[32,1536]{1,0:T(8,128)(2,1)}, bf16[32,1536]{1,0:T(8,128)(2,1)S(1)}, u32[]{:S(2)}, u32[]{:S(2)}) %collective-permute-start.14) | collective-permute-done | bytes 98336 | tf_op jit(solution)/shard_map/ppermute | solution.py:373
  198.6 1.8 collective-permute-done.10.refs_3_
  200.4 0.6 copy-done.14
  201.1 0.3 copy-done.2
  201.3 5.9 %shard_map.133 = (bf16[128,1536]{1,0:T(8,128)(2,1)}, bf16[128,1536]{1,0:T(8,128)(2,1)}, bf16[128,1536]{1,0:T(8,128)(2,1)}, bf16[128,1536]{1,0:T(8,128)(2,1)}) custom-call(s32[1]{0:T(128)} %bitcast.me, bf16[128,3072]{1,0:T(8,128)(2,1)} %bitcast.22, bf16[768,1536]{1,0:T(8,128)(2,1)} %all-gather.2.cloned.1.call-done.w_own.refs_10_, bf16[768,1536]{1,0:T(8,128)(2,1)} %copy-done, ...), custom_call_target="tpu_custom_call" | custom-call | tf_op jit(solution)/shard_map/pallas_call | solution.py:274
  (53 shorter events, 0.2 us)
Async XLA Ops:
  7.2 119.5 %all-gather.2.cloned.1.call-start = ((), (), s32[]{:S(2)}) async-start(), calls=%async_computation.4 | async-start | bytes 2506752 | tf_op jit(solution)/shard_map/all_gather | solution.py:301
  11.7 37.6 %all-to-all-start = ((bf16[8,16,3968]{2,1,0:T(8,128)(2,1)}), bf16[8,16,3968]{2,1,0:T(8,128)(2,1)S(1)}, u32[]{:S(2)}, u32[]{:S(2)}) async-start(bf16[8,16,3968]{2,1,0:T(8,128)(2,1)} %bitcast.23), calls=%async_computation | async-start | bytes 2031616 | tf_op jit(solution)/shard_map/all_to_all | solution.py:312
  17.6 25.3 %collective-permute-start.1 = (bf16[32,3840]{1,0:T(8,128)(2,1)}, bf16[32,3840]{1,0:T(8,128)(2,1)S(1)}, u32[]{:S(2)}, u32[]{:S(2)}) collective-permute-start(bf16[32,3840]{1,0:T(8,128)(2,1)} %get-tuple-element.36), channel_id=1, source_target_pairs={{0,1},{1,0},{2,3},{3,2},{4,5},{5,4},{6,7},{7,6},{8,9},{9,8},{10,11... | collective-permute-start | bytes 737288 | tf_op jit(solution)/shard_map/ppermute | solution.py:313
  18.7 24.2 %collective-permute-start.2 = (bf16[32,3840]{1,0:T(8,128)(2,1)}, bf16[32,3840]{1,0:T(8,128)(2,1)S(1)}, u32[]{:S(2)}, u32[]{:S(2)}) collective-permute-start(bf16[32,3840]{1,0:T(8,128)(2,1)} %get-tuple-element.37), channel_id=1, source_target_pairs={{0,2},{1,3},{2,0},{3,1},{4,6},{5,7},{6,4},{7,5},{8,10},{9,11},{10,... | collective-permute-start | bytes 737288 | tf_op jit(solution)/shard_map/ppermute | solution.py:313
  21.2 23.2 %collective-permute-start.3 = (bf16[32,3840]{1,0:T(8,128)(2,1)}, bf16[32,3840]{1,0:T(8,128)(2,1)S(1)}, u32[]{:S(2)}, u32[]{:S(2)}) collective-permute-start(bf16[32,3840]{1,0:T(8,128)(2,1)} %get-tuple-element.38), channel_id=1, source_target_pairs={{0,3},{1,2},{2,1},{3,0},{4,7},{5,6},{6,5},{7,4},{8,11},{9,10},{10,... | collective-permute-start | bytes 737288 | tf_op jit(solution)/shard_map/ppermute | solution.py:313
  21.9 7.3 %collective-permute-start.4 = (bf16[32,1536]{1,0:T(8,128)(2,1)}, bf16[32,1536]{1,0:T(8,128)(2,1)S(1)}, u32[]{:S(2)}, u32[]{:S(2)}) collective-permute-start(bf16[32,1536]{1,0:T(8,128)(2,1)} %get-tuple-element.39), channel_id=1, source_target_pairs={{0,4},{1,5},{2,6},{3,7},{4,8},{5,9},{6,10},{7,11},{8,12},{9,13},{1... | collective-permute-start | bytes 294920 | tf_op jit(solution)/shard_map/ppermute | solution.py:314
  25.4 9.8 %collective-permute-start.5 = (bf16[32,1536]{1,0:T(8,128)(2,1)}, bf16[32,1536]{1,0:T(8,128)(2,1)S(1)}, u32[]{:S(2)}, u32[]{:S(2)}) collective-permute-start(bf16[32,1536]{1,0:T(8,128)(2,1)} %get-tuple-element.40), channel_id=1, source_target_pairs={{0,5},{1,4},{2,7},{3,6},{4,9},{5,8},{6,11},{7,10},{8,13},{9,12},{1... | collective-permute-start | bytes 294920 | tf_op jit(solution)/shard_map/ppermute | solution.py:314
  29.2 15.2 %copy-start.6 = (bf16[32,1536]{1,0:T(8,128)(2,1)}, bf16[32,1536]{1,0:T(8,128)(2,1)S(1)}, u32[]{:S(2)}) copy-start(bf16[32,1536]{1,0:T(8,128)(2,1)S(1)} %collective-permute-done.4.refs_4_) | copy-start | bytes 294916
  29.3 11.0 %collective-permute-start.6 = (bf16[32,1536]{1,0:T(8,128)(2,1)}, bf16[32,1536]{1,0:T(8,128)(2,1)S(1)}, u32[]{:S(2)}, u32[]{:S(2)}) collective-permute-start(bf16[32,1536]{1,0:T(8,128)(2,1)} %get-tuple-element.41), channel_id=1, source_target_pairs={{0,6},{1,7},{2,4},{3,5},{4,10},{5,11},{6,8},{7,9},{8,14},{9,15},{1... | collective-permute-start | bytes 294920 | tf_op jit(solution)/shard_map/ppermute | solution.py:314
  35.2 9.3 %copy-start.7 = (bf16[32,1536]{1,0:T(8,128)(2,1)}, bf16[32,1536]{1,0:T(8,128)(2,1)S(1)}, u32[]{:S(2)}) copy-start(bf16[32,1536]{1,0:T(8,128)(2,1)S(1)} %collective-permute-done.5.refs_5_) | copy-start | bytes 294916
  35.2 7.7 %collective-permute-start.7 = (bf16[32,1536]{1,0:T(8,128)(2,1)}, bf16[32,1536]{1,0:T(8,128)(2,1)S(1)}, u32[]{:S(2)}, u32[]{:S(2)}) collective-permute-start(bf16[32,1536]{1,0:T(8,128)(2,1)} %get-tuple-element.42), channel_id=1, source_target_pairs={{0,7},{1,6},{2,5},{3,4},{4,11},{5,10},{6,9},{7,8},{8,15},{9,14},{1... | collective-permute-start | bytes 294920 | tf_op jit(solution)/shard_map/ppermute | solution.py:314
  40.3 4.2 %copy-start.8 = (bf16[32,1536]{1,0:T(8,128)(2,1)}, bf16[32,1536]{1,0:T(8,128)(2,1)S(1)}, u32[]{:S(2)}) copy-start(bf16[32,1536]{1,0:T(8,128)(2,1)S(1)} %collective-permute-done.6.refs_6_) | copy-start | bytes 294916
  42.9 1.5 copy-start.9
  42.9 1.5 copy-start.3
  42.9 1.5 copy-start.4
  44.4 0.7 copy-start.5
  49.3 4.6 %collective-permute-start.16 = (bf16[128,1536]{1,0:T(8,128)(2,1)}, bf16[128,1536]{1,0:T(8,128)(2,1)S(1)}, u32[]{:S(2)}, u32[]{:S(2)}) collective-permute-start(bf16[128,1536]{1,0:T(8,128)(2,1)} %get-tuple-element.58), channel_id=1, source_target_pairs={{0,1},{1,0},{2,3},{3,2},{4,5},{5,4},{6,7},{7,6},{8,9},{9,8},{10,11... | collective-permute-start | bytes 1179656 | tf_op jit(solution)/shard_map/ppermute | solution.py:330
  49.3 1.0 copy-start.1
  53.5 2.1 collective-permute-start.15
  54.0 1.6 copy-start.10
  55.5 0.7 copy-start.11
  59.8 71.2 %all-to-all-start.2 = ((bf16[8,192,768]{2,1,0:T(8,128)(2,1)}), bf16[8,192,768]{2,1,0:T(8,128)(2,1)}, u32[]{:S(2)}, u32[]{:S(2)}) async-start(bf16[8,192,768]{2,1,0:T(8,128)(2,1)} %bitcast.18), calls=%async_computation.2 | async-start | bytes 4718592 | tf_op jit(solution)/shard_map/all_to_all | solution.py:338
  126.7 29.1 %collective-permute-start = (bf16[768,1536]{1,0:T(8,128)(2,1)}, bf16[768,1536]{1,0:T(8,128)(2,1)S(1)}, u32[]{:S(2)}, u32[]{:S(2)}) collective-permute-start(bf16[768,1536]{1,0:T(8,128)(2,1)} %all-gather.2.cloned.1.call-done.w_own.refs_10_), channel_id=1, source_target_pairs={{0,1},{1,0},{2,3},{3,2},{4,5},{5,4},{6,7},{7,6},{8,9},{9,8},{10,11... | collective-permute-start | bytes 7077896 | tf_op jit(solution)/shard_map/ppermute | solution.py:302
  133.9 19.6 %all-to-all-start.3 = ((bf16[16,12,768]{2,1,0:T(8,128)(2,1)}), bf16[16,12,768]{2,1,0:T(8,128)(2,1)S(1)}, u32[]{:S(2)}, u32[]{:S(2)}) async-start(bf16[16,12,768]{2,1,0:T(8,128)(2,1)} %reshape.64), calls=%async_computation.3 | async-start | bytes 786432 | tf_op jit(solution)/shard_map/all_to_all | solution.py:341
  153.6 29.6 %collective-permute-start.17 = (f32[6,768]{1,0:T(8,128)S(1)}, f32[6,768]{1,0:T(8,128)S(1)}, u32[]{:S(2)}, u32[]{:S(2)}) collective-permute-start(f32[6,768]{1,0:T(8,128)S(1)} %constant_dynamic-slice_fusion), channel_id=1, source_target_pairs={{0,1},{1,0},{2,3},{3,2},{4,5},{5,4},{6,7},{7,6},{8,9},{9,8},{10,11... | collective-permute-start | bytes 55304 | tf_op jit(solution)/shard_map/ppermute | solution.py:347
  155.8 1.4 copy-start
  157.2 11.3 %copy-start.19 = (s32[16,7]{0,1:T(8,128)S(1)}, s32[16,7]{0,1:T(8,128)}, u32[]{:S(2)}) copy-start(s32[16,7]{0,1:T(8,128)} %param.14) | copy-start | bytes 1348
  163.7 36.7 %all-to-all-start.1 = ((bf16[8,16,3072]{2,1,0:T(8,128)(2,1)}), bf16[8,16,3072]{2,1,0:T(8,128)(2,1)S(1)}, u32[]{:S(2)}, u32[]{:S(2)}) async-start(bf16[8,16,3072]{2,1,0:T(8,128)(2,1)} %bitcast.21), calls=%async_computation.1 | async-start | bytes 1572864 | tf_op jit(solution)/shard_map/all_to_all | solution.py:371
  180.6 6.4 %collective-permute-start.11 = (bf16[32,1536]{1,0:T(8,128)(2,1)}, bf16[32,1536]{1,0:T(8,128)(2,1)S(1)}, u32[]{:S(2)}, u32[]{:S(2)}) collective-permute-start(bf16[32,1536]{1,0:T(8,128)(2,1)} %get-tuple-element.49), channel_id=1, source_target_pairs={{4,0},{5,1},{6,2},{7,3},{8,4},{9,5},{10,6},{11,7},{12,8},{13,9},{1... | collective-permute-start | bytes 294920 | tf_op jit(solution)/shard_map/ppermute | solution.py:373
  181.9 7.7 %collective-permute-start.12 = (bf16[32,1536]{1,0:T(8,128)(2,1)}, bf16[32,1536]{1,0:T(8,128)(2,1)S(1)}, u32[]{:S(2)}, u32[]{:S(2)}) collective-permute-start(bf16[32,1536]{1,0:T(8,128)(2,1)} %get-tuple-element.50), channel_id=1, source_target_pairs={{5,0},{4,1},{7,2},{6,3},{9,4},{8,5},{11,6},{10,7},{13,8},{12,9},{1... | collective-permute-start | bytes 294920 | tf_op jit(solution)/shard_map/ppermute | solution.py:373
  183.2 15.4 %collective-permute-start.8 = (bf16[32,3072]{1,0:T(8,128)(2,1)}, bf16[32,3072]{1,0:T(8,128)(2,1)S(1)}, u32[]{:S(2)}, u32[]{:S(2)}) collective-permute-start(bf16[32,3072]{1,0:T(8,128)(2,1)} %get-tuple-element.46), channel_id=1, source_target_pairs={{0,1},{1,0},{2,3},{3,2},{4,5},{5,4},{6,7},{7,6},{8,9},{9,8},{10,11... | collective-permute-start | bytes 589832 | tf_op jit(solution)/shard_map/ppermute | solution.py:372
  183.6 15.0 %collective-permute-start.9 = (bf16[32,3072]{1,0:T(8,128)(2,1)}, bf16[32,3072]{1,0:T(8,128)(2,1)S(1)}, u32[]{:S(2)}, u32[]{:S(2)}) collective-permute-start(bf16[32,3072]{1,0:T(8,128)(2,1)} %get-tuple-element.47), channel_id=1, source_target_pairs={{0,2},{1,3},{2,0},{3,1},{4,6},{5,7},{6,4},{7,5},{8,10},{9,11},{10,... | collective-permute-start | bytes 589832 | tf_op jit(solution)/shard_map/ppermute | solution.py:372
  184.5 15.8 %collective-permute-start.10 = (bf16[32,3072]{1,0:T(8,128)(2,1)}, bf16[32,3072]{1,0:T(8,128)(2,1)S(1)}, u32[]{:S(2)}, u32[]{:S(2)}) collective-permute-start(bf16[32,3072]{1,0:T(8,128)(2,1)} %get-tuple-element.48), channel_id=1, source_target_pairs={{0,3},{1,2},{2,1},{3,0},{4,7},{5,6},{6,5},{7,4},{8,11},{9,10},{10,... | collective-permute-start | bytes 589832 | tf_op jit(solution)/shard_map/ppermute | solution.py:372
  186.9 13.4 %copy-start.15 = (bf16[32,1536]{1,0:T(8,128)(2,1)}, bf16[32,1536]{1,0:T(8,128)(2,1)S(1)}, u32[]{:S(2)}) copy-start(bf16[32,1536]{1,0:T(8,128)(2,1)S(1)} %collective-permute-done.11.refs_4_) | copy-start | bytes 294916
  186.9 8.1 %collective-permute-start.13 = (bf16[32,1536]{1,0:T(8,128)(2,1)}, bf16[32,1536]{1,0:T(8,128)(2,1)S(1)}, u32[]{:S(2)}, u32[]{:S(2)}) collective-permute-start(bf16[32,1536]{1,0:T(8,128)(2,1)} %get-tuple-element.51), channel_id=1, source_target_pairs={{6,0},{7,1},{4,2},{5,3},{10,4},{11,5},{8,6},{9,7},{14,8},{15,9},{1... | collective-permute-start | bytes 294920 | tf_op jit(solution)/shard_map/ppermute | solution.py:373
  189.6 10.8 %copy-start.16 = (bf16[32,1536]{1,0:T(8,128)(2,1)}, bf16[32,1536]{1,0:T(8,128)(2,1)S(1)}, u32[]{:S(2)}) copy-start(bf16[32,1536]{1,0:T(8,128)(2,1)S(1)} %collective-permute-done.12.refs_5_) | copy-start | bytes 294916
  189.6 9.0 %collective-permute-start.14 = (bf16[32,1536]{1,0:T(8,128)(2,1)}, bf16[32,1536]{1,0:T(8,128)(2,1)S(1)}, u32[]{:S(2)}, u32[]{:S(2)}) collective-permute-start(bf16[32,1536]{1,0:T(8,128)(2,1)} %get-tuple-element.52), channel_id=1, source_target_pairs={{7,0},{6,1},{5,2},{4,3},{11,4},{10,5},{9,6},{8,7},{15,8},{14,9},{1... | collective-permute-start | bytes 294920 | tf_op jit(solution)/shard_map/ppermute | solution.py:373
  195.0 5.4 %copy-start.17 = (bf16[32,1536]{1,0:T(8,128)(2,1)}, bf16[32,1536]{1,0:T(8,128)(2,1)S(1)}, u32[]{:S(2)}) copy-start(bf16[32,1536]{1,0:T(8,128)(2,1)S(1)} %collective-permute-done.13.refs_6_) | copy-start | bytes 294916
  198.6 1.8 copy-start.18
  198.6 1.8 copy-start.12
  198.6 1.8 copy-start.13
  200.4 0.7 copy-start.14
  200.4 1.0 copy-start.2
Sparse Core Ops, SparseCore 0:
  10.6 116.0 all-gather.1

commit v3 on v2

--- a/solution.py
+++ b/solution.py
@@ -166,18 +166,24 @@
         out_ref[i * CW : (i + 1) * CW, :] = (dot_tn(left, right) * scale).astype(BF)
 
 
-def fetch_weight(me, own, other, held, sem, first, count):
-    size = held.shape[0] // count
-    core = me[0] % 2
+def fetch_weight(me, own, others, held, sem, first, count):
+    size = held.shape[0] // (4 * count)
+    core, y = me[0] % 2, me[0] // 2
     copies = []
-    for i in range(count // 2):
-        for which_at, (which, ref) in enumerate(((core, own), (1 - core, other))):
-            start = pl.multiple_of((2 * i + which) * size, 16)
-            copies.append(
-                pltpu.make_async_copy(
-                    ref.at[pl.ds((first // 2 + i) * size, size)], held.at[pl.ds(start, size)], sem.at[2 * i + which_at]
+    for z in range(count):
+        other = others[z * len(others) // count]
+        for e in range(2):
+            for n, (which, ref, place) in enumerate(
+                ((core, own, 2 * (first + z) + e), (1 - core, other, 2 * (z % (count // len(others))) + e))
+            ):
+                start = pl.multiple_of((4 * z + 2 * (y ^ e) + which) * size, 16)
+                copies.append(
+                    pltpu.make_async_copy(
+                        ref.at[pl.ds(place * size, size)],
+                        held.at[pl.ds(start, size)],
+                        sem.at[4 * z + 2 * e + n],
+                    )
                 )
-            )
     for copy in copies:
         copy.start()
     return copies
@@ -194,27 +200,31 @@
     return dq, dk, dv
 
 
-def view_backward_kernel(blocks, me, x, kept, prob_ref, w_own, w_other, out_ref, w, sem):
-    copies = fetch_weight(me, w_own, w_other, w, sem, 0, blocks // 2)
-    out_ref[:, :CW] = kept[:, :CW]
+def view_backward_kernel(depth, me, cam, x, kept, prob_ref, w_own, w_other, *rest):
+    out_refs, (held, w, sem) = rest[:-3], rest[-3:]
+    copies = fetch_weight(me, w_own, (w_other,), w, sem, 0, depth // 2)
+    held[:, :CW] = kept[:, :CW]
     for copy in copies:
         copy.wait()
     grad = dot_nt(x[:, 3 * CW : 5 * CW], w[...]).astype(BF)
     for j in range(PAIRS):
         at = [slice(i * CW + 128 * j, i * CW + 128 * (j + 1)) for i in range(4)]
         dq, dk, dv = backward_pair(x[:, at[0]], x[:, at[1]], x[:, at[2]], grad[:, at[0]], prob_ref[j])
-        out_ref[:, at[1]] = dq.astype(BF)
-        out_ref[:, at[2]] = dk.astype(BF)
-        out_ref[:, at[3]] = dv.astype(BF)
-
-
-def time_backward_kernel(blocks, me, *refs):
+        held[:, at[1]] = dq.astype(BF)
+        held[:, at[2]] = dk.astype(BF)
+        held[:, at[3]] = dv.astype(BF)
+    size = held.shape[0] // len(out_refs)
+    for d, out in enumerate(out_refs):
+        out[...] = held[pl.ds(pl.multiple_of((cam[0] ^ d) * size, size), size), :]
+
+
+def time_backward_kernel(depth, me, *refs):
     x, prev = refs[:GROUP], refs[GROUP : 2 * GROUP]
     kept, prob_ref, w_own, w_other = refs[2 * GROUP : 2 * GROUP + 4]
     out_refs = refs[2 * GROUP + 4 : 3 * GROUP + 4]
     back_refs = refs[3 * GROUP + 4 : 4 * GROUP + 4]
     w, sem = refs[4 * GROUP + 4 :]
-    copies = fetch_weight(me, w_own, w_other, w, sem, blocks // 2, blocks // 2)
+    copies = fetch_weight(me, w_own, (w_other,), w, sem, depth // 2, depth // 2)
     size = x[0].shape[0]
     rows = GROUP * size
 
@@ -239,10 +249,13 @@
         store(out_refs, at[3], dv[rows:])
 
 
-def finish_kernel(blocks, me, view, w_own, w_other, action, *refs):
-    time, back = refs[:GROUP], refs[GROUP : 2 * GROUP]
-    pred_ref, dq_ref, dk_ref, dv_ref, w, sem = refs[2 * GROUP :]
-    copies = fetch_weight(me, w_own, w_other, w, sem, 0, blocks)
+def finish_kernel(depth, cams, me, cam, w_own, w_view, w_time, action, *refs):
+    time, back, blocks = refs[:GROUP], refs[GROUP : 2 * GROUP], refs[2 * GROUP : 2 * GROUP + cams]
+    pred_ref, dq_ref, dk_ref, dv_ref, view, w, sem = refs[2 * GROUP + cams :]
+    copies = fetch_weight(me, w_own, (w_view, w_time), w, sem, 0, depth)
+    size = blocks[0].shape[0]
+    for d, part in enumerate(blocks):
+        view[pl.ds(pl.multiple_of((cam[0] ^ d) * size, size), size), :] = part[...]
     rows = view.shape[0]
     frames = rows // 8
     row = iota((rows, rows), 0)
@@ -271,7 +284,7 @@
 
 def call(kernel, outs, specs, *args, scratch=()):
     specs = [whole(arg.shape) if spec is VM else spec for spec, arg in zip(specs, args)]
-    return pl.pallas_call(
+    return list(pl.pallas_call(
         kernel,
         out_shape=[jax.ShapeDtypeStruct(shape, kind) for shape, kind in outs],
         in_specs=specs,
@@ -279,7 +292,7 @@
         grid=(1,),
         scratch_shapes=list(scratch),
         compiler_params=params(),
-    )(*args)
+    )(*args))
 
 
 def shards(queries, keys, values, cam_valid, windows, actions, act_table, w_out, cotangent):
@@ -298,8 +311,13 @@
     inward = [[((i + GROUP) ^ d, i) for i in range(tm - GROUP)] for d in range(GROUP)]
     within = [[(i, i ^ d) for i in range(tm)] for d in range(GROUP)]
 
-    w_own = lax.all_gather(w_out, "tm", axis=0, tiled=True, axis_index_groups=same_core)
-    w_other = lax.ppermute(w_own, "tm", swap)
+    depth = tm // GROUP
+    along_z = [[GROUP * i + j for i in range(depth)] for j in range(GROUP)]
+    beside = [(i, i ^ (tm + 2)) for i in range(cams * tm)]
+    w_both = jnp.concatenate([w_out, lax.ppermute(w_out, ("cam", "tm"), beside)], axis=0)
+    w_own = lax.all_gather(w_both, "tm", axis=0, tiled=True, axis_index_groups=along_z)
+    w_view = lax.ppermute(w_own[:CW // 2], "tm", swap)
+    w_time = lax.ppermute(w_own[CW // 2:], "tm", swap)
     q, k, v, ct = (a.reshape(rows, width) for a in (queries, keys, values, cotangent))
     packed = call(
         pack_kernel,
@@ -312,6 +330,11 @@
     view_x = lax.all_to_all(view_send, "cam", 0, 0, tiled=True)
     time_x = [time_send[0]] + [lax.ppermute(time_send[d], "tm", within[d]) for d in range(1, GROUP)]
     prev = [lax.ppermute(kv_send[d], "tm", onward[d]) for d in range(GROUP)]
+
+    codes = jnp.arange(act_table.shape[1])
+    one_hot = (actions[:, :, None] == codes[None, None, :]).astype(BF).reshape(frames, -1)
+    action_sum = jnp.dot(one_hot, act_table.reshape(-1, width), preferred_element_type=F32)
+    view_x, action_sum = lax.optimization_barrier((view_x, action_sum))
 
     kept_view, view_swap, prob_view = call(
         view_forward_kernel,
@@ -336,6 +359,24 @@
         kept_view, view_swap, kept_time, time_swap,
     )
     part = lax.all_to_all(part.reshape(cams, width // cams, CW), "cam", 0, 0, tiled=True)
+    half_weight = [pltpu.VMEM((CW, width), BF), pltpu.SemaphoreType.DMA((tm // 2,))]
+    cam = lax.axis_index("cam").reshape(1)
+    share = rows // cams
+    view_out = call(
+        functools.partial(view_backward_kernel, depth),
+        [((share, 4 * CW), BF)] * cams,
+        [SM, SM] + [VM] * 3 + [ANY] * 2,
+        me, cam, view_x, kept_view, prob_view, w_own, w_view,
+        scratch=[pltpu.VMEM((rows, 4 * CW), BF)] + half_weight,
+    )
+    returned = call(
+        functools.partial(time_backward_kernel, depth),
+        [((block, 4 * CW), BF)] * GROUP + [((block, 2 * CW), BF)] * GROUP,
+        [SM] + [VM] * (2 * GROUP + 2) + [ANY] * 2,
+        me, *time_x, *prev, kept_time, prob_time, w_own, w_time,
+        scratch=half_weight,
+    )
+    part, view_out[0], returned[0] = lax.optimization_barrier((part, view_out[0], returned[0]))
     part = jnp.sum(part.astype(F32), axis=0).astype(BF)
     chips = tm // 2
     part = lax.all_to_all(
@@ -349,34 +390,21 @@
         [jnp.where(core == 0, mine, theirs), jnp.where(core == 0, theirs, mine)], axis=1
     )
 
-    codes = jnp.arange(act_table.shape[1])
-    one_hot = (actions[:, :, None] == codes[None, None, :]).astype(BF).reshape(frames, -1)
-    action_sum = jnp.dot(one_hot, act_table.reshape(-1, width), preferred_element_type=F32)
-
-    half_weight = [pltpu.VMEM((CW, width), BF), pltpu.SemaphoreType.DMA((tm // 2,))]
-    (view_back,) = call(
-        functools.partial(view_backward_kernel, tm),
-        [((rows, 4 * CW), BF)],
-        [SM] + [VM] * 3 + [ANY] * 2,
-        me, view_x, kept_view, prob_view, w_own, w_other,
-        scratch=half_weight,
-    )
-    returned = call(
-        functools.partial(time_backward_kernel, tm),
-        [((block, 4 * CW), BF)] * GROUP + [((block, 2 * CW), BF)] * GROUP,
-        [SM] + [VM] * (2 * GROUP + 2) + [ANY] * 2,
-        me, *time_x, *prev, kept_time, prob_time, w_own, w_other,
-        scratch=half_weight,
-    )
-    view_back = lax.all_to_all(view_back, "cam", 0, 0, tiled=True)
+    view_back = [view_out[0]] + [
+        lax.ppermute(view_out[d], "cam", [(i, i ^ d) for i in range(cams)]) for d in range(1, cams)
+    ]
     time_back = [returned[0]] + [lax.ppermute(returned[d], "tm", within[d]) for d in range(1, GROUP)]
     back = [lax.ppermute(returned[GROUP + d], "tm", inward[d]) for d in range(GROUP)]
     outs = call(
-        functools.partial(finish_kernel, tm),
+        functools.partial(finish_kernel, depth, cams),
         [((rows, width), BF)] * 4,
-        [SM, VM] + [ANY] * 2 + [VM] * (2 * GROUP + 1),
-        me, view_back, w_own, w_other, action_sum, *time_back, *back,
-        scratch=[pltpu.VMEM((width, width), BF), pltpu.SemaphoreType.DMA((tm,))],
+        [SM, SM] + [ANY] * 3 + [VM] * (2 * GROUP + 1 + cams),
+        me, cam, w_own, w_view, w_time, action_sum, *time_back, *back, *view_back,
+        scratch=[
+            pltpu.VMEM((rows, 4 * CW), BF),
+            pltpu.VMEM((width, width), BF),
+            pltpu.SemaphoreType.DMA((tm,)),
+        ],
     )
     return tuple(a.reshape(1, frames, tokens, width) for a in outs) + (grad_out_weight,)
 

time: 216 us -> 178 us (0.82)
  the two profiles are of different devices: /device:TPU:1 before, /device:TPU:193 now
where the time goes in v3:
time: 178 us; the launch traced here: 177 us
  starting transfers between devices  73.8 us (41%)
  waiting for transfers between devices  37.4 us (21%)
  Pallas kernels  35.1 us (20%)
  between operations  14.5 us (8%)
  local copies, waits for them, and re-layouts  9.04 us (5%)
  matrix products  4.09 us (2%)
  other arithmetic  2.78 us (2%)
    pallas_call x7, Pallas kernels, call(): pl.pallas_call(kernel, out_shape=[jax.ShapeDtypeStruct(shape, kind) for s...  35.1 us
    ppermute x4, starting transfers between devices, shards(): lax.ppermute(returned[GROUP + d], 'tm', inward[d])  20.7 us
    ppermute x4, starting transfers between devices, shards(): prev = [lax.ppermute(kv_send[d], 'tm', onward[d]) for d in range(GROUP)]  11.4 us
    all_to_all x1, waiting for transfers between devices, shards(): lax.all_to_all(part.reshape(cams, width // cams, CW), 'cam', 0, 0, tiled=...  10.9 us
    all_to_all x1, starting transfers between devices, shards(): lax.all_to_all(part.reshape(chips, width // cams // chips, CW), 'tm', 0,...  9.88 us
    ppermute x7, starting transfers between devices, shards(): lax.ppermute(view_out[d], 'cam', [(i, i ^ d) for i in range(cams)])  9.19 us
    ppermute x3, waiting for transfers between devices, shards(): lax.ppermute(time_send[d], 'tm', within[d])  6.73 us
    ppermute x4, waiting for transfers between devices, shards(): lax.ppermute(returned[GROUP + d], 'tm', inward[d])  5.89 us
  transfers between devices with their start and end apart: 31, of which 10 were waited for; matrix products, arithmetic and copies ran while one was open for 4% of the time, Pallas kernels for 20%

profile of v3, /device:TPU:193, one launch (start us, length us, event | category | flops | bytes accessed | tf_op | source)
XLA Modules:
  0.0 176.8 jit_solution(16647440442806800252)
XLA Ops:
  7.2 2.8 %collective-permute-start = (bf16[48,1536]{1,0:T(8,128)(2,1)}, bf16[48,1536]{1,0:T(8,128)(2,1)S(1)}, u32[]{:S(2)}, u32[]{:S(2)}) collective-permute-start(bf16[48,1536]{1,0:T(8,128)(2,1)} %param.16), channel_id=1, source_target_pairs={{0,34},{1,35},{2,32},{3,33},{4,38},{5,39},{6,36},{7,37},{8,42},{9,... | collective-permute-start | bytes 442376 | tf_op jit(solution)/shard_map/ppermute | solution.py:317
  10.0 3.5 %collective-permute-done = bf16[48,1536]{1,0:T(8,128)(2,1)S(1)} collective-permute-done((bf16[48,1536]{1,0:T(8,128)(2,1)}, bf16[48,1536]{1,0:T(8,128)(2,1)S(1)}, u32[]{:S(2)}, u32[]{:S(2)}) %collective-permute-start) | collective-permute-done | bytes 147488 | tf_op jit(solution)/shard_map/ppermute | solution.py:317
  13.6 1.6 pad_maximum_fusion
  15.3 3.8 %shard_map.128 = (bf16[128,3968]{1,0:T(8,128)(2,1)}, bf16[32,3840]{1,0:T(8,128)(2,1)}, bf16[32,3840]{1,0:T(8,128)(2,1)}, bf16[32,3840]{1,0:T(8,128)(2,1)}, bf16[...) custom-call(s32[1]{0:T(128)} %bitcast.me, ...), custom_call_target="tpu_custom_call" | custom-call | tf_op jit(solution)/shard_map/pallas_call | solution.py:287
  19.1 4.0 %all-to-all-start = ((bf16[8,16,3968]{2,1,0:T(8,128)(2,1)}), bf16[8,16,3968]{2,1,0:T(8,128)(2,1)S(1)}, u32[]{:S(2)}, u32[]{:S(2)}) async-start(bf16[8,16,3968]{2,1,0:T(8,128)(2,1)} %bitcast.20), calls=%async_computation | async-start | bytes 2031616 | tf_op jit(solution)/shard_map/all_to_all | solution.py:330
  23.1 2.6 %collective-permute-start.7 = (bf16[32,1536]{1,0:T(8,128)(2,1)}, bf16[32,1536]{1,0:T(8,128)(2,1)S(1)}, u32[]{:S(2)}, u32[]{:S(2)}) collective-permute-start(bf16[32,1536]{1,0:T(8,128)(2,1)} %get-tuple-element.54), channel_id=1, source_target_pairs={{0,4},{1,5},{2,6},{3,7},{4,8},{5,9},{6,10},{7,11},{8,12},{9,13},{1... | collective-permute-start | bytes 294920 | tf_op jit(solution)/shard_map/ppermute | solution.py:332
  25.8 2.9 %collective-permute-start.8 = (bf16[32,1536]{1,0:T(8,128)(2,1)}, bf16[32,1536]{1,0:T(8,128)(2,1)S(1)}, u32[]{:S(2)}, u32[]{:S(2)}) collective-permute-start(bf16[32,1536]{1,0:T(8,128)(2,1)} %get-tuple-element.55), channel_id=1, source_target_pairs={{0,5},{1,4},{2,7},{3,6},{4,9},{5,8},{6,11},{7,10},{8,13},{9,12},{1... | collective-permute-start | bytes 294920 | tf_op jit(solution)/shard_map/ppermute | solution.py:332
  28.7 2.9 %collective-permute-start.9 = (bf16[32,1536]{1,0:T(8,128)(2,1)}, bf16[32,1536]{1,0:T(8,128)(2,1)S(1)}, u32[]{:S(2)}, u32[]{:S(2)}) collective-permute-start(bf16[32,1536]{1,0:T(8,128)(2,1)} %get-tuple-element.56), channel_id=1, source_target_pairs={{0,6},{1,7},{2,4},{3,5},{4,10},{5,11},{6,8},{7,9},{8,14},{9,15},{1... | collective-permute-start | bytes 294920 | tf_op jit(solution)/shard_map/ppermute | solution.py:332
  31.6 3.0 %collective-permute-start.10 = (bf16[32,1536]{1,0:T(8,128)(2,1)}, bf16[32,1536]{1,0:T(8,128)(2,1)S(1)}, u32[]{:S(2)}, u32[]{:S(2)}) collective-permute-start(bf16[32,1536]{1,0:T(8,128)(2,1)} %get-tuple-element.57), channel_id=1, source_target_pairs={{0,7},{1,6},{2,5},{3,4},{4,11},{5,10},{6,9},{7,8},{8,15},{9,14},{1... | collective-permute-start | bytes 294920 | tf_op jit(solution)/shard_map/ppermute | solution.py:332
  34.6 1.1 collective-permute-start.4
  35.7 1.6 collective-permute-start.5
  37.6 3.0 %collective-permute-start.6 = (bf16[32,3840]{1,0:T(8,128)(2,1)}, bf16[32,3840]{1,0:T(8,128)(2,1)S(1)}, u32[]{:S(2)}, u32[]{:S(2)}) collective-permute-start(bf16[32,3840]{1,0:T(8,128)(2,1)} %get-tuple-element.53), channel_id=1, source_target_pairs={{0,3},{1,2},{2,1},{3,0},{4,7},{5,6},{6,5},{7,4},{8,11},{9,10},{10,... | collective-permute-start | bytes 737288 | tf_op jit(solution)/shard_map/ppermute | solution.py:331
  40.6 4.1 %convolution_bitcast_fusion.action = f32[16,1536]{1,0:T(8,128)} fusion(bf16[7,256,1536]{2,1,0:T(8,128)(2,1)} %param.15, s32[16,7]{0,1:T(8,128)S(1)} %copy-done.25), kind=kOutput, calls=%fused_computation | convolution fusion | flops 88109056 | bytes 5603776 | tf_op jit(solution)/shard_map/dot_general | solution.py:336
  44.7 4.0 %collective-permute-done.10.refs_7_ = bf16[32,1536]{1,0:T(8,128)(2,1)S(1)} collective-permute-done((bf16[32,1536]{1,0:T(8,128)(2,1)}, bf16[32,1536]{1,0:T(8,128)(2,1)S(1)}, u32[]{:S(2)}, u32[]{:S(2)}) %collective-permute-start.10) | collective-permute-done | bytes 98336 | tf_op jit(solution)/shard_map/ppermute | solution.py:332
  48.6 1.5 collective-permute-done.5.refs_2_
  50.1 5.3 %collective-permute-done.6.refs_3_ = bf16[32,3840]{1,0:T(8,128)(2,1)S(1)} collective-permute-done((bf16[32,3840]{1,0:T(8,128)(2,1)}, bf16[32,3840]{1,0:T(8,128)(2,1)S(1)}, u32[]{:S(2)}, u32[]{:S(2)}) %collective-permute-start.6) | collective-permute-done | bytes 245792 | tf_op jit(solution)/shard_map/ppermute | solution.py:331
  55.4 0.7 copy-done.4
  56.1 4.2 %shard_map.130 = (bf16[128,1536]{1,0:T(8,128)(2,1)}, bf16[128,1536]{1,0:T(8,128)(2,1)}, f32[6,256,256]{2,1,0:T(8,128)}) custom-call(s32[12]{0:T(128)} %windows.1, s32[1]{0:T(128)} %bitcast.me, s32[1]{0:T(128)} %bitcast.9.block, bf16[32,3840]{1,0:T(8,128)(2,1)} %get-tuple-element.50.refs_0_, bf16[32,3840]{1,0:T(8,128)(2,1)} %copy-done.2, ...), custom_call_target="tpu_custom_call" | custom-call | tf_op jit(solution)/shard_map/pallas_call | solution.py:287
  60.7 1.0 copy-done
  61.6 3.1 %shard_map.129 = (bf16[128,1536]{1,0:T(8,128)(2,1)}, bf16[128,1536]{1,0:T(8,128)(2,1)}, f32[6,256,128]{2,1,0:T(8,128)}) custom-call(s32[1]{0:T(128)} %bitcast.me, bf16[128,3968]{1,0:T(8,128)(2,1)} %bitcast.18), custom_call_target="tpu_custom_call" | custom-call | tf_op jit(solution)/shard_map/pallas_call | solution.py:287
  64.9 1.8 %collective-permute-done.3.other_view = bf16[128,1536]{1,0:T(8,128)(2,1)S(1)} collective-permute-done((bf16[128,1536]{1,0:T(8,128)(2,1)}, bf16[128,1536]{1,0:T(8,128)(2,1)S(1)}, u32[]{:S(2)}, u32[]{:S(2)}) %collective-permute-start.3) | collective-permute-done | bytes 393248 | tf_op jit(solution)/shard_map/ppermute | solution.py:352
  66.7 0.7 copy-done.10
  67.5 3.6 %shard_map.131 = bf16[1536,768]{1,0:T(8,128)(2,1)} custom-call(bf16[128,1536]{1,0:T(8,128)(2,1)} %get-tuple-element.48.own_view.kept, bf16[128,1536]{1,0:T(8,128)(2,1)} %copy-done.10, bf16[128,1536]{1,0:T(8,128)(2,1)} %get-tuple-element.58.own_time.refs_8_, bf16[128,1536]{1,0:T(8,128)(2,1)} %copy-done.9), custom_call_target="tpu_custom_call" | custom-call | tf_op jit(solution)/shard_map/pallas_call | solution.py:287
  71.1 3.9 %all-to-all-start.1 = ((bf16[8,192,768]{2,1,0:T(8,128)(2,1)}), bf16[8,192,768]{2,1,0:T(8,128)(2,1)S(1)}, u32[]{:S(2)}, u32[]{:S(2)}) async-start(bf16[8,192,768]{2,1,0:T(8,128)(2,1)} %bitcast.17), calls=%async_computation.1 | async-start | bytes 4718592 | tf_op jit(solution)/shard_map/all_to_all | solution.py:361
  75.0 3.3 %fusion.1 = (bf16[384,1536]{1,0:T(8,128)(2,1)}, bf16[384,1536]{1,0:T(8,128)(2,1)}) fusion(bf16[768,1536]{1,0:T(8,128)(2,1)} %all-gather.2.cloned.1.call-done.w_own.refs_10_), kind=kLoop, calls=%fused_computation.9 | loop fusion | bytes 4718592 | tf_op jit(solution)/shard_map/slice | solution.py:320
  78.8 4.2 %collective-permute-done.2.refs_11_.w_time = bf16[384,1536]{1,0:T(8,128)(2,1)S(1)} collective-permute-done((bf16[384,1536]{1,0:T(8,128)(2,1)}, bf16[384,1536]{1,0:T(8,128)(2,1)S(1)}, u32[]{:S(2)}, u32[]{:S(2)}) %collective-permute-start.2) | collective-permute-done | bytes 1179680 | tf_op jit(solution)/shard_map/ppermute | solution.py:320
  83.1 1.1 copy-done.1
  84.2 8.0 %shard_map.133 = (bf16[32,3072]{1,0:T(8,128)(2,1)}, bf16[32,3072]{1,0:T(8,128)(2,1)}, bf16[32,3072]{1,0:T(8,128)(2,1)}, bf16[32,3072]{1,0:T(8,128)(2,1)}, bf16[3...) custom-call(s32[1]{0:T(128)} %bitcast.me, ...), custom_call_target="tpu_custom_call" | custom-call | tf_op jit(solution)/shard_map/pallas_call | solution.py:287
  92.2 6.5 %shard_map.132 = (bf16[16,3072]{1,0:T(8,128)(2,1)}, bf16[16,3072]{1,0:T(8,128)(2,1)}, bf16[16,3072]{1,0:T(8,128)(2,1)}, bf16[16,3072]{1,0:T(8,128)(2,1)}, bf16[1...) custom-call(s32[1]{0:T(128)} %bitcast.me, s32[1]{0:T(128)} %bitcast.1.cam, ...), custom_call_target="tpu_custom_call" | custom-call | tf_op jit(solution)/shard_map/pallas_call | solution.py:287
  98.7 10.9 %all-to-all-done.1 = bf16[8,192,768]{2,1,0:T(8,128)(2,1)S(1)} async-done(((bf16[8,192,768]{2,1,0:T(8,128)(2,1)}), bf16[8,192,768]{2,1,0:T(8,128)(2,1)S(1)}, u32[]{:S(2)}, u32[]{:S(2)}) %all-to-all-start.1) | async-done | bytes 2359328 | tf_op jit(solution)/shard_map/all_to_all | solution.py:361
  110.0 0.8 reshape.66
  110.8 9.9 %all-to-all-start.2 = ((bf16[16,12,768]{2,1,0:T(8,128)(2,1)}), bf16[16,12,768]{2,1,0:T(8,128)(2,1)S(1)}, u32[]{:S(2)}, u32[]{:S(2)}) async-start(bf16[16,12,768]{2,1,0:T(8,128)(2,1)} %reshape.66), calls=%async_computation.2 | async-start | bytes 786432 | tf_op jit(solution)/shard_map/all_to_all | solution.py:382
  120.8 2.5 %collective-permute-start.21 = (bf16[16,3072]{1,0:T(8,128)(2,1)}, bf16[16,3072]{1,0:T(8,128)(2,1)S(1)}, u32[]{:S(2)}, u32[]{:S(2)}) collective-permute-start(bf16[16,3072]{1,0:T(8,128)(2,1)} %get-tuple-element.75), channel_id=1, source_target_pairs={{0,96},{32,64},{64,32},{96,0},{128,224},{160,192},{192,160},{224,1... | collective-permute-start | bytes 294920 | tf_op jit(solution)/shard_map/ppermute | solution.py:394
  123.3 2.8 %collective-permute-start.23 = (bf16[16,3072]{1,0:T(8,128)(2,1)}, bf16[16,3072]{1,0:T(8,128)(2,1)S(1)}, u32[]{:S(2)}, u32[]{:S(2)}) collective-permute-start(bf16[16,3072]{1,0:T(8,128)(2,1)} %get-tuple-element.77), channel_id=1, source_target_pairs={{0,160},{32,128},{64,224},{96,192},{128,32},{160,0},{192,96},{224,... | collective-permute-start | bytes 294920 | tf_op jit(solution)/shard_map/ppermute | solution.py:394
  126.6 3.3 %collective-permute-start.25 = (bf16[16,3072]{1,0:T(8,128)(2,1)}, bf16[16,3072]{1,0:T(8,128)(2,1)S(1)}, u32[]{:S(2)}, u32[]{:S(2)}) collective-permute-start(bf16[16,3072]{1,0:T(8,128)(2,1)} %get-tuple-element.79), channel_id=1, source_target_pairs={{0,224},{32,192},{64,160},{96,128},{128,96},{160,64},{192,32},{224... | collective-permute-start | bytes 294920 | tf_op jit(solution)/shard_map/ppermute | solution.py:394
  129.9 3.1 %collective-permute-start.15 = (bf16[32,1536]{1,0:T(8,128)(2,1)}, bf16[32,1536]{1,0:T(8,128)(2,1)S(1)}, u32[]{:S(2)}, u32[]{:S(2)}) collective-permute-start(bf16[32,1536]{1,0:T(8,128)(2,1)} %get-tuple-element.68), channel_id=1, source_target_pairs={{4,0},{5,1},{6,2},{7,3},{8,4},{9,5},{10,6},{11,7},{12,8},{13,9},{1... | collective-permute-start | bytes 294920 | tf_op jit(solution)/shard_map/ppermute | solution.py:397
  133.0 11.1 %collective-permute-start.16 = (bf16[32,1536]{1,0:T(8,128)(2,1)S(1)}, bf16[32,1536]{1,0:T(8,128)(2,1)S(1)}, u32[]{:S(2)}, u32[]{:S(2)}) collective-permute-start(bf16[32,1536]{1,0:T(8,128)(2,1)S(1)} %copy-done.31), channel_id=1, source_target_pairs={{5,0},{4,1},{7,2},{6,3},{9,4},{8,5},{11,6},{10,7},{13,8},{12,9},{1... | collective-permute-start | bytes 294920 | tf_op jit(solution)/shard_map/ppermute | solution.py:397
  144.3 3.2 %collective-permute-start.13 = (bf16[32,3072]{1,0:T(8,128)(2,1)S(1)}, bf16[32,3072]{1,0:T(8,128)(2,1)S(1)}, u32[]{:S(2)}, u32[]{:S(2)}) collective-permute-start(bf16[32,3072]{1,0:T(8,128)(2,1)S(1)} %copy-done.27), channel_id=1, source_target_pairs={{0,2},{1,3},{2,0},{3,1},{4,6},{5,7},{6,4},{7,5},{8,10},{9,11},{10,... | collective-permute-start | bytes 589832 | tf_op jit(solution)/shard_map/ppermute | solution.py:396
  147.6 0.5 collective-permute-start.14
  148.2 4.6 %collective-permute-start.17 = (bf16[32,1536]{1,0:T(8,128)(2,1)S(1)}, bf16[32,1536]{1,0:T(8,128)(2,1)S(1)}, u32[]{:S(2)}, u32[]{:S(2)}) collective-permute-start(bf16[32,1536]{1,0:T(8,128)(2,1)S(1)} %copy-done.30), channel_id=1, source_target_pairs={{6,0},{7,1},{4,2},{5,3},{10,4},{11,5},{8,6},{9,7},{14,8},{15,9},{1... | collective-permute-start | bytes 294920 | tf_op jit(solution)/shard_map/ppermute | solution.py:397
  152.8 1.9 %collective-permute-start.18 = (bf16[32,1536]{1,0:T(8,128)(2,1)S(1)}, bf16[32,1536]{1,0:T(8,128)(2,1)S(1)}, u32[]{:S(2)}, u32[]{:S(2)}) collective-permute-start(bf16[32,1536]{1,0:T(8,128)(2,1)S(1)} %copy-done.29), channel_id=1, source_target_pairs={{7,0},{6,1},{5,2},{4,3},{11,4},{10,5},{9,6},{8,7},{15,8},{14,9},{1... | collective-permute-start | bytes 294920 | tf_op jit(solution)/shard_map/ppermute | solution.py:397
  154.8 1.9 %collective-permute-done.17.refs_6_ = bf16[32,1536]{1,0:T(8,128)(2,1)S(1)} collective-permute-done((bf16[32,1536]{1,0:T(8,128)(2,1)S(1)}, bf16[32,1536]{1,0:T(8,128)(2,1)S(1)}, u32[]{:S(2)}, u32[]{:S(2)}) %collective-permute-start.17) | collective-permute-done | bytes 98336 | tf_op jit(solution)/shard_map/ppermute | solution.py:397
  156.6 1.2 collective-permute-start.26
  157.8 4.0 %collective-permute-done.18.refs_7_ = bf16[32,1536]{1,0:T(8,128)(2,1)S(1)} collective-permute-done((bf16[32,1536]{1,0:T(8,128)(2,1)S(1)}, bf16[32,1536]{1,0:T(8,128)(2,1)S(1)}, u32[]{:S(2)}, u32[]{:S(2)}) %collective-permute-start.18) | collective-permute-done | bytes 98336 | tf_op jit(solution)/shard_map/ppermute | solution.py:397
  162.0 0.5 copy-done.24
  162.7 0.7 copy-done.13
  163.4 5.9 %shard_map.134 = (bf16[128,1536]{1,0:T(8,128)(2,1)}, bf16[128,1536]{1,0:T(8,128)(2,1)}, bf16[128,1536]{1,0:T(8,128)(2,1)}, bf16[128,1536]{1,0:T(8,128)(2,1)}) custom-call(s32[1]{0:T(128)} %bitcast.me, s32[1]{0:T(128)} %bitcast.1.cam, bf16[768,1536]{1,0:T(8,128)(2,1)} %all-gather.2.cloned.1.call-done.w_own.refs_10_, ...), custom_call_target="tpu_custom_call" | custom-call | tf_op jit(solution)/shard_map/pallas_call | solution.py:287
  169.3 0.6 pad_maximum_fusion.1
  (95 shorter events, 2.9 us)
Async XLA Ops:
  7.2 33.4 %copy-start.25 = (s32[16,7]{0,1:T(8,128)S(1)}, s32[16,7]{0,1:T(8,128)}, u32[]{:S(2)}) copy-start(s32[16,7]{0,1:T(8,128)} %param.14) | copy-start | bytes 1348
  7.2 67.9 %all-gather.2.cloned.1.call-start = ((), (), s32[]{:S(2)}) async-start(), calls=%async_computation.3 | async-start | bytes 2654208 | tf_op jit(solution)/shard_map/all_gather | solution.py:318
  7.2 6.4 %collective-permute-start = (bf16[48,1536]{1,0:T(8,128)(2,1)}, bf16[48,1536]{1,0:T(8,128)(2,1)S(1)}, u32[]{:S(2)}, u32[]{:S(2)}) collective-permute-start(bf16[48,1536]{1,0:T(8,128)(2,1)} %param.16), channel_id=1, source_target_pairs={{0,34},{1,35},{2,32},{3,33},{4,38},{5,39},{6,36},{7,37},{8,42},{9,... | collective-permute-start | bytes 442376 | tf_op jit(solution)/shard_map/ppermute | solution.py:317
  19.1 41.6 %all-to-all-start = ((bf16[8,16,3968]{2,1,0:T(8,128)(2,1)}), bf16[8,16,3968]{2,1,0:T(8,128)(2,1)S(1)}, u32[]{:S(2)}, u32[]{:S(2)}) async-start(bf16[8,16,3968]{2,1,0:T(8,128)(2,1)} %bitcast.20), calls=%async_computation | async-start | bytes 2031616 | tf_op jit(solution)/shard_map/all_to_all | solution.py:330
  23.1 12.6 %collective-permute-start.7 = (bf16[32,1536]{1,0:T(8,128)(2,1)}, bf16[32,1536]{1,0:T(8,128)(2,1)S(1)}, u32[]{:S(2)}, u32[]{:S(2)}) collective-permute-start(bf16[32,1536]{1,0:T(8,128)(2,1)} %get-tuple-element.54), channel_id=1, source_target_pairs={{0,4},{1,5},{2,6},{3,7},{4,8},{5,9},{6,10},{7,11},{8,12},{9,13},{1... | collective-permute-start | bytes 294920 | tf_op jit(solution)/shard_map/ppermute | solution.py:332
  25.8 11.8 %collective-permute-start.8 = (bf16[32,1536]{1,0:T(8,128)(2,1)}, bf16[32,1536]{1,0:T(8,128)(2,1)S(1)}, u32[]{:S(2)}, u32[]{:S(2)}) collective-permute-start(bf16[32,1536]{1,0:T(8,128)(2,1)} %get-tuple-element.55), channel_id=1, source_target_pairs={{0,5},{1,4},{2,7},{3,6},{4,9},{5,8},{6,11},{7,10},{8,13},{9,12},{1... | collective-permute-start | bytes 294920 | tf_op jit(solution)/shard_map/ppermute | solution.py:332
  28.7 15.9 %collective-permute-start.9 = (bf16[32,1536]{1,0:T(8,128)(2,1)}, bf16[32,1536]{1,0:T(8,128)(2,1)S(1)}, u32[]{:S(2)}, u32[]{:S(2)}) collective-permute-start(bf16[32,1536]{1,0:T(8,128)(2,1)} %get-tuple-element.56), channel_id=1, source_target_pairs={{0,6},{1,7},{2,4},{3,5},{4,10},{5,11},{6,8},{7,9},{8,14},{9,15},{1... | collective-permute-start | bytes 294920 | tf_op jit(solution)/shard_map/ppermute | solution.py:332
  31.6 17.0 %collective-permute-start.10 = (bf16[32,1536]{1,0:T(8,128)(2,1)}, bf16[32,1536]{1,0:T(8,128)(2,1)S(1)}, u32[]{:S(2)}, u32[]{:S(2)}) collective-permute-start(bf16[32,1536]{1,0:T(8,128)(2,1)} %get-tuple-element.57), channel_id=1, source_target_pairs={{0,7},{1,6},{2,5},{3,4},{4,11},{5,10},{6,9},{7,8},{8,15},{9,14},{1... | collective-permute-start | bytes 294920 | tf_op jit(solution)/shard_map/ppermute | solution.py:332
  34.6 14.0 %collective-permute-start.4 = (bf16[32,3840]{1,0:T(8,128)(2,1)}, bf16[32,3840]{1,0:T(8,128)(2,1)S(1)}, u32[]{:S(2)}, u32[]{:S(2)}) collective-permute-start(bf16[32,3840]{1,0:T(8,128)(2,1)} %get-tuple-element.51), channel_id=1, source_target_pairs={{0,1},{1,0},{2,3},{3,2},{4,5},{5,4},{6,7},{7,6},{8,9},{9,8},{10,11... | collective-permute-start | bytes 737288 | tf_op jit(solution)/shard_map/ppermute | solution.py:331
  35.7 14.4 %collective-permute-start.5 = (bf16[32,3840]{1,0:T(8,128)(2,1)}, bf16[32,3840]{1,0:T(8,128)(2,1)S(1)}, u32[]{:S(2)}, u32[]{:S(2)}) collective-permute-start(bf16[32,3840]{1,0:T(8,128)(2,1)} %get-tuple-element.52), channel_id=1, source_target_pairs={{0,2},{1,3},{2,0},{3,1},{4,6},{5,7},{6,4},{7,5},{8,10},{9,11},{10,... | collective-permute-start | bytes 737288 | tf_op jit(solution)/shard_map/ppermute | solution.py:331
  37.6 17.8 %collective-permute-start.6 = (bf16[32,3840]{1,0:T(8,128)(2,1)}, bf16[32,3840]{1,0:T(8,128)(2,1)S(1)}, u32[]{:S(2)}, u32[]{:S(2)}) collective-permute-start(bf16[32,3840]{1,0:T(8,128)(2,1)} %get-tuple-element.53), channel_id=1, source_target_pairs={{0,3},{1,2},{2,1},{3,0},{4,7},{5,6},{6,5},{7,4},{8,11},{9,10},{10,... | collective-permute-start | bytes 737288 | tf_op jit(solution)/shard_map/ppermute | solution.py:331
  44.7 10.7 %copy-start.7 = (bf16[32,1536]{1,0:T(8,128)(2,1)}, bf16[32,1536]{1,0:T(8,128)(2,1)S(1)}, u32[]{:S(2)}) copy-start(bf16[32,1536]{1,0:T(8,128)(2,1)S(1)} %collective-permute-done.9.refs_6_) | copy-start | bytes 294916
  60.3 4.6 %collective-permute-start.11 = (bf16[128,1536]{1,0:T(8,128)(2,1)}, bf16[128,1536]{1,0:T(8,128)(2,1)S(1)}, u32[]{:S(2)}, u32[]{:S(2)}) collective-permute-start(bf16[128,1536]{1,0:T(8,128)(2,1)} %get-tuple-element.59), channel_id=1, source_target_pairs={{0,1},{1,0},{2,3},{3,2},{4,5},{5,4},{6,7},{7,6},{8,9},{9,8},{10,11... | collective-permute-start | bytes 1179656 | tf_op jit(solution)/shard_map/ppermute | solution.py:353
  64.8 1.9 %collective-permute-start.3 = (bf16[128,1536]{1,0:T(8,128)(2,1)}, bf16[128,1536]{1,0:T(8,128)(2,1)S(1)}, u32[]{:S(2)}, u32[]{:S(2)}) collective-permute-start(bf16[128,1536]{1,0:T(8,128)(2,1)} %get-tuple-element.49), channel_id=1, source_target_pairs={{0,1},{1,0},{2,3},{3,2},{4,5},{5,4},{6,7},{7,6},{8,9},{9,8},{10,11... | collective-permute-start | bytes 1179656 | tf_op jit(solution)/shard_map/ppermute | solution.py:352
  71.1 38.5 %all-to-all-start.1 = ((bf16[8,192,768]{2,1,0:T(8,128)(2,1)}), bf16[8,192,768]{2,1,0:T(8,128)(2,1)S(1)}, u32[]{:S(2)}, u32[]{:S(2)}) async-start(bf16[8,192,768]{2,1,0:T(8,128)(2,1)} %bitcast.17), calls=%async_computation.1 | async-start | bytes 4718592 | tf_op jit(solution)/shard_map/all_to_all | solution.py:361
  78.3 4.7 %collective-permute-start.2 = (bf16[384,1536]{1,0:T(8,128)(2,1)}, bf16[384,1536]{1,0:T(8,128)(2,1)S(1)}, u32[]{:S(2)}, u32[]{:S(2)}) collective-permute-start(bf16[384,1536]{1,0:T(8,128)(2,1)} %get-tuple-element.85), channel_id=1, source_target_pairs={{0,1},{1,0},{2,3},{3,2},{4,5},{5,4},{6,7},{7,6},{8,9},{9,8},{10,11... | collective-permute-start | bytes 3538952 | tf_op jit(solution)/shard_map/ppermute | solution.py:320
  78.8 13.3 %collective-permute-start.1 = (bf16[384,1536]{1,0:T(8,128)(2,1)}, bf16[384,1536]{1,0:T(8,128)(2,1)}, u32[]{:S(2)}, u32[]{:S(2)}) collective-permute-start(bf16[384,1536]{1,0:T(8,128)(2,1)} %get-tuple-element.86), channel_id=1, source_target_pairs={{0,1},{1,0},{2,3},{3,2},{4,5},{5,4},{6,7},{7,6},{8,9},{9,8},{10,11... | collective-permute-start | bytes 3538952 | tf_op jit(solution)/shard_map/ppermute | solution.py:319
  98.6 34.4 %copy-start.31 = (bf16[32,1536]{1,0:T(8,128)(2,1)S(1)}, bf16[32,1536]{1,0:T(8,128)(2,1)}, u32[]{:S(2)}) copy-start(bf16[32,1536]{1,0:T(8,128)(2,1)} %get-tuple-element.69) | copy-start | bytes 294916
  98.6 45.5 %copy-start.28 = (bf16[32,3072]{1,0:T(8,128)(2,1)S(1)}, bf16[32,3072]{1,0:T(8,128)(2,1)}, u32[]{:S(2)}) copy-start(bf16[32,3072]{1,0:T(8,128)(2,1)} %get-tuple-element.65) | copy-start | bytes 589828
  98.7 45.7 %copy-start.27 = (bf16[32,3072]{1,0:T(8,128)(2,1)S(1)}, bf16[32,3072]{1,0:T(8,128)(2,1)}, u32[]{:S(2)}) copy-start(bf16[32,3072]{1,0:T(8,128)(2,1)} %get-tuple-element.66) | copy-start | bytes 589828
  98.7 48.9 %copy-start.26 = (bf16[32,3072]{1,0:T(8,128)(2,1)S(1)}, bf16[32,3072]{1,0:T(8,128)(2,1)}, u32[]{:S(2)}) copy-start(bf16[32,3072]{1,0:T(8,128)(2,1)} %get-tuple-element.67) | copy-start | bytes 589828
  98.7 49.5 %copy-start.30 = (bf16[32,1536]{1,0:T(8,128)(2,1)S(1)}, bf16[32,1536]{1,0:T(8,128)(2,1)}, u32[]{:S(2)}) copy-start(bf16[32,1536]{1,0:T(8,128)(2,1)} %get-tuple-element.70) | copy-start | bytes 294916
  98.7 54.1 %copy-start.29 = (bf16[32,1536]{1,0:T(8,128)(2,1)S(1)}, bf16[32,1536]{1,0:T(8,128)(2,1)}, u32[]{:S(2)}) copy-start(bf16[32,1536]{1,0:T(8,128)(2,1)} %get-tuple-element.71) | copy-start | bytes 294916
  110.8 37.3 %all-to-all-start.2 = ((bf16[16,12,768]{2,1,0:T(8,128)(2,1)}), bf16[16,12,768]{2,1,0:T(8,128)(2,1)S(1)}, u32[]{:S(2)}, u32[]{:S(2)}) async-start(bf16[16,12,768]{2,1,0:T(8,128)(2,1)} %reshape.66), calls=%async_computation.2 | async-start | bytes 786432 | tf_op jit(solution)/shard_map/all_to_all | solution.py:382
  120.7 5.4 %collective-permute-start.19 = (bf16[16,3072]{1,0:T(8,128)(2,1)}, bf16[16,3072]{1,0:T(8,128)(2,1)S(1)}, u32[]{:S(2)}, u32[]{:S(2)}) collective-permute-start(bf16[16,3072]{1,0:T(8,128)(2,1)} %get-tuple-element.73), channel_id=1, source_target_pairs={{0,32},{32,0},{64,96},{96,64},{128,160},{160,128},{192,224},{224,1... | collective-permute-start | bytes 294920 | tf_op jit(solution)/shard_map/ppermute | solution.py:394
  120.7 5.9 %collective-permute-start.20 = (bf16[16,3072]{1,0:T(8,128)(2,1)}, bf16[16,3072]{1,0:T(8,128)(2,1)S(1)}, u32[]{:S(2)}, u32[]{:S(2)}) collective-permute-start(bf16[16,3072]{1,0:T(8,128)(2,1)} %get-tuple-element.74), channel_id=1, source_target_pairs={{0,64},{32,96},{64,0},{96,32},{128,192},{160,224},{192,128},{224,1... | collective-permute-start | bytes 294920 | tf_op jit(solution)/shard_map/ppermute | solution.py:394
  120.8 9.1 %collective-permute-start.21 = (bf16[16,3072]{1,0:T(8,128)(2,1)}, bf16[16,3072]{1,0:T(8,128)(2,1)S(1)}, u32[]{:S(2)}, u32[]{:S(2)}) collective-permute-start(bf16[16,3072]{1,0:T(8,128)(2,1)} %get-tuple-element.75), channel_id=1, source_target_pairs={{0,96},{32,64},{64,32},{96,0},{128,224},{160,192},{192,160},{224,1... | collective-permute-start | bytes 294920 | tf_op jit(solution)/shard_map/ppermute | solution.py:394
  123.3 9.7 %collective-permute-start.22 = (bf16[16,3072]{1,0:T(8,128)(2,1)}, bf16[16,3072]{1,0:T(8,128)(2,1)S(1)}, u32[]{:S(2)}, u32[]{:S(2)}) collective-permute-start(bf16[16,3072]{1,0:T(8,128)(2,1)} %get-tuple-element.76), channel_id=1, source_target_pairs={{0,128},{32,160},{64,192},{96,224},{128,0},{160,32},{192,64},{224,... | collective-permute-start | bytes 294920 | tf_op jit(solution)/shard_map/ppermute | solution.py:394
  123.3 20.8 %collective-permute-start.23 = (bf16[16,3072]{1,0:T(8,128)(2,1)}, bf16[16,3072]{1,0:T(8,128)(2,1)S(1)}, u32[]{:S(2)}, u32[]{:S(2)}) collective-permute-start(bf16[16,3072]{1,0:T(8,128)(2,1)} %get-tuple-element.77), channel_id=1, source_target_pairs={{0,160},{32,128},{64,224},{96,192},{128,32},{160,0},{192,96},{224,... | collective-permute-start | bytes 294920 | tf_op jit(solution)/shard_map/ppermute | solution.py:394
  126.1 35.8 %copy-start.14 = (bf16[16,3072]{1,0:T(8,128)(2,1)}, bf16[16,3072]{1,0:T(8,128)(2,1)S(1)}, u32[]{:S(2)}) copy-start(bf16[16,3072]{1,0:T(8,128)(2,1)S(1)} %collective-permute-done.19.refs_9_) | copy-start | bytes 294916
  126.1 18.2 %collective-permute-start.24 = (bf16[16,3072]{1,0:T(8,128)(2,1)}, bf16[16,3072]{1,0:T(8,128)(2,1)S(1)}, u32[]{:S(2)}, u32[]{:S(2)}) collective-permute-start(bf16[16,3072]{1,0:T(8,128)(2,1)} %get-tuple-element.78), channel_id=1, source_target_pairs={{0,192},{32,224},{64,128},{96,160},{128,64},{160,96},{192,0},{224,... | collective-permute-start | bytes 294920 | tf_op jit(solution)/shard_map/ppermute | solution.py:394
  126.6 35.3 %copy-start.15 = (bf16[16,3072]{1,0:T(8,128)(2,1)}, bf16[16,3072]{1,0:T(8,128)(2,1)S(1)}, u32[]{:S(2)}) copy-start(bf16[16,3072]{1,0:T(8,128)(2,1)S(1)} %collective-permute-done.20.refs_10_) | copy-start | bytes 294916
  126.6 21.0 %collective-permute-start.25 = (bf16[16,3072]{1,0:T(8,128)(2,1)}, bf16[16,3072]{1,0:T(8,128)(2,1)S(1)}, u32[]{:S(2)}, u32[]{:S(2)}) collective-permute-start(bf16[16,3072]{1,0:T(8,128)(2,1)} %get-tuple-element.79), channel_id=1, source_target_pairs={{0,224},{32,192},{64,160},{96,128},{128,96},{160,64},{192,32},{224... | collective-permute-start | bytes 294920 | tf_op jit(solution)/shard_map/ppermute | solution.py:394
  129.9 32.0 %copy-start.16 = (bf16[16,3072]{1,0:T(8,128)(2,1)}, bf16[16,3072]{1,0:T(8,128)(2,1)S(1)}, u32[]{:S(2)}) copy-start(bf16[16,3072]{1,0:T(8,128)(2,1)S(1)} %collective-permute-done.21.refs_11_) | copy-start | bytes 294916
  129.9 18.3 %collective-permute-start.15 = (bf16[32,1536]{1,0:T(8,128)(2,1)}, bf16[32,1536]{1,0:T(8,128)(2,1)S(1)}, u32[]{:S(2)}, u32[]{:S(2)}) collective-permute-start(bf16[32,1536]{1,0:T(8,128)(2,1)} %get-tuple-element.68), channel_id=1, source_target_pairs={{4,0},{5,1},{6,2},{7,3},{8,4},{9,5},{10,6},{11,7},{12,8},{13,9},{1... | collective-permute-start | bytes 294920 | tf_op jit(solution)/shard_map/ppermute | solution.py:397
  133.0 28.9 %copy-start.17 = (bf16[16,3072]{1,0:T(8,128)(2,1)}, bf16[16,3072]{1,0:T(8,128)(2,1)S(1)}, u32[]{:S(2)}) copy-start(bf16[16,3072]{1,0:T(8,128)(2,1)S(1)} %collective-permute-done.22.refs_12_) | copy-start | bytes 294916
  133.0 19.8 %collective-permute-start.16 = (bf16[32,1536]{1,0:T(8,128)(2,1)S(1)}, bf16[32,1536]{1,0:T(8,128)(2,1)S(1)}, u32[]{:S(2)}, u32[]{:S(2)}) collective-permute-start(bf16[32,1536]{1,0:T(8,128)(2,1)S(1)} %copy-done.31), channel_id=1, source_target_pairs={{5,0},{4,1},{7,2},{6,3},{9,4},{8,5},{11,6},{10,7},{13,8},{12,9},{1... | collective-permute-start | bytes 294920 | tf_op jit(solution)/shard_map/ppermute | solution.py:397
  144.2 17.8 %copy-start.18 = (bf16[16,3072]{1,0:T(8,128)(2,1)}, bf16[16,3072]{1,0:T(8,128)(2,1)S(1)}, u32[]{:S(2)}) copy-start(bf16[16,3072]{1,0:T(8,128)(2,1)S(1)} %collective-permute-done.23.refs_13_) | copy-start | bytes 294916
  144.2 17.7 %collective-permute-start.12 = (bf16[32,3072]{1,0:T(8,128)(2,1)S(1)}, bf16[32,3072]{1,0:T(8,128)(2,1)S(1)}, u32[]{:S(2)}, u32[]{:S(2)}) collective-permute-start(bf16[32,3072]{1,0:T(8,128)(2,1)S(1)} %copy-done.28), channel_id=1, source_target_pairs={{0,1},{1,0},{2,3},{3,2},{4,5},{5,4},{6,7},{7,6},{8,9},{9,8},{10,11... | collective-permute-start | bytes 589832 | tf_op jit(solution)/shard_map/ppermute | solution.py:396
  144.3 17.6 %copy-start.19 = (bf16[16,3072]{1,0:T(8,128)(2,1)}, bf16[16,3072]{1,0:T(8,128)(2,1)S(1)}, u32[]{:S(2)}) copy-start(bf16[16,3072]{1,0:T(8,128)(2,1)S(1)} %collective-permute-done.24.refs_14_) | copy-start | bytes 294916
  144.3 17.5 %collective-permute-start.13 = (bf16[32,3072]{1,0:T(8,128)(2,1)S(1)}, bf16[32,3072]{1,0:T(8,128)(2,1)S(1)}, u32[]{:S(2)}, u32[]{:S(2)}) collective-permute-start(bf16[32,3072]{1,0:T(8,128)(2,1)S(1)} %copy-done.27), channel_id=1, source_target_pairs={{0,2},{1,3},{2,0},{3,1},{4,6},{5,7},{6,4},{7,5},{8,10},{9,11},{10,... | collective-permute-start | bytes 589832 | tf_op jit(solution)/shard_map/ppermute | solution.py:396
  147.6 14.4 %copy-start.20 = (bf16[16,3072]{1,0:T(8,128)(2,1)}, bf16[16,3072]{1,0:T(8,128)(2,1)S(1)}, u32[]{:S(2)}) copy-start(bf16[16,3072]{1,0:T(8,128)(2,1)S(1)} %collective-permute-done.25.refs_15_) | copy-start | bytes 294916
  147.6 14.3 %collective-permute-start.14 = (bf16[32,3072]{1,0:T(8,128)(2,1)S(1)}, bf16[32,3072]{1,0:T(8,128)(2,1)S(1)}, u32[]{:S(2)}, u32[]{:S(2)}) collective-permute-start(bf16[32,3072]{1,0:T(8,128)(2,1)S(1)} %copy-done.26), channel_id=1, source_target_pairs={{0,3},{1,2},{2,1},{3,0},{4,7},{5,6},{6,5},{7,4},{8,11},{9,10},{10,... | collective-permute-start | bytes 589832 | tf_op jit(solution)/shard_map/ppermute | solution.py:396
  148.2 13.8 %copy-start.21 = (bf16[32,1536]{1,0:T(8,128)(2,1)}, bf16[32,1536]{1,0:T(8,128)(2,1)S(1)}, u32[]{:S(2)}) copy-start(bf16[32,1536]{1,0:T(8,128)(2,1)S(1)} %collective-permute-done.15.refs_4_) | copy-start | bytes 294916
  148.2 8.4 %collective-permute-start.17 = (bf16[32,1536]{1,0:T(8,128)(2,1)S(1)}, bf16[32,1536]{1,0:T(8,128)(2,1)S(1)}, u32[]{:S(2)}, u32[]{:S(2)}) collective-permute-start(bf16[32,1536]{1,0:T(8,128)(2,1)S(1)} %copy-done.30), channel_id=1, source_target_pairs={{6,0},{7,1},{4,2},{5,3},{10,4},{11,5},{8,6},{9,7},{14,8},{15,9},{1... | collective-permute-start | bytes 294920 | tf_op jit(solution)/shard_map/ppermute | solution.py:397
  152.8 9.2 %copy-start.22 = (bf16[32,1536]{1,0:T(8,128)(2,1)}, bf16[32,1536]{1,0:T(8,128)(2,1)S(1)}, u32[]{:S(2)}) copy-start(bf16[32,1536]{1,0:T(8,128)(2,1)S(1)} %collective-permute-done.16.refs_5_) | copy-start | bytes 294916
  152.8 9.0 %collective-permute-start.18 = (bf16[32,1536]{1,0:T(8,128)(2,1)S(1)}, bf16[32,1536]{1,0:T(8,128)(2,1)S(1)}, u32[]{:S(2)}, u32[]{:S(2)}) collective-permute-start(bf16[32,1536]{1,0:T(8,128)(2,1)S(1)} %copy-done.29), channel_id=1, source_target_pairs={{7,0},{6,1},{5,2},{4,3},{11,4},{10,5},{9,6},{8,7},{15,8},{14,9},{1... | collective-permute-start | bytes 294920 | tf_op jit(solution)/shard_map/ppermute | solution.py:397
  156.6 12.6 %collective-permute-start.26 = (f32[6,768]{1,0:T(8,128)S(1)}, f32[6,768]{1,0:T(8,128)S(1)}, u32[]{:S(2)}, u32[]{:S(2)}) collective-permute-start(f32[6,768]{1,0:T(8,128)S(1)} %constant_dynamic-slice_fusion), channel_id=1, source_target_pairs={{0,1},{1,0},{2,3},{3,2},{4,5},{5,4},{6,7},{7,6},{8,9},{9,8},{10,11... | collective-permute-start | bytes 55304 | tf_op jit(solution)/shard_map/ppermute | solution.py:388
  (15 other events, 48.3 us)
Sparse Core Ops, SparseCore 0:
  15.4 44.6 all-gather.1

commit v4 on v3

v4 whole, which is shorter than its diff:
```python
import functools
import math

import jax
import jax.numpy as jnp
from jax import lax
from jax.experimental import pallas as pl
from jax.experimental.pallas import tpu as pltpu
from jax.sharding import PartitionSpec as P

HC = 12
HT = 12
HD = 64
WIN = 64
CW = HC * HD
GROUP = 4
PAIR = 2
SCALE = HD ** (-0.5)
BF = jnp.bfloat16
F32 = jnp.float32
PAIRS = HC // 2
VM = pl.BlockSpec(memory_space=pltpu.VMEM)
ANY = pl.BlockSpec(memory_space=pl.ANY)
SM = pl.BlockSpec(memory_space=pltpu.SMEM)


def iota(shape, dim):
    return lax.broadcasted_iota(jnp.int32, shape, dim)


def dot_nt(a, b):
    return lax.dot_general(a, b, (((1,), (1,)), ((), ())), preferred_element_type=F32)


def dot_tn(a, b):
    return lax.dot_general(a, b, (((0,), (0,)), ((), ())), preferred_element_type=F32)


def dot_nn(a, b):
    return jnp.dot(a, b, preferred_element_type=F32)


def split_pair(rows):
    low = iota(rows.shape, 1) < HD
    zero = jnp.zeros_like(rows)
    return jnp.concatenate([jnp.where(low, rows, zero), jnp.where(low, zero, rows)], axis=0)


def join_pair(rows):
    count = rows.shape[0] // 2
    low = iota((count, rows.shape[1]), 1) < HD
    return jnp.where(low, rows[:count], rows[count:])


def softmax_pair(q, k, mask):
    scores = dot_nt(split_pair(q), k) * SCALE
    scores = jnp.where(mask, scores, -jnp.inf)
    largest = jnp.max(scores, axis=1, keepdims=True)
    e = jnp.exp(scores - largest)
    return e / jnp.sum(e, axis=1, keepdims=True)


def pack_kernel(me, valid, q, k, v, ct, view_ref, *rest):
    kv_refs, qct_refs, (held, sems) = rest[:PAIR], rest[PAIR : 2 * PAIR], rest[2 * PAIR :]
    copies = [pltpu.make_async_copy(ref, held.at[i], sems.at[i]) for i, ref in enumerate((q, k, v, ct))]
    for copy in copies:
        copy.start()
    rows = q.shape[0]
    frames = rows // 8
    block = 4 * frames
    row = iota((rows, rows), 0)
    col = iota((rows, rows), 1)
    source = ((row // 4) % frames) * 8 + 4 * ((row // block) ^ (me[0] % 2)) + row % 4
    perm = jnp.where(col == source, 1.0, 0.0).astype(BF)
    frame = iota((rows, 128), 0) // 8
    flags = jnp.zeros((rows, 128), F32)
    for f in range(frames):
        flags = jnp.where(frame == f, valid[0, f].astype(F32), flags)
    view_ref[:, 5 * CW :] = jnp.where(flags > 0.5, 1.0, 0.0).astype(BF)
    for i in range(4):
        copies[i].wait()
        if i < 3:
            view_ref[:, i * CW : (i + 1) * CW] = held[i, :, :CW]
            moved = dot_nn(perm, held[i, :, CW:]).astype(BF)
        else:
            view_ref[:, 3 * CW : 5 * CW] = held[i]
            moved = dot_nn(perm, held[i]).astype(BF)
        for d in range(PAIR):
            part = moved[d * block : (d + 1) * block]
            if i in (1, 2):
                kv_refs[d][:, (i - 1) * CW : i * CW] = part
            elif i == 0:
                qct_refs[d][:, :CW] = part
            else:
                qct_refs[d][:, CW:] = part


def view_mask(flags):
    rows = flags.shape[0]
    pick = jnp.where(iota((8, 128), 1) == 0, 1.0, 0.0).astype(BF)
    valid_row = dot_nt(pick, flags)[:1]
    r = iota((2 * rows, rows), 0) % rows
    c = iota((2 * rows, rows), 1)
    same_frame = ((r // 8) % 2) == ((c // 8) % 2)
    return same_frame & ((valid_row > 0.5) | (r // 16 == c // 16))


def keep_for_weight(attn, ct, core, own_ref, send_ref):
    own_ref[:, :CW] = attn
    send_ref[:, :CW] = attn
    own_ref[:, CW:] = jnp.where(core == 0, ct[:, :CW], ct[:, CW:])
    send_ref[:, CW:] = jnp.where(core == 0, ct[:, CW:], ct[:, :CW])


def view_forward_kernel(me, x, own_ref, send_ref, prob_ref):
    mask = view_mask(x[:, 5 * CW :])
    attn = []
    for j in range(PAIRS):
        q = x[:, 128 * j : 128 * (j + 1)]
        k = x[:, CW + 128 * j : CW + 128 * (j + 1)]
        v = x[:, 2 * CW + 128 * j : 2 * CW + 128 * (j + 1)]
        prob = softmax_pair(q, k, mask)
        prob_ref[j] = prob
        attn.append(join_pair(dot_nn(prob.astype(BF), v)).astype(BF))
    keep_for_weight(jnp.concatenate(attn, axis=1), x[:, 3 * CW : 5 * CW], me[0] % 2, own_ref, send_ref)


def rows_of(refs, columns):
    return jnp.concatenate([ref[:, columns] for ref in refs], axis=0)


def time_forward_kernel(windows, me, pair, q0, q1, far, near, own, own_ref, send_ref, prob_ref):
    qct, kv = (q0, q1), (far, near, own)
    size = q0.shape[0]
    rows = PAIR * size
    shape = (2 * rows, 3 * rows)
    r = iota(shape, 0)
    c = iota(shape, 1)
    second = r >= rows
    core = me[0] % 2
    span = size // 2

    def frame_of(row):
        return ((row // size) ^ core) * (size // 4) + (row % size) // 4

    key_frame = frame_of(c % rows) + span * (c // rows) - 2 * span
    gap = frame_of(r % rows) - key_frame
    base = (r % 4 == c % 4) & (gap >= 0) & (key_frame + span * pair[0] >= 0)
    attn = []
    for j in range(PAIRS):
        at = [slice(i * CW + 128 * j, i * CW + 128 * (j + 1)) for i in range(2)]
        limit = jnp.where(second, windows[2 * j + 1], windows[2 * j])
        prob = softmax_pair(rows_of(qct, at[0]), rows_of(kv, at[0]), base & (gap < limit))
        prob_ref[j] = prob
        attn.append(join_pair(dot_nn(prob.astype(BF), rows_of(kv, at[1]))).astype(BF))
    keep_for_weight(jnp.concatenate(attn, axis=1), rows_of(qct, slice(CW, 3 * CW)), core, own_ref, send_ref)


def weight_kernel(scale, own_view, other_view, own_time, other_time, out_ref):
    for i, (own, other) in enumerate(((own_view, other_view), (own_time, other_time))):
        left = jnp.concatenate([own[:, :CW], other[:, :CW]], axis=0)
        right = jnp.concatenate([own[:, CW:], other[:, CW:]], axis=0)
        out_ref[i * CW : (i + 1) * CW, :] = (dot_tn(left, right) * scale).astype(BF)


def fetch_weight(me, own, others, held, sem, first, count):
    size = held.shape[0] // (4 * count)
    core, y = me[0] % 2, me[0] // 2
    copies = []
    for z in range(count):
        other = others[z * len(others) // count]
        for e in range(2):
            for n, (which, ref, place) in enumerate(
                ((core, own, 2 * (first + z) + e), (1 - core, other, 2 * (z % (count // len(others))) + e))
            ):
                start = pl.multiple_of((4 * z + 2 * (y ^ e) + which) * size, 16)
                copies.append(
                    pltpu.make_async_copy(
                        ref.at[pl.ds(place * size, size)],
                        held.at[pl.ds(start, size)],
                        sem.at[4 * z + 2 * e + n],
                    )
                )
    for copy in copies:
        copy.start()
    return copies


def backward_pair(q, k, v, g, prob):
    g2 = split_pair(g)
    grad_prob = dot_nt(g2, v)
    total = jnp.sum(prob * grad_prob, axis=1, keepdims=True)
    grad_scores = (prob * (grad_prob - total)).astype(BF)
    dq = join_pair(dot_nn(grad_scores, k)) * SCALE
    dk = dot_tn(grad_scores, split_pair(q)) * SCALE
    dv = dot_tn(prob.astype(BF), g2)
    return dq, dk, dv


def view_backward_kernel(depth, me, x, kept, prob_ref, w_own, w_other, out_ref, w, sem):
    copies = fetch_weight(me, w_own, (w_other,), w, sem, 0, depth // 2)
    out_ref[:, :CW] = kept[:, :CW]
    for copy in copies:
        copy.wait()
    grad = dot_nt(x[:, 3 * CW : 5 * CW], w[...]).astype(BF)
    for j in range(PAIRS):
        at = [slice(i * CW + 128 * j, i * CW + 128 * (j + 1)) for i in range(4)]
        dq, dk, dv = backward_pair(x[:, at[0]], x[:, at[1]], x[:, at[2]], grad[:, at[0]], prob_ref[j])
        out_ref[:, at[1]] = dq.astype(BF)
        out_ref[:, at[2]] = dk.astype(BF)
        out_ref[:, at[3]] = dv.astype(BF)


def time_backward_kernel(depth, me, q0, q1, far, near, own, prob_ref, w_own, w_other, *rest):
    dq_ref, own_ref, near_ref, far_ref, w, sem = rest
    qct, kv = (q0, q1), (far, near, own)
    copies = fetch_weight(me, w_own, (w_other,), w, sem, depth // 2, depth // 2)
    rows = PAIR * q0.shape[0]
    for copy in copies:
        copy.wait()
    grad = dot_nt(rows_of(qct, slice(CW, 3 * CW)), w[...]).astype(BF)
    for j in range(PAIRS):
        at = [slice(i * CW + 128 * j, i * CW + 128 * (j + 1)) for i in range(2)]
        dq, dk, dv = backward_pair(
            rows_of(qct, at[0]), rows_of(kv, at[0]), rows_of(kv, at[1]), grad[:, at[0]], prob_ref[j]
        )
        dq_ref[:, at[0]] = dq.astype(BF)
        for part, value in zip(at, (dk, dv)):
            far_ref[:, part] = value[:rows].astype(BF)
            near_ref[:, part] = value[rows : 2 * rows].astype(BF)
            own_ref[:, part] = value[2 * rows :]


def time_sum_kernel(kept, dq, own, near, far, *outs):
    size = outs[0].shape[0]
    for d, out in enumerate(outs):
        part = slice(d * size, (d + 1) * size)
        out[:, :CW] = kept[part, :CW]
        out[:, CW : 2 * CW] = dq[part]
        out[:, 2 * CW :] = (own[part] + near[part].astype(F32) + far[part].astype(F32)).astype(BF)


def action_kernel(actions, table, out_ref):
    total = None
    for d in range(table.shape[0]):
        codes = iota((actions.shape[0], table.shape[1]), 1)
        one_hot = jnp.where(actions[:, d : d + 1] == codes, 1.0, 0.0).astype(BF)
        term = dot_nn(one_hot, table[d])
        total = term if total is None else total + term
    out_ref[...] = total


def camera_sum_kernel(parts, out_ref, held):
    total = parts[0].astype(F32)
    for i in range(1, parts.shape[0]):
        total = total + parts[i].astype(F32)
    held[...] = total
    size = out_ref.shape[1]
    for i in range(out_ref.shape[0]):
        out_ref[i] = held[i * size : (i + 1) * size, :].astype(BF)


def finish_kernel(depth, me, w_own, w_view, w_time, action, t0, t1, view, *rest):
    time = (t0, t1)
    pred_ref, dq_ref, dk_ref, dv_ref, w, sem = rest
    copies = fetch_weight(me, w_own, (w_view, w_time), w, sem, 0, depth)
    rows = view.shape[0]
    frames = rows // 8
    row = iota((rows, rows), 0)
    col = iota((rows, rows), 1)
    source = (((row % 8) // 4) ^ (me[0] % 2)) * 4 * frames + (row // 8) * 4 + row % 4
    perm = jnp.where(col == source, 1.0, 0.0).astype(BF)
    for i, ref in enumerate((dq_ref, dk_ref, dv_ref), 1):
        part = slice(i * CW, (i + 1) * CW)
        ref[:, :CW] = view[:, part]
        ref[:, CW:] = dot_nn(perm, rows_of(time, part)).astype(BF)
    attn_time = dot_nn(perm, rows_of(time, slice(0, CW))).astype(BF)
    for copy in copies:
        copy.wait()
    mixed = dot_nn(view[:, :CW], w[:CW]) + dot_nn(attn_time, w[CW:])
    total = mixed.reshape(frames, 8, 2 * CW) + action[...][:, None, :]
    pred_ref[...] = total.reshape(rows, 2 * CW).astype(BF)


def call(kernel, outs, specs, *args, scratch=()):
    return list(
        pl.pallas_call(
            kernel,
            out_shape=[jax.ShapeDtypeStruct(shape, kind) for shape, kind in outs],
            in_specs=specs,
            out_specs=[VM] * len(outs),
            scratch_shapes=list(scratch),
            compiler_params=pltpu.CompilerParams(vmem_limit_bytes=20 * 1024 * 1024),
        )(*args)
    )


def shards(queries, keys, values, cam_valid, windows, actions, act_table, w_out, cotangent):
    _, frames, tokens, width = queries.shape
    rows = frames * tokens
    block = rows // PAIR
    cams = lax.axis_size("cam")
    tm = lax.axis_size("tm")
    at_tm = lax.axis_index("tm")
    core = at_tm % 2
    me = (at_tm % GROUP).reshape(1)
    pair = (at_tm // PAIR).reshape(1)
    depth = tm // GROUP
    same_core = [[2 * i + j for i in range(tm // 2)] for j in range(2)]
    along_z = [[GROUP * i + j for i in range(depth)] for j in range(GROUP)]
    swap = [(i, i ^ 1) for i in range(tm)]
    beside = [(i, i ^ (tm + 2)) for i in range(cams * tm)]

    w_beside = lax.ppermute(w_out, ("cam", "tm"), beside)
    q, k, v, ct = (a.reshape(rows, width) for a in (queries, keys, values, cotangent))
    packed = call(
        pack_kernel,
        [((rows, 5 * CW + 128), BF)] + [((block, 2 * CW), BF)] * PAIR + [((block, 3 * CW), BF)] * PAIR,
        [SM, SM] + [ANY] * 4,
        me, cam_valid, q, k, v, ct,
        scratch=[pltpu.VMEM((4, rows, width), BF), pltpu.SemaphoreType.DMA((4,))],
    )
    view_send, kv, qct = packed[0], packed[1 : PAIR + 1], packed[PAIR + 1 :]
    w_beside, view_send = lax.optimization_barrier((w_beside, view_send))
    w_both = jnp.concatenate([w_out, w_beside], axis=0)
    w_own = lax.all_gather(w_both, "tm", axis=0, tiled=True, axis_index_groups=along_z)
    view_x = lax.all_to_all(view_send, "cam", 0, 0, tiled=True)
    own = jnp.concatenate([kv[0], lax.ppermute(kv[1], "tm", swap)], axis=0)
    near = lax.ppermute(own, "tm", [(i, i + 2) for i in range(tm - 2)])
    far = lax.ppermute(own, "tm", [(i, i + 4) for i in range(tm - 4)])
    q0, q1 = qct[0], lax.ppermute(qct[1], "tm", swap)

    (action_sum,) = call(action_kernel, [((frames, width), F32)], [VM] * 2, actions, act_table)
    view_x, action_sum = lax.optimization_barrier((view_x, action_sum))
    kept_view, view_swap, prob_view = call(
        view_forward_kernel,
        [((rows, 2 * CW), BF)] * 2 + [((PAIRS, 2 * rows, rows), F32)],
        [SM, VM],
        me, view_x,
    )
    kept_time, time_swap, prob_time = call(
        time_forward_kernel,
        [((rows, 2 * CW), BF)] * 2 + [((PAIRS, 2 * rows, 3 * rows), F32)],
        [SM] * 3 + [VM] * 5,
        windows, me, pair, q0, q1, far, near, own,
    )

    view_swap = lax.ppermute(view_swap, "tm", swap)
    time_swap = lax.ppermute(time_swap, "tm", swap)
    grad_norm = 1.0 / math.sqrt(cams * tm * rows)
    (part,) = call(
        functools.partial(weight_kernel, grad_norm),
        [((width, CW), BF)],
        [VM] * 4,
        kept_view, view_swap, kept_time, time_swap,
    )
    part = lax.all_to_all(part.reshape(cams, width // cams, CW), "cam", 0, 0, tiled=True)

    w_view = lax.ppermute(w_own[: CW // 2], "tm", swap)
    w_time = lax.ppermute(w_own[CW // 2 :], "tm", swap)
    half_weight = [pltpu.VMEM((CW, width), BF), pltpu.SemaphoreType.DMA((tm // 2,))]
    (view_out,) = call(
        functools.partial(view_backward_kernel, depth),
        [((rows, 4 * CW), BF)],
        [SM] + [VM] * 3 + [ANY] * 2,
        me, view_x, kept_view, prob_view, w_own, w_view,
        scratch=half_weight,
    )
    q0, view_out = lax.optimization_barrier((q0, view_out))
    view_back = lax.all_to_all(view_out, "cam", 0, 0, tiled=True)
    dq_time, own_grad, near_grad, far_grad = call(
        functools.partial(time_backward_kernel, depth),
        [((rows, CW), BF), ((rows, 2 * CW), F32), ((rows, 2 * CW), BF), ((rows, 2 * CW), BF)],
        [SM] + [VM] * 6 + [ANY] * 2,
        me, q0, q1, far, near, own, prob_time, w_own, w_time,
        scratch=half_weight,
    )
    part, near_grad = lax.optimization_barrier((part, near_grad))
    near_grad = lax.ppermute(near_grad, "tm", [(i + 2, i) for i in range(tm - 2)])
    far_grad = lax.ppermute(far_grad, "tm", [(i + 4, i) for i in range(tm - 4)])

    chips = tm // 2
    (part,) = call(
        camera_sum_kernel,
        [((chips, width // cams // chips, CW), BF)],
        [VM],
        part,
        scratch=[pltpu.VMEM((width // cams, CW), F32)],
    )
    part = lax.all_to_all(part, "tm", 0, 0, tiled=True, axis_index_groups=same_core)
    part = jnp.sum(part.astype(F32), axis=0)
    final = width // cams // tm
    mine = lax.dynamic_slice_in_dim(part, core * final, final, 0)
    theirs = lax.ppermute(lax.dynamic_slice_in_dim(part, (1 - core) * final, final, 0), "tm", swap)
    grad_out_weight = jnp.concatenate(
        [jnp.where(core == 0, mine, theirs), jnp.where(core == 0, theirs, mine)], axis=1
    )

    t0, t1 = call(
        time_sum_kernel, [((block, 4 * CW), BF)] * PAIR, [VM] * 5, kept_time, dq_time, own_grad, near_grad, far_grad
    )
    t1 = lax.ppermute(t1, "tm", swap)
    outs = call(
        functools.partial(finish_kernel, depth),
        [((rows, width), BF)] * 4,
        [SM] + [ANY] * 3 + [VM] * 4,
        me, w_own, w_view, w_time, action_sum, t0, t1, view_back,
        scratch=[pltpu.VMEM((width, width), BF), pltpu.SemaphoreType.DMA((tm,))],
    )
    return tuple(a.reshape(1, frames, tokens, width) for a in outs) + (grad_out_weight,)


def solution(mesh):
    in_specs = (
        P("cam", "tm", None, None),
        P("cam", "tm", None, None),
        P("cam", "tm", None, None),
        P("cam", "tm"),
        P(),
        P("tm", None),
        P(),
        P("tm", None),
        P("cam", "tm", None, None),
    )
    out_specs = (
        P("cam", "tm", None, None),
        P("cam", "tm", None, None),
        P("cam", "tm", None, None),
        P("cam", "tm", None, None),
        P(("cam", "tm"), None),
    )
    return jax.shard_map(shards, mesh=mesh, in_specs=in_specs, out_specs=out_specs, check_vma=False)
```

time: 178 us -> 196 us (1.10)
  the two profiles are of different devices: /device:TPU:193 before, /device:TPU:17 now
where the time goes in v4:
time: 196 us; the launch traced here: 195 us
  waiting for transfers between devices  60.4 us (31%)
  starting transfers between devices  52.1 us (27%)
  Pallas kernels  38.1 us (19%)
  local copies, waits for them, and re-layouts  25.6 us (13%)
  between operations  14.4 us (7%)
  other arithmetic  4.28 us (2%)
    pallas_call x10, Pallas kernels, call(): pl.pallas_call(kernel, out_shape=[jax.ShapeDtypeStruct(shape, kind) for s...  38.1 us
    unnamed x88, local copies, waits for them, and re-layouts  23.1 us
    ppermute x1, waiting for transfers between devices, shards(): far = lax.ppermute(own, 'tm', [(i, i + 4) for i in range(tm - 4)])  16.9 us
    all_to_all x1, starting transfers between devices, shards(): lax.all_to_all(part, 'tm', 0, 0, tiled=True, axis_index_groups=same_core)  12.6 us
    all_to_all x1, waiting for transfers between devices, shards(): lax.all_to_all(part.reshape(cams, width // cams, CW), 'cam', 0, 0, tiled=...  12.4 us
    ppermute x1, waiting for transfers between devices, shards(): lax.ppermute(near_grad, 'tm', [(i + 2, i) for i in range(tm - 2)])  12.1 us
    all_to_all x1, waiting for transfers between devices, shards(): lax.all_to_all(part, 'tm', 0, 0, tiled=True, axis_index_groups=same_core)  7.69 us
    all_to_all x1, starting transfers between devices, shards(): lax.all_to_all(part.reshape(cams, width // cams, CW), 'cam', 0, 0, tiled=...  7.24 us
  transfers between devices with their start and end apart: 18, of which 9 were waited for; matrix products, arithmetic and copies ran while one was open for 3% of the time, Pallas kernels for 13%

profile of v4, /device:TPU:17, one launch (start us, length us, event | category | flops | bytes accessed | tf_op | source)
XLA Modules:
  0.0 195.0 jit_solution(11847433921222474197)
XLA Ops:
  7.5 1.0 copy-done.29
  8.5 1.0 copy-done.30
  9.5 1.0 copy-done.31
  10.5 1.0 copy-done.32
  12.1 3.3 %shard_map.128 = (bf16[128,3968]{1,0:T(8,128)(2,1)}, bf16[64,1536]{1,0:T(8,128)(2,1)S(1)}, bf16[64,1536]{1,0:T(8,128)(2,1)S(1)}, bf16[64,2304]{1,0:T(8,128)(2,1)S(1)}, bf16[64,2304]{1,0:T(8,128)(2,1)}) custom-call(s32[1]{0:T(128)} %bitcast.me, s32[1,16]{1,0:T(1,128)S(1)} %copy-done.37, bf16[128,1536]{1,0:T(8,128)(2,1)S(1)} %bitcast.18, ...), custom_call_target="tpu_custom_call" | custom-call | tf_op jit(solution)/shard_map/pallas_call | solution.py:287
  15.4 1.8 pad_maximum_fusion
  17.2 4.6 %all-to-all-start = ((bf16[8,16,3968]{2,1,0:T(8,128)(2,1)}), bf16[8,16,3968]{2,1,0:T(8,128)(2,1)S(1)}, u32[]{:S(2)}, u32[]{:S(2)}) async-start(bf16[8,16,3968]{2,1,0:T(8,128)(2,1)} %bitcast.5), calls=%async_computation | async-start | bytes 2031616 | tf_op jit(solution)/shard_map/all_to_all | solution.py:327
  21.8 1.1 collective-permute-start.4
  23.0 1.1 collective-permute-done.4
  24.0 5.4 %collective-permute-start.6 = (bf16[128,1536]{1,0:T(8,128)(2,1)S(1)}, bf16[128,1536]{1,0:T(8,128)(2,1)S(1)}, u32[]{:S(2)}, u32[]{:S(2)}) collective-permute-start(bf16[128,1536]{1,0:T(8,128)(2,1)S(1)} %constant_dynamic-update-slice_fusion.own), channel_id=1, source_target_pairs={{0,2},{1,3},{2,4},{3,5},{4,6},{5,7},{6,8},{7,9},{8,10},{9,11},{10,... | collective-permute-start | bytes 1179656 | tf_op jit(solution)/shard_map/ppermute | solution.py:329
  29.4 3.6 %collective-permute-start.5 = (bf16[128,1536]{1,0:T(8,128)(2,1)S(1)}, bf16[128,1536]{1,0:T(8,128)(2,1)S(1)}, u32[]{:S(2)}, u32[]{:S(2)}) collective-permute-start(bf16[128,1536]{1,0:T(8,128)(2,1)S(1)} %constant_dynamic-update-slice_fusion.own), channel_id=1, source_target_pairs={{0,4},{1,5},{2,6},{3,7},{4,8},{5,9},{6,10},{7,11},{8,12},{9,13},{1... | collective-permute-start | bytes 1179656 | tf_op jit(solution)/shard_map/ppermute | solution.py:330
  33.0 1.0 collective-permute-start.3
  34.1 2.6 %copy-done.1 = bf16[7,256,1536]{2,1,0:T(8,128)(2,1)S(1)} copy-done((bf16[7,256,1536]{2,1,0:T(8,128)(2,1)S(1)}, bf16[7,256,1536]{2,1,0:T(8,128)(2,1)}, u32[]{:S(2)}) %copy-start.1) | copy-done | bytes 5505048
  37.6 6.1 %collective-permute-done.6.near = bf16[128,1536]{1,0:T(8,128)(2,1)S(1)} collective-permute-done((bf16[128,1536]{1,0:T(8,128)(2,1)S(1)}, bf16[128,1536]{1,0:T(8,128)(2,1)S(1)}, u32[]{:S(2)}, u32[]{:S(2)}) %collective-permute-start.6) | collective-permute-done | bytes 393248 | tf_op jit(solution)/shard_map/ppermute | solution.py:329
  43.7 16.9 %collective-permute-done.5.far = bf16[128,1536]{1,0:T(8,128)(2,1)S(1)} collective-permute-done((bf16[128,1536]{1,0:T(8,128)(2,1)S(1)}, bf16[128,1536]{1,0:T(8,128)(2,1)S(1)}, u32[]{:S(2)}, u32[]{:S(2)}) %collective-permute-start.5) | collective-permute-done | bytes 393248 | tf_op jit(solution)/shard_map/ppermute | solution.py:330
  60.5 4.0 %shard_map.130 = (bf16[128,1536]{1,0:T(8,128)(2,1)S(1)}, bf16[128,1536]{1,0:T(8,128)(2,1)}, f32[6,256,384]{2,1,0:T(8,128)S(1)}) custom-call(s32[12]{0:T(128)S(1)} %copy-done.38, s32[1]{0:T(128)} %bitcast.me, s32[1]{0:T(128)} %bitcast.7.pair, bf16[64,2304]{1,0:T(8,128)(2,1)S(1)} %get-tuple-element.46.q0, bf16[64,2304]{1,0:T(8,128)(2,1)S(1)} %collective-permute-done.3.q1, ...), custom_call_target="tpu_custom_call" | custom-call | tf_op jit(solution)/shard_map/pallas_call | solution.py:287
  64.5 1.5 copy-done.9
  66.0 2.8 %collective-permute-start.8 = (bf16[128,1536]{1,0:T(8,128)(2,1)}, bf16[128,1536]{1,0:T(8,128)(2,1)S(1)}, u32[]{:S(2)}, u32[]{:S(2)}) collective-permute-start(bf16[128,1536]{1,0:T(8,128)(2,1)} %get-tuple-element.51), channel_id=1, source_target_pairs={{0,1},{1,0},{2,3},{3,2},{4,5},{5,4},{6,7},{7,6},{8,9},{9,8},{10,11... | collective-permute-start | bytes 1179656 | tf_op jit(solution)/shard_map/ppermute | solution.py:349
  69.6 0.9 copy-done.23
  70.5 1.7 collective-permute-done.7.other_view
  72.2 2.2 %shard_map.134 = bf16[1536,768]{1,0:T(8,128)(2,1)} custom-call(bf16[128,1536]{1,0:T(8,128)(2,1)S(1)} %get-tuple-element.44.kept.own_view, bf16[128,1536]{1,0:T(8,128)(2,1)S(1)} %collective-permute-done.7.other_view, bf16[128,1536]{1,0:T(8,128)(2,1)S(1)} %get-tuple-element.42.own_time.kept, bf16[128,1536]{1,0:T(8,128)(2,1)S(1)} %collective-permute-done.8.other_time), custom_call_target="tpu_custom_call" | custom-call | tf_op jit(solution)/shard_map/pallas_call | solution.py:287
  75.2 7.2 %all-to-all-start.1 = ((bf16[8,192,768]{2,1,0:T(8,128)(2,1)}), bf16[8,192,768]{2,1,0:T(8,128)(2,1)}, u32[]{:S(2)}, u32[]{:S(2)}) async-start(bf16[8,192,768]{2,1,0:T(8,128)(2,1)} %bitcast.8), calls=%async_computation.1 | async-start | bytes 4718592 | tf_op jit(solution)/shard_map/all_to_all | solution.py:357
  82.5 1.9 fusion
  85.2 2.2 %collective-permute-done.1.w_other.w_view = bf16[384,1536]{1,0:T(8,128)(2,1)S(1)} collective-permute-done((bf16[384,1536]{1,0:T(8,128)(2,1)S(1)}, bf16[384,1536]{1,0:T(8,128)(2,1)S(1)}, u32[]{:S(2)}, u32[]{:S(2)}) %collective-permute-start.1) | collective-permute-done | bytes 1179680 | tf_op jit(solution)/shard_map/ppermute | solution.py:359
  87.5 5.4 %shard_map.132 = bf16[128,3072]{1,0:T(8,128)(2,1)S(1)} custom-call(s32[1]{0:T(128)} %bitcast.me, bf16[128,3968]{1,0:T(8,128)(2,1)S(1)} %bitcast.16, bf16[128,1536]{1,0:T(8,128)(2,1)S(1)} %copy-done.16, f32[6,256,128]{2,1,0:T(8,128)S(1)} %copy-done.24, bf16[768,1536]{1,0:T(8,128)(2,1)S(1)} %copy-done, bf16[384,1536]{1,0:T(8,128)(2,1)S(1)} %collective-permute-done.1.w_other.w_view), custom_call_target="tpu_custom_call" | custom-call | tf_op jit(solution)/shard_map/pallas_call | solution.py:287
  92.9 0.9 copy-done.6
  93.8 6.8 %shard_map.133 = (bf16[128,768]{1,0:T(8,128)(2,1)S(1)}, f32[128,1536]{1,0:T(8,128)S(1)}, bf16[128,1536]{1,0:T(8,128)(2,1)S(1)}, bf16[128,1536]{1,0:T(8,128)(2,1)S(1)}) custom-call(s32[1]{0:T(128)} %bitcast.me, bf16[64,2304]{1,0:T(8,128)(2,1)S(1)} %copy-done.20, bf16[64,2304]{1,0:T(8,128)(2,1)S(1)} %copy-done.22, bf16[128,1536]{1,0:T(8,128)(2,1)S(1)} %copy-done.14, ...), custom_call_target="tpu_custom_call" | custom-call | tf_op jit(solution)/shard_map/pallas_call | solution.py:287
  100.6 1.0 copy-done.4
  101.7 1.0 copy-done.25
  104.8 12.4 %all-to-all-done.1.parts = bf16[8,192,768]{2,1,0:T(8,128)(2,1)} async-done(((bf16[8,192,768]{2,1,0:T(8,128)(2,1)}), bf16[8,192,768]{2,1,0:T(8,128)(2,1)}, u32[]{:S(2)}, u32[]{:S(2)}) %all-to-all-start.1) | async-done | bytes 2359328 | tf_op jit(solution)/shard_map/all_to_all | solution.py:357
  117.2 2.9 %shard_map.137 = bf16[16,12,768]{2,1,0:T(8,128)(2,1)} custom-call(bf16[8,192,768]{2,1,0:T(8,128)(2,1)} %all-to-all-done.1.parts), custom_call_target="tpu_custom_call" | custom-call | tf_op jit(solution)/shard_map/pallas_call | solution.py:287
  120.1 12.6 %all-to-all-start.3 = ((bf16[16,12,768]{2,1,0:T(8,128)(2,1)}), bf16[16,12,768]{2,1,0:T(8,128)(2,1)}, u32[]{:S(2)}, u32[]{:S(2)}) async-start(bf16[16,12,768]{2,1,0:T(8,128)(2,1)} %shard_map.137), calls=%async_computation.3 | async-start | bytes 786432 | tf_op jit(solution)/shard_map/all_to_all | solution.py:390
  132.7 1.4 collective-permute-start.10
  134.2 2.1 %collective-permute-start.9 = (bf16[128,1536]{1,0:T(8,128)(2,1)}, bf16[128,1536]{1,0:T(8,128)(2,1)}, u32[]{:S(2)}, u32[]{:S(2)}) collective-permute-start(bf16[128,1536]{1,0:T(8,128)(2,1)} %copy-done.39), channel_id=1, source_target_pairs={{2,0},{3,1},{4,2},{5,3},{6,4},{7,5},{8,6},{9,7},{10,8},{11,9},{12,... | collective-permute-start | bytes 1179656 | tf_op jit(solution)/shard_map/ppermute | solution.py:379
  136.3 7.7 %all-to-all-done.3 = bf16[16,12,768]{2,1,0:T(8,128)(2,1)} async-done(((bf16[16,12,768]{2,1,0:T(8,128)(2,1)}), bf16[16,12,768]{2,1,0:T(8,128)(2,1)}, u32[]{:S(2)}, u32[]{:S(2)}) %all-to-all-start.3) | async-done | bytes 294944 | tf_op jit(solution)/shard_map/all_to_all | solution.py:390
  143.9 4.2 %all-to-all-start.2 = ((bf16[8,16,3072]{2,1,0:T(8,128)(2,1)}), bf16[8,16,3072]{2,1,0:T(8,128)(2,1)}, u32[]{:S(2)}, u32[]{:S(2)}) async-start(bf16[8,16,3072]{2,1,0:T(8,128)(2,1)} %bitcast.17), calls=%async_computation.2 | async-start | bytes 1572864 | tf_op jit(solution)/shard_map/all_to_all | solution.py:370
  148.2 1.1 convert_reduce_fusion
  150.5 3.2 %collective-permute-start.12 = (f32[6,768]{1,0:T(8,128)}, f32[6,768]{1,0:T(8,128)}, u32[]{:S(2)}, u32[]{:S(2)}) collective-permute-start(f32[6,768]{1,0:T(8,128)} %constant_dynamic-slice_fusion), channel_id=1, source_target_pairs={{0,1},{1,0},{2,3},{3,2},{4,5},{5,4},{6,7},{7,6},{8,9},{9,8},{10,11... | collective-permute-start | bytes 55304 | tf_op jit(solution)/shard_map/ppermute | solution.py:394
  153.7 12.1 %collective-permute-done.9.near = bf16[128,1536]{1,0:T(8,128)(2,1)} collective-permute-done((bf16[128,1536]{1,0:T(8,128)(2,1)}, bf16[128,1536]{1,0:T(8,128)(2,1)}, u32[]{:S(2)}, u32[]{:S(2)}) %collective-permute-start.9) | collective-permute-done | bytes 393248 | tf_op jit(solution)/shard_map/ppermute | solution.py:379
  165.9 1.0 copy-done.18
  166.9 1.1 copy-done.26
  168.0 0.9 copy-done.36
  168.9 1.9 shard_map.135
  171.6 1.7 collective-permute-start.11
  175.0 1.3 copy-done.5
  176.3 1.0 copy-done.28
  177.2 0.9 copy-done.34
  178.1 10.0 %shard_map.136 = (bf16[128,1536]{1,0:T(8,128)(2,1)}, bf16[128,1536]{1,0:T(8,128)(2,1)}, bf16[128,1536]{1,0:T(8,128)(2,1)}, bf16[128,1536]{1,0:T(8,128)(2,1)}) custom-call(s32[1]{0:T(128)} %bitcast.me, bf16[768,1536]{1,0:T(8,128)(2,1)S(1)} %copy-done, bf16[384,1536]{1,0:T(8,128)(2,1)S(1)} %copy-done.3, bf16[384,1536]{1,0:T(8,128)(2,1)S(1)} %copy-done.5, ...), custom_call_target="tpu_custom_call" | custom-call | tf_op jit(solution)/shard_map/pallas_call | solution.py:287
  (94 shorter events, 10.2 us)
Async XLA Ops:
  7.2 75.3 %all-gather.2.cloned.1.call-start = ((), (), s32[]{:S(2)}) async-start(), calls=%async_computation.4 | async-start | bytes 2654208 | tf_op jit(solution)/shard_map/all_gather | solution.py:326
  7.2 8.2 %collective-permute-start = (bf16[48,1536]{1,0:T(8,128)(2,1)}, bf16[48,1536]{1,0:T(8,128)(2,1)S(1)}, u32[]{:S(2)}, u32[]{:S(2)}) collective-permute-start(bf16[48,1536]{1,0:T(8,128)(2,1)} %param.16), channel_id=1, source_target_pairs={{0,34},{1,35},{2,32},{3,33},{4,38},{5,39},{6,36},{7,37},{8,42},{9,... | collective-permute-start | bytes 442376 | tf_op jit(solution)/shard_map/ppermute | solution.py:314
  7.5 1.0 copy-start.29
  8.5 1.0 copy-start.30
  9.5 1.0 copy-start.31
  12.1 21.9 %copy-start.42 = (s32[16,7]{0,1:T(8,128)S(1)}, s32[16,7]{0,1:T(8,128)}, u32[]{:S(2)}) copy-start(s32[16,7]{0,1:T(8,128)} %param.14) | copy-start | bytes 1348
  15.4 45.1 %copy-start.19 = (bf16[64,2304]{1,0:T(8,128)(2,1)}, bf16[64,2304]{1,0:T(8,128)(2,1)S(1)}, u32[]{:S(2)}) copy-start(bf16[64,2304]{1,0:T(8,128)(2,1)S(1)} %get-tuple-element.46.q0) | copy-start | bytes 884740
  17.2 51.6 %all-to-all-start = ((bf16[8,16,3968]{2,1,0:T(8,128)(2,1)}), bf16[8,16,3968]{2,1,0:T(8,128)(2,1)S(1)}, u32[]{:S(2)}, u32[]{:S(2)}) async-start(bf16[8,16,3968]{2,1,0:T(8,128)(2,1)} %bitcast.5), calls=%async_computation | async-start | bytes 2031616 | tf_op jit(solution)/shard_map/all_to_all | solution.py:327
  21.8 2.2 %collective-permute-start.4 = (bf16[64,1536]{1,0:T(8,128)(2,1)S(1)}, bf16[64,1536]{1,0:T(8,128)(2,1)S(1)}, u32[]{:S(2)}, u32[]{:S(2)}) collective-permute-start(bf16[64,1536]{1,0:T(8,128)(2,1)S(1)} %get-tuple-element.41), channel_id=1, source_target_pairs={{0,1},{1,0},{2,3},{3,2},{4,5},{5,4},{6,7},{7,6},{8,9},{9,8},{10,11... | collective-permute-start | bytes 589832 | tf_op jit(solution)/shard_map/ppermute | solution.py:328
  24.0 36.5 %copy-start.7 = (bf16[128,1536]{1,0:T(8,128)(2,1)}, bf16[128,1536]{1,0:T(8,128)(2,1)S(1)}, u32[]{:S(2)}) copy-start(bf16[128,1536]{1,0:T(8,128)(2,1)S(1)} %constant_dynamic-update-slice_fusion.own) | copy-start | bytes 1179652
  24.0 19.6 %collective-permute-start.6 = (bf16[128,1536]{1,0:T(8,128)(2,1)S(1)}, bf16[128,1536]{1,0:T(8,128)(2,1)S(1)}, u32[]{:S(2)}, u32[]{:S(2)}) collective-permute-start(bf16[128,1536]{1,0:T(8,128)(2,1)S(1)} %constant_dynamic-update-slice_fusion.own), channel_id=1, source_target_pairs={{0,2},{1,3},{2,4},{3,5},{4,6},{5,7},{6,8},{7,9},{8,10},{9,11},{10,... | collective-permute-start | bytes 1179656 | tf_op jit(solution)/shard_map/ppermute | solution.py:329
  29.4 31.1 %collective-permute-start.5 = (bf16[128,1536]{1,0:T(8,128)(2,1)S(1)}, bf16[128,1536]{1,0:T(8,128)(2,1)S(1)}, u32[]{:S(2)}, u32[]{:S(2)}) collective-permute-start(bf16[128,1536]{1,0:T(8,128)(2,1)S(1)} %constant_dynamic-update-slice_fusion.own), channel_id=1, source_target_pairs={{0,4},{1,5},{2,6},{3,7},{4,8},{5,9},{6,10},{7,11},{8,12},{9,13},{1... | collective-permute-start | bytes 1179656 | tf_op jit(solution)/shard_map/ppermute | solution.py:330
  33.0 4.5 %collective-permute-start.3 = (bf16[64,2304]{1,0:T(8,128)(2,1)}, bf16[64,2304]{1,0:T(8,128)(2,1)S(1)}, u32[]{:S(2)}, u32[]{:S(2)}) collective-permute-start(bf16[64,2304]{1,0:T(8,128)(2,1)} %get-tuple-element.39), channel_id=1, source_target_pairs={{0,1},{1,0},{2,3},{3,2},{4,5},{5,4},{6,7},{7,6},{8,9},{9,8},{10,11... | collective-permute-start | bytes 884744 | tf_op jit(solution)/shard_map/ppermute | solution.py:331
  34.1 2.6 %copy-start.1 = (bf16[7,256,1536]{2,1,0:T(8,128)(2,1)S(1)}, bf16[7,256,1536]{2,1,0:T(8,128)(2,1)}, u32[]{:S(2)}) copy-start(bf16[7,256,1536]{2,1,0:T(8,128)(2,1)} %table.1) | copy-start | bytes 16515076
  36.7 23.9 %copy-start.38 = (s32[12]{0:T(128)S(1)}, s32[12]{0:T(128)}, u32[]{:S(2)}) copy-start(s32[12]{0:T(128)} %windows.1) | copy-start | bytes 148
  37.5 28.4 %copy-start.33 = (f32[16,1536]{1,0:T(8,128)}, f32[16,1536]{1,0:T(8,128)S(1)}, u32[]{:S(2)}) copy-start(f32[16,1536]{1,0:T(8,128)S(1)} %shard_map.129.action) | copy-start | bytes 294916
  37.5 36.9 %copy-start.21 = (bf16[64,2304]{1,0:T(8,128)(2,1)}, bf16[64,2304]{1,0:T(8,128)(2,1)S(1)}, u32[]{:S(2)}) copy-start(bf16[64,2304]{1,0:T(8,128)(2,1)S(1)} %collective-permute-done.3.q1) | copy-start | bytes 884740
  43.7 30.8 %copy-start.11 = (bf16[128,1536]{1,0:T(8,128)(2,1)}, bf16[128,1536]{1,0:T(8,128)(2,1)S(1)}, u32[]{:S(2)}) copy-start(bf16[128,1536]{1,0:T(8,128)(2,1)S(1)} %collective-permute-done.6.near) | copy-start | bytes 1179652
  60.5 13.9 %copy-start.13 = (bf16[128,1536]{1,0:T(8,128)(2,1)}, bf16[128,1536]{1,0:T(8,128)(2,1)S(1)}, u32[]{:S(2)}) copy-start(bf16[128,1536]{1,0:T(8,128)(2,1)S(1)} %collective-permute-done.5.far) | copy-start | bytes 1179652
  64.5 1.5 copy-start.9
  66.0 8.5 %copy-start.17 = (bf16[128,1536]{1,0:T(8,128)(2,1)}, bf16[128,1536]{1,0:T(8,128)(2,1)S(1)}, u32[]{:S(2)}) copy-start(bf16[128,1536]{1,0:T(8,128)(2,1)S(1)} %get-tuple-element.42.own_time.kept) | copy-start | bytes 1179652
  66.0 4.5 %collective-permute-start.8 = (bf16[128,1536]{1,0:T(8,128)(2,1)}, bf16[128,1536]{1,0:T(8,128)(2,1)S(1)}, u32[]{:S(2)}, u32[]{:S(2)}) collective-permute-start(bf16[128,1536]{1,0:T(8,128)(2,1)} %get-tuple-element.51), channel_id=1, source_target_pairs={{0,1},{1,0},{2,3},{3,2},{4,5},{5,4},{6,7},{7,6},{8,9},{9,8},{10,11... | collective-permute-start | bytes 1179656 | tf_op jit(solution)/shard_map/ppermute | solution.py:349
  70.5 1.7 collective-permute-start.7
  75.2 42.0 %all-to-all-start.1 = ((bf16[8,192,768]{2,1,0:T(8,128)(2,1)}), bf16[8,192,768]{2,1,0:T(8,128)(2,1)}, u32[]{:S(2)}, u32[]{:S(2)}) async-start(bf16[8,192,768]{2,1,0:T(8,128)(2,1)} %bitcast.8), calls=%async_computation.1 | async-start | bytes 4718592 | tf_op jit(solution)/shard_map/all_to_all | solution.py:357
  82.5 5.0 %copy-start = (bf16[768,1536]{1,0:T(8,128)(2,1)S(1)}, bf16[768,1536]{1,0:T(8,128)(2,1)}, u32[]{:S(2)}) copy-start(bf16[768,1536]{1,0:T(8,128)(2,1)} %all-gather.2.cloned.1.call-done.w_own) | copy-start | bytes 7077892
  82.5 5.0 %copy-start.16 = (bf16[128,1536]{1,0:T(8,128)(2,1)S(1)}, bf16[128,1536]{1,0:T(8,128)(2,1)}, u32[]{:S(2)}) copy-start(bf16[128,1536]{1,0:T(8,128)(2,1)} %copy-done.15) | copy-start | bytes 1179652
  82.5 4.9 %copy-start.24 = (f32[6,256,128]{2,1,0:T(8,128)S(1)}, f32[6,256,128]{2,1,0:T(8,128)}, u32[]{:S(2)}) copy-start(f32[6,256,128]{2,1,0:T(8,128)} %copy-done.23) | copy-start | bytes 2359300
  84.4 3.0 %collective-permute-start.1 = (bf16[384,1536]{1,0:T(8,128)(2,1)S(1)}, bf16[384,1536]{1,0:T(8,128)(2,1)S(1)}, u32[]{:S(2)}, u32[]{:S(2)}) collective-permute-start(bf16[384,1536]{1,0:T(8,128)(2,1)S(1)} %get-tuple-element.64), channel_id=1, source_target_pairs={{0,1},{1,0},{2,3},{3,2},{4,5},{5,4},{6,7},{7,6},{8,9},{9,8},{10,11... | collective-permute-start | bytes 3538952 | tf_op jit(solution)/shard_map/ppermute | solution.py:359
  85.0 8.8 %collective-permute-start.2 = (bf16[384,1536]{1,0:T(8,128)(2,1)S(1)}, bf16[384,1536]{1,0:T(8,128)(2,1)S(1)}, u32[]{:S(2)}, u32[]{:S(2)}) collective-permute-start(bf16[384,1536]{1,0:T(8,128)(2,1)S(1)} %get-tuple-element.63), channel_id=1, source_target_pairs={{0,1},{1,0},{2,3},{3,2},{4,5},{5,4},{6,7},{7,6},{8,9},{9,8},{10,11... | collective-permute-start | bytes 3538952 | tf_op jit(solution)/shard_map/ppermute | solution.py:360
  87.4 5.5 %copy-start.2 = (bf16[384,1536]{1,0:T(8,128)(2,1)}, bf16[384,1536]{1,0:T(8,128)(2,1)S(1)}, u32[]{:S(2)}) copy-start(bf16[384,1536]{1,0:T(8,128)(2,1)S(1)} %collective-permute-done.1.w_other.w_view) | copy-start | bytes 3538948
  87.4 6.3 %copy-start.8 = (bf16[128,1536]{1,0:T(8,128)(2,1)S(1)}, bf16[128,1536]{1,0:T(8,128)(2,1)}, u32[]{:S(2)}) copy-start(bf16[128,1536]{1,0:T(8,128)(2,1)} %copy-done.7) | copy-start | bytes 1179652
  87.5 6.3 %copy-start.10 = (f32[6,256,384]{2,1,0:T(8,128)S(1)}, f32[6,256,384]{2,1,0:T(8,128)}, u32[]{:S(2)}) copy-start(f32[6,256,384]{2,1,0:T(8,128)} %copy-done.9) | copy-start | bytes 7077892
  87.5 6.3 %copy-start.12 = (bf16[128,1536]{1,0:T(8,128)(2,1)S(1)}, bf16[128,1536]{1,0:T(8,128)(2,1)}, u32[]{:S(2)}) copy-start(bf16[128,1536]{1,0:T(8,128)(2,1)} %copy-done.11) | copy-start | bytes 1179652
  87.5 6.3 %copy-start.14 = (bf16[128,1536]{1,0:T(8,128)(2,1)S(1)}, bf16[128,1536]{1,0:T(8,128)(2,1)}, u32[]{:S(2)}) copy-start(bf16[128,1536]{1,0:T(8,128)(2,1)} %copy-done.13) | copy-start | bytes 1179652
  87.5 6.3 %copy-start.20 = (bf16[64,2304]{1,0:T(8,128)(2,1)S(1)}, bf16[64,2304]{1,0:T(8,128)(2,1)}, u32[]{:S(2)}) copy-start(bf16[64,2304]{1,0:T(8,128)(2,1)} %copy-done.19) | copy-start | bytes 884740
  87.5 6.3 %copy-start.22 = (bf16[64,2304]{1,0:T(8,128)(2,1)S(1)}, bf16[64,2304]{1,0:T(8,128)(2,1)}, u32[]{:S(2)}) copy-start(bf16[64,2304]{1,0:T(8,128)(2,1)} %copy-done.21) | copy-start | bytes 884740
  100.6 1.0 copy-start.4
  120.1 23.8 %all-to-all-start.3 = ((bf16[16,12,768]{2,1,0:T(8,128)(2,1)}), bf16[16,12,768]{2,1,0:T(8,128)(2,1)}, u32[]{:S(2)}, u32[]{:S(2)}) async-start(bf16[16,12,768]{2,1,0:T(8,128)(2,1)} %shard_map.137), calls=%async_computation.3 | async-start | bytes 786432 | tf_op jit(solution)/shard_map/all_to_all | solution.py:390
  132.7 42.2 %copy-start.3 = (bf16[384,1536]{1,0:T(8,128)(2,1)S(1)}, bf16[384,1536]{1,0:T(8,128)(2,1)}, u32[]{:S(2)}) copy-start(bf16[384,1536]{1,0:T(8,128)(2,1)} %copy-done.2) | copy-start | bytes 3538948
  132.7 21.0 %collective-permute-start.10 = (bf16[128,1536]{1,0:T(8,128)(2,1)}, bf16[128,1536]{1,0:T(8,128)(2,1)}, u32[]{:S(2)}, u32[]{:S(2)}) collective-permute-start(bf16[128,1536]{1,0:T(8,128)(2,1)} %copy-done.40), channel_id=1, source_target_pairs={{4,0},{5,1},{6,2},{7,3},{8,4},{9,5},{10,6},{11,7},{12,8},{13,9},{1... | collective-permute-start | bytes 1179656 | tf_op jit(solution)/shard_map/ppermute | solution.py:380
  134.2 31.7 %collective-permute-start.9 = (bf16[128,1536]{1,0:T(8,128)(2,1)}, bf16[128,1536]{1,0:T(8,128)(2,1)}, u32[]{:S(2)}, u32[]{:S(2)}) collective-permute-start(bf16[128,1536]{1,0:T(8,128)(2,1)} %copy-done.39), channel_id=1, source_target_pairs={{2,0},{3,1},{4,2},{5,3},{6,4},{7,5},{8,6},{9,7},{10,8},{11,9},{12,... | collective-permute-start | bytes 1179656 | tf_op jit(solution)/shard_map/ppermute | solution.py:379
  143.9 30.8 %all-to-all-start.2 = ((bf16[8,16,3072]{2,1,0:T(8,128)(2,1)}), bf16[8,16,3072]{2,1,0:T(8,128)(2,1)}, u32[]{:S(2)}, u32[]{:S(2)}) async-start(bf16[8,16,3072]{2,1,0:T(8,128)(2,1)} %bitcast.17), calls=%async_computation.2 | async-start | bytes 1572864 | tf_op jit(solution)/shard_map/all_to_all | solution.py:370
  150.5 22.8 %collective-permute-start.12 = (f32[6,768]{1,0:T(8,128)}, f32[6,768]{1,0:T(8,128)}, u32[]{:S(2)}, u32[]{:S(2)}) collective-permute-start(f32[6,768]{1,0:T(8,128)} %constant_dynamic-slice_fusion), channel_id=1, source_target_pairs={{0,1},{1,0},{2,3},{3,2},{4,5},{5,4},{6,7},{7,6},{8,9},{9,8},{10,11... | collective-permute-start | bytes 55304 | tf_op jit(solution)/shard_map/ppermute | solution.py:394
  165.9 1.0 copy-start.18
  166.8 1.1 copy-start.26
  171.6 3.4 %collective-permute-start.11 = (bf16[64,3072]{1,0:T(8,128)(2,1)}, bf16[64,3072]{1,0:T(8,128)(2,1)}, u32[]{:S(2)}, u32[]{:S(2)}) collective-permute-start(bf16[64,3072]{1,0:T(8,128)(2,1)} %get-tuple-element.56), channel_id=1, source_target_pairs={{0,1},{1,0},{2,3},{3,2},{4,5},{5,4},{6,7},{7,6},{8,9},{9,8},{10,11... | collective-permute-start | bytes 1179656 | tf_op jit(solution)/shard_map/ppermute | solution.py:402
  175.0 1.3 copy-start.5
  176.2 1.0 copy-start.28
  (13 other events, 10.5 us)
Sparse Core Ops, SparseCore 0:
  17.3 57.2 all-gather.1

commit v5 on v4

--- a/solution.py
+++ b/solution.py
@@ -163,27 +163,28 @@
         out_ref[i * CW : (i + 1) * CW, :] = (dot_tn(left, right) * scale).astype(BF)
 
 
-def fetch_weight(me, own, others, held, sem, first, count):
-    size = held.shape[0] // (4 * count)
+def fetch_weight(me, z, own, others, held, sem):
+    depth = len(own)
+    size = own[0].shape[0] // 2
     core, y = me[0] % 2, me[0] // 2
     copies = []
-    for z in range(count):
-        other = others[z * len(others) // count]
-        for e in range(2):
-            for n, (which, ref, place) in enumerate(
-                ((core, own, 2 * (first + z) + e), (1 - core, other, 2 * (z % (count // len(others))) + e))
-            ):
-                start = pl.multiple_of((4 * z + 2 * (y ^ e) + which) * size, 16)
+    for i in range(depth):
+        place = lax.rem(z[0] + offset(i, depth), depth)
+        for n, (which, ref) in enumerate(((core, own[i]), (1 - core, others[i]))):
+            for e in range(2):
+                start = pl.multiple_of((4 * place + 2 * (y ^ e) + which) * size, 16)
                 copies.append(
                     pltpu.make_async_copy(
-                        ref.at[pl.ds(place * size, size)],
-                        held.at[pl.ds(start, size)],
-                        sem.at[4 * z + 2 * e + n],
+                        ref.at[pl.ds(e * size, size)], held.at[pl.ds(start, size)], sem.at[4 * i + 2 * n + e]
                     )
                 )
     for copy in copies:
         copy.start()
     return copies
+
+
+def offset(i, depth):
+    return (i + 1) // 2 if i % 2 == 0 else depth - (i + 1) // 2
 
 
 def backward_pair(q, k, v, g, prob):
@@ -197,27 +198,27 @@
     return dq, dk, dv
 
 
-def view_backward_kernel(depth, me, x, kept, prob_ref, w_own, w_other, out_ref, w, sem):
-    copies = fetch_weight(me, w_own, (w_other,), w, sem, 0, depth // 2)
+def view_backward_kernel(depth, me, z, x, kept, prob_ref, *rest):
+    own, others, (out_ref, full_ref, w, sem, full_sem) = rest[:depth], rest[depth : 2 * depth], rest[2 * depth :]
+    copies = fetch_weight(me, z, own, others, w, sem)
     out_ref[:, :CW] = kept[:, :CW]
     for copy in copies:
         copy.wait()
-    grad = dot_nt(x[:, 3 * CW : 5 * CW], w[...]).astype(BF)
+    full = pltpu.make_async_copy(w, full_ref, full_sem)
+    full.start()
+    grad = dot_nt(x[:, 3 * CW : 5 * CW], w[:CW]).astype(BF)
     for j in range(PAIRS):
         at = [slice(i * CW + 128 * j, i * CW + 128 * (j + 1)) for i in range(4)]
         dq, dk, dv = backward_pair(x[:, at[0]], x[:, at[1]], x[:, at[2]], grad[:, at[0]], prob_ref[j])
         out_ref[:, at[1]] = dq.astype(BF)
         out_ref[:, at[2]] = dk.astype(BF)
         out_ref[:, at[3]] = dv.astype(BF)
-
-
-def time_backward_kernel(depth, me, q0, q1, far, near, own, prob_ref, w_own, w_other, *rest):
-    dq_ref, own_ref, near_ref, far_ref, w, sem = rest
+    full.wait()
+
+
+def time_backward_kernel(q0, q1, far, near, own, prob_ref, w, dq_ref, own_ref, near_ref, far_ref):
     qct, kv = (q0, q1), (far, near, own)
-    copies = fetch_weight(me, w_own, (w_other,), w, sem, depth // 2, depth // 2)
     rows = PAIR * q0.shape[0]
-    for copy in copies:
-        copy.wait()
     grad = dot_nt(rows_of(qct, slice(CW, 3 * CW)), w[...]).astype(BF)
     for j in range(PAIRS):
         at = [slice(i * CW + 128 * j, i * CW + 128 * (j + 1)) for i in range(2)]
@@ -260,10 +261,8 @@
         out_ref[i] = held[i * size : (i + 1) * size, :].astype(BF)
 
 
-def finish_kernel(depth, me, w_own, w_view, w_time, action, t0, t1, view, *rest):
+def finish_kernel(me, w, action, t0, t1, view, pred_ref, dq_ref, dk_ref, dv_ref):
     time = (t0, t1)
-    pred_ref, dq_ref, dk_ref, dv_ref, w, sem = rest
-    copies = fetch_weight(me, w_own, (w_view, w_time), w, sem, 0, depth)
     rows = view.shape[0]
     frames = rows // 8
     row = iota((rows, rows), 0)
@@ -275,22 +274,27 @@
         ref[:, :CW] = view[:, part]
         ref[:, CW:] = dot_nn(perm, rows_of(time, part)).astype(BF)
     attn_time = dot_nn(perm, rows_of(time, slice(0, CW))).astype(BF)
-    for copy in copies:
-        copy.wait()
     mixed = dot_nn(view[:, :CW], w[:CW]) + dot_nn(attn_time, w[CW:])
     total = mixed.reshape(frames, 8, 2 * CW) + action[...][:, None, :]
     pred_ref[...] = total.reshape(rows, 2 * CW).astype(BF)
 
 
-def call(kernel, outs, specs, *args, scratch=()):
+def whole(shape):
+    return pl.BlockSpec(shape, lambda *at: (0,) * len(shape))
+
+
+def call(kernel, outs, specs, *args, scratch=(), kept=0):
+    specs = [whole(arg.shape) if spec is VM else spec for spec, arg in zip(specs, args)]
+    count = len(outs) - kept
     return list(
         pl.pallas_call(
             kernel,
             out_shape=[jax.ShapeDtypeStruct(shape, kind) for shape, kind in outs],
             in_specs=specs,
-            out_specs=[VM] * len(outs),
+            out_specs=[whole(shape) for shape, _ in outs[:count]] + [ANY] * kept,
+            grid=(1,),
             scratch_shapes=list(scratch),
-            compiler_params=pltpu.CompilerParams(vmem_limit_bytes=20 * 1024 * 1024),
+            compiler_params=pltpu.CompilerParams(vmem_limit_bytes=56 * 1024 * 1024),
         )(*args)
     )
 
@@ -305,9 +309,11 @@
     core = at_tm % 2
     me = (at_tm % GROUP).reshape(1)
     pair = (at_tm // PAIR).reshape(1)
+    group = (at_tm // GROUP).reshape(1)
     depth = tm // GROUP
     same_core = [[2 * i + j for i in range(tm // 2)] for j in range(2)]
-    along_z = [[GROUP * i + j for i in range(depth)] for j in range(GROUP)]
+    up = [(i, (i + GROUP) % tm) for i in range(tm)]
+    down = [(i, (i - GROUP) % tm) for i in range(tm)]
     swap = [(i, i ^ 1) for i in range(tm)]
     beside = [(i, i ^ (tm + 2)) for i in range(cams * tm)]
 
@@ -323,15 +329,36 @@
     view_send, kv, qct = packed[0], packed[1 : PAIR + 1], packed[PAIR + 1 :]
     w_beside, view_send = lax.optimization_barrier((w_beside, view_send))
     w_both = jnp.concatenate([w_out, w_beside], axis=0)
-    w_own = lax.all_gather(w_both, "tm", axis=0, tiled=True, axis_index_groups=along_z)
     view_x = lax.all_to_all(view_send, "cam", 0, 0, tiled=True)
+    w_own, w_other = [w_both], []
+
+    def pass_on(first, last):
+        for i in range(first, min(last, depth)):
+            w_own.append(lax.ppermute(w_own[max(i - 2, 0)], "tm", up if i % 2 else down))
+
+    def swap_blocks(last):
+        for block_rows in w_own[len(w_other) : last]:
+            w_other.append(lax.ppermute(block_rows, "tm", swap))
+
+    def tie(value):
+        value, w_own[:], w_other[:] = lax.optimization_barrier((value, w_own[:], w_other[:]))
+        return value
+
+    pass_on(1, 3)
+    swap_blocks(1)
     own = jnp.concatenate([kv[0], lax.ppermute(kv[1], "tm", swap)], axis=0)
     near = lax.ppermute(own, "tm", [(i, i + 2) for i in range(tm - 2)])
     far = lax.ppermute(own, "tm", [(i, i + 4) for i in range(tm - 4)])
     q0, q1 = qct[0], lax.ppermute(qct[1], "tm", swap)
 
+    q0 = tie(q0)
+    pass_on(3, 5)
+    swap_blocks(3)
     (action_sum,) = call(action_kernel, [((frames, width), F32)], [VM] * 2, actions, act_table)
     view_x, action_sum = lax.optimization_barrier((view_x, action_sum))
+    near, far = tie((near, far))
+    pass_on(5, 7)
+    swap_blocks(5)
     kept_view, view_swap, prob_view = call(
         view_forward_kernel,
         [((rows, 2 * CW), BF)] * 2 + [((PAIRS, 2 * rows, rows), F32)],
@@ -345,6 +372,9 @@
         windows, me, pair, q0, q1, far, near, own,
     )
 
+    kept_view = tie(kept_view)
+    pass_on(7, depth)
+    swap_blocks(depth)
     view_swap = lax.ppermute(view_swap, "tm", swap)
     time_swap = lax.ppermute(time_swap, "tm", swap)
     grad_norm = 1.0 / math.sqrt(cams * tm * rows)
@@ -356,24 +386,21 @@
     )
     part = lax.all_to_all(part.reshape(cams, width // cams, CW), "cam", 0, 0, tiled=True)
 
-    w_view = lax.ppermute(w_own[: CW // 2], "tm", swap)
-    w_time = lax.ppermute(w_own[CW // 2 :], "tm", swap)
-    half_weight = [pltpu.VMEM((CW, width), BF), pltpu.SemaphoreType.DMA((tm // 2,))]
-    (view_out,) = call(
+    view_out, w_full = call(
         functools.partial(view_backward_kernel, depth),
-        [((rows, 4 * CW), BF)],
-        [SM] + [VM] * 3 + [ANY] * 2,
-        me, view_x, kept_view, prob_view, w_own, w_view,
-        scratch=half_weight,
+        [((rows, 4 * CW), BF), ((width, width), BF)],
+        [SM] * 2 + [VM] * 3 + [ANY] * (2 * depth),
+        me, group, view_x, kept_view, prob_view, *w_own, *w_other,
+        scratch=[pltpu.VMEM((width, width), BF), pltpu.SemaphoreType.DMA((tm,)), pltpu.SemaphoreType.DMA],
+        kept=1,
     )
     q0, view_out = lax.optimization_barrier((q0, view_out))
     view_back = lax.all_to_all(view_out, "cam", 0, 0, tiled=True)
     dq_time, own_grad, near_grad, far_grad = call(
-        functools.partial(time_backward_kernel, depth),
+        time_backward_kernel,
         [((rows, CW), BF), ((rows, 2 * CW), F32), ((rows, 2 * CW), BF), ((rows, 2 * CW), BF)],
-        [SM] + [VM] * 6 + [ANY] * 2,
-        me, q0, q1, far, near, own, prob_time, w_own, w_time,
-        scratch=half_weight,
+        [VM] * 6 + [pl.BlockSpec((CW, width), lambda *at: (1, 0))],
+        q0, q1, far, near, own, prob_time, w_full,
     )
     part, near_grad = lax.optimization_barrier((part, near_grad))
     near_grad = lax.ppermute(near_grad, "tm", [(i + 2, i) for i in range(tm - 2)])
@@ -387,6 +414,7 @@
         part,
         scratch=[pltpu.VMEM((width // cams, CW), F32)],
     )
+    part, view_back, near_grad, far_grad = lax.optimization_barrier((part, view_back, near_grad, far_grad))
     part = lax.all_to_all(part, "tm", 0, 0, tiled=True, axis_index_groups=same_core)
     part = jnp.sum(part.astype(F32), axis=0)
     final = width // cams // tm
@@ -401,11 +429,10 @@
     )
     t1 = lax.ppermute(t1, "tm", swap)
     outs = call(
-        functools.partial(finish_kernel, depth),
+        finish_kernel,
         [((rows, width), BF)] * 4,
-        [SM] + [ANY] * 3 + [VM] * 4,
-        me, w_own, w_view, w_time, action_sum, t0, t1, view_back,
-        scratch=[pltpu.VMEM((width, width), BF), pltpu.SemaphoreType.DMA((tm,))],
+        [SM] + [VM] * 5,
+        me, w_full, action_sum, t0, t1, view_back,
     )
     return tuple(a.reshape(1, frames, tokens, width) for a in outs) + (grad_out_weight,)
 

time: 196 us -> 191 us (0.974)
  the two profiles are of different devices: /device:TPU:17 before, /device:TPU:1 now
where the time goes in v5:
time: 191 us; the launch traced here: 190 us
  starting transfers between devices  70 us (37%)
  waiting for transfers between devices  65.1 us (34%)
  Pallas kernels  45.7 us (24%)
  local copies, waits for them, and re-layouts  7.57 us (4%)
    pallas_call x10, Pallas kernels, call(): pl.pallas_call(kernel, out_shape=[jax.ShapeDtypeStruct(shape, kind) for s...  45.7 us
    ppermute x7, waiting for transfers between devices, pass_on(): lax.ppermute(w_own[max(i - 2, 0)], 'tm', up if i % 2 else down)  21.3 us
    ppermute x7, starting transfers between devices, pass_on(): lax.ppermute(w_own[max(i - 2, 0)], 'tm', up if i % 2 else down)  15.7 us
    ppermute x1, waiting for transfers between devices, shards(): lax.ppermute(near_grad, 'tm', [(i + 2, i) for i in range(tm - 2)])  15.4 us
    all_to_all x1, waiting for transfers between devices, shards(): lax.all_to_all(part.reshape(cams, width // cams, CW), 'cam', 0, 0, tiled=...  13.8 us
    all_to_all x1, starting transfers between devices, shards(): lax.all_to_all(part, 'tm', 0, 0, tiled=True, axis_index_groups=same_core)  12.7 us
    ppermute x8, starting transfers between devices, swap_blocks(): w_other.append(lax.ppermute(block_rows, 'tm', swap))  8.47 us
    unnamed x53, local copies, waits for them, and re-layouts  7.53 us
  transfers between devices with their start and end apart: 30, of which 10 were waited for; matrix products, arithmetic and copies ran while one was open for 1% of the time, Pallas kernels for 22%

profile of v5, /device:TPU:1, one launch (start us, length us, event | category | flops | bytes accessed | tf_op | source)
XLA Modules:
  0.0 190.0 jit_solution(7688603064584246058)
XLA Ops:
  0.6 3.7 %collective-permute-start = (bf16[48,1536]{1,0:T(8,128)(2,1)}, bf16[48,1536]{1,0:T(8,128)(2,1)S(1)}, u32[]{:S(2)}, u32[]{:S(2)}) collective-permute-start(bf16[48,1536]{1,0:T(8,128)(2,1)} %param.16), channel_id=1, source_target_pairs={{0,34},{1,35},{2,32},{3,33},{4,38},{5,39},{6,36},{7,37},{8,42},{9,... | collective-permute-start | bytes 442376 | tf_op jit(solution)/shard_map/ppermute | solution.py:320
  4.3 3.8 %shard_map.128 = (bf16[128,3968]{1,0:T(8,128)(2,1)}, bf16[64,1536]{1,0:T(8,128)(2,1)}, bf16[64,1536]{1,0:T(8,128)(2,1)}, bf16[64,2304]{1,0:T(8,128)(2,1)}, bf16[64,2304]{1,0:T(8,128)(2,1)}) custom-call(s32[1]{0:T(128)} %bitcast.me, s32[1,16]{1,0:T(1,128)} %valid.1, bf16[128,1536]{1,0:T(8,128)(2,1)} %bitcast.22, bf16[128,1536]{1,0:T(8,128)(2,1)} %bitcast.23, ...), custom_call_target="tpu_custom_call" | custom-call | tf_op jit(solution)/shard_map/pallas_call | solution.py:290
  8.1 1.0 collective-permute-start.1
  9.2 0.9 constant_dynamic-update-slice_fusion.1
  10.1 0.9 constant_dynamic-update-slice_fusion.3
  11.0 4.0 %all-to-all-start = ((bf16[8,16,3968]{2,1,0:T(8,128)(2,1)}), bf16[8,16,3968]{2,1,0:T(8,128)(2,1)S(1)}, u32[]{:S(2)}, u32[]{:S(2)}) async-start(bf16[8,16,3968]{2,1,0:T(8,128)(2,1)} %bitcast.20), calls=%async_computation | async-start | bytes 2031616 | tf_op jit(solution)/shard_map/all_to_all | solution.py:332
  15.1 2.8 %collective-permute-start.2 = (bf16[128,1536]{1,0:T(8,128)(2,1)S(1)}, bf16[128,1536]{1,0:T(8,128)(2,1)S(1)}, u32[]{:S(2)}, u32[]{:S(2)}) collective-permute-start(bf16[128,1536]{1,0:T(8,128)(2,1)S(1)} %constant_dynamic-update-slice_fusion.own), channel_id=1, source_target_pairs={{0,2},{1,3},{2,4},{3,5},{4,6},{5,7},{6,8},{7,9},{8,10},{9,11},{10,... | collective-permute-start | bytes 1179656 | tf_op jit(solution)/shard_map/ppermute | solution.py:350
  17.9 1.7 collective-permute-start.4
  19.6 4.0 %collective-permute-start.5 = (bf16[96,1536]{1,0:T(8,128)(2,1)S(1)}, bf16[96,1536]{1,0:T(8,128)(2,1)S(1)}, u32[]{:S(2)}, u32[]{:S(2)}) collective-permute-start(bf16[96,1536]{1,0:T(8,128)(2,1)S(1)} %constant_dynamic-update-slice_fusion.2.rest_0_), channel_id=1, source_target_pairs={{0,28},{1,29},{2,30},{3,31},{4,0},{5,1},{6,2},{7,3},{8,4},{9,5},{1... | collective-permute-start | bytes 884744 | tf_op jit(solution)/shard_map/ppermute | solution.py:337
  23.6 1.8 collective-permute-start.6
  25.5 1.3 collective-permute-start.3
  26.8 2.6 %collective-permute-done.4.rest_1_ = bf16[96,1536]{1,0:T(8,128)(2,1)S(1)} collective-permute-done((bf16[96,1536]{1,0:T(8,128)(2,1)S(1)}, bf16[96,1536]{1,0:T(8,128)(2,1)S(1)}, u32[]{:S(2)}, u32[]{:S(2)}) %collective-permute-start.4) | collective-permute-done | bytes 294944 | tf_op jit(solution)/shard_map/ppermute | solution.py:337
  29.5 2.3 %collective-permute-start.9 = (bf16[96,1536]{1,0:T(8,128)(2,1)S(1)}, bf16[96,1536]{1,0:T(8,128)(2,1)S(1)}, u32[]{:S(2)}, u32[]{:S(2)}) collective-permute-start(bf16[96,1536]{1,0:T(8,128)(2,1)S(1)} %collective-permute-done.4.rest_1_), channel_id=1, source_target_pairs={{0,1},{1,0},{2,3},{3,2},{4,5},{5,4},{6,7},{7,6},{8,9},{9,8},{10,11... | collective-permute-start | bytes 884744 | tf_op jit(solution)/shard_map/ppermute | solution.py:341
  31.7 2.9 %collective-permute-start.8 = (bf16[96,1536]{1,0:T(8,128)(2,1)S(1)}, bf16[96,1536]{1,0:T(8,128)(2,1)S(1)}, u32[]{:S(2)}, u32[]{:S(2)}) collective-permute-start(bf16[96,1536]{1,0:T(8,128)(2,1)S(1)} %collective-permute-done.5.rest_2_), channel_id=1, source_target_pairs={{0,28},{1,29},{2,30},{3,31},{4,0},{5,1},{6,2},{7,3},{8,4},{9,5},{1... | collective-permute-start | bytes 884744 | tf_op jit(solution)/shard_map/ppermute | solution.py:337
  34.7 0.8 collective-permute-start.10
  36.2 5.6 %collective-permute-done.7.rest_3_ = bf16[96,1536]{1,0:T(8,128)(2,1)} collective-permute-done((bf16[96,1536]{1,0:T(8,128)(2,1)S(1)}, bf16[96,1536]{1,0:T(8,128)(2,1)}, u32[]{:S(2)}, u32[]{:S(2)}) %collective-permute-start.7) | collective-permute-done | bytes 294944 | tf_op jit(solution)/shard_map/ppermute | solution.py:337
  43.4 2.4 %collective-permute-start.11 = (bf16[96,1536]{1,0:T(8,128)(2,1)}, bf16[96,1536]{1,0:T(8,128)(2,1)}, u32[]{:S(2)}, u32[]{:S(2)}) collective-permute-start(bf16[96,1536]{1,0:T(8,128)(2,1)} %collective-permute-done.7.rest_3_), channel_id=1, source_target_pairs={{0,4},{1,5},{2,6},{3,7},{4,8},{5,9},{6,10},{7,11},{8,12},{9,13},{1... | collective-permute-start | bytes 884744 | tf_op jit(solution)/shard_map/ppermute | solution.py:337
  46.5 4.1 %shard_map.129.action = f32[16,1536]{1,0:T(8,128)} custom-call(s32[16,7]{1,0:T(8,128)} %copy.14.actions, bf16[7,256,1536]{2,1,0:T(8,128)(2,1)} %table.1), custom_call_target="tpu_custom_call" | custom-call | tf_op jit(solution)/shard_map/pallas_call | solution.py:290
  51.3 5.7 %shard_map.132 = (bf16[128,1536]{1,0:T(8,128)(2,1)}, bf16[128,1536]{1,0:T(8,128)(2,1)}, f32[6,256,384]{2,1,0:T(8,128)}) custom-call(s32[12]{0:T(128)} %windows.1, s32[1]{0:T(128)} %bitcast.me, s32[1]{0:T(128)} %bitcast.8.pair, bf16[64,2304]{1,0:T(8,128)(2,1)} %get-tuple-element.110.q0, bf16[64,2304]{1,0:T(8,128)(2,1)} %copy-done.6, ...), custom_call_target="tpu_custom_call" | custom-call | tf_op jit(solution)/shard_map/pallas_call | solution.py:290
  57.1 0.8 collective-permute-start.21
  57.8 1.0 copy-done.1
  58.8 3.2 %shard_map.130 = (bf16[128,1536]{1,0:T(8,128)(2,1)}, bf16[128,1536]{1,0:T(8,128)(2,1)}, f32[6,256,128]{2,1,0:T(8,128)}) custom-call(s32[1]{0:T(128)} %bitcast.me, bf16[128,3968]{1,0:T(8,128)(2,1)} %bitcast.17), custom_call_target="tpu_custom_call" | custom-call | tf_op jit(solution)/shard_map/pallas_call | solution.py:290
  62.5 2.9 %collective-permute-start.12 = (bf16[96,1536]{1,0:T(8,128)(2,1)S(1)}, bf16[96,1536]{1,0:T(8,128)(2,1)S(1)}, u32[]{:S(2)}, u32[]{:S(2)}) collective-permute-start(bf16[96,1536]{1,0:T(8,128)(2,1)S(1)} %copy-done.18), channel_id=1, source_target_pairs={{0,28},{1,29},{2,30},{3,31},{4,0},{5,1},{6,2},{7,3},{8,4},{9,5},{1... | collective-permute-start | bytes 884744 | tf_op jit(solution)/shard_map/ppermute | solution.py:337
  65.6 6.1 %collective-permute-done.12.rest_6_ = bf16[96,1536]{1,0:T(8,128)(2,1)S(1)} collective-permute-done((bf16[96,1536]{1,0:T(8,128)(2,1)S(1)}, bf16[96,1536]{1,0:T(8,128)(2,1)S(1)}, u32[]{:S(2)}, u32[]{:S(2)}) %collective-permute-start.12) | collective-permute-done | bytes 294944 | tf_op jit(solution)/shard_map/ppermute | solution.py:337
  71.9 0.8 copy-done.11
  72.8 3.6 %shard_map.134 = bf16[1536,768]{1,0:T(8,128)(2,1)} custom-call(bf16[128,1536]{1,0:T(8,128)(2,1)} %get-tuple-element.88.kept.own_view, bf16[128,1536]{1,0:T(8,128)(2,1)} %copy-done.12, bf16[128,1536]{1,0:T(8,128)(2,1)} %get-tuple-element.108.own_time.kept, bf16[128,1536]{1,0:T(8,128)(2,1)} %copy-done.11), custom_call_target="tpu_custom_call" | custom-call | tf_op jit(solution)/shard_map/pallas_call | solution.py:290
  76.4 4.5 %all-to-all-start.1 = ((bf16[8,192,768]{2,1,0:T(8,128)(2,1)}), bf16[8,192,768]{2,1,0:T(8,128)(2,1)S(1)}, u32[]{:S(2)}, u32[]{:S(2)}) async-start(bf16[8,192,768]{2,1,0:T(8,128)(2,1)} %bitcast.16), calls=%async_computation.1 | async-start | bytes 4718592 | tf_op jit(solution)/shard_map/all_to_all | solution.py:387
  81.0 1.7 collective-permute-start.15
  82.7 1.1 collective-permute-start.16
  83.8 7.1 %collective-permute-done.15.rest_7_ = bf16[96,1536]{1,0:T(8,128)(2,1)S(1)} collective-permute-done((bf16[96,1536]{1,0:T(8,128)(2,1)}, bf16[96,1536]{1,0:T(8,128)(2,1)S(1)}, u32[]{:S(2)}, u32[]{:S(2)}) %collective-permute-start.15) | collective-permute-done | bytes 294944 | tf_op jit(solution)/shard_map/ppermute | solution.py:337
  90.9 1.7 collective-permute-start.18
  92.5 1.3 collective-permute-done.18.rest_15_
  93.9 7.3 %shard_map.131 = (bf16[128,3072]{1,0:T(8,128)(2,1)}, bf16[1536,1536]{1,0:T(8,128)(2,1)}) custom-call(s32[1]{0:T(128)} %bitcast.me, s32[1]{0:T(128)} %bitcast.1.z, bf16[128,3968]{1,0:T(8,128)(2,1)} %bitcast.18, bf16[128,1536]{1,0:T(8,128)(2,1)} %get-tuple-element.88.kept.own_view, f32[6,256,128]{2,1,0:T(8,128)} %get-tuple-element.89.prob_ref, ...), custom_call_target="tpu_custom_call" | custom-call | tf_op jit(solution)/shard_map/pallas_call | solution.py:290
  101.2 13.8 %all-to-all-done.1.parts = bf16[8,192,768]{2,1,0:T(8,128)(2,1)S(1)} async-done(((bf16[8,192,768]{2,1,0:T(8,128)(2,1)}), bf16[8,192,768]{2,1,0:T(8,128)(2,1)S(1)}, u32[]{:S(2)}, u32[]{:S(2)}) %all-to-all-start.1) | async-done | bytes 2359328 | tf_op jit(solution)/shard_map/all_to_all | solution.py:387
  115.1 3.5 %all-to-all-start.2 = ((bf16[8,16,3072]{2,1,0:T(8,128)(2,1)}), bf16[8,16,3072]{2,1,0:T(8,128)(2,1)S(1)}, u32[]{:S(2)}, u32[]{:S(2)}) async-start(bf16[8,16,3072]{2,1,0:T(8,128)(2,1)} %bitcast.21), calls=%async_computation.2 | async-start | bytes 1572864 | tf_op jit(solution)/shard_map/all_to_all | solution.py:398
  118.6 7.5 %shard_map.133 = (bf16[128,768]{1,0:T(8,128)(2,1)}, f32[128,1536]{1,0:T(8,128)}, bf16[128,1536]{1,0:T(8,128)(2,1)}, bf16[128,1536]{1,0:T(8,128)(2,1)}) custom-call(bf16[64,2304]{1,0:T(8,128)(2,1)} %get-tuple-element.110.q0, bf16[64,2304]{1,0:T(8,128)(2,1)} %copy-done.6, bf16[128,1536]{1,0:T(8,128)(2,1)} %copy-done.5, bf16[128,1536]{1,0:T(8,128)(2,1)} %copy-done.4, ...), custom_call_target="tpu_custom_call" | custom-call | tf_op jit(solution)/shard_map/pallas_call | solution.py:290
  126.1 1.3 collective-permute-start.23
  127.4 1.3 collective-permute-start.22
  128.7 2.9 %shard_map.135 = bf16[16,12,768]{2,1,0:T(8,128)(2,1)} custom-call(bf16[8,192,768]{2,1,0:T(8,128)(2,1)} %copy-done), custom_call_target="tpu_custom_call" | custom-call | tf_op jit(solution)/shard_map/pallas_call | solution.py:290
  131.6 6.3 %collective-permute-done.23.far = bf16[128,1536]{1,0:T(8,128)(2,1)S(1)} collective-permute-done((bf16[128,1536]{1,0:T(8,128)(2,1)}, bf16[128,1536]{1,0:T(8,128)(2,1)S(1)}, u32[]{:S(2)}, u32[]{:S(2)}) %collective-permute-start.23) | collective-permute-done | bytes 393248 | tf_op jit(solution)/shard_map/ppermute | solution.py:407
  138.0 15.4 %collective-permute-done.22.near = bf16[128,1536]{1,0:T(8,128)(2,1)S(1)} collective-permute-done((bf16[128,1536]{1,0:T(8,128)(2,1)}, bf16[128,1536]{1,0:T(8,128)(2,1)S(1)}, u32[]{:S(2)}, u32[]{:S(2)}) %collective-permute-start.22) | collective-permute-done | bytes 393248 | tf_op jit(solution)/shard_map/ppermute | solution.py:406
  153.4 12.7 %all-to-all-start.3 = ((bf16[16,12,768]{2,1,0:T(8,128)(2,1)}), bf16[16,12,768]{2,1,0:T(8,128)(2,1)S(1)}, u32[]{:S(2)}, u32[]{:S(2)}) async-start(bf16[16,12,768]{2,1,0:T(8,128)(2,1)} %shard_map.135), calls=%async_computation.3 | async-start | bytes 786432 | tf_op jit(solution)/shard_map/all_to_all | solution.py:418
  166.1 2.5 %shard_map.136 = (bf16[64,3072]{1,0:T(8,128)(2,1)}, bf16[64,3072]{1,0:T(8,128)(2,1)}) custom-call(bf16[128,1536]{1,0:T(8,128)(2,1)} %get-tuple-element.108.own_time.kept, bf16[128,768]{1,0:T(8,128)(2,1)} %get-tuple-element.112.dq, f32[128,1536]{1,0:T(8,128)} %get-tuple-element.113.own, bf16[128,1536]{1,0:T(8,128)(2,1)} %copy-done.10, bf16[128,1536]{1,0:T(8,128)(2,1)} %copy-done.9), custom_call_target="tpu_custom_call" | custom-call | tf_op jit(solution)/shard_map/pallas_call | solution.py:290
  168.7 3.2 %collective-permute-start.24 = (bf16[64,3072]{1,0:T(8,128)(2,1)}, bf16[64,3072]{1,0:T(8,128)(2,1)S(1)}, u32[]{:S(2)}, u32[]{:S(2)}) collective-permute-start(bf16[64,3072]{1,0:T(8,128)(2,1)} %get-tuple-element.124), channel_id=1, source_target_pairs={{0,1},{1,0},{2,3},{3,2},{4,5},{5,4},{6,7},{7,6},{8,9},{9,8},{10,11... | collective-permute-start | bytes 1179656 | tf_op jit(solution)/shard_map/ppermute | solution.py:430
  171.8 6.7 %all-to-all-done.3 = bf16[16,12,768]{2,1,0:T(8,128)(2,1)S(1)} async-done(((bf16[16,12,768]{2,1,0:T(8,128)(2,1)}), bf16[16,12,768]{2,1,0:T(8,128)(2,1)S(1)}, u32[]{:S(2)}, u32[]{:S(2)}) %all-to-all-start.3) | async-done | bytes 294944 | tf_op jit(solution)/shard_map/all_to_all | solution.py:418
  178.6 5.1 %collective-permute-start.25 = (f32[6,768]{1,0:T(8,128)S(1)}, f32[6,768]{1,0:T(8,128)S(1)}, u32[]{:S(2)}, u32[]{:S(2)}) collective-permute-start(f32[6,768]{1,0:T(8,128)S(1)} %constant_dynamic-slice_fusion), channel_id=1, source_target_pairs={{0,1},{1,0},{2,3},{3,2},{4,5},{5,4},{6,7},{7,6},{8,9},{9,8},{10,11... | collective-permute-start | bytes 55304 | tf_op jit(solution)/shard_map/ppermute | solution.py:422
  183.7 0.8 copy-done.8
  184.4 4.9 %shard_map.137 = (bf16[128,1536]{1,0:T(8,128)(2,1)}, bf16[128,1536]{1,0:T(8,128)(2,1)}, bf16[128,1536]{1,0:T(8,128)(2,1)}, bf16[128,1536]{1,0:T(8,128)(2,1)}) custom-call(s32[1]{0:T(128)} %bitcast.me, bf16[1536,1536]{1,0:T(8,128)(2,1)} %get-tuple-element.102.w, f32[16,1536]{1,0:T(8,128)} %shard_map.129.action, bf16[64,3072]{1,0:T(8,128)(2,1)} %get-tuple-element.123.t0, ...), custom_call_target="tpu_custom_call" | custom-call | tf_op jit(solution)/shard_map/pallas_call | solution.py:290
  (81 shorter events, 5.7 us)
Async XLA Ops:
  0.6 10.4 %collective-permute-start = (bf16[48,1536]{1,0:T(8,128)(2,1)}, bf16[48,1536]{1,0:T(8,128)(2,1)S(1)}, u32[]{:S(2)}, u32[]{:S(2)}) collective-permute-start(bf16[48,1536]{1,0:T(8,128)(2,1)} %param.16), channel_id=1, source_target_pairs={{0,34},{1,35},{2,32},{3,33},{4,38},{5,39},{6,36},{7,37},{8,42},{9,... | collective-permute-start | bytes 442376 | tf_op jit(solution)/shard_map/ppermute | solution.py:320
  4.3 41.5 %copy-start.24 = (s32[16,7]{0,1:T(8,128)S(1)}, s32[16,7]{0,1:T(8,128)}, u32[]{:S(2)}) copy-start(s32[16,7]{0,1:T(8,128)} %param.14) | copy-start | bytes 1348
  8.1 7.0 %collective-permute-start.1 = (bf16[64,1536]{1,0:T(8,128)(2,1)}, bf16[64,1536]{1,0:T(8,128)(2,1)S(1)}, u32[]{:S(2)}, u32[]{:S(2)}) collective-permute-start(bf16[64,1536]{1,0:T(8,128)(2,1)} %get-tuple-element.73), channel_id=1, source_target_pairs={{0,1},{1,0},{2,3},{3,2},{4,5},{5,4},{6,7},{7,6},{8,9},{9,8},{10,11... | collective-permute-start | bytes 589832 | tf_op jit(solution)/shard_map/ppermute | solution.py:349
  11.0 46.8 %all-to-all-start = ((bf16[8,16,3968]{2,1,0:T(8,128)(2,1)}), bf16[8,16,3968]{2,1,0:T(8,128)(2,1)S(1)}, u32[]{:S(2)}, u32[]{:S(2)}) async-start(bf16[8,16,3968]{2,1,0:T(8,128)(2,1)} %bitcast.20), calls=%async_computation | async-start | bytes 2031616 | tf_op jit(solution)/shard_map/all_to_all | solution.py:332
  15.1 35.4 %copy-start.3 = (bf16[128,1536]{1,0:T(8,128)(2,1)}, bf16[128,1536]{1,0:T(8,128)(2,1)S(1)}, u32[]{:S(2)}) copy-start(bf16[128,1536]{1,0:T(8,128)(2,1)S(1)} %constant_dynamic-update-slice_fusion.own) | copy-start | bytes 1179652
  15.1 19.6 %collective-permute-start.2 = (bf16[128,1536]{1,0:T(8,128)(2,1)S(1)}, bf16[128,1536]{1,0:T(8,128)(2,1)S(1)}, u32[]{:S(2)}, u32[]{:S(2)}) collective-permute-start(bf16[128,1536]{1,0:T(8,128)(2,1)S(1)} %constant_dynamic-update-slice_fusion.own), channel_id=1, source_target_pairs={{0,2},{1,3},{2,4},{3,5},{4,6},{5,7},{6,8},{7,9},{8,10},{9,11},{10,... | collective-permute-start | bytes 1179656 | tf_op jit(solution)/shard_map/ppermute | solution.py:350
  17.9 32.6 %copy-start.7 = (bf16[96,1536]{1,0:T(8,128)(2,1)}, bf16[96,1536]{1,0:T(8,128)(2,1)S(1)}, u32[]{:S(2)}) copy-start(bf16[96,1536]{1,0:T(8,128)(2,1)S(1)} %constant_dynamic-update-slice_fusion.2.rest_0_) | copy-start | bytes 884740
  17.9 11.4 %collective-permute-start.4 = (bf16[96,1536]{1,0:T(8,128)(2,1)S(1)}, bf16[96,1536]{1,0:T(8,128)(2,1)S(1)}, u32[]{:S(2)}, u32[]{:S(2)}) collective-permute-start(bf16[96,1536]{1,0:T(8,128)(2,1)S(1)} %constant_dynamic-update-slice_fusion.2.rest_0_), channel_id=1, source_target_pairs={{0,4},{1,5},{2,6},{3,7},{4,8},{5,9},{6,10},{7,11},{8,12},{9,13},{1... | collective-permute-start | bytes 884744 | tf_op jit(solution)/shard_map/ppermute | solution.py:337
  19.6 9.7 %collective-permute-start.5 = (bf16[96,1536]{1,0:T(8,128)(2,1)S(1)}, bf16[96,1536]{1,0:T(8,128)(2,1)S(1)}, u32[]{:S(2)}, u32[]{:S(2)}) collective-permute-start(bf16[96,1536]{1,0:T(8,128)(2,1)S(1)} %constant_dynamic-update-slice_fusion.2.rest_0_), channel_id=1, source_target_pairs={{0,28},{1,29},{2,30},{3,31},{4,0},{5,1},{6,2},{7,3},{8,4},{9,5},{1... | collective-permute-start | bytes 884744 | tf_op jit(solution)/shard_map/ppermute | solution.py:337
  23.6 5.7 %collective-permute-start.6 = (bf16[96,1536]{1,0:T(8,128)(2,1)S(1)}, bf16[96,1536]{1,0:T(8,128)(2,1)S(1)}, u32[]{:S(2)}, u32[]{:S(2)}) collective-permute-start(bf16[96,1536]{1,0:T(8,128)(2,1)S(1)} %constant_dynamic-update-slice_fusion.2.rest_0_), channel_id=1, source_target_pairs={{0,1},{1,0},{2,3},{3,2},{4,5},{5,4},{6,7},{7,6},{8,9},{9,8},{10,11... | collective-permute-start | bytes 884744 | tf_op jit(solution)/shard_map/ppermute | solution.py:341
  25.5 10.0 %collective-permute-start.3 = (bf16[128,1536]{1,0:T(8,128)(2,1)S(1)}, bf16[128,1536]{1,0:T(8,128)(2,1)S(1)}, u32[]{:S(2)}, u32[]{:S(2)}) collective-permute-start(bf16[128,1536]{1,0:T(8,128)(2,1)S(1)} %constant_dynamic-update-slice_fusion.own), channel_id=1, source_target_pairs={{0,4},{1,5},{2,6},{3,7},{4,8},{5,9},{6,10},{7,11},{8,12},{9,13},{1... | collective-permute-start | bytes 1179656 | tf_op jit(solution)/shard_map/ppermute | solution.py:351
  29.3 21.2 %copy-start.13 = (bf16[96,1536]{1,0:T(8,128)(2,1)}, bf16[96,1536]{1,0:T(8,128)(2,1)S(1)}, u32[]{:S(2)}) copy-start(bf16[96,1536]{1,0:T(8,128)(2,1)S(1)} %collective-permute-done.4.rest_1_) | copy-start | bytes 884740
  29.4 21.2 %copy-start.14 = (bf16[96,1536]{1,0:T(8,128)(2,1)}, bf16[96,1536]{1,0:T(8,128)(2,1)S(1)}, u32[]{:S(2)}) copy-start(bf16[96,1536]{1,0:T(8,128)(2,1)S(1)} %collective-permute-done.5.rest_2_) | copy-start | bytes 884740
  29.4 6.1 %copy-start.15 = (bf16[96,1536]{1,0:T(8,128)(2,1)}, bf16[96,1536]{1,0:T(8,128)(2,1)S(1)}, u32[]{:S(2)}) copy-start(bf16[96,1536]{1,0:T(8,128)(2,1)S(1)} %collective-permute-done.6.rest_8_) | copy-start | bytes 884740
  29.4 12.4 %collective-permute-start.7 = (bf16[96,1536]{1,0:T(8,128)(2,1)S(1)}, bf16[96,1536]{1,0:T(8,128)(2,1)}, u32[]{:S(2)}, u32[]{:S(2)}) collective-permute-start(bf16[96,1536]{1,0:T(8,128)(2,1)S(1)} %collective-permute-done.4.rest_1_), channel_id=1, source_target_pairs={{0,4},{1,5},{2,6},{3,7},{4,8},{5,9},{6,10},{7,11},{8,12},{9,13},{1... | collective-permute-start | bytes 884744 | tf_op jit(solution)/shard_map/ppermute | solution.py:337
  29.5 12.3 %collective-permute-start.9 = (bf16[96,1536]{1,0:T(8,128)(2,1)S(1)}, bf16[96,1536]{1,0:T(8,128)(2,1)S(1)}, u32[]{:S(2)}, u32[]{:S(2)}) collective-permute-start(bf16[96,1536]{1,0:T(8,128)(2,1)S(1)} %collective-permute-done.4.rest_1_), channel_id=1, source_target_pairs={{0,1},{1,0},{2,3},{3,2},{4,5},{5,4},{6,7},{7,6},{8,9},{9,8},{10,11... | collective-permute-start | bytes 884744 | tf_op jit(solution)/shard_map/ppermute | solution.py:341
  31.7 10.1 %collective-permute-start.8 = (bf16[96,1536]{1,0:T(8,128)(2,1)S(1)}, bf16[96,1536]{1,0:T(8,128)(2,1)S(1)}, u32[]{:S(2)}, u32[]{:S(2)}) collective-permute-start(bf16[96,1536]{1,0:T(8,128)(2,1)S(1)} %collective-permute-done.5.rest_2_), channel_id=1, source_target_pairs={{0,28},{1,29},{2,30},{3,31},{4,0},{5,1},{6,2},{7,3},{8,4},{9,5},{1... | collective-permute-start | bytes 884744 | tf_op jit(solution)/shard_map/ppermute | solution.py:337
  34.7 15.9 %copy-start.4 = (bf16[128,1536]{1,0:T(8,128)(2,1)}, bf16[128,1536]{1,0:T(8,128)(2,1)S(1)}, u32[]{:S(2)}) copy-start(bf16[128,1536]{1,0:T(8,128)(2,1)S(1)} %collective-permute-done.2.near) | copy-start | bytes 1179652
  34.7 7.1 %collective-permute-start.10 = (bf16[96,1536]{1,0:T(8,128)(2,1)S(1)}, bf16[96,1536]{1,0:T(8,128)(2,1)S(1)}, u32[]{:S(2)}, u32[]{:S(2)}) collective-permute-start(bf16[96,1536]{1,0:T(8,128)(2,1)S(1)} %collective-permute-done.5.rest_2_), channel_id=1, source_target_pairs={{0,1},{1,0},{2,3},{3,2},{4,5},{5,4},{6,7},{7,6},{8,9},{9,8},{10,11... | collective-permute-start | bytes 884744 | tf_op jit(solution)/shard_map/ppermute | solution.py:341
  35.5 15.1 %copy-start.5 = (bf16[128,1536]{1,0:T(8,128)(2,1)}, bf16[128,1536]{1,0:T(8,128)(2,1)S(1)}, u32[]{:S(2)}) copy-start(bf16[128,1536]{1,0:T(8,128)(2,1)S(1)} %collective-permute-done.3.far) | copy-start | bytes 1179652
  35.5 15.1 %collective-permute-start.19 = (bf16[64,2304]{1,0:T(8,128)(2,1)}, bf16[64,2304]{1,0:T(8,128)(2,1)S(1)}, u32[]{:S(2)}, u32[]{:S(2)}) collective-permute-start(bf16[64,2304]{1,0:T(8,128)(2,1)} %get-tuple-element.105), channel_id=1, source_target_pairs={{0,1},{1,0},{2,3},{3,2},{4,5},{5,4},{6,7},{7,6},{8,9},{9,8},{10,11... | collective-permute-start | bytes 884744 | tf_op jit(solution)/shard_map/ppermute | solution.py:352
  43.4 22.0 %collective-permute-start.11 = (bf16[96,1536]{1,0:T(8,128)(2,1)}, bf16[96,1536]{1,0:T(8,128)(2,1)}, u32[]{:S(2)}, u32[]{:S(2)}) collective-permute-start(bf16[96,1536]{1,0:T(8,128)(2,1)} %collective-permute-done.7.rest_3_), channel_id=1, source_target_pairs={{0,4},{1,5},{2,6},{3,7},{4,8},{5,9},{6,10},{7,11},{8,12},{9,13},{1... | collective-permute-start | bytes 884744 | tf_op jit(solution)/shard_map/ppermute | solution.py:337
  50.6 11.9 %copy-start.18 = (bf16[96,1536]{1,0:T(8,128)(2,1)S(1)}, bf16[96,1536]{1,0:T(8,128)(2,1)}, u32[]{:S(2)}) copy-start(bf16[96,1536]{1,0:T(8,128)(2,1)} %copy-done.17) | copy-start | bytes 884740
  57.1 14.7 %collective-permute-start.21 = (bf16[128,1536]{1,0:T(8,128)(2,1)}, bf16[128,1536]{1,0:T(8,128)(2,1)S(1)}, u32[]{:S(2)}, u32[]{:S(2)}) collective-permute-start(bf16[128,1536]{1,0:T(8,128)(2,1)} %get-tuple-element.115), channel_id=1, source_target_pairs={{0,1},{1,0},{2,3},{3,2},{4,5},{5,4},{6,7},{7,6},{8,9},{9,8},{10,11... | collective-permute-start | bytes 1179656 | tf_op jit(solution)/shard_map/ppermute | solution.py:379
  57.8 1.0 copy-start.1
  62.0 9.9 %collective-permute-start.20 = (bf16[128,1536]{1,0:T(8,128)(2,1)}, bf16[128,1536]{1,0:T(8,128)(2,1)S(1)}, u32[]{:S(2)}, u32[]{:S(2)}) collective-permute-start(bf16[128,1536]{1,0:T(8,128)(2,1)} %get-tuple-element.114), channel_id=1, source_target_pairs={{0,1},{1,0},{2,3},{3,2},{4,5},{5,4},{6,7},{7,6},{8,9},{9,8},{10,11... | collective-permute-start | bytes 1179656 | tf_op jit(solution)/shard_map/ppermute | solution.py:378
  62.0 9.8 %collective-permute-start.13 = (bf16[96,1536]{1,0:T(8,128)(2,1)}, bf16[96,1536]{1,0:T(8,128)(2,1)S(1)}, u32[]{:S(2)}, u32[]{:S(2)}) collective-permute-start(bf16[96,1536]{1,0:T(8,128)(2,1)} %collective-permute-done.7.rest_3_), channel_id=1, source_target_pairs={{0,1},{1,0},{2,3},{3,2},{4,5},{5,4},{6,7},{7,6},{8,9},{9,8},{10,11... | collective-permute-start | bytes 884744 | tf_op jit(solution)/shard_map/ppermute | solution.py:341
  62.5 9.3 %collective-permute-start.12 = (bf16[96,1536]{1,0:T(8,128)(2,1)S(1)}, bf16[96,1536]{1,0:T(8,128)(2,1)S(1)}, u32[]{:S(2)}, u32[]{:S(2)}) collective-permute-start(bf16[96,1536]{1,0:T(8,128)(2,1)S(1)} %copy-done.18), channel_id=1, source_target_pairs={{0,28},{1,29},{2,30},{3,31},{4,0},{5,1},{6,2},{7,3},{8,4},{9,5},{1... | collective-permute-start | bytes 884744 | tf_op jit(solution)/shard_map/ppermute | solution.py:337
  65.4 6.4 %collective-permute-start.14 = (bf16[96,1536]{1,0:T(8,128)(2,1)S(1)}, bf16[96,1536]{1,0:T(8,128)(2,1)S(1)}, u32[]{:S(2)}, u32[]{:S(2)}) collective-permute-start(bf16[96,1536]{1,0:T(8,128)(2,1)S(1)} %copy-done.18), channel_id=1, source_target_pairs={{0,1},{1,0},{2,3},{3,2},{4,5},{5,4},{6,7},{7,6},{8,9},{9,8},{10,11... | collective-permute-start | bytes 884744 | tf_op jit(solution)/shard_map/ppermute | solution.py:341
  71.8 22.1 %copy-start.21 = (bf16[96,1536]{1,0:T(8,128)(2,1)}, bf16[96,1536]{1,0:T(8,128)(2,1)S(1)}, u32[]{:S(2)}) copy-start(bf16[96,1536]{1,0:T(8,128)(2,1)S(1)} %collective-permute-done.12.rest_6_) | copy-start | bytes 884740
  71.8 22.1 %copy-start.20 = (bf16[96,1536]{1,0:T(8,128)(2,1)}, bf16[96,1536]{1,0:T(8,128)(2,1)S(1)}, u32[]{:S(2)}) copy-start(bf16[96,1536]{1,0:T(8,128)(2,1)S(1)} %collective-permute-done.13.rest_11_) | copy-start | bytes 884740
  71.8 4.6 %copy-start.22 = (bf16[96,1536]{1,0:T(8,128)(2,1)}, bf16[96,1536]{1,0:T(8,128)(2,1)S(1)}, u32[]{:S(2)}) copy-start(bf16[96,1536]{1,0:T(8,128)(2,1)S(1)} %collective-permute-done.14.rest_12_) | copy-start | bytes 884740
  76.4 38.6 %all-to-all-start.1 = ((bf16[8,192,768]{2,1,0:T(8,128)(2,1)}), bf16[8,192,768]{2,1,0:T(8,128)(2,1)S(1)}, u32[]{:S(2)}, u32[]{:S(2)}) async-start(bf16[8,192,768]{2,1,0:T(8,128)(2,1)} %bitcast.16), calls=%async_computation.1 | async-start | bytes 4718592 | tf_op jit(solution)/shard_map/all_to_all | solution.py:387
  81.0 9.9 %collective-permute-start.15 = (bf16[96,1536]{1,0:T(8,128)(2,1)}, bf16[96,1536]{1,0:T(8,128)(2,1)S(1)}, u32[]{:S(2)}, u32[]{:S(2)}) collective-permute-start(bf16[96,1536]{1,0:T(8,128)(2,1)} %collective-permute-done.11.rest_5_), channel_id=1, source_target_pairs={{0,4},{1,5},{2,6},{3,7},{4,8},{5,9},{6,10},{7,11},{8,12},{9,13},{1... | collective-permute-start | bytes 884744 | tf_op jit(solution)/shard_map/ppermute | solution.py:337
  82.7 9.9 %collective-permute-start.16 = (bf16[96,1536]{1,0:T(8,128)(2,1)}, bf16[96,1536]{1,0:T(8,128)(2,1)}, u32[]{:S(2)}, u32[]{:S(2)}) collective-permute-start(bf16[96,1536]{1,0:T(8,128)(2,1)} %collective-permute-done.11.rest_5_), channel_id=1, source_target_pairs={{0,1},{1,0},{2,3},{3,2},{4,5},{5,4},{6,7},{7,6},{8,9},{9,8},{10,11... | collective-permute-start | bytes 884744 | tf_op jit(solution)/shard_map/ppermute | solution.py:341
  83.8 8.7 %collective-permute-start.17 = (bf16[96,1536]{1,0:T(8,128)(2,1)S(1)}, bf16[96,1536]{1,0:T(8,128)(2,1)}, u32[]{:S(2)}, u32[]{:S(2)}) collective-permute-start(bf16[96,1536]{1,0:T(8,128)(2,1)S(1)} %collective-permute-done.12.rest_6_), channel_id=1, source_target_pairs={{0,1},{1,0},{2,3},{3,2},{4,5},{5,4},{6,7},{7,6},{8,9},{9,8},{10,11... | collective-permute-start | bytes 884744 | tf_op jit(solution)/shard_map/ppermute | solution.py:341
  90.9 3.0 %copy-start.23 = (bf16[96,1536]{1,0:T(8,128)(2,1)}, bf16[96,1536]{1,0:T(8,128)(2,1)S(1)}, u32[]{:S(2)}) copy-start(bf16[96,1536]{1,0:T(8,128)(2,1)S(1)} %collective-permute-done.15.rest_7_) | copy-start | bytes 884740
  90.9 3.0 %collective-permute-start.18 = (bf16[96,1536]{1,0:T(8,128)(2,1)S(1)}, bf16[96,1536]{1,0:T(8,128)(2,1)}, u32[]{:S(2)}, u32[]{:S(2)}) collective-permute-start(bf16[96,1536]{1,0:T(8,128)(2,1)S(1)} %collective-permute-done.15.rest_7_), channel_id=1, source_target_pairs={{0,1},{1,0},{2,3},{3,2},{4,5},{5,4},{6,7},{7,6},{8,9},{9,8},{10,11... | collective-permute-start | bytes 884744 | tf_op jit(solution)/shard_map/ppermute | solution.py:341
  115.1 11.1 %copy-start = (bf16[8,192,768]{2,1,0:T(8,128)(2,1)}, bf16[8,192,768]{2,1,0:T(8,128)(2,1)S(1)}, u32[]{:S(2)}) copy-start(bf16[8,192,768]{2,1,0:T(8,128)(2,1)S(1)} %all-to-all-done.1.parts) | copy-start | bytes 7077892
  115.1 22.9 %all-to-all-start.2 = ((bf16[8,16,3072]{2,1,0:T(8,128)(2,1)}), bf16[8,16,3072]{2,1,0:T(8,128)(2,1)S(1)}, u32[]{:S(2)}, u32[]{:S(2)}) async-start(bf16[8,16,3072]{2,1,0:T(8,128)(2,1)} %bitcast.21), calls=%async_computation.2 | async-start | bytes 1572864 | tf_op jit(solution)/shard_map/all_to_all | solution.py:398
  126.1 11.9 %collective-permute-start.23 = (bf16[128,1536]{1,0:T(8,128)(2,1)}, bf16[128,1536]{1,0:T(8,128)(2,1)S(1)}, u32[]{:S(2)}, u32[]{:S(2)}) collective-permute-start(bf16[128,1536]{1,0:T(8,128)(2,1)} %get-tuple-element.120), channel_id=1, source_target_pairs={{4,0},{5,1},{6,2},{7,3},{8,4},{9,5},{10,6},{11,7},{12,8},{13,9},{1... | collective-permute-start | bytes 1179656 | tf_op jit(solution)/shard_map/ppermute | solution.py:407
  127.4 26.0 %collective-permute-start.22 = (bf16[128,1536]{1,0:T(8,128)(2,1)}, bf16[128,1536]{1,0:T(8,128)(2,1)S(1)}, u32[]{:S(2)}, u32[]{:S(2)}) collective-permute-start(bf16[128,1536]{1,0:T(8,128)(2,1)} %get-tuple-element.119), channel_id=1, source_target_pairs={{2,0},{3,1},{4,2},{5,3},{6,4},{7,5},{8,6},{9,7},{10,8},{11,9},{12,... | collective-permute-start | bytes 1179656 | tf_op jit(solution)/shard_map/ppermute | solution.py:406
  138.0 28.1 %copy-start.9 = (bf16[128,1536]{1,0:T(8,128)(2,1)}, bf16[128,1536]{1,0:T(8,128)(2,1)S(1)}, u32[]{:S(2)}) copy-start(bf16[128,1536]{1,0:T(8,128)(2,1)S(1)} %collective-permute-done.23.far) | copy-start | bytes 1179652
  138.0 45.7 %copy-start.2 = (bf16[8,16,3072]{2,1,0:T(8,128)(2,1)}, bf16[8,16,3072]{2,1,0:T(8,128)(2,1)S(1)}, u32[]{:S(2)}) copy-start(bf16[8,16,3072]{2,1,0:T(8,128)(2,1)S(1)} %all-to-all-done.2) | copy-start | bytes 2359300
  153.4 12.7 %copy-start.10 = (bf16[128,1536]{1,0:T(8,128)(2,1)}, bf16[128,1536]{1,0:T(8,128)(2,1)S(1)}, u32[]{:S(2)}) copy-start(bf16[128,1536]{1,0:T(8,128)(2,1)S(1)} %collective-permute-done.22.near) | copy-start | bytes 1179652
  153.4 25.1 %all-to-all-start.3 = ((bf16[16,12,768]{2,1,0:T(8,128)(2,1)}), bf16[16,12,768]{2,1,0:T(8,128)(2,1)S(1)}, u32[]{:S(2)}, u32[]{:S(2)}) async-start(bf16[16,12,768]{2,1,0:T(8,128)(2,1)} %shard_map.135), calls=%async_computation.3 | async-start | bytes 786432 | tf_op jit(solution)/shard_map/all_to_all | solution.py:418
  168.7 15.0 %collective-permute-start.24 = (bf16[64,3072]{1,0:T(8,128)(2,1)}, bf16[64,3072]{1,0:T(8,128)(2,1)S(1)}, u32[]{:S(2)}, u32[]{:S(2)}) collective-permute-start(bf16[64,3072]{1,0:T(8,128)(2,1)} %get-tuple-element.124), channel_id=1, source_target_pairs={{0,1},{1,0},{2,3},{3,2},{4,5},{5,4},{6,7},{7,6},{8,9},{9,8},{10,11... | collective-permute-start | bytes 1179656 | tf_op jit(solution)/shard_map/ppermute | solution.py:430
  178.6 10.7 %collective-permute-start.25 = (f32[6,768]{1,0:T(8,128)S(1)}, f32[6,768]{1,0:T(8,128)S(1)}, u32[]{:S(2)}, u32[]{:S(2)}) collective-permute-start(f32[6,768]{1,0:T(8,128)S(1)} %constant_dynamic-slice_fusion), channel_id=1, source_target_pairs={{0,1},{1,0},{2,3},{3,2},{4,5},{5,4},{6,7},{7,6},{8,9},{9,8},{10,11... | collective-permute-start | bytes 55304 | tf_op jit(solution)/shard_map/ppermute | solution.py:422
  (7 other events, 5.6 us)

commit v6 on v5

--- a/solution.py
+++ b/solution.py
@@ -198,28 +198,17 @@
     return dq, dk, dv
 
 
-def view_backward_kernel(depth, me, z, x, kept, prob_ref, *rest):
-    own, others, (out_ref, full_ref, w, sem, full_sem) = rest[:depth], rest[depth : 2 * depth], rest[2 * depth :]
-    copies = fetch_weight(me, z, own, others, w, sem)
-    out_ref[:, :CW] = kept[:, :CW]
+def time_backward_kernel(depth, me, z, q0, q1, far, near, own, prob_ref, *rest):
+    w_own, w_other, rest = rest[:depth], rest[depth : 2 * depth], rest[2 * depth :]
+    dq_ref, own_ref, near_ref, far_ref, full_ref, w, sem, full_sem = rest
+    copies = fetch_weight(me, z, w_own, w_other, w, sem)
+    qct, kv = (q0, q1), (far, near, own)
+    rows = PAIR * q0.shape[0]
     for copy in copies:
         copy.wait()
     full = pltpu.make_async_copy(w, full_ref, full_sem)
     full.start()
-    grad = dot_nt(x[:, 3 * CW : 5 * CW], w[:CW]).astype(BF)
-    for j in range(PAIRS):
-        at = [slice(i * CW + 128 * j, i * CW + 128 * (j + 1)) for i in range(4)]
-        dq, dk, dv = backward_pair(x[:, at[0]], x[:, at[1]], x[:, at[2]], grad[:, at[0]], prob_ref[j])
-        out_ref[:, at[1]] = dq.astype(BF)
-        out_ref[:, at[2]] = dk.astype(BF)
-        out_ref[:, at[3]] = dv.astype(BF)
-    full.wait()
-
-
-def time_backward_kernel(q0, q1, far, near, own, prob_ref, w, dq_ref, own_ref, near_ref, far_ref):
-    qct, kv = (q0, q1), (far, near, own)
-    rows = PAIR * q0.shape[0]
-    grad = dot_nt(rows_of(qct, slice(CW, 3 * CW)), w[...]).astype(BF)
+    grad = dot_nt(rows_of(qct, slice(CW, 3 * CW)), w[CW:]).astype(BF)
     for j in range(PAIRS):
         at = [slice(i * CW + 128 * j, i * CW + 128 * (j + 1)) for i in range(2)]
         dq, dk, dv = backward_pair(
@@ -230,6 +219,22 @@
             far_ref[:, part] = value[:rows].astype(BF)
             near_ref[:, part] = value[rows : 2 * rows].astype(BF)
             own_ref[:, part] = value[2 * rows :]
+    full.wait()
+
+
+def view_backward_kernel(cam, x, kept, prob_ref, w, *rest):
+    out_refs, held = rest[:-1], rest[-1]
+    held[:, :CW] = kept[:, :CW]
+    grad = dot_nt(x[:, 3 * CW : 5 * CW], w[...]).astype(BF)
+    for j in range(PAIRS):
+        at = [slice(i * CW + 128 * j, i * CW + 128 * (j + 1)) for i in range(4)]
+        dq, dk, dv = backward_pair(x[:, at[0]], x[:, at[1]], x[:, at[2]], grad[:, at[0]], prob_ref[j])
+        held[:, at[1]] = dq.astype(BF)
+        held[:, at[2]] = dk.astype(BF)
+        held[:, at[3]] = dv.astype(BF)
+    size = held.shape[0] // len(out_refs)
+    for d, out in enumerate(out_refs):
+        out[...] = held[pl.ds(pl.multiple_of((cam[0] ^ d) * size, size), size), :]
 
 
 def time_sum_kernel(kept, dq, own, near, far, *outs):
@@ -261,8 +266,12 @@
         out_ref[i] = held[i * size : (i + 1) * size, :].astype(BF)
 
 
-def finish_kernel(me, w, action, t0, t1, view, pred_ref, dq_ref, dk_ref, dv_ref):
+def finish_kernel(cams, me, cam, w, action, t0, t1, *rest):
+    blocks, (pred_ref, dq_ref, dk_ref, dv_ref, view) = rest[:cams], rest[cams:]
     time = (t0, t1)
+    share = blocks[0].shape[0]
+    for d, part in enumerate(blocks):
+        view[pl.ds(pl.multiple_of((cam[0] ^ d) * share, share), share), :] = part[...]
     rows = view.shape[0]
     frames = rows // 8
     row = iota((rows, rows), 0)
@@ -344,19 +353,18 @@
         value, w_own[:], w_other[:] = lax.optimization_barrier((value, w_own[:], w_other[:]))
         return value
 
-    pass_on(1, 3)
-    swap_blocks(1)
     own = jnp.concatenate([kv[0], lax.ppermute(kv[1], "tm", swap)], axis=0)
+    q0, q1 = qct[0], lax.ppermute(qct[1], "tm", swap)
+
+    own = tie(own)
     near = lax.ppermute(own, "tm", [(i, i + 2) for i in range(tm - 2)])
     far = lax.ppermute(own, "tm", [(i, i + 4) for i in range(tm - 4)])
-    q0, q1 = qct[0], lax.ppermute(qct[1], "tm", swap)
-
-    q0 = tie(q0)
+    pass_on(1, 3)
+    (action_sum,) = call(action_kernel, [((frames, width), F32)], [VM] * 2, actions, act_table)
+    near, far = tie((near, far))
     pass_on(3, 5)
-    swap_blocks(3)
-    (action_sum,) = call(action_kernel, [((frames, width), F32)], [VM] * 2, actions, act_table)
-    view_x, action_sum = lax.optimization_barrier((view_x, action_sum))
-    near, far = tie((near, far))
+    swap_blocks(1)
+    view_x = tie(view_x)
     pass_on(5, 7)
     swap_blocks(5)
     kept_view, view_swap, prob_view = call(
@@ -372,7 +380,6 @@
         windows, me, pair, q0, q1, far, near, own,
     )
 
-    kept_view = tie(kept_view)
     pass_on(7, depth)
     swap_blocks(depth)
     view_swap = lax.ppermute(view_swap, "tm", swap)
@@ -386,25 +393,30 @@
     )
     part = lax.all_to_all(part.reshape(cams, width // cams, CW), "cam", 0, 0, tiled=True)
 
-    view_out, w_full = call(
-        functools.partial(view_backward_kernel, depth),
-        [((rows, 4 * CW), BF), ((width, width), BF)],
-        [SM] * 2 + [VM] * 3 + [ANY] * (2 * depth),
-        me, group, view_x, kept_view, prob_view, *w_own, *w_other,
+    q0, action_sum = lax.optimization_barrier((q0, action_sum))
+    dq_time, own_grad, near_grad, far_grad, w_full = call(
+        functools.partial(time_backward_kernel, depth),
+        [((rows, CW), BF), ((rows, 2 * CW), F32)] + [((rows, 2 * CW), BF)] * 2 + [((width, width), BF)],
+        [SM] * 2 + [VM] * 6 + [ANY] * (2 * depth),
+        me, group, q0, q1, far, near, own, prob_time, *w_own, *w_other,
         scratch=[pltpu.VMEM((width, width), BF), pltpu.SemaphoreType.DMA((tm,)), pltpu.SemaphoreType.DMA],
         kept=1,
     )
-    q0, view_out = lax.optimization_barrier((q0, view_out))
-    view_back = lax.all_to_all(view_out, "cam", 0, 0, tiled=True)
-    dq_time, own_grad, near_grad, far_grad = call(
-        time_backward_kernel,
-        [((rows, CW), BF), ((rows, 2 * CW), F32), ((rows, 2 * CW), BF), ((rows, 2 * CW), BF)],
-        [VM] * 6 + [pl.BlockSpec((CW, width), lambda *at: (1, 0))],
-        q0, q1, far, near, own, prob_time, w_full,
-    )
-    part, near_grad = lax.optimization_barrier((part, near_grad))
+    view_x, near_grad = lax.optimization_barrier((view_x, near_grad))
     near_grad = lax.ppermute(near_grad, "tm", [(i + 2, i) for i in range(tm - 2)])
     far_grad = lax.ppermute(far_grad, "tm", [(i + 4, i) for i in range(tm - 4)])
+    cam = lax.axis_index("cam").reshape(1)
+    view_out = call(
+        view_backward_kernel,
+        [((rows // cams, 4 * CW), BF)] * cams,
+        [SM] + [VM] * 3 + [pl.BlockSpec((CW, width), lambda *at: (0, 0))],
+        cam, view_x, kept_view, prob_view, w_full,
+        scratch=[pltpu.VMEM((rows, 4 * CW), BF)],
+    )
+    view_back = [view_out[0]] + [
+        lax.ppermute(view_out[d], "cam", [(i, i ^ d) for i in range(cams)]) for d in range(1, cams)
+    ]
+    part, near_grad, far_grad, view_back[1] = lax.optimization_barrier((part, near_grad, far_grad, view_back[1]))
 
     chips = tm // 2
     (part,) = call(
@@ -414,7 +426,6 @@
         part,
         scratch=[pltpu.VMEM((width // cams, CW), F32)],
     )
-    part, view_back, near_grad, far_grad = lax.optimization_barrier((part, view_back, near_grad, far_grad))
     part = lax.all_to_all(part, "tm", 0, 0, tiled=True, axis_index_groups=same_core)
     part = jnp.sum(part.astype(F32), axis=0)
     final = width // cams // tm
@@ -429,10 +440,11 @@
     )
     t1 = lax.ppermute(t1, "tm", swap)
     outs = call(
-        finish_kernel,
+        functools.partial(finish_kernel, cams),
         [((rows, width), BF)] * 4,
-        [SM] + [VM] * 5,
-        me, w_full, action_sum, t0, t1, view_back,
+        [SM] * 2 + [VM] * (4 + cams),
+        me, cam, w_full, action_sum, t0, t1, *view_back,
+        scratch=[pltpu.VMEM((rows, 4 * CW), BF)],
     )
     return tuple(a.reshape(1, frames, tokens, width) for a in outs) + (grad_out_weight,)
 

time: 191 us -> 177 us (0.927)
  waiting for transfers between devices: 65.1 us -> 54.6 us
  starting transfers between devices: 70 us -> 67.3 us
  local copies, waits for them, and re-layouts: 7.57 us -> 5.41 us
    all_to_all x1, waiting for transfers between devices: 13.8 us -> 0.01 us  [shards(): lax.all_to_all(part.reshape(cams, width // cams, CW), 'cam', 0, 0, tiled=...]
    ppermute x0 -> x7, starting transfers between devices: none -> 9.56 us  [shards(): lax.ppermute(view_out[d], 'cam', [(i, i ^ d) for i in range(cams)])]
    all_to_all x1, starting transfers between devices: 12.7 us -> 5.74 us  [shards(): lax.all_to_all(part, 'tm', 0, 0, tiled=True, axis_index_groups=same_core)]
    ppermute x0 -> x7, waiting for transfers between devices: none -> 6.25 us  [shards(): lax.ppermute(view_out[d], 'cam', [(i, i ^ d) for i in range(cams)])]
    all_to_all x1 -> x0, starting transfers between devices: 3.55 us -> none  [shards(): view_back = lax.all_to_all(view_out, 'cam', 0, 0, tiled=True)]
    ppermute x7, starting transfers between devices: 15.7 us -> 12.4 us  [pass_on(): lax.ppermute(w_own[max(i - 2, 0)], 'tm', up if i % 2 else down)]
    ppermute x7, waiting for transfers between devices: 21.3 us -> 18.3 us  [pass_on(): lax.ppermute(w_own[max(i - 2, 0)], 'tm', up if i % 2 else down)]
    ppermute x1, waiting for transfers between devices: 6.34 us -> 9.39 us  [shards(): far_grad = lax.ppermute(far_grad, 'tm', [(i + 4, i) for i in range(tm - 4)])]
  transfers between devices with their start and end apart: 30 -> 36, of which waited for: 10 -> 9; matrix products, arithmetic and copies ran while one was open for 1% -> 0% of each run, Pallas kernels for 22% -> 22%
where the time goes in v6:
time: 177 us; the launch traced here: 175 us
  starting transfers between devices  67.3 us (38%)
  waiting for transfers between devices  54.6 us (31%)
  Pallas kernels  45.8 us (26%)
  local copies, waits for them, and re-layouts  5.41 us (3%)
    pallas_call x10, Pallas kernels, call(): pl.pallas_call(kernel, out_shape=[jax.ShapeDtypeStruct(shape, kind) for s...  45.8 us
    ppermute x7, waiting for transfers between devices, pass_on(): lax.ppermute(w_own[max(i - 2, 0)], 'tm', up if i % 2 else down)  18.3 us
    ppermute x1, waiting for transfers between devices, shards(): lax.ppermute(near_grad, 'tm', [(i + 2, i) for i in range(tm - 2)])  13 us
    ppermute x7, starting transfers between devices, pass_on(): lax.ppermute(w_own[max(i - 2, 0)], 'tm', up if i % 2 else down)  12.4 us
    ppermute x7, starting transfers between devices, shards(): lax.ppermute(view_out[d], 'cam', [(i, i ^ d) for i in range(cams)])  9.56 us
    ppermute x1, waiting for transfers between devices, shards(): far_grad = lax.ppermute(far_grad, 'tm', [(i + 4, i) for i in range(tm - 4)])  9.39 us
    ppermute x8, starting transfers between devices, swap_blocks(): w_other.append(lax.ppermute(block_rows, 'tm', swap))  9.12 us
    ppermute x7, waiting for transfers between devices, shards(): lax.ppermute(view_out[d], 'cam', [(i, i ^ d) for i in range(cams)])  6.25 us
  transfers between devices with their start and end apart: 36, of which 9 were waited for; matrix products, arithmetic and copies ran while one was open for 0% of the time, Pallas kernels for 22%

profile of v6, /device:TPU:1, one launch (start us, length us, event | category | flops | bytes accessed | tf_op | source)
XLA Modules:
  0.0 174.9 jit_solution(13348539722068996625)
XLA Ops:
  0.6 3.7 %collective-permute-start.2 = (bf16[48,1536]{1,0:T(8,128)(2,1)}, bf16[48,1536]{1,0:T(8,128)(2,1)S(1)}, u32[]{:S(2)}, u32[]{:S(2)}) collective-permute-start(bf16[48,1536]{1,0:T(8,128)(2,1)} %param.16), channel_id=1, source_target_pairs={{0,34},{1,35},{2,32},{3,33},{4,38},{5,39},{6,36},{7,37},{8,42},{9,... | collective-permute-start | bytes 442376 | tf_op jit(solution)/shard_map/ppermute | solution.py:329
  4.3 3.7 %shard_map.128 = (bf16[128,3968]{1,0:T(8,128)(2,1)}, bf16[64,1536]{1,0:T(8,128)(2,1)}, bf16[64,1536]{1,0:T(8,128)(2,1)}, bf16[64,2304]{1,0:T(8,128)(2,1)}, bf16[64,2304]{1,0:T(8,128)(2,1)}) custom-call(s32[1]{0:T(128)} %bitcast.me, s32[1,16]{1,0:T(1,128)} %valid.1, bf16[128,1536]{1,0:T(8,128)(2,1)} %bitcast.19, bf16[128,1536]{1,0:T(8,128)(2,1)} %bitcast.20, ...), custom_call_target="tpu_custom_call" | custom-call | tf_op jit(solution)/shard_map/pallas_call | solution.py:299
  8.0 1.0 collective-permute-start.1
  9.1 4.0 %all-to-all-start = ((bf16[8,16,3968]{2,1,0:T(8,128)(2,1)}), bf16[8,16,3968]{2,1,0:T(8,128)(2,1)S(1)}, u32[]{:S(2)}, u32[]{:S(2)}) async-start(bf16[8,16,3968]{2,1,0:T(8,128)(2,1)} %bitcast.18), calls=%async_computation | async-start | bytes 2031616 | tf_op jit(solution)/shard_map/all_to_all | solution.py:341
  13.2 4.2 %collective-permute-start.3 = (bf16[128,1536]{1,0:T(8,128)(2,1)S(1)}, bf16[128,1536]{1,0:T(8,128)(2,1)S(1)}, u32[]{:S(2)}, u32[]{:S(2)}) collective-permute-start(bf16[128,1536]{1,0:T(8,128)(2,1)S(1)} %pad_maximum_fusion.own), channel_id=1, source_target_pairs={{0,2},{1,3},{2,4},{3,5},{4,6},{5,7},{6,8},{7,9},{8,10},{9,11},{10,... | collective-permute-start | bytes 1179656 | tf_op jit(solution)/shard_map/ppermute | solution.py:360
  17.4 3.5 %collective-permute-start.4 = (bf16[128,1536]{1,0:T(8,128)(2,1)S(1)}, bf16[128,1536]{1,0:T(8,128)(2,1)S(1)}, u32[]{:S(2)}, u32[]{:S(2)}) collective-permute-start(bf16[128,1536]{1,0:T(8,128)(2,1)S(1)} %pad_maximum_fusion.own), channel_id=1, source_target_pairs={{0,4},{1,5},{2,6},{3,7},{4,8},{5,9},{6,10},{7,11},{8,12},{9,13},{1... | collective-permute-start | bytes 1179656 | tf_op jit(solution)/shard_map/ppermute | solution.py:361
  21.0 1.7 collective-permute-start.5
  22.6 1.8 %collective-permute-start.6 = (bf16[96,1536]{1,0:T(8,128)(2,1)S(1)}, bf16[96,1536]{1,0:T(8,128)(2,1)S(1)}, u32[]{:S(2)}, u32[]{:S(2)}) collective-permute-start(bf16[96,1536]{1,0:T(8,128)(2,1)S(1)} %pad_maximum_fusion.1.rest_0_), channel_id=1, source_target_pairs={{0,28},{1,29},{2,30},{3,31},{4,0},{5,1},{6,2},{7,3},{8,4},{9,5},{1... | collective-permute-start | bytes 884744 | tf_op jit(solution)/shard_map/ppermute | solution.py:346
  24.4 2.4 %collective-permute-start = (bf16[64,2304]{1,0:T(8,128)(2,1)}, bf16[64,2304]{1,0:T(8,128)(2,1)S(1)}, u32[]{:S(2)}, u32[]{:S(2)}) collective-permute-start(bf16[64,2304]{1,0:T(8,128)(2,1)} %get-tuple-element.61), channel_id=1, source_target_pairs={{0,1},{1,0},{2,3},{3,2},{4,5},{5,4},{6,7},{7,6},{8,9},{9,8},{10,11... | collective-permute-start | bytes 884744 | tf_op jit(solution)/shard_map/ppermute | solution.py:357
  26.8 6.7 %collective-permute-done.5.rest_1_ = bf16[96,1536]{1,0:T(8,128)(2,1)S(1)} collective-permute-done((bf16[96,1536]{1,0:T(8,128)(2,1)S(1)}, bf16[96,1536]{1,0:T(8,128)(2,1)S(1)}, u32[]{:S(2)}, u32[]{:S(2)}) %collective-permute-start.5) | collective-permute-done | bytes 294944 | tf_op jit(solution)/shard_map/ppermute | solution.py:346
  33.6 2.3 %collective-permute-start.7 = (bf16[96,1536]{1,0:T(8,128)(2,1)S(1)}, bf16[96,1536]{1,0:T(8,128)(2,1)}, u32[]{:S(2)}, u32[]{:S(2)}) collective-permute-start(bf16[96,1536]{1,0:T(8,128)(2,1)S(1)} %collective-permute-done.5.rest_1_), channel_id=1, source_target_pairs={{0,4},{1,5},{2,6},{3,7},{4,8},{5,9},{6,10},{7,11},{8,12},{9,13},{1... | collective-permute-start | bytes 884744 | tf_op jit(solution)/shard_map/ppermute | solution.py:346
  35.9 4.0 %collective-permute-start.8 = (bf16[96,1536]{1,0:T(8,128)(2,1)S(1)}, bf16[96,1536]{1,0:T(8,128)(2,1)}, u32[]{:S(2)}, u32[]{:S(2)}) collective-permute-start(bf16[96,1536]{1,0:T(8,128)(2,1)S(1)} %collective-permute-done.6.rest_2_), channel_id=1, source_target_pairs={{0,28},{1,29},{2,30},{3,31},{4,0},{5,1},{6,2},{7,3},{8,4},{9,5},{1... | collective-permute-start | bytes 884744 | tf_op jit(solution)/shard_map/ppermute | solution.py:346
  39.9 3.3 %collective-permute-start.9 = (bf16[96,1536]{1,0:T(8,128)(2,1)S(1)}, bf16[96,1536]{1,0:T(8,128)(2,1)}, u32[]{:S(2)}, u32[]{:S(2)}) collective-permute-start(bf16[96,1536]{1,0:T(8,128)(2,1)S(1)} %pad_maximum_fusion.1.rest_0_), channel_id=1, source_target_pairs={{0,1},{1,0},{2,3},{3,2},{4,5},{5,4},{6,7},{7,6},{8,9},{9,8},{10,11... | collective-permute-start | bytes 884744 | tf_op jit(solution)/shard_map/ppermute | solution.py:350
  43.9 5.8 %shard_map.130 = (bf16[128,1536]{1,0:T(8,128)(2,1)}, bf16[128,1536]{1,0:T(8,128)(2,1)}, f32[6,256,384]{2,1,0:T(8,128)}) custom-call(s32[12]{0:T(128)} %windows.1, s32[1]{0:T(128)} %bitcast.me, s32[1]{0:T(128)} %bitcast.7.pair, bf16[64,2304]{1,0:T(8,128)(2,1)} %get-tuple-element.60.q0, bf16[64,2304]{1,0:T(8,128)(2,1)} %copy-done.5, ...), custom_call_target="tpu_custom_call" | custom-call | tf_op jit(solution)/shard_map/pallas_call | solution.py:299
  49.8 1.0 copy-done.1
  50.8 3.2 %shard_map.132 = (bf16[128,1536]{1,0:T(8,128)(2,1)}, bf16[128,1536]{1,0:T(8,128)(2,1)}, f32[6,256,128]{2,1,0:T(8,128)}) custom-call(s32[1]{0:T(128)} %bitcast.me, bf16[128,3968]{1,0:T(8,128)(2,1)} %bitcast.16), custom_call_target="tpu_custom_call" | custom-call | tf_op jit(solution)/shard_map/pallas_call | solution.py:299
  54.5 1.6 collective-permute-done.20.other_view
  56.0 0.8 copy-done.11
  56.8 3.6 %shard_map.133 = bf16[1536,768]{1,0:T(8,128)(2,1)} custom-call(bf16[128,1536]{1,0:T(8,128)(2,1)} %get-tuple-element.87.own_view.kept, bf16[128,1536]{1,0:T(8,128)(2,1)} %copy-done.11, bf16[128,1536]{1,0:T(8,128)(2,1)} %get-tuple-element.83.own_time.kept, bf16[128,1536]{1,0:T(8,128)(2,1)} %copy-done.10), custom_call_target="tpu_custom_call" | custom-call | tf_op jit(solution)/shard_map/pallas_call | solution.py:299
  60.4 4.7 %all-to-all-start.1 = ((bf16[8,192,768]{2,1,0:T(8,128)(2,1)}), bf16[8,192,768]{2,1,0:T(8,128)(2,1)S(1)}, u32[]{:S(2)}, u32[]{:S(2)}) async-start(bf16[8,192,768]{2,1,0:T(8,128)(2,1)} %bitcast.15), calls=%async_computation.1 | async-start | bytes 4718592 | tf_op jit(solution)/shard_map/all_to_all | solution.py:394
  65.0 2.7 %collective-permute-start.11 = (bf16[96,1536]{1,0:T(8,128)(2,1)}, bf16[96,1536]{1,0:T(8,128)(2,1)}, u32[]{:S(2)}, u32[]{:S(2)}) collective-permute-start(bf16[96,1536]{1,0:T(8,128)(2,1)} %collective-permute-done.8.rest_4_), channel_id=1, source_target_pairs={{0,28},{1,29},{2,30},{3,31},{4,0},{5,1},{6,2},{7,3},{8,4},{9,5},{1... | collective-permute-start | bytes 884744 | tf_op jit(solution)/shard_map/ppermute | solution.py:346
  67.7 1.2 collective-permute-start.13
  68.9 5.4 %collective-permute-done.10.rest_5_ = bf16[96,1536]{1,0:T(8,128)(2,1)S(1)} collective-permute-done((bf16[96,1536]{1,0:T(8,128)(2,1)}, bf16[96,1536]{1,0:T(8,128)(2,1)S(1)}, u32[]{:S(2)}, u32[]{:S(2)}) %collective-permute-start.10) | collective-permute-done | bytes 294944 | tf_op jit(solution)/shard_map/ppermute | solution.py:346
  74.4 1.5 collective-permute-start.15
  76.5 6.1 %collective-permute-done.12.rest_7_ = bf16[96,1536]{1,0:T(8,128)(2,1)} collective-permute-done((bf16[96,1536]{1,0:T(8,128)(2,1)S(1)}, bf16[96,1536]{1,0:T(8,128)(2,1)}, u32[]{:S(2)}, u32[]{:S(2)}) %collective-permute-start.12) | collective-permute-done | bytes 294944 | tf_op jit(solution)/shard_map/ppermute | solution.py:346
  82.7 2.4 %collective-permute-start.19 = (bf16[96,1536]{1,0:T(8,128)(2,1)}, bf16[96,1536]{1,0:T(8,128)(2,1)}, u32[]{:S(2)}, u32[]{:S(2)}) collective-permute-start(bf16[96,1536]{1,0:T(8,128)(2,1)} %collective-permute-done.12.rest_7_), channel_id=1, source_target_pairs={{0,1},{1,0},{2,3},{3,2},{4,5},{5,4},{6,7},{7,6},{8,9},{9,8},{10,11... | collective-permute-start | bytes 884744 | tf_op jit(solution)/shard_map/ppermute | solution.py:350
  85.8 4.1 %shard_map.129.action = f32[16,1536]{1,0:T(8,128)} custom-call(s32[16,7]{1,0:T(8,128)} %copy.14.actions, bf16[7,256,1536]{2,1,0:T(8,128)(2,1)} %table.1), custom_call_target="tpu_custom_call" | custom-call | tf_op jit(solution)/shard_map/pallas_call | solution.py:299
  89.9 9.7 %shard_map.131 = (bf16[128,768]{1,0:T(8,128)(2,1)}, f32[128,1536]{1,0:T(8,128)}, bf16[128,1536]{1,0:T(8,128)(2,1)}, bf16[128,1536]{1,0:T(8,128)(2,1)}, bf16[1536,1536]{1,0:T(8,128)(2,1)}) custom-call(s32[1]{0:T(128)} %bitcast.me, s32[1]{0:T(128)} %bitcast.2.z, bf16[64,2304]{1,0:T(8,128)(2,1)} %get-tuple-element.60.q0, bf16[64,2304]{1,0:T(8,128)(2,1)} %copy-done.5, ...), custom_call_target="tpu_custom_call" | custom-call | tf_op jit(solution)/shard_map/pallas_call | solution.py:299
  99.6 1.3 collective-permute-start.22
  100.9 1.3 collective-permute-start.23
  102.2 5.3 %shard_map.134 = (bf16[16,3072]{1,0:T(8,128)(2,1)}, bf16[16,3072]{1,0:T(8,128)(2,1)}, bf16[16,3072]{1,0:T(8,128)(2,1)}, bf16[16,3072]{1,0:T(8,128)(2,1)}, bf16[1...) custom-call(s32[1]{0:T(128)} %bitcast.1.cam, ...), custom_call_target="tpu_custom_call" | custom-call | tf_op jit(solution)/shard_map/pallas_call | solution.py:299
  107.5 1.2 collective-permute-start.24
  108.8 3.5 %collective-permute-done.24.rest_1_ = bf16[16,3072]{1,0:T(8,128)(2,1)S(1)} collective-permute-done((bf16[16,3072]{1,0:T(8,128)(2,1)}, bf16[16,3072]{1,0:T(8,128)(2,1)S(1)}, u32[]{:S(2)}, u32[]{:S(2)}) %collective-permute-start.24) | collective-permute-done | bytes 98336 | tf_op jit(solution)/shard_map/ppermute | solution.py:417
  112.3 13.0 %collective-permute-done.22.near = bf16[128,1536]{1,0:T(8,128)(2,1)S(1)} collective-permute-done((bf16[128,1536]{1,0:T(8,128)(2,1)}, bf16[128,1536]{1,0:T(8,128)(2,1)S(1)}, u32[]{:S(2)}, u32[]{:S(2)}) %collective-permute-start.22) | collective-permute-done | bytes 393248 | tf_op jit(solution)/shard_map/ppermute | solution.py:406
  125.3 9.4 %collective-permute-done.23.far = bf16[128,1536]{1,0:T(8,128)(2,1)S(1)} collective-permute-done((bf16[128,1536]{1,0:T(8,128)(2,1)}, bf16[128,1536]{1,0:T(8,128)(2,1)S(1)}, u32[]{:S(2)}, u32[]{:S(2)}) %collective-permute-start.23) | collective-permute-done | bytes 393248 | tf_op jit(solution)/shard_map/ppermute | solution.py:407
  134.7 1.4 copy-done
  136.1 3.0 %shard_map.137 = bf16[16,12,768]{2,1,0:T(8,128)(2,1)} custom-call(bf16[8,192,768]{2,1,0:T(8,128)(2,1)} %copy-done), custom_call_target="tpu_custom_call" | custom-call | tf_op jit(solution)/shard_map/pallas_call | solution.py:299
  139.1 5.7 %all-to-all-start.2 = ((bf16[16,12,768]{2,1,0:T(8,128)(2,1)}), bf16[16,12,768]{2,1,0:T(8,128)(2,1)S(1)}, u32[]{:S(2)}, u32[]{:S(2)}) async-start(bf16[16,12,768]{2,1,0:T(8,128)(2,1)} %shard_map.137), calls=%async_computation.2 | async-start | bytes 786432 | tf_op jit(solution)/shard_map/all_to_all | solution.py:429
  144.9 2.5 %shard_map.135 = (bf16[64,3072]{1,0:T(8,128)(2,1)}, bf16[64,3072]{1,0:T(8,128)(2,1)}) custom-call(bf16[128,1536]{1,0:T(8,128)(2,1)} %get-tuple-element.83.own_time.kept, bf16[128,768]{1,0:T(8,128)(2,1)} %get-tuple-element.84.dq, f32[128,1536]{1,0:T(8,128)} %get-tuple-element.85.own, bf16[128,1536]{1,0:T(8,128)(2,1)} %copy-done.7, bf16[128,1536]{1,0:T(8,128)(2,1)} %copy-done.8), custom_call_target="tpu_custom_call" | custom-call | tf_op jit(solution)/shard_map/pallas_call | solution.py:299
  147.4 1.1 collective-permute-start.25
  148.5 1.1 collective-permute-start.26
  150.2 2.7 %collective-permute-start.28 = (bf16[16,3072]{1,0:T(8,128)(2,1)S(1)}, bf16[16,3072]{1,0:T(8,128)(2,1)S(1)}, u32[]{:S(2)}, u32[]{:S(2)}) collective-permute-start(bf16[16,3072]{1,0:T(8,128)(2,1)S(1)} %copy-done.30), channel_id=1, source_target_pairs={{0,128},{32,160},{64,192},{96,224},{128,0},{160,32},{192,64},{224,... | collective-permute-start | bytes 294920 | tf_op jit(solution)/shard_map/ppermute | solution.py:417
  152.9 0.9 collective-permute-start.29
  153.8 6.1 %all-to-all-done.2 = bf16[16,12,768]{2,1,0:T(8,128)(2,1)S(1)} async-done(((bf16[16,12,768]{2,1,0:T(8,128)(2,1)}), bf16[16,12,768]{2,1,0:T(8,128)(2,1)S(1)}, u32[]{:S(2)}, u32[]{:S(2)}) %all-to-all-start.2) | async-done | bytes 294944 | tf_op jit(solution)/shard_map/all_to_all | solution.py:429
  160.0 2.4 %collective-permute-start.30 = (bf16[16,3072]{1,0:T(8,128)(2,1)S(1)}, bf16[16,3072]{1,0:T(8,128)(2,1)S(1)}, u32[]{:S(2)}, u32[]{:S(2)}) collective-permute-start(bf16[16,3072]{1,0:T(8,128)(2,1)S(1)} %copy-done.28), channel_id=1, source_target_pairs={{0,192},{32,224},{64,128},{96,160},{128,64},{160,96},{192,0},{224,... | collective-permute-start | bytes 294920 | tf_op jit(solution)/shard_map/ppermute | solution.py:417
  163.1 2.7 %collective-permute-start.32 = (f32[6,768]{1,0:T(8,128)S(1)}, f32[6,768]{1,0:T(8,128)S(1)}, u32[]{:S(2)}, u32[]{:S(2)}) collective-permute-start(f32[6,768]{1,0:T(8,128)S(1)} %constant_dynamic-slice_fusion), channel_id=1, source_target_pairs={{0,1},{1,0},{2,3},{3,2},{4,5},{5,4},{6,7},{7,6},{8,9},{9,8},{10,11... | collective-permute-start | bytes 55304 | tf_op jit(solution)/shard_map/ppermute | solution.py:433
  165.8 2.7 %collective-permute-done.31.rest_7_ = bf16[16,3072]{1,0:T(8,128)(2,1)S(1)} collective-permute-done((bf16[16,3072]{1,0:T(8,128)(2,1)S(1)}, bf16[16,3072]{1,0:T(8,128)(2,1)S(1)}, u32[]{:S(2)}, u32[]{:S(2)}) %collective-permute-start.31) | collective-permute-done | bytes 98336 | tf_op jit(solution)/shard_map/ppermute | solution.py:417
  169.3 4.9 %shard_map.136 = (bf16[128,1536]{1,0:T(8,128)(2,1)}, bf16[128,1536]{1,0:T(8,128)(2,1)}, bf16[128,1536]{1,0:T(8,128)(2,1)}, bf16[128,1536]{1,0:T(8,128)(2,1)}) custom-call(s32[1]{0:T(128)} %bitcast.me, s32[1]{0:T(128)} %bitcast.1.cam, bf16[1536,1536]{1,0:T(8,128)(2,1)} %get-tuple-element.81.w, f32[16,1536]{1,0:T(8,128)} %shard_map.129.action, ...), custom_call_target="tpu_custom_call" | custom-call | tf_op jit(solution)/shard_map/pallas_call | solution.py:299
  (103 shorter events, 5.4 us)
Async XLA Ops:
  0.6 8.4 %collective-permute-start.2 = (bf16[48,1536]{1,0:T(8,128)(2,1)}, bf16[48,1536]{1,0:T(8,128)(2,1)S(1)}, u32[]{:S(2)}, u32[]{:S(2)}) collective-permute-start(bf16[48,1536]{1,0:T(8,128)(2,1)} %param.16), channel_id=1, source_target_pairs={{0,34},{1,35},{2,32},{3,33},{4,38},{5,39},{6,36},{7,37},{8,42},{9,... | collective-permute-start | bytes 442376 | tf_op jit(solution)/shard_map/ppermute | solution.py:329
  8.0 5.1 %collective-permute-start.1 = (bf16[64,1536]{1,0:T(8,128)(2,1)}, bf16[64,1536]{1,0:T(8,128)(2,1)S(1)}, u32[]{:S(2)}, u32[]{:S(2)}) collective-permute-start(bf16[64,1536]{1,0:T(8,128)(2,1)} %get-tuple-element.63), channel_id=1, source_target_pairs={{0,1},{1,0},{2,3},{3,2},{4,5},{5,4},{6,7},{7,6},{8,9},{9,8},{10,11... | collective-permute-start | bytes 589832 | tf_op jit(solution)/shard_map/ppermute | solution.py:356
  9.1 40.7 %all-to-all-start = ((bf16[8,16,3968]{2,1,0:T(8,128)(2,1)}), bf16[8,16,3968]{2,1,0:T(8,128)(2,1)S(1)}, u32[]{:S(2)}, u32[]{:S(2)}) async-start(bf16[8,16,3968]{2,1,0:T(8,128)(2,1)} %bitcast.18), calls=%async_computation | async-start | bytes 2031616 | tf_op jit(solution)/shard_map/all_to_all | solution.py:341
  13.1 47.3 %copy-start.6 = (bf16[96,1536]{1,0:T(8,128)(2,1)}, bf16[96,1536]{1,0:T(8,128)(2,1)S(1)}, u32[]{:S(2)}) copy-start(bf16[96,1536]{1,0:T(8,128)(2,1)S(1)} %pad_maximum_fusion.1.rest_0_) | copy-start | bytes 884740
  13.2 30.0 %copy-start.2 = (bf16[128,1536]{1,0:T(8,128)(2,1)}, bf16[128,1536]{1,0:T(8,128)(2,1)S(1)}, u32[]{:S(2)}) copy-start(bf16[128,1536]{1,0:T(8,128)(2,1)S(1)} %pad_maximum_fusion.own) | copy-start | bytes 1179652
  13.2 20.4 %collective-permute-start.3 = (bf16[128,1536]{1,0:T(8,128)(2,1)S(1)}, bf16[128,1536]{1,0:T(8,128)(2,1)S(1)}, u32[]{:S(2)}, u32[]{:S(2)}) collective-permute-start(bf16[128,1536]{1,0:T(8,128)(2,1)S(1)} %pad_maximum_fusion.own), channel_id=1, source_target_pairs={{0,2},{1,3},{2,4},{3,5},{4,6},{5,7},{6,8},{7,9},{8,10},{9,11},{10,... | collective-permute-start | bytes 1179656 | tf_op jit(solution)/shard_map/ppermute | solution.py:360
  17.4 16.2 %collective-permute-start.4 = (bf16[128,1536]{1,0:T(8,128)(2,1)S(1)}, bf16[128,1536]{1,0:T(8,128)(2,1)S(1)}, u32[]{:S(2)}, u32[]{:S(2)}) collective-permute-start(bf16[128,1536]{1,0:T(8,128)(2,1)S(1)} %pad_maximum_fusion.own), channel_id=1, source_target_pairs={{0,4},{1,5},{2,6},{3,7},{4,8},{5,9},{6,10},{7,11},{8,12},{9,13},{1... | collective-permute-start | bytes 1179656 | tf_op jit(solution)/shard_map/ppermute | solution.py:361
  21.0 12.6 %collective-permute-start.5 = (bf16[96,1536]{1,0:T(8,128)(2,1)S(1)}, bf16[96,1536]{1,0:T(8,128)(2,1)S(1)}, u32[]{:S(2)}, u32[]{:S(2)}) collective-permute-start(bf16[96,1536]{1,0:T(8,128)(2,1)S(1)} %pad_maximum_fusion.1.rest_0_), channel_id=1, source_target_pairs={{0,4},{1,5},{2,6},{3,7},{4,8},{5,9},{6,10},{7,11},{8,12},{9,13},{1... | collective-permute-start | bytes 884744 | tf_op jit(solution)/shard_map/ppermute | solution.py:346
  22.6 10.9 %collective-permute-start.6 = (bf16[96,1536]{1,0:T(8,128)(2,1)S(1)}, bf16[96,1536]{1,0:T(8,128)(2,1)S(1)}, u32[]{:S(2)}, u32[]{:S(2)}) collective-permute-start(bf16[96,1536]{1,0:T(8,128)(2,1)S(1)} %pad_maximum_fusion.1.rest_0_), channel_id=1, source_target_pairs={{0,28},{1,29},{2,30},{3,31},{4,0},{5,1},{6,2},{7,3},{8,4},{9,5},{1... | collective-permute-start | bytes 884744 | tf_op jit(solution)/shard_map/ppermute | solution.py:346
  24.4 18.8 %collective-permute-start = (bf16[64,2304]{1,0:T(8,128)(2,1)}, bf16[64,2304]{1,0:T(8,128)(2,1)S(1)}, u32[]{:S(2)}, u32[]{:S(2)}) collective-permute-start(bf16[64,2304]{1,0:T(8,128)(2,1)} %get-tuple-element.61), channel_id=1, source_target_pairs={{0,1},{1,0},{2,3},{3,2},{4,5},{5,4},{6,7},{7,6},{8,9},{9,8},{10,11... | collective-permute-start | bytes 884744 | tf_op jit(solution)/shard_map/ppermute | solution.py:357
  33.5 56.3 %copy-start.12 = (bf16[96,1536]{1,0:T(8,128)(2,1)}, bf16[96,1536]{1,0:T(8,128)(2,1)S(1)}, u32[]{:S(2)}) copy-start(bf16[96,1536]{1,0:T(8,128)(2,1)S(1)} %collective-permute-done.5.rest_1_) | copy-start | bytes 884740
  33.5 56.3 %copy-start.13 = (bf16[96,1536]{1,0:T(8,128)(2,1)}, bf16[96,1536]{1,0:T(8,128)(2,1)S(1)}, u32[]{:S(2)}) copy-start(bf16[96,1536]{1,0:T(8,128)(2,1)S(1)} %collective-permute-done.6.rest_2_) | copy-start | bytes 884740
  33.6 16.2 %collective-permute-start.7 = (bf16[96,1536]{1,0:T(8,128)(2,1)S(1)}, bf16[96,1536]{1,0:T(8,128)(2,1)}, u32[]{:S(2)}, u32[]{:S(2)}) collective-permute-start(bf16[96,1536]{1,0:T(8,128)(2,1)S(1)} %collective-permute-done.5.rest_1_), channel_id=1, source_target_pairs={{0,4},{1,5},{2,6},{3,7},{4,8},{5,9},{6,10},{7,11},{8,12},{9,13},{1... | collective-permute-start | bytes 884744 | tf_op jit(solution)/shard_map/ppermute | solution.py:346
  35.9 13.9 %collective-permute-start.8 = (bf16[96,1536]{1,0:T(8,128)(2,1)S(1)}, bf16[96,1536]{1,0:T(8,128)(2,1)}, u32[]{:S(2)}, u32[]{:S(2)}) collective-permute-start(bf16[96,1536]{1,0:T(8,128)(2,1)S(1)} %collective-permute-done.6.rest_2_), channel_id=1, source_target_pairs={{0,28},{1,29},{2,30},{3,31},{4,0},{5,1},{6,2},{7,3},{8,4},{9,5},{1... | collective-permute-start | bytes 884744 | tf_op jit(solution)/shard_map/ppermute | solution.py:346
  39.9 9.9 %collective-permute-start.9 = (bf16[96,1536]{1,0:T(8,128)(2,1)S(1)}, bf16[96,1536]{1,0:T(8,128)(2,1)}, u32[]{:S(2)}, u32[]{:S(2)}) collective-permute-start(bf16[96,1536]{1,0:T(8,128)(2,1)S(1)} %pad_maximum_fusion.1.rest_0_), channel_id=1, source_target_pairs={{0,1},{1,0},{2,3},{3,2},{4,5},{5,4},{6,7},{7,6},{8,9},{9,8},{10,11... | collective-permute-start | bytes 884744 | tf_op jit(solution)/shard_map/ppermute | solution.py:350
  49.8 4.7 %collective-permute-start.21 = (bf16[128,1536]{1,0:T(8,128)(2,1)}, bf16[128,1536]{1,0:T(8,128)(2,1)S(1)}, u32[]{:S(2)}, u32[]{:S(2)}) collective-permute-start(bf16[128,1536]{1,0:T(8,128)(2,1)} %get-tuple-element.89), channel_id=1, source_target_pairs={{0,1},{1,0},{2,3},{3,2},{4,5},{5,4},{6,7},{7,6},{8,9},{9,8},{10,11... | collective-permute-start | bytes 1179656 | tf_op jit(solution)/shard_map/ppermute | solution.py:386
  54.0 2.1 %collective-permute-start.20 = (bf16[128,1536]{1,0:T(8,128)(2,1)}, bf16[128,1536]{1,0:T(8,128)(2,1)S(1)}, u32[]{:S(2)}, u32[]{:S(2)}) collective-permute-start(bf16[128,1536]{1,0:T(8,128)(2,1)} %get-tuple-element.88), channel_id=1, source_target_pairs={{0,1},{1,0},{2,3},{3,2},{4,5},{5,4},{6,7},{7,6},{8,9},{9,8},{10,11... | collective-permute-start | bytes 1179656 | tf_op jit(solution)/shard_map/ppermute | solution.py:385
  60.4 24.7 %copy-start.26 = (s32[16,7]{0,1:T(8,128)S(1)}, s32[16,7]{0,1:T(8,128)}, u32[]{:S(2)}) copy-start(s32[16,7]{0,1:T(8,128)} %param.14) | copy-start | bytes 1348
  60.4 74.3 %all-to-all-start.1 = ((bf16[8,192,768]{2,1,0:T(8,128)(2,1)}), bf16[8,192,768]{2,1,0:T(8,128)(2,1)S(1)}, u32[]{:S(2)}, u32[]{:S(2)}) async-start(bf16[8,192,768]{2,1,0:T(8,128)(2,1)} %bitcast.15), calls=%async_computation.1 | async-start | bytes 4718592 | tf_op jit(solution)/shard_map/all_to_all | solution.py:394
  65.0 9.3 %collective-permute-start.10 = (bf16[96,1536]{1,0:T(8,128)(2,1)}, bf16[96,1536]{1,0:T(8,128)(2,1)S(1)}, u32[]{:S(2)}, u32[]{:S(2)}) collective-permute-start(bf16[96,1536]{1,0:T(8,128)(2,1)} %collective-permute-done.7.rest_3_), channel_id=1, source_target_pairs={{0,4},{1,5},{2,6},{3,7},{4,8},{5,9},{6,10},{7,11},{8,12},{9,13},{1... | collective-permute-start | bytes 884744 | tf_op jit(solution)/shard_map/ppermute | solution.py:346
  65.0 10.8 %collective-permute-start.11 = (bf16[96,1536]{1,0:T(8,128)(2,1)}, bf16[96,1536]{1,0:T(8,128)(2,1)}, u32[]{:S(2)}, u32[]{:S(2)}) collective-permute-start(bf16[96,1536]{1,0:T(8,128)(2,1)} %collective-permute-done.8.rest_4_), channel_id=1, source_target_pairs={{0,28},{1,29},{2,30},{3,31},{4,0},{5,1},{6,2},{7,3},{8,4},{9,5},{1... | collective-permute-start | bytes 884744 | tf_op jit(solution)/shard_map/ppermute | solution.py:346
  67.7 8.3 %collective-permute-start.13 = (bf16[96,1536]{1,0:T(8,128)(2,1)S(1)}, bf16[96,1536]{1,0:T(8,128)(2,1)S(1)}, u32[]{:S(2)}, u32[]{:S(2)}) collective-permute-start(bf16[96,1536]{1,0:T(8,128)(2,1)S(1)} %collective-permute-done.5.rest_1_), channel_id=1, source_target_pairs={{0,1},{1,0},{2,3},{3,2},{4,5},{5,4},{6,7},{7,6},{8,9},{9,8},{10,11... | collective-permute-start | bytes 884744 | tf_op jit(solution)/shard_map/ppermute | solution.py:350
  68.9 7.5 %collective-permute-start.14 = (bf16[96,1536]{1,0:T(8,128)(2,1)S(1)}, bf16[96,1536]{1,0:T(8,128)(2,1)S(1)}, u32[]{:S(2)}, u32[]{:S(2)}) collective-permute-start(bf16[96,1536]{1,0:T(8,128)(2,1)S(1)} %collective-permute-done.6.rest_2_), channel_id=1, source_target_pairs={{0,1},{1,0},{2,3},{3,2},{4,5},{5,4},{6,7},{7,6},{8,9},{9,8},{10,11... | collective-permute-start | bytes 884744 | tf_op jit(solution)/shard_map/ppermute | solution.py:350
  74.4 15.5 %copy-start.14 = (bf16[96,1536]{1,0:T(8,128)(2,1)}, bf16[96,1536]{1,0:T(8,128)(2,1)S(1)}, u32[]{:S(2)}) copy-start(bf16[96,1536]{1,0:T(8,128)(2,1)S(1)} %collective-permute-done.10.rest_5_) | copy-start | bytes 884740
  74.4 8.3 %collective-permute-start.12 = (bf16[96,1536]{1,0:T(8,128)(2,1)S(1)}, bf16[96,1536]{1,0:T(8,128)(2,1)}, u32[]{:S(2)}, u32[]{:S(2)}) collective-permute-start(bf16[96,1536]{1,0:T(8,128)(2,1)S(1)} %collective-permute-done.10.rest_5_), channel_id=1, source_target_pairs={{0,4},{1,5},{2,6},{3,7},{4,8},{5,9},{6,10},{7,11},{8,12},{9,13},{1... | collective-permute-start | bytes 884744 | tf_op jit(solution)/shard_map/ppermute | solution.py:346
  74.4 15.5 %collective-permute-start.15 = (bf16[96,1536]{1,0:T(8,128)(2,1)}, bf16[96,1536]{1,0:T(8,128)(2,1)}, u32[]{:S(2)}, u32[]{:S(2)}) collective-permute-start(bf16[96,1536]{1,0:T(8,128)(2,1)} %collective-permute-done.7.rest_3_), channel_id=1, source_target_pairs={{0,1},{1,0},{2,3},{3,2},{4,5},{5,4},{6,7},{7,6},{8,9},{9,8},{10,11... | collective-permute-start | bytes 884744 | tf_op jit(solution)/shard_map/ppermute | solution.py:350
  75.9 14.0 %collective-permute-start.16 = (bf16[96,1536]{1,0:T(8,128)(2,1)}, bf16[96,1536]{1,0:T(8,128)(2,1)}, u32[]{:S(2)}, u32[]{:S(2)}) collective-permute-start(bf16[96,1536]{1,0:T(8,128)(2,1)} %collective-permute-done.8.rest_4_), channel_id=1, source_target_pairs={{0,1},{1,0},{2,3},{3,2},{4,5},{5,4},{6,7},{7,6},{8,9},{9,8},{10,11... | collective-permute-start | bytes 884744 | tf_op jit(solution)/shard_map/ppermute | solution.py:350
  76.0 13.9 %collective-permute-start.17 = (bf16[96,1536]{1,0:T(8,128)(2,1)S(1)}, bf16[96,1536]{1,0:T(8,128)(2,1)}, u32[]{:S(2)}, u32[]{:S(2)}) collective-permute-start(bf16[96,1536]{1,0:T(8,128)(2,1)S(1)} %collective-permute-done.10.rest_5_), channel_id=1, source_target_pairs={{0,1},{1,0},{2,3},{3,2},{4,5},{5,4},{6,7},{7,6},{8,9},{9,8},{10,11... | collective-permute-start | bytes 884744 | tf_op jit(solution)/shard_map/ppermute | solution.py:350
  76.4 13.5 %collective-permute-start.18 = (bf16[96,1536]{1,0:T(8,128)(2,1)}, bf16[96,1536]{1,0:T(8,128)(2,1)}, u32[]{:S(2)}, u32[]{:S(2)}) collective-permute-start(bf16[96,1536]{1,0:T(8,128)(2,1)} %collective-permute-done.11.rest_6_), channel_id=1, source_target_pairs={{0,1},{1,0},{2,3},{3,2},{4,5},{5,4},{6,7},{7,6},{8,9},{9,8},{10,11... | collective-permute-start | bytes 884744 | tf_op jit(solution)/shard_map/ppermute | solution.py:350
  82.7 7.3 %collective-permute-start.19 = (bf16[96,1536]{1,0:T(8,128)(2,1)}, bf16[96,1536]{1,0:T(8,128)(2,1)}, u32[]{:S(2)}, u32[]{:S(2)}) collective-permute-start(bf16[96,1536]{1,0:T(8,128)(2,1)} %collective-permute-done.12.rest_7_), channel_id=1, source_target_pairs={{0,1},{1,0},{2,3},{3,2},{4,5},{5,4},{6,7},{7,6},{8,9},{9,8},{10,11... | collective-permute-start | bytes 884744 | tf_op jit(solution)/shard_map/ppermute | solution.py:350
  99.6 25.7 %collective-permute-start.22 = (bf16[128,1536]{1,0:T(8,128)(2,1)}, bf16[128,1536]{1,0:T(8,128)(2,1)S(1)}, u32[]{:S(2)}, u32[]{:S(2)}) collective-permute-start(bf16[128,1536]{1,0:T(8,128)(2,1)} %get-tuple-element.91), channel_id=1, source_target_pairs={{2,0},{3,1},{4,2},{5,3},{6,4},{7,5},{8,6},{9,7},{10,8},{11,9},{12,... | collective-permute-start | bytes 1179656 | tf_op jit(solution)/shard_map/ppermute | solution.py:406
  100.9 33.7 %collective-permute-start.23 = (bf16[128,1536]{1,0:T(8,128)(2,1)}, bf16[128,1536]{1,0:T(8,128)(2,1)S(1)}, u32[]{:S(2)}, u32[]{:S(2)}) collective-permute-start(bf16[128,1536]{1,0:T(8,128)(2,1)} %get-tuple-element.92), channel_id=1, source_target_pairs={{4,0},{5,1},{6,2},{7,3},{8,4},{9,5},{10,6},{11,7},{12,8},{13,9},{1... | collective-permute-start | bytes 1179656 | tf_op jit(solution)/shard_map/ppermute | solution.py:407
  107.5 42.6 %copy-start.30 = (bf16[16,3072]{1,0:T(8,128)(2,1)S(1)}, bf16[16,3072]{1,0:T(8,128)(2,1)}, u32[]{:S(2)}) copy-start(bf16[16,3072]{1,0:T(8,128)(2,1)} %get-tuple-element.104) | copy-start | bytes 294916
  107.5 45.3 %copy-start.29 = (bf16[16,3072]{1,0:T(8,128)(2,1)S(1)}, bf16[16,3072]{1,0:T(8,128)(2,1)}, u32[]{:S(2)}) copy-start(bf16[16,3072]{1,0:T(8,128)(2,1)} %get-tuple-element.105) | copy-start | bytes 294916
  107.5 4.7 %collective-permute-start.24 = (bf16[16,3072]{1,0:T(8,128)(2,1)}, bf16[16,3072]{1,0:T(8,128)(2,1)S(1)}, u32[]{:S(2)}, u32[]{:S(2)}) collective-permute-start(bf16[16,3072]{1,0:T(8,128)(2,1)} %get-tuple-element.95), channel_id=1, source_target_pairs={{0,32},{32,0},{64,96},{96,64},{128,160},{160,128},{192,224},{224,1... | collective-permute-start | bytes 294920 | tf_op jit(solution)/shard_map/ppermute | solution.py:417
  112.3 56.3 %copy-start.19 = (bf16[16,3072]{1,0:T(8,128)(2,1)}, bf16[16,3072]{1,0:T(8,128)(2,1)S(1)}, u32[]{:S(2)}) copy-start(bf16[16,3072]{1,0:T(8,128)(2,1)S(1)} %collective-permute-done.24.rest_1_) | copy-start | bytes 294916
  125.3 19.6 %copy-start.7 = (bf16[128,1536]{1,0:T(8,128)(2,1)}, bf16[128,1536]{1,0:T(8,128)(2,1)S(1)}, u32[]{:S(2)}) copy-start(bf16[128,1536]{1,0:T(8,128)(2,1)S(1)} %collective-permute-done.22.near) | copy-start | bytes 1179652
  139.1 20.9 %copy-start.28 = (bf16[16,3072]{1,0:T(8,128)(2,1)S(1)}, bf16[16,3072]{1,0:T(8,128)(2,1)}, u32[]{:S(2)}) copy-start(bf16[16,3072]{1,0:T(8,128)(2,1)} %get-tuple-element.106) | copy-start | bytes 294916
  139.1 23.3 %copy-start.27 = (bf16[16,3072]{1,0:T(8,128)(2,1)S(1)}, bf16[16,3072]{1,0:T(8,128)(2,1)}, u32[]{:S(2)}) copy-start(bf16[16,3072]{1,0:T(8,128)(2,1)} %get-tuple-element.107) | copy-start | bytes 294916
  139.1 20.8 %all-to-all-start.2 = ((bf16[16,12,768]{2,1,0:T(8,128)(2,1)}), bf16[16,12,768]{2,1,0:T(8,128)(2,1)S(1)}, u32[]{:S(2)}, u32[]{:S(2)}) async-start(bf16[16,12,768]{2,1,0:T(8,128)(2,1)} %shard_map.137), calls=%async_computation.2 | async-start | bytes 786432 | tf_op jit(solution)/shard_map/all_to_all | solution.py:429
  147.4 21.1 %collective-permute-start.25 = (bf16[64,3072]{1,0:T(8,128)(2,1)}, bf16[64,3072]{1,0:T(8,128)(2,1)S(1)}, u32[]{:S(2)}, u32[]{:S(2)}) collective-permute-start(bf16[64,3072]{1,0:T(8,128)(2,1)} %get-tuple-element.99), channel_id=1, source_target_pairs={{0,1},{1,0},{2,3},{3,2},{4,5},{5,4},{6,7},{7,6},{8,9},{9,8},{10,11... | collective-permute-start | bytes 1179656 | tf_op jit(solution)/shard_map/ppermute | solution.py:441
  148.5 11.5 %collective-permute-start.26 = (bf16[16,3072]{1,0:T(8,128)(2,1)}, bf16[16,3072]{1,0:T(8,128)(2,1)S(1)}, u32[]{:S(2)}, u32[]{:S(2)}) collective-permute-start(bf16[16,3072]{1,0:T(8,128)(2,1)} %get-tuple-element.102), channel_id=1, source_target_pairs={{0,64},{32,96},{64,0},{96,32},{128,192},{160,224},{192,128},{224,1... | collective-permute-start | bytes 294920 | tf_op jit(solution)/shard_map/ppermute | solution.py:417
  149.6 12.8 %collective-permute-start.27 = (bf16[16,3072]{1,0:T(8,128)(2,1)}, bf16[16,3072]{1,0:T(8,128)(2,1)S(1)}, u32[]{:S(2)}, u32[]{:S(2)}) collective-permute-start(bf16[16,3072]{1,0:T(8,128)(2,1)} %get-tuple-element.103), channel_id=1, source_target_pairs={{0,96},{32,64},{64,32},{96,0},{128,224},{160,192},{192,160},{224,1... | collective-permute-start | bytes 294920 | tf_op jit(solution)/shard_map/ppermute | solution.py:417
  150.2 12.9 %collective-permute-start.28 = (bf16[16,3072]{1,0:T(8,128)(2,1)S(1)}, bf16[16,3072]{1,0:T(8,128)(2,1)S(1)}, u32[]{:S(2)}, u32[]{:S(2)}) collective-permute-start(bf16[16,3072]{1,0:T(8,128)(2,1)S(1)} %copy-done.30), channel_id=1, source_target_pairs={{0,128},{32,160},{64,192},{96,224},{128,0},{160,32},{192,64},{224,... | collective-permute-start | bytes 294920 | tf_op jit(solution)/shard_map/ppermute | solution.py:417
  152.9 12.9 %collective-permute-start.29 = (bf16[16,3072]{1,0:T(8,128)(2,1)S(1)}, bf16[16,3072]{1,0:T(8,128)(2,1)S(1)}, u32[]{:S(2)}, u32[]{:S(2)}) collective-permute-start(bf16[16,3072]{1,0:T(8,128)(2,1)S(1)} %copy-done.29), channel_id=1, source_target_pairs={{0,160},{32,128},{64,224},{96,192},{128,32},{160,0},{192,96},{224,... | collective-permute-start | bytes 294920 | tf_op jit(solution)/shard_map/ppermute | solution.py:417
  160.0 5.8 %collective-permute-start.30 = (bf16[16,3072]{1,0:T(8,128)(2,1)S(1)}, bf16[16,3072]{1,0:T(8,128)(2,1)S(1)}, u32[]{:S(2)}, u32[]{:S(2)}) collective-permute-start(bf16[16,3072]{1,0:T(8,128)(2,1)S(1)} %copy-done.28), channel_id=1, source_target_pairs={{0,192},{32,224},{64,128},{96,160},{128,64},{160,96},{192,0},{224,... | collective-permute-start | bytes 294920 | tf_op jit(solution)/shard_map/ppermute | solution.py:417
  162.4 6.1 %collective-permute-start.31 = (bf16[16,3072]{1,0:T(8,128)(2,1)S(1)}, bf16[16,3072]{1,0:T(8,128)(2,1)S(1)}, u32[]{:S(2)}, u32[]{:S(2)}) collective-permute-start(bf16[16,3072]{1,0:T(8,128)(2,1)S(1)} %copy-done.27), channel_id=1, source_target_pairs={{0,224},{32,192},{64,160},{96,128},{128,96},{160,64},{192,32},{224... | collective-permute-start | bytes 294920 | tf_op jit(solution)/shard_map/ppermute | solution.py:417
  163.1 11.2 %collective-permute-start.32 = (f32[6,768]{1,0:T(8,128)S(1)}, f32[6,768]{1,0:T(8,128)S(1)}, u32[]{:S(2)}, u32[]{:S(2)}) collective-permute-start(f32[6,768]{1,0:T(8,128)S(1)} %constant_dynamic-slice_fusion), channel_id=1, source_target_pairs={{0,1},{1,0},{2,3},{3,2},{4,5},{5,4},{6,7},{7,6},{8,9},{9,8},{10,11... | collective-permute-start | bytes 55304 | tf_op jit(solution)/shard_map/ppermute | solution.py:433
  (19 other events, 92.7 us)

commit v7 on v6

--- a/solution.py
+++ b/solution.py
@@ -381,6 +381,7 @@
     )
 
     pass_on(7, depth)
+    w_own[-1], action_sum = lax.optimization_barrier((w_own[-1], action_sum))
     swap_blocks(depth)
     view_swap = lax.ppermute(view_swap, "tm", swap)
     time_swap = lax.ppermute(time_swap, "tm", swap)
@@ -393,7 +394,6 @@
     )
     part = lax.all_to_all(part.reshape(cams, width // cams, CW), "cam", 0, 0, tiled=True)
 
-    q0, action_sum = lax.optimization_barrier((q0, action_sum))
     dq_time, own_grad, near_grad, far_grad, w_full = call(
         functools.partial(time_backward_kernel, depth),
         [((rows, CW), BF), ((rows, 2 * CW), F32)] + [((rows, 2 * CW), BF)] * 2 + [((width, width), BF)],
@@ -402,7 +402,17 @@
         scratch=[pltpu.VMEM((width, width), BF), pltpu.SemaphoreType.DMA((tm,)), pltpu.SemaphoreType.DMA],
         kept=1,
     )
-    view_x, near_grad = lax.optimization_barrier((view_x, near_grad))
+    part, near_grad = lax.optimization_barrier((part, near_grad))
+    chips = tm // 2
+    (part,) = call(
+        camera_sum_kernel,
+        [((chips, width // cams // chips, CW), BF)],
+        [VM],
+        part,
+        scratch=[pltpu.VMEM((width // cams, CW), F32)],
+    )
+    view_x, part = lax.optimization_barrier((view_x, part))
+    part = lax.all_to_all(part, "tm", 0, 0, tiled=True, axis_index_groups=same_core)
     near_grad = lax.ppermute(near_grad, "tm", [(i + 2, i) for i in range(tm - 2)])
     far_grad = lax.ppermute(far_grad, "tm", [(i + 4, i) for i in range(tm - 4)])
     cam = lax.axis_index("cam").reshape(1)
@@ -416,17 +426,10 @@
     view_back = [view_out[0]] + [
         lax.ppermute(view_out[d], "cam", [(i, i ^ d) for i in range(cams)]) for d in range(1, cams)
     ]
-    part, near_grad, far_grad, view_back[1] = lax.optimization_barrier((part, near_grad, far_grad, view_back[1]))
-
-    chips = tm // 2
-    (part,) = call(
-        camera_sum_kernel,
-        [((chips, width // cams // chips, CW), BF)],
-        [VM],
-        part,
-        scratch=[pltpu.VMEM((width // cams, CW), F32)],
-    )
-    part = lax.all_to_all(part, "tm", 0, 0, tiled=True, axis_index_groups=same_core)
+
+    part, near_grad, far_grad, view_back[1:4] = lax.optimization_barrier(
+        (part, near_grad, far_grad, view_back[1:4])
+    )
     part = jnp.sum(part.astype(F32), axis=0)
     final = width // cams // tm
     mine = lax.dynamic_slice_in_dim(part, core * final, final, 0)

time: 177 us -> 171 us (0.966)
  the two profiles are of different devices: /device:TPU:1 before, /device:TPU:113 now
where the time goes in v7:
time: 171 us; the launch traced here: 170 us
  starting transfers between devices  64.3 us (38%)
  waiting for transfers between devices  52.2 us (31%)
  Pallas kernels  45.7 us (27%)
  local copies, waits for them, and re-layouts  6.12 us (4%)
    pallas_call x10, Pallas kernels, call(): pl.pallas_call(kernel, out_shape=[jax.ShapeDtypeStruct(shape, kind) for s...  45.7 us
    ppermute x7, waiting for transfers between devices, pass_on(): lax.ppermute(w_own[max(i - 2, 0)], 'tm', up if i % 2 else down)  30 us
    ppermute x7, starting transfers between devices, shards(): lax.ppermute(view_out[d], 'cam', [(i, i ^ d) for i in range(cams)])  9.22 us
    ppermute x7, starting transfers between devices, pass_on(): lax.ppermute(w_own[max(i - 2, 0)], 'tm', up if i % 2 else down)  8.27 us
    ppermute x1, waiting for transfers between devices, shards(): lax.ppermute(near_grad, 'tm', [(i + 2, i) for i in range(tm - 2)])  8.16 us
    all_to_all x1, starting transfers between devices, shards(): lax.all_to_all(part, 'tm', 0, 0, tiled=True, axis_index_groups=same_core)  7.96 us
    ppermute x1, waiting for transfers between devices, shards(): far_grad = lax.ppermute(far_grad, 'tm', [(i + 4, i) for i in range(tm - 4)])  7.45 us
    ppermute x8, starting transfers between devices, swap_blocks(): w_other.append(lax.ppermute(block_rows, 'tm', swap))  7.36 us
  transfers between devices with their start and end apart: 36, of which 12 were waited for; matrix products, arithmetic and copies ran while one was open for 1% of the time, Pallas kernels for 20%

profile of v7, /device:TPU:113, one launch (start us, length us, event | category | flops | bytes accessed | tf_op | source)
XLA Modules:
  0.0 170.1 jit_solution(11536156705098020689)
XLA Ops:
  0.9 3.7 %shard_map.128 = (bf16[128,3968]{1,0:T(8,128)(2,1)}, bf16[64,1536]{1,0:T(8,128)(2,1)}, bf16[64,1536]{1,0:T(8,128)(2,1)}, bf16[64,2304]{1,0:T(8,128)(2,1)}, bf16[64,2304]{1,0:T(8,128)(2,1)}) custom-call(s32[1]{0:T(128)} %bitcast.me, s32[1,16]{1,0:T(1,128)} %valid.1, bf16[128,1536]{1,0:T(8,128)(2,1)} %bitcast.19, bf16[128,1536]{1,0:T(8,128)(2,1)} %bitcast.20, ...), custom_call_target="tpu_custom_call" | custom-call | tf_op jit(solution)/shard_map/pallas_call | solution.py:299
  4.6 1.0 collective-permute-start.1
  5.7 6.0 %all-to-all-start = ((bf16[8,16,3968]{2,1,0:T(8,128)(2,1)}), bf16[8,16,3968]{2,1,0:T(8,128)(2,1)S(1)}, u32[]{:S(2)}, u32[]{:S(2)}) async-start(bf16[8,16,3968]{2,1,0:T(8,128)(2,1)} %bitcast.18), calls=%async_computation | async-start | bytes 2031616 | tf_op jit(solution)/shard_map/all_to_all | solution.py:341
  11.7 5.2 %collective-permute-start.3 = (bf16[128,1536]{1,0:T(8,128)(2,1)S(1)}, bf16[128,1536]{1,0:T(8,128)(2,1)S(1)}, u32[]{:S(2)}, u32[]{:S(2)}) collective-permute-start(bf16[128,1536]{1,0:T(8,128)(2,1)S(1)} %pad_maximum_fusion.own), channel_id=1, source_target_pairs={{0,2},{1,3},{2,4},{3,5},{4,6},{5,7},{6,8},{7,9},{8,10},{9,11},{10,... | collective-permute-start | bytes 1179656 | tf_op jit(solution)/shard_map/ppermute | solution.py:360
  16.9 2.6 %collective-permute-start.4 = (bf16[128,1536]{1,0:T(8,128)(2,1)S(1)}, bf16[128,1536]{1,0:T(8,128)(2,1)S(1)}, u32[]{:S(2)}, u32[]{:S(2)}) collective-permute-start(bf16[128,1536]{1,0:T(8,128)(2,1)S(1)} %pad_maximum_fusion.own), channel_id=1, source_target_pairs={{0,4},{1,5},{2,6},{3,7},{4,8},{5,9},{6,10},{7,11},{8,12},{9,13},{1... | collective-permute-start | bytes 1179656 | tf_op jit(solution)/shard_map/ppermute | solution.py:361
  19.5 0.8 collective-permute-start.5
  20.4 0.7 collective-permute-start.6
  21.1 1.7 collective-permute-start
  22.7 22.2 %collective-permute-done.5.rest_1_ = bf16[96,1536]{1,0:T(8,128)(2,1)S(1)} collective-permute-done((bf16[96,1536]{1,0:T(8,128)(2,1)S(1)}, bf16[96,1536]{1,0:T(8,128)(2,1)S(1)}, u32[]{:S(2)}, u32[]{:S(2)}) %collective-permute-start.5) | collective-permute-done | bytes 294944 | tf_op jit(solution)/shard_map/ppermute | solution.py:346
  45.0 3.0 %collective-permute-start.7 = (bf16[96,1536]{1,0:T(8,128)(2,1)S(1)}, bf16[96,1536]{1,0:T(8,128)(2,1)}, u32[]{:S(2)}, u32[]{:S(2)}) collective-permute-start(bf16[96,1536]{1,0:T(8,128)(2,1)S(1)} %collective-permute-done.5.rest_1_), channel_id=1, source_target_pairs={{0,4},{1,5},{2,6},{3,7},{4,8},{5,9},{6,10},{7,11},{8,12},{9,13},{1... | collective-permute-start | bytes 884744 | tf_op jit(solution)/shard_map/ppermute | solution.py:346
  48.0 1.7 collective-permute-start.9
  49.6 0.7 copy-done.5
  50.4 5.8 %shard_map.129 = (bf16[128,1536]{1,0:T(8,128)(2,1)}, bf16[128,1536]{1,0:T(8,128)(2,1)}, f32[6,256,384]{2,1,0:T(8,128)}) custom-call(s32[12]{0:T(128)} %windows.1, s32[1]{0:T(128)} %bitcast.me, s32[1]{0:T(128)} %bitcast.7.pair, bf16[64,2304]{1,0:T(8,128)(2,1)} %get-tuple-element.63.q0, bf16[64,2304]{1,0:T(8,128)(2,1)} %copy-done.5, ...), custom_call_target="tpu_custom_call" | custom-call | tf_op jit(solution)/shard_map/pallas_call | solution.py:299
  56.2 1.0 copy-done.1
  57.2 3.2 %shard_map.132 = (bf16[128,1536]{1,0:T(8,128)(2,1)}, bf16[128,1536]{1,0:T(8,128)(2,1)}, f32[6,256,128]{2,1,0:T(8,128)}) custom-call(s32[1]{0:T(128)} %bitcast.me, bf16[128,3968]{1,0:T(8,128)(2,1)} %bitcast.16), custom_call_target="tpu_custom_call" | custom-call | tf_op jit(solution)/shard_map/pallas_call | solution.py:299
  60.4 2.5 %collective-permute-start.20 = (bf16[128,1536]{1,0:T(8,128)(2,1)}, bf16[128,1536]{1,0:T(8,128)(2,1)S(1)}, u32[]{:S(2)}, u32[]{:S(2)}) collective-permute-start(bf16[128,1536]{1,0:T(8,128)(2,1)} %get-tuple-element.92), channel_id=1, source_target_pairs={{0,1},{1,0},{2,3},{3,2},{4,5},{5,4},{6,7},{7,6},{8,9},{9,8},{10,11... | collective-permute-start | bytes 1179656 | tf_op jit(solution)/shard_map/ppermute | solution.py:386
  62.9 1.6 collective-permute-done.20.other_view
  64.4 0.8 copy-done.11
  65.2 3.6 %shard_map.133 = bf16[1536,768]{1,0:T(8,128)(2,1)} custom-call(bf16[128,1536]{1,0:T(8,128)(2,1)} %get-tuple-element.91.own_view.kept, bf16[128,1536]{1,0:T(8,128)(2,1)} %copy-done.11, bf16[128,1536]{1,0:T(8,128)(2,1)} %get-tuple-element.87.own_time.kept, bf16[128,1536]{1,0:T(8,128)(2,1)} %copy-done.10), custom_call_target="tpu_custom_call" | custom-call | tf_op jit(solution)/shard_map/pallas_call | solution.py:299
  68.8 5.4 %all-to-all-start.1 = ((bf16[8,192,768]{2,1,0:T(8,128)(2,1)}), bf16[8,192,768]{2,1,0:T(8,128)(2,1)S(1)}, u32[]{:S(2)}, u32[]{:S(2)}) async-start(bf16[8,192,768]{2,1,0:T(8,128)(2,1)} %bitcast.15), calls=%async_computation.1 | async-start | bytes 4718592 | tf_op jit(solution)/shard_map/all_to_all | solution.py:395
  74.2 1.3 collective-permute-start.10
  75.5 6.8 %collective-permute-done.10.rest_5_ = bf16[96,1536]{1,0:T(8,128)(2,1)S(1)} collective-permute-done((bf16[96,1536]{1,0:T(8,128)(2,1)}, bf16[96,1536]{1,0:T(8,128)(2,1)S(1)}, u32[]{:S(2)}, u32[]{:S(2)}) %collective-permute-start.10) | collective-permute-done | bytes 294944 | tf_op jit(solution)/shard_map/ppermute | solution.py:346
  82.3 2.5 %collective-permute-start.12 = (bf16[96,1536]{1,0:T(8,128)(2,1)S(1)}, bf16[96,1536]{1,0:T(8,128)(2,1)}, u32[]{:S(2)}, u32[]{:S(2)}) collective-permute-start(bf16[96,1536]{1,0:T(8,128)(2,1)S(1)} %collective-permute-done.10.rest_5_), channel_id=1, source_target_pairs={{0,4},{1,5},{2,6},{3,7},{4,8},{5,9},{6,10},{7,11},{8,12},{9,13},{1... | collective-permute-start | bytes 884744 | tf_op jit(solution)/shard_map/ppermute | solution.py:346
  84.8 1.8 %collective-permute-start.13 = (bf16[96,1536]{1,0:T(8,128)(2,1)S(1)}, bf16[96,1536]{1,0:T(8,128)(2,1)}, u32[]{:S(2)}, u32[]{:S(2)}) collective-permute-start(bf16[96,1536]{1,0:T(8,128)(2,1)S(1)} %collective-permute-done.5.rest_1_), channel_id=1, source_target_pairs={{0,1},{1,0},{2,3},{3,2},{4,5},{5,4},{6,7},{7,6},{8,9},{9,8},{10,11... | collective-permute-start | bytes 884744 | tf_op jit(solution)/shard_map/ppermute | solution.py:350
  87.3 4.1 %shard_map.130.action = f32[16,1536]{1,0:T(8,128)} custom-call(s32[16,7]{1,0:T(8,128)} %copy.14.actions, bf16[7,256,1536]{2,1,0:T(8,128)(2,1)} %table.1), custom_call_target="tpu_custom_call" | custom-call | tf_op jit(solution)/shard_map/pallas_call | solution.py:299
  92.0 1.0 collective-permute-done.11.rest_6_
  93.0 2.7 %collective-permute-start.17 = (bf16[96,1536]{1,0:T(8,128)(2,1)S(1)}, bf16[96,1536]{1,0:T(8,128)(2,1)}, u32[]{:S(2)}, u32[]{:S(2)}) collective-permute-start(bf16[96,1536]{1,0:T(8,128)(2,1)S(1)} %collective-permute-done.10.rest_5_), channel_id=1, source_target_pairs={{0,1},{1,0},{2,3},{3,2},{4,5},{5,4},{6,7},{7,6},{8,9},{9,8},{10,11... | collective-permute-start | bytes 884744 | tf_op jit(solution)/shard_map/ppermute | solution.py:350
  96.3 0.8 collective-permute-done.17.rest_13_
  98.8 9.7 %shard_map.131 = (bf16[128,768]{1,0:T(8,128)(2,1)}, f32[128,1536]{1,0:T(8,128)}, bf16[128,1536]{1,0:T(8,128)(2,1)}, bf16[128,1536]{1,0:T(8,128)(2,1)}, bf16[1536,1536]{1,0:T(8,128)(2,1)}) custom-call(s32[1]{0:T(128)} %bitcast.me, s32[1]{0:T(128)} %bitcast.2.z, bf16[64,2304]{1,0:T(8,128)(2,1)} %get-tuple-element.63.q0, bf16[64,2304]{1,0:T(8,128)(2,1)} %copy-done.5, ...), custom_call_target="tpu_custom_call" | custom-call | tf_op jit(solution)/shard_map/pallas_call | solution.py:299
  108.7 1.4 copy-done
  110.1 2.9 %shard_map.134 = bf16[16,12,768]{2,1,0:T(8,128)(2,1)} custom-call(bf16[8,192,768]{2,1,0:T(8,128)(2,1)} %copy-done), custom_call_target="tpu_custom_call" | custom-call | tf_op jit(solution)/shard_map/pallas_call | solution.py:299
  113.0 8.0 %all-to-all-start.2 = ((bf16[16,12,768]{2,1,0:T(8,128)(2,1)}), bf16[16,12,768]{2,1,0:T(8,128)(2,1)S(1)}, u32[]{:S(2)}, u32[]{:S(2)}) async-start(bf16[16,12,768]{2,1,0:T(8,128)(2,1)} %shard_map.134), calls=%async_computation.2 | async-start | bytes 786432 | tf_op jit(solution)/shard_map/all_to_all | solution.py:415
  121.0 2.2 %collective-permute-start.23 = (bf16[128,1536]{1,0:T(8,128)(2,1)S(1)}, bf16[128,1536]{1,0:T(8,128)(2,1)S(1)}, u32[]{:S(2)}, u32[]{:S(2)}) collective-permute-start(bf16[128,1536]{1,0:T(8,128)(2,1)S(1)} %copy-done.28), channel_id=1, source_target_pairs={{4,0},{5,1},{6,2},{7,3},{8,4},{9,5},{10,6},{11,7},{12,8},{13,9},{1... | collective-permute-start | bytes 1179656 | tf_op jit(solution)/shard_map/ppermute | solution.py:417
  123.2 2.2 %collective-permute-start.22 = (bf16[128,1536]{1,0:T(8,128)(2,1)S(1)}, bf16[128,1536]{1,0:T(8,128)(2,1)S(1)}, u32[]{:S(2)}, u32[]{:S(2)}) collective-permute-start(bf16[128,1536]{1,0:T(8,128)(2,1)S(1)} %copy-done.27), channel_id=1, source_target_pairs={{2,0},{3,1},{4,2},{5,3},{6,4},{7,5},{8,6},{9,7},{10,8},{11,9},{12,... | collective-permute-start | bytes 1179656 | tf_op jit(solution)/shard_map/ppermute | solution.py:416
  125.4 5.3 %shard_map.135 = (bf16[16,3072]{1,0:T(8,128)(2,1)}, bf16[16,3072]{1,0:T(8,128)(2,1)}, bf16[16,3072]{1,0:T(8,128)(2,1)}, bf16[16,3072]{1,0:T(8,128)(2,1)}, bf16[1...) custom-call(s32[1]{0:T(128)} %bitcast.1.cam, ...), custom_call_target="tpu_custom_call" | custom-call | tf_op jit(solution)/shard_map/pallas_call | solution.py:299
  131.1 0.7 collective-permute-start.25
  131.8 1.5 collective-permute-start.26
  133.3 7.4 %collective-permute-done.23.far = bf16[128,1536]{1,0:T(8,128)(2,1)S(1)} collective-permute-done((bf16[128,1536]{1,0:T(8,128)(2,1)S(1)}, bf16[128,1536]{1,0:T(8,128)(2,1)S(1)}, u32[]{:S(2)}, u32[]{:S(2)}) %collective-permute-start.23) | collective-permute-done | bytes 393248 | tf_op jit(solution)/shard_map/ppermute | solution.py:417
  141.1 8.2 %collective-permute-done.22.near = bf16[128,1536]{1,0:T(8,128)(2,1)S(1)} collective-permute-done((bf16[128,1536]{1,0:T(8,128)(2,1)S(1)}, bf16[128,1536]{1,0:T(8,128)(2,1)S(1)}, u32[]{:S(2)}, u32[]{:S(2)}) %collective-permute-start.22) | collective-permute-done | bytes 393248 | tf_op jit(solution)/shard_map/ppermute | solution.py:416
  149.3 1.3 collective-permute-start.32
  150.7 1.5 collective-permute-start.28
  152.1 2.5 %collective-permute-start.29 = (bf16[16,3072]{1,0:T(8,128)(2,1)}, bf16[16,3072]{1,0:T(8,128)(2,1)S(1)}, u32[]{:S(2)}, u32[]{:S(2)}) collective-permute-start(bf16[16,3072]{1,0:T(8,128)(2,1)} %get-tuple-element.113), channel_id=1, source_target_pairs={{0,160},{32,128},{64,224},{96,192},{128,32},{160,0},{192,96},{224,... | collective-permute-start | bytes 294920 | tf_op jit(solution)/shard_map/ppermute | solution.py:427
  154.6 1.1 collective-permute-start.30
  155.7 1.5 collective-permute-start.31
  157.2 2.5 %shard_map.136 = (bf16[64,3072]{1,0:T(8,128)(2,1)}, bf16[64,3072]{1,0:T(8,128)(2,1)}) custom-call(bf16[128,1536]{1,0:T(8,128)(2,1)} %get-tuple-element.87.own_time.kept, bf16[128,768]{1,0:T(8,128)(2,1)} %get-tuple-element.88.dq, f32[128,1536]{1,0:T(8,128)} %get-tuple-element.89.own, bf16[128,1536]{1,0:T(8,128)(2,1)} %copy-done.8, bf16[128,1536]{1,0:T(8,128)(2,1)} %copy-done.7), custom_call_target="tpu_custom_call" | custom-call | tf_op jit(solution)/shard_map/pallas_call | solution.py:299
  159.8 1.2 collective-permute-start.27
  161.7 2.7 %collective-permute-done.31.rest_7_ = bf16[16,3072]{1,0:T(8,128)(2,1)S(1)} collective-permute-done((bf16[16,3072]{1,0:T(8,128)(2,1)}, bf16[16,3072]{1,0:T(8,128)(2,1)S(1)}, u32[]{:S(2)}, u32[]{:S(2)}) %collective-permute-start.31) | collective-permute-done | bytes 98336 | tf_op jit(solution)/shard_map/ppermute | solution.py:427
  165.2 4.9 %shard_map.137 = (bf16[128,1536]{1,0:T(8,128)(2,1)}, bf16[128,1536]{1,0:T(8,128)(2,1)}, bf16[128,1536]{1,0:T(8,128)(2,1)}, bf16[128,1536]{1,0:T(8,128)(2,1)}) custom-call(s32[1]{0:T(128)} %bitcast.me, s32[1]{0:T(128)} %bitcast.1.cam, bf16[1536,1536]{1,0:T(8,128)(2,1)} %get-tuple-element.85.w, f32[16,1536]{1,0:T(8,128)} %shard_map.130.action, ...), custom_call_target="tpu_custom_call" | custom-call | tf_op jit(solution)/shard_map/pallas_call | solution.py:299
  (99 shorter events, 6.3 us)
Async XLA Ops:
  0.6 11.0 %copy-start.18 = (bf16[48,1536]{1,0:T(8,128)(2,1)S(1)}, bf16[48,1536]{1,0:T(8,128)(2,1)}, u32[]{:S(2)}) copy-start(bf16[48,1536]{1,0:T(8,128)(2,1)} %param.16) | copy-start | bytes 442372
  0.6 5.0 %collective-permute-start.2 = (bf16[48,1536]{1,0:T(8,128)(2,1)}, bf16[48,1536]{1,0:T(8,128)(2,1)S(1)}, u32[]{:S(2)}, u32[]{:S(2)}) collective-permute-start(bf16[48,1536]{1,0:T(8,128)(2,1)} %param.16), channel_id=1, source_target_pairs={{0,34},{1,35},{2,32},{3,33},{4,38},{5,39},{6,36},{7,37},{8,42},{9,... | collective-permute-start | bytes 442376 | tf_op jit(solution)/shard_map/ppermute | solution.py:329
  4.6 7.0 %collective-permute-start.1 = (bf16[64,1536]{1,0:T(8,128)(2,1)}, bf16[64,1536]{1,0:T(8,128)(2,1)S(1)}, u32[]{:S(2)}, u32[]{:S(2)}) collective-permute-start(bf16[64,1536]{1,0:T(8,128)(2,1)} %get-tuple-element.66), channel_id=1, source_target_pairs={{0,1},{1,0},{2,3},{3,2},{4,5},{5,4},{6,7},{7,6},{8,9},{9,8},{10,11... | collective-permute-start | bytes 589832 | tf_op jit(solution)/shard_map/ppermute | solution.py:356
  5.7 50.6 %all-to-all-start = ((bf16[8,16,3968]{2,1,0:T(8,128)(2,1)}), bf16[8,16,3968]{2,1,0:T(8,128)(2,1)S(1)}, u32[]{:S(2)}, u32[]{:S(2)}) async-start(bf16[8,16,3968]{2,1,0:T(8,128)(2,1)} %bitcast.18), calls=%async_computation | async-start | bytes 2031616 | tf_op jit(solution)/shard_map/all_to_all | solution.py:341
  11.6 57.2 %copy-start.6 = (bf16[96,1536]{1,0:T(8,128)(2,1)}, bf16[96,1536]{1,0:T(8,128)(2,1)S(1)}, u32[]{:S(2)}) copy-start(bf16[96,1536]{1,0:T(8,128)(2,1)S(1)} %pad_maximum_fusion.1.rest_0_) | copy-start | bytes 884740
  11.7 37.9 %copy-start.2 = (bf16[128,1536]{1,0:T(8,128)(2,1)}, bf16[128,1536]{1,0:T(8,128)(2,1)S(1)}, u32[]{:S(2)}) copy-start(bf16[128,1536]{1,0:T(8,128)(2,1)S(1)} %pad_maximum_fusion.own) | copy-start | bytes 1179652
  11.7 33.2 %collective-permute-start.3 = (bf16[128,1536]{1,0:T(8,128)(2,1)S(1)}, bf16[128,1536]{1,0:T(8,128)(2,1)S(1)}, u32[]{:S(2)}, u32[]{:S(2)}) collective-permute-start(bf16[128,1536]{1,0:T(8,128)(2,1)S(1)} %pad_maximum_fusion.own), channel_id=1, source_target_pairs={{0,2},{1,3},{2,4},{3,5},{4,6},{5,7},{6,8},{7,9},{8,10},{9,11},{10,... | collective-permute-start | bytes 1179656 | tf_op jit(solution)/shard_map/ppermute | solution.py:360
  16.9 28.1 %collective-permute-start.4 = (bf16[128,1536]{1,0:T(8,128)(2,1)S(1)}, bf16[128,1536]{1,0:T(8,128)(2,1)S(1)}, u32[]{:S(2)}, u32[]{:S(2)}) collective-permute-start(bf16[128,1536]{1,0:T(8,128)(2,1)S(1)} %pad_maximum_fusion.own), channel_id=1, source_target_pairs={{0,4},{1,5},{2,6},{3,7},{4,8},{5,9},{6,10},{7,11},{8,12},{9,13},{1... | collective-permute-start | bytes 1179656 | tf_op jit(solution)/shard_map/ppermute | solution.py:361
  19.5 25.4 %collective-permute-start.5 = (bf16[96,1536]{1,0:T(8,128)(2,1)S(1)}, bf16[96,1536]{1,0:T(8,128)(2,1)S(1)}, u32[]{:S(2)}, u32[]{:S(2)}) collective-permute-start(bf16[96,1536]{1,0:T(8,128)(2,1)S(1)} %pad_maximum_fusion.1.rest_0_), channel_id=1, source_target_pairs={{0,4},{1,5},{2,6},{3,7},{4,8},{5,9},{6,10},{7,11},{8,12},{9,13},{1... | collective-permute-start | bytes 884744 | tf_op jit(solution)/shard_map/ppermute | solution.py:346
  20.4 24.6 %collective-permute-start.6 = (bf16[96,1536]{1,0:T(8,128)(2,1)S(1)}, bf16[96,1536]{1,0:T(8,128)(2,1)S(1)}, u32[]{:S(2)}, u32[]{:S(2)}) collective-permute-start(bf16[96,1536]{1,0:T(8,128)(2,1)S(1)} %pad_maximum_fusion.1.rest_0_), channel_id=1, source_target_pairs={{0,28},{1,29},{2,30},{3,31},{4,0},{5,1},{6,2},{7,3},{8,4},{9,5},{1... | collective-permute-start | bytes 884744 | tf_op jit(solution)/shard_map/ppermute | solution.py:346
  21.1 28.5 %collective-permute-start = (bf16[64,2304]{1,0:T(8,128)(2,1)}, bf16[64,2304]{1,0:T(8,128)(2,1)S(1)}, u32[]{:S(2)}, u32[]{:S(2)}) collective-permute-start(bf16[64,2304]{1,0:T(8,128)(2,1)} %get-tuple-element.64), channel_id=1, source_target_pairs={{0,1},{1,0},{2,3},{3,2},{4,5},{5,4},{6,7},{7,6},{8,9},{9,8},{10,11... | collective-permute-start | bytes 884744 | tf_op jit(solution)/shard_map/ppermute | solution.py:357
  45.0 46.4 %copy-start.12 = (bf16[96,1536]{1,0:T(8,128)(2,1)}, bf16[96,1536]{1,0:T(8,128)(2,1)S(1)}, u32[]{:S(2)}) copy-start(bf16[96,1536]{1,0:T(8,128)(2,1)S(1)} %collective-permute-done.5.rest_1_) | copy-start | bytes 884740
  45.0 46.4 %copy-start.13 = (bf16[96,1536]{1,0:T(8,128)(2,1)}, bf16[96,1536]{1,0:T(8,128)(2,1)S(1)}, u32[]{:S(2)}) copy-start(bf16[96,1536]{1,0:T(8,128)(2,1)S(1)} %collective-permute-done.6.rest_2_) | copy-start | bytes 884740
  45.0 11.2 %collective-permute-start.7 = (bf16[96,1536]{1,0:T(8,128)(2,1)S(1)}, bf16[96,1536]{1,0:T(8,128)(2,1)}, u32[]{:S(2)}, u32[]{:S(2)}) collective-permute-start(bf16[96,1536]{1,0:T(8,128)(2,1)S(1)} %collective-permute-done.5.rest_1_), channel_id=1, source_target_pairs={{0,4},{1,5},{2,6},{3,7},{4,8},{5,9},{6,10},{7,11},{8,12},{9,13},{1... | collective-permute-start | bytes 884744 | tf_op jit(solution)/shard_map/ppermute | solution.py:346
  48.0 8.2 %collective-permute-start.8 = (bf16[96,1536]{1,0:T(8,128)(2,1)S(1)}, bf16[96,1536]{1,0:T(8,128)(2,1)}, u32[]{:S(2)}, u32[]{:S(2)}) collective-permute-start(bf16[96,1536]{1,0:T(8,128)(2,1)S(1)} %collective-permute-done.6.rest_2_), channel_id=1, source_target_pairs={{0,28},{1,29},{2,30},{3,31},{4,0},{5,1},{6,2},{7,3},{8,4},{9,5},{1... | collective-permute-start | bytes 884744 | tf_op jit(solution)/shard_map/ppermute | solution.py:346
  48.0 8.2 %collective-permute-start.9 = (bf16[96,1536]{1,0:T(8,128)(2,1)S(1)}, bf16[96,1536]{1,0:T(8,128)(2,1)}, u32[]{:S(2)}, u32[]{:S(2)}) collective-permute-start(bf16[96,1536]{1,0:T(8,128)(2,1)S(1)} %pad_maximum_fusion.1.rest_0_), channel_id=1, source_target_pairs={{0,1},{1,0},{2,3},{3,2},{4,5},{5,4},{6,7},{7,6},{8,9},{9,8},{10,11... | collective-permute-start | bytes 884744 | tf_op jit(solution)/shard_map/ppermute | solution.py:350
  56.2 6.7 %collective-permute-start.21 = (bf16[128,1536]{1,0:T(8,128)(2,1)}, bf16[128,1536]{1,0:T(8,128)(2,1)S(1)}, u32[]{:S(2)}, u32[]{:S(2)}) collective-permute-start(bf16[128,1536]{1,0:T(8,128)(2,1)} %get-tuple-element.93), channel_id=1, source_target_pairs={{0,1},{1,0},{2,3},{3,2},{4,5},{5,4},{6,7},{7,6},{8,9},{9,8},{10,11... | collective-permute-start | bytes 1179656 | tf_op jit(solution)/shard_map/ppermute | solution.py:387
  60.4 4.0 %collective-permute-start.20 = (bf16[128,1536]{1,0:T(8,128)(2,1)}, bf16[128,1536]{1,0:T(8,128)(2,1)S(1)}, u32[]{:S(2)}, u32[]{:S(2)}) collective-permute-start(bf16[128,1536]{1,0:T(8,128)(2,1)} %get-tuple-element.92), channel_id=1, source_target_pairs={{0,1},{1,0},{2,3},{3,2},{4,5},{5,4},{6,7},{7,6},{8,9},{9,8},{10,11... | collective-permute-start | bytes 1179656 | tf_op jit(solution)/shard_map/ppermute | solution.py:386
  68.8 17.8 %copy-start.26 = (s32[16,7]{0,1:T(8,128)S(1)}, s32[16,7]{0,1:T(8,128)}, u32[]{:S(2)}) copy-start(s32[16,7]{0,1:T(8,128)} %param.14) | copy-start | bytes 1348
  68.8 39.8 %all-to-all-start.1 = ((bf16[8,192,768]{2,1,0:T(8,128)(2,1)}), bf16[8,192,768]{2,1,0:T(8,128)(2,1)S(1)}, u32[]{:S(2)}, u32[]{:S(2)}) async-start(bf16[8,192,768]{2,1,0:T(8,128)(2,1)} %bitcast.15), calls=%async_computation.1 | async-start | bytes 4718592 | tf_op jit(solution)/shard_map/all_to_all | solution.py:395
  74.2 8.1 %collective-permute-start.10 = (bf16[96,1536]{1,0:T(8,128)(2,1)}, bf16[96,1536]{1,0:T(8,128)(2,1)S(1)}, u32[]{:S(2)}, u32[]{:S(2)}) collective-permute-start(bf16[96,1536]{1,0:T(8,128)(2,1)} %collective-permute-done.7.rest_3_), channel_id=1, source_target_pairs={{0,4},{1,5},{2,6},{3,7},{4,8},{5,9},{6,10},{7,11},{8,12},{9,13},{1... | collective-permute-start | bytes 884744 | tf_op jit(solution)/shard_map/ppermute | solution.py:346
  82.3 9.6 %collective-permute-start.12 = (bf16[96,1536]{1,0:T(8,128)(2,1)S(1)}, bf16[96,1536]{1,0:T(8,128)(2,1)}, u32[]{:S(2)}, u32[]{:S(2)}) collective-permute-start(bf16[96,1536]{1,0:T(8,128)(2,1)S(1)} %collective-permute-done.10.rest_5_), channel_id=1, source_target_pairs={{0,4},{1,5},{2,6},{3,7},{4,8},{5,9},{6,10},{7,11},{8,12},{9,13},{1... | collective-permute-start | bytes 884744 | tf_op jit(solution)/shard_map/ppermute | solution.py:346
  84.8 8.2 %collective-permute-start.11 = (bf16[96,1536]{1,0:T(8,128)(2,1)}, bf16[96,1536]{1,0:T(8,128)(2,1)}, u32[]{:S(2)}, u32[]{:S(2)}) collective-permute-start(bf16[96,1536]{1,0:T(8,128)(2,1)} %collective-permute-done.8.rest_4_), channel_id=1, source_target_pairs={{0,28},{1,29},{2,30},{3,31},{4,0},{5,1},{6,2},{7,3},{8,4},{9,5},{1... | collective-permute-start | bytes 884744 | tf_op jit(solution)/shard_map/ppermute | solution.py:346
  84.8 11.0 %collective-permute-start.13 = (bf16[96,1536]{1,0:T(8,128)(2,1)S(1)}, bf16[96,1536]{1,0:T(8,128)(2,1)}, u32[]{:S(2)}, u32[]{:S(2)}) collective-permute-start(bf16[96,1536]{1,0:T(8,128)(2,1)S(1)} %collective-permute-done.5.rest_1_), channel_id=1, source_target_pairs={{0,1},{1,0},{2,3},{3,2},{4,5},{5,4},{6,7},{7,6},{8,9},{9,8},{10,11... | collective-permute-start | bytes 884744 | tf_op jit(solution)/shard_map/ppermute | solution.py:350
  86.6 9.2 %collective-permute-start.14 = (bf16[96,1536]{1,0:T(8,128)(2,1)S(1)}, bf16[96,1536]{1,0:T(8,128)(2,1)}, u32[]{:S(2)}, u32[]{:S(2)}) collective-permute-start(bf16[96,1536]{1,0:T(8,128)(2,1)S(1)} %collective-permute-done.6.rest_2_), channel_id=1, source_target_pairs={{0,1},{1,0},{2,3},{3,2},{4,5},{5,4},{6,7},{7,6},{8,9},{9,8},{10,11... | collective-permute-start | bytes 884744 | tf_op jit(solution)/shard_map/ppermute | solution.py:350
  91.4 4.9 %collective-permute-start.15 = (bf16[96,1536]{1,0:T(8,128)(2,1)}, bf16[96,1536]{1,0:T(8,128)(2,1)}, u32[]{:S(2)}, u32[]{:S(2)}) collective-permute-start(bf16[96,1536]{1,0:T(8,128)(2,1)} %collective-permute-done.7.rest_3_), channel_id=1, source_target_pairs={{0,1},{1,0},{2,3},{3,2},{4,5},{5,4},{6,7},{7,6},{8,9},{9,8},{10,11... | collective-permute-start | bytes 884744 | tf_op jit(solution)/shard_map/ppermute | solution.py:350
  91.9 4.4 %collective-permute-start.16 = (bf16[96,1536]{1,0:T(8,128)(2,1)}, bf16[96,1536]{1,0:T(8,128)(2,1)}, u32[]{:S(2)}, u32[]{:S(2)}) collective-permute-start(bf16[96,1536]{1,0:T(8,128)(2,1)} %collective-permute-done.8.rest_4_), channel_id=1, source_target_pairs={{0,1},{1,0},{2,3},{3,2},{4,5},{5,4},{6,7},{7,6},{8,9},{9,8},{10,11... | collective-permute-start | bytes 884744 | tf_op jit(solution)/shard_map/ppermute | solution.py:350
  93.0 4.1 %collective-permute-start.17 = (bf16[96,1536]{1,0:T(8,128)(2,1)S(1)}, bf16[96,1536]{1,0:T(8,128)(2,1)}, u32[]{:S(2)}, u32[]{:S(2)}) collective-permute-start(bf16[96,1536]{1,0:T(8,128)(2,1)S(1)} %collective-permute-done.10.rest_5_), channel_id=1, source_target_pairs={{0,1},{1,0},{2,3},{3,2},{4,5},{5,4},{6,7},{7,6},{8,9},{9,8},{10,11... | collective-permute-start | bytes 884744 | tf_op jit(solution)/shard_map/ppermute | solution.py:350
  95.8 1.8 %collective-permute-start.18 = (bf16[96,1536]{1,0:T(8,128)(2,1)}, bf16[96,1536]{1,0:T(8,128)(2,1)S(1)}, u32[]{:S(2)}, u32[]{:S(2)}) collective-permute-start(bf16[96,1536]{1,0:T(8,128)(2,1)} %collective-permute-done.11.rest_6_), channel_id=1, source_target_pairs={{0,1},{1,0},{2,3},{3,2},{4,5},{5,4},{6,7},{7,6},{8,9},{9,8},{10,11... | collective-permute-start | bytes 884744 | tf_op jit(solution)/shard_map/ppermute | solution.py:350
  95.9 2.2 %collective-permute-start.19 = (bf16[96,1536]{1,0:T(8,128)(2,1)}, bf16[96,1536]{1,0:T(8,128)(2,1)S(1)}, u32[]{:S(2)}, u32[]{:S(2)}) collective-permute-start(bf16[96,1536]{1,0:T(8,128)(2,1)} %collective-permute-done.12.rest_7_), channel_id=1, source_target_pairs={{0,1},{1,0},{2,3},{3,2},{4,5},{5,4},{6,7},{7,6},{8,9},{9,8},{10,11... | collective-permute-start | bytes 884744 | tf_op jit(solution)/shard_map/ppermute | solution.py:350
  108.4 12.5 %copy-start.28 = (bf16[128,1536]{1,0:T(8,128)(2,1)S(1)}, bf16[128,1536]{1,0:T(8,128)(2,1)}, u32[]{:S(2)}) copy-start(bf16[128,1536]{1,0:T(8,128)(2,1)} %get-tuple-element.98) | copy-start | bytes 1179652
  108.4 14.7 %copy-start.27 = (bf16[128,1536]{1,0:T(8,128)(2,1)S(1)}, bf16[128,1536]{1,0:T(8,128)(2,1)}, u32[]{:S(2)}) copy-start(bf16[128,1536]{1,0:T(8,128)(2,1)} %get-tuple-element.97) | copy-start | bytes 1179652
  113.0 36.2 %all-to-all-start.2 = ((bf16[16,12,768]{2,1,0:T(8,128)(2,1)}), bf16[16,12,768]{2,1,0:T(8,128)(2,1)S(1)}, u32[]{:S(2)}, u32[]{:S(2)}) async-start(bf16[16,12,768]{2,1,0:T(8,128)(2,1)} %shard_map.134), calls=%async_computation.2 | async-start | bytes 786432 | tf_op jit(solution)/shard_map/all_to_all | solution.py:415
  121.0 19.8 %collective-permute-start.23 = (bf16[128,1536]{1,0:T(8,128)(2,1)S(1)}, bf16[128,1536]{1,0:T(8,128)(2,1)S(1)}, u32[]{:S(2)}, u32[]{:S(2)}) collective-permute-start(bf16[128,1536]{1,0:T(8,128)(2,1)S(1)} %copy-done.28), channel_id=1, source_target_pairs={{4,0},{5,1},{6,2},{7,3},{8,4},{9,5},{10,6},{11,7},{12,8},{13,9},{1... | collective-permute-start | bytes 1179656 | tf_op jit(solution)/shard_map/ppermute | solution.py:417
  123.2 26.0 %collective-permute-start.22 = (bf16[128,1536]{1,0:T(8,128)(2,1)S(1)}, bf16[128,1536]{1,0:T(8,128)(2,1)S(1)}, u32[]{:S(2)}, u32[]{:S(2)}) collective-permute-start(bf16[128,1536]{1,0:T(8,128)(2,1)S(1)} %copy-done.27), channel_id=1, source_target_pairs={{2,0},{3,1},{4,2},{5,3},{6,4},{7,5},{8,6},{9,7},{10,8},{11,9},{12,... | collective-permute-start | bytes 1179656 | tf_op jit(solution)/shard_map/ppermute | solution.py:416
  130.7 10.3 %collective-permute-start.24 = (bf16[16,3072]{1,0:T(8,128)(2,1)}, bf16[16,3072]{1,0:T(8,128)(2,1)S(1)}, u32[]{:S(2)}, u32[]{:S(2)}) collective-permute-start(bf16[16,3072]{1,0:T(8,128)(2,1)} %get-tuple-element.101), channel_id=1, source_target_pairs={{0,32},{32,0},{64,96},{96,64},{128,160},{160,128},{192,224},{224,1... | collective-permute-start | bytes 294920 | tf_op jit(solution)/shard_map/ppermute | solution.py:427
  131.1 10.0 %collective-permute-start.25 = (bf16[16,3072]{1,0:T(8,128)(2,1)}, bf16[16,3072]{1,0:T(8,128)(2,1)S(1)}, u32[]{:S(2)}, u32[]{:S(2)}) collective-permute-start(bf16[16,3072]{1,0:T(8,128)(2,1)} %get-tuple-element.102), channel_id=1, source_target_pairs={{0,64},{32,96},{64,0},{96,32},{128,192},{160,224},{192,128},{224,1... | collective-permute-start | bytes 294920 | tf_op jit(solution)/shard_map/ppermute | solution.py:427
  131.8 9.2 %collective-permute-start.26 = (bf16[16,3072]{1,0:T(8,128)(2,1)}, bf16[16,3072]{1,0:T(8,128)(2,1)S(1)}, u32[]{:S(2)}, u32[]{:S(2)}) collective-permute-start(bf16[16,3072]{1,0:T(8,128)(2,1)} %get-tuple-element.103), channel_id=1, source_target_pairs={{0,96},{32,64},{64,32},{96,0},{128,224},{160,192},{192,160},{224,1... | collective-permute-start | bytes 294920 | tf_op jit(solution)/shard_map/ppermute | solution.py:427
  140.8 16.4 %copy-start.7 = (bf16[128,1536]{1,0:T(8,128)(2,1)}, bf16[128,1536]{1,0:T(8,128)(2,1)S(1)}, u32[]{:S(2)}) copy-start(bf16[128,1536]{1,0:T(8,128)(2,1)S(1)} %collective-permute-done.23.far) | copy-start | bytes 1179652
  141.0 23.3 %copy-start.19 = (bf16[16,3072]{1,0:T(8,128)(2,1)}, bf16[16,3072]{1,0:T(8,128)(2,1)S(1)}, u32[]{:S(2)}) copy-start(bf16[16,3072]{1,0:T(8,128)(2,1)S(1)} %collective-permute-done.24.rest_1_) | copy-start | bytes 294916
  141.0 23.3 %copy-start.20 = (bf16[16,3072]{1,0:T(8,128)(2,1)}, bf16[16,3072]{1,0:T(8,128)(2,1)S(1)}, u32[]{:S(2)}) copy-start(bf16[16,3072]{1,0:T(8,128)(2,1)S(1)} %collective-permute-done.25.rest_2_) | copy-start | bytes 294916
  141.0 23.3 %copy-start.21 = (bf16[16,3072]{1,0:T(8,128)(2,1)}, bf16[16,3072]{1,0:T(8,128)(2,1)S(1)}, u32[]{:S(2)}) copy-start(bf16[16,3072]{1,0:T(8,128)(2,1)S(1)} %collective-permute-done.26.rest_3_) | copy-start | bytes 294916
  149.3 10.5 %collective-permute-start.32 = (f32[6,768]{1,0:T(8,128)S(1)}, f32[6,768]{1,0:T(8,128)S(1)}, u32[]{:S(2)}, u32[]{:S(2)}) collective-permute-start(f32[6,768]{1,0:T(8,128)S(1)} %constant_dynamic-slice_fusion), channel_id=1, source_target_pairs={{0,1},{1,0},{2,3},{3,2},{4,5},{5,4},{6,7},{7,6},{8,9},{9,8},{10,11... | collective-permute-start | bytes 55304 | tf_op jit(solution)/shard_map/ppermute | solution.py:436
  150.7 11.0 %collective-permute-start.28 = (bf16[16,3072]{1,0:T(8,128)(2,1)}, bf16[16,3072]{1,0:T(8,128)(2,1)S(1)}, u32[]{:S(2)}, u32[]{:S(2)}) collective-permute-start(bf16[16,3072]{1,0:T(8,128)(2,1)} %get-tuple-element.112), channel_id=1, source_target_pairs={{0,128},{32,160},{64,192},{96,224},{128,0},{160,32},{192,64},{224,... | collective-permute-start | bytes 294920 | tf_op jit(solution)/shard_map/ppermute | solution.py:427
  152.1 9.5 %collective-permute-start.29 = (bf16[16,3072]{1,0:T(8,128)(2,1)}, bf16[16,3072]{1,0:T(8,128)(2,1)S(1)}, u32[]{:S(2)}, u32[]{:S(2)}) collective-permute-start(bf16[16,3072]{1,0:T(8,128)(2,1)} %get-tuple-element.113), channel_id=1, source_target_pairs={{0,160},{32,128},{64,224},{96,192},{128,32},{160,0},{192,96},{224,... | collective-permute-start | bytes 294920 | tf_op jit(solution)/shard_map/ppermute | solution.py:427
  154.6 7.1 %collective-permute-start.30 = (bf16[16,3072]{1,0:T(8,128)(2,1)}, bf16[16,3072]{1,0:T(8,128)(2,1)S(1)}, u32[]{:S(2)}, u32[]{:S(2)}) collective-permute-start(bf16[16,3072]{1,0:T(8,128)(2,1)} %get-tuple-element.114), channel_id=1, source_target_pairs={{0,192},{32,224},{64,128},{96,160},{128,64},{160,96},{192,0},{224,... | collective-permute-start | bytes 294920 | tf_op jit(solution)/shard_map/ppermute | solution.py:427
  155.7 8.7 %collective-permute-start.31 = (bf16[16,3072]{1,0:T(8,128)(2,1)}, bf16[16,3072]{1,0:T(8,128)(2,1)S(1)}, u32[]{:S(2)}, u32[]{:S(2)}) collective-permute-start(bf16[16,3072]{1,0:T(8,128)(2,1)} %get-tuple-element.115), channel_id=1, source_target_pairs={{0,224},{32,192},{64,160},{96,128},{128,96},{160,64},{192,32},{224... | collective-permute-start | bytes 294920 | tf_op jit(solution)/shard_map/ppermute | solution.py:427
  159.8 4.6 %collective-permute-start.27 = (bf16[64,3072]{1,0:T(8,128)(2,1)}, bf16[64,3072]{1,0:T(8,128)(2,1)S(1)}, u32[]{:S(2)}, u32[]{:S(2)}) collective-permute-start(bf16[64,3072]{1,0:T(8,128)(2,1)} %get-tuple-element.107), channel_id=1, source_target_pairs={{0,1},{1,0},{2,3},{3,2},{4,5},{5,4},{6,7},{7,6},{8,9},{9,8},{10,11... | collective-permute-start | bytes 1179656 | tf_op jit(solution)/shard_map/ppermute | solution.py:444
  (17 other events, 51.8 us)

commit v8 on v6

--- a/solution.py
+++ b/solution.py
@@ -381,6 +381,7 @@
     )
 
     pass_on(7, depth)
+    w_own[-1], action_sum = lax.optimization_barrier((w_own[-1], action_sum))
     swap_blocks(depth)
     view_swap = lax.ppermute(view_swap, "tm", swap)
     time_swap = lax.ppermute(time_swap, "tm", swap)
@@ -393,7 +394,6 @@
     )
     part = lax.all_to_all(part.reshape(cams, width // cams, CW), "cam", 0, 0, tiled=True)
 
-    q0, action_sum = lax.optimization_barrier((q0, action_sum))
     dq_time, own_grad, near_grad, far_grad, w_full = call(
         functools.partial(time_backward_kernel, depth),
         [((rows, CW), BF), ((rows, 2 * CW), F32)] + [((rows, 2 * CW), BF)] * 2 + [((width, width), BF)],
@@ -413,11 +413,7 @@
         cam, view_x, kept_view, prob_view, w_full,
         scratch=[pltpu.VMEM((rows, 4 * CW), BF)],
     )
-    view_back = [view_out[0]] + [
-        lax.ppermute(view_out[d], "cam", [(i, i ^ d) for i in range(cams)]) for d in range(1, cams)
-    ]
-    part, near_grad, far_grad, view_back[1] = lax.optimization_barrier((part, near_grad, far_grad, view_back[1]))
-
+    part, view_out[0] = lax.optimization_barrier((part, view_out[0]))
     chips = tm // 2
     (part,) = call(
         camera_sum_kernel,
@@ -427,6 +423,13 @@
         scratch=[pltpu.VMEM((width // cams, CW), F32)],
     )
     part = lax.all_to_all(part, "tm", 0, 0, tiled=True, axis_index_groups=same_core)
+    view_back = [view_out[0]] + [
+        lax.ppermute(view_out[d], "cam", [(i, i ^ d) for i in range(cams)]) for d in range(1, cams)
+    ]
+
+    part, near_grad, far_grad, view_back[1:4] = lax.optimization_barrier(
+        (part, near_grad, far_grad, view_back[1:4])
+    )
     part = jnp.sum(part.astype(F32), axis=0)
     final = width // cams // tm
     mine = lax.dynamic_slice_in_dim(part, core * final, final, 0)

time: 177 us -> 178 us (level)
  starting transfers between devices: 67.3 us -> 77.7 us
  waiting for transfers between devices: 54.6 us -> 45.7 us
    all_to_all x1, starting transfers between devices: 5.74 us -> 19.4 us  [shards(): lax.all_to_all(part, 'tm', 0, 0, tiled=True, axis_index_groups=same_core)]
    all_to_all x1, waiting for transfers between devices: 6.11 us -> 0.01 us  [shards(): lax.all_to_all(part, 'tm', 0, 0, tiled=True, axis_index_groups=same_core)]
    ppermute x1, waiting for transfers between devices: 13 us -> 9.03 us  [shards(): lax.ppermute(near_grad, 'tm', [(i + 2, i) for i in range(tm - 2)])]
    ppermute x7, waiting for transfers between devices: 18.3 us -> 16 us  [pass_on(): lax.ppermute(w_own[max(i - 2, 0)], 'tm', up if i % 2 else down)]
    ppermute x8, waiting for transfers between devices: 0.02 us -> 2.06 us  [swap_blocks(): w_other.append(lax.ppermute(block_rows, 'tm', swap))]
    ppermute x8, starting transfers between devices: 9.12 us -> 7.22 us  [swap_blocks(): w_other.append(lax.ppermute(block_rows, 'tm', swap))]
    unnamed x63 -> x67, local copies, waits for them, and re-layouts: 5.41 us -> 6.08 us
  transfers between devices with their start and end apart: 36 -> 36, of which waited for: 9 -> 14; matrix products, arithmetic and copies ran while one was open for 0% -> 1% of each run, Pallas kernels for 22% -> 19%
where the time goes in v8:
time: 178 us; the launch traced here: 177 us
  starting transfers between devices  77.7 us (44%)
  Pallas kernels  45.7 us (26%)
  waiting for transfers between devices  45.7 us (26%)
  local copies, waits for them, and re-layouts  6.09 us (3%)
    pallas_call x10, Pallas kernels, call(): pl.pallas_call(kernel, out_shape=[jax.ShapeDtypeStruct(shape, kind) for s...  45.7 us
    all_to_all x1, starting transfers between devices, shards(): lax.all_to_all(part, 'tm', 0, 0, tiled=True, axis_index_groups=same_core)  19.4 us
    ppermute x7, waiting for transfers between devices, pass_on(): lax.ppermute(w_own[max(i - 2, 0)], 'tm', up if i % 2 else down)  16 us
    ppermute x7, starting transfers between devices, pass_on(): lax.ppermute(w_own[max(i - 2, 0)], 'tm', up if i % 2 else down)  12.5 us
    ppermute x7, starting transfers between devices, shards(): lax.ppermute(view_out[d], 'cam', [(i, i ^ d) for i in range(cams)])  9.28 us
    ppermute x1, waiting for transfers between devices, shards(): far_grad = lax.ppermute(far_grad, 'tm', [(i + 4, i) for i in range(tm - 4)])  9.08 us
    ppermute x1, waiting for transfers between devices, shards(): lax.ppermute(near_grad, 'tm', [(i + 2, i) for i in range(tm - 2)])  9.03 us
    ppermute x7, waiting for transfers between devices, shards(): lax.ppermute(view_out[d], 'cam', [(i, i ^ d) for i in range(cams)])  7.85 us
  transfers between devices with their start and end apart: 36, of which 14 were waited for; matrix products, arithmetic and copies ran while one was open for 1% of the time, Pallas kernels for 19%

profile of v8, /device:TPU:1, one launch (start us, length us, event | category | flops | bytes accessed | tf_op | source)
XLA Modules:
  0.0 176.9 jit_solution(16905375796590853057)
XLA Ops:
  0.6 3.7 %collective-permute-start.2 = (bf16[48,1536]{1,0:T(8,128)(2,1)}, bf16[48,1536]{1,0:T(8,128)(2,1)S(1)}, u32[]{:S(2)}, u32[]{:S(2)}) collective-permute-start(bf16[48,1536]{1,0:T(8,128)(2,1)} %param.16), channel_id=1, source_target_pairs={{0,34},{1,35},{2,32},{3,33},{4,38},{5,39},{6,36},{7,37},{8,42},{9,... | collective-permute-start | bytes 442376 | tf_op jit(solution)/shard_map/ppermute | solution.py:329
  4.3 3.7 %shard_map.128 = (bf16[128,3968]{1,0:T(8,128)(2,1)}, bf16[64,1536]{1,0:T(8,128)(2,1)}, bf16[64,1536]{1,0:T(8,128)(2,1)}, bf16[64,2304]{1,0:T(8,128)(2,1)}, bf16[64,2304]{1,0:T(8,128)(2,1)}) custom-call(s32[1]{0:T(128)} %bitcast.me, s32[1,16]{1,0:T(1,128)} %valid.1, bf16[128,1536]{1,0:T(8,128)(2,1)} %bitcast.19, bf16[128,1536]{1,0:T(8,128)(2,1)} %bitcast.20, ...), custom_call_target="tpu_custom_call" | custom-call | tf_op jit(solution)/shard_map/pallas_call | solution.py:299
  8.0 1.0 collective-permute-start.1
  9.1 4.0 %all-to-all-start = ((bf16[8,16,3968]{2,1,0:T(8,128)(2,1)}), bf16[8,16,3968]{2,1,0:T(8,128)(2,1)S(1)}, u32[]{:S(2)}, u32[]{:S(2)}) async-start(bf16[8,16,3968]{2,1,0:T(8,128)(2,1)} %bitcast.18), calls=%async_computation | async-start | bytes 2031616 | tf_op jit(solution)/shard_map/all_to_all | solution.py:341
  13.2 4.2 %collective-permute-start.3 = (bf16[128,1536]{1,0:T(8,128)(2,1)S(1)}, bf16[128,1536]{1,0:T(8,128)(2,1)S(1)}, u32[]{:S(2)}, u32[]{:S(2)}) collective-permute-start(bf16[128,1536]{1,0:T(8,128)(2,1)S(1)} %pad_maximum_fusion.own), channel_id=1, source_target_pairs={{0,2},{1,3},{2,4},{3,5},{4,6},{5,7},{6,8},{7,9},{8,10},{9,11},{10,... | collective-permute-start | bytes 1179656 | tf_op jit(solution)/shard_map/ppermute | solution.py:360
  17.4 3.5 %collective-permute-start.4 = (bf16[128,1536]{1,0:T(8,128)(2,1)S(1)}, bf16[128,1536]{1,0:T(8,128)(2,1)S(1)}, u32[]{:S(2)}, u32[]{:S(2)}) collective-permute-start(bf16[128,1536]{1,0:T(8,128)(2,1)S(1)} %pad_maximum_fusion.own), channel_id=1, source_target_pairs={{0,4},{1,5},{2,6},{3,7},{4,8},{5,9},{6,10},{7,11},{8,12},{9,13},{1... | collective-permute-start | bytes 1179656 | tf_op jit(solution)/shard_map/ppermute | solution.py:361
  21.0 1.7 collective-permute-start.5
  22.6 1.8 %collective-permute-start.6 = (bf16[96,1536]{1,0:T(8,128)(2,1)S(1)}, bf16[96,1536]{1,0:T(8,128)(2,1)S(1)}, u32[]{:S(2)}, u32[]{:S(2)}) collective-permute-start(bf16[96,1536]{1,0:T(8,128)(2,1)S(1)} %pad_maximum_fusion.1.rest_0_), channel_id=1, source_target_pairs={{0,28},{1,29},{2,30},{3,31},{4,0},{5,1},{6,2},{7,3},{8,4},{9,5},{1... | collective-permute-start | bytes 884744 | tf_op jit(solution)/shard_map/ppermute | solution.py:346
  24.4 2.4 %collective-permute-start = (bf16[64,2304]{1,0:T(8,128)(2,1)}, bf16[64,2304]{1,0:T(8,128)(2,1)S(1)}, u32[]{:S(2)}, u32[]{:S(2)}) collective-permute-start(bf16[64,2304]{1,0:T(8,128)(2,1)} %get-tuple-element.64), channel_id=1, source_target_pairs={{0,1},{1,0},{2,3},{3,2},{4,5},{5,4},{6,7},{7,6},{8,9},{9,8},{10,11... | collective-permute-start | bytes 884744 | tf_op jit(solution)/shard_map/ppermute | solution.py:357
  26.8 6.7 %collective-permute-done.5.rest_1_ = bf16[96,1536]{1,0:T(8,128)(2,1)S(1)} collective-permute-done((bf16[96,1536]{1,0:T(8,128)(2,1)S(1)}, bf16[96,1536]{1,0:T(8,128)(2,1)S(1)}, u32[]{:S(2)}, u32[]{:S(2)}) %collective-permute-start.5) | collective-permute-done | bytes 294944 | tf_op jit(solution)/shard_map/ppermute | solution.py:346
  33.6 2.3 %collective-permute-start.7 = (bf16[96,1536]{1,0:T(8,128)(2,1)S(1)}, bf16[96,1536]{1,0:T(8,128)(2,1)}, u32[]{:S(2)}, u32[]{:S(2)}) collective-permute-start(bf16[96,1536]{1,0:T(8,128)(2,1)S(1)} %collective-permute-done.5.rest_1_), channel_id=1, source_target_pairs={{0,4},{1,5},{2,6},{3,7},{4,8},{5,9},{6,10},{7,11},{8,12},{9,13},{1... | collective-permute-start | bytes 884744 | tf_op jit(solution)/shard_map/ppermute | solution.py:346
  35.9 4.0 %collective-permute-start.8 = (bf16[96,1536]{1,0:T(8,128)(2,1)S(1)}, bf16[96,1536]{1,0:T(8,128)(2,1)}, u32[]{:S(2)}, u32[]{:S(2)}) collective-permute-start(bf16[96,1536]{1,0:T(8,128)(2,1)S(1)} %collective-permute-done.6.rest_2_), channel_id=1, source_target_pairs={{0,28},{1,29},{2,30},{3,31},{4,0},{5,1},{6,2},{7,3},{8,4},{9,5},{1... | collective-permute-start | bytes 884744 | tf_op jit(solution)/shard_map/ppermute | solution.py:346
  39.9 3.3 %collective-permute-start.9 = (bf16[96,1536]{1,0:T(8,128)(2,1)S(1)}, bf16[96,1536]{1,0:T(8,128)(2,1)}, u32[]{:S(2)}, u32[]{:S(2)}) collective-permute-start(bf16[96,1536]{1,0:T(8,128)(2,1)S(1)} %pad_maximum_fusion.1.rest_0_), channel_id=1, source_target_pairs={{0,1},{1,0},{2,3},{3,2},{4,5},{5,4},{6,7},{7,6},{8,9},{9,8},{10,11... | collective-permute-start | bytes 884744 | tf_op jit(solution)/shard_map/ppermute | solution.py:350
  43.2 0.7 copy-done.5
  43.9 5.8 %shard_map.129 = (bf16[128,1536]{1,0:T(8,128)(2,1)}, bf16[128,1536]{1,0:T(8,128)(2,1)}, f32[6,256,384]{2,1,0:T(8,128)}) custom-call(s32[12]{0:T(128)} %windows.1, s32[1]{0:T(128)} %bitcast.me, s32[1]{0:T(128)} %bitcast.7.pair, bf16[64,2304]{1,0:T(8,128)(2,1)} %get-tuple-element.63.q0, bf16[64,2304]{1,0:T(8,128)(2,1)} %copy-done.5, ...), custom_call_target="tpu_custom_call" | custom-call | tf_op jit(solution)/shard_map/pallas_call | solution.py:299
  49.8 1.0 copy-done.1
  50.8 3.2 %shard_map.132 = (bf16[128,1536]{1,0:T(8,128)(2,1)}, bf16[128,1536]{1,0:T(8,128)(2,1)}, f32[6,256,128]{2,1,0:T(8,128)}) custom-call(s32[1]{0:T(128)} %bitcast.me, bf16[128,3968]{1,0:T(8,128)(2,1)} %bitcast.16), custom_call_target="tpu_custom_call" | custom-call | tf_op jit(solution)/shard_map/pallas_call | solution.py:299
  54.5 1.6 collective-permute-done.20.other_view
  56.0 0.8 copy-done.11
  56.8 3.6 %shard_map.133 = bf16[1536,768]{1,0:T(8,128)(2,1)} custom-call(bf16[128,1536]{1,0:T(8,128)(2,1)} %get-tuple-element.91.own_view.kept, bf16[128,1536]{1,0:T(8,128)(2,1)} %copy-done.11, bf16[128,1536]{1,0:T(8,128)(2,1)} %get-tuple-element.87.own_time.kept, bf16[128,1536]{1,0:T(8,128)(2,1)} %copy-done.10), custom_call_target="tpu_custom_call" | custom-call | tf_op jit(solution)/shard_map/pallas_call | solution.py:299
  60.4 4.7 %all-to-all-start.1 = ((bf16[8,192,768]{2,1,0:T(8,128)(2,1)}), bf16[8,192,768]{2,1,0:T(8,128)(2,1)S(1)}, u32[]{:S(2)}, u32[]{:S(2)}) async-start(bf16[8,192,768]{2,1,0:T(8,128)(2,1)} %bitcast.15), calls=%async_computation.1 | async-start | bytes 4718592 | tf_op jit(solution)/shard_map/all_to_all | solution.py:395
  65.1 9.3 %collective-permute-done.10.rest_5_ = bf16[96,1536]{1,0:T(8,128)(2,1)S(1)} collective-permute-done((bf16[96,1536]{1,0:T(8,128)(2,1)}, bf16[96,1536]{1,0:T(8,128)(2,1)S(1)}, u32[]{:S(2)}, u32[]{:S(2)}) %collective-permute-start.10) | collective-permute-done | bytes 294944 | tf_op jit(solution)/shard_map/ppermute | solution.py:346
  74.4 2.7 %collective-permute-start.11 = (bf16[96,1536]{1,0:T(8,128)(2,1)}, bf16[96,1536]{1,0:T(8,128)(2,1)}, u32[]{:S(2)}, u32[]{:S(2)}) collective-permute-start(bf16[96,1536]{1,0:T(8,128)(2,1)} %collective-permute-done.8.rest_4_), channel_id=1, source_target_pairs={{0,28},{1,29},{2,30},{3,31},{4,0},{5,1},{6,2},{7,3},{8,4},{9,5},{1... | collective-permute-start | bytes 884744 | tf_op jit(solution)/shard_map/ppermute | solution.py:346
  77.1 2.1 %collective-permute-start.13 = (bf16[96,1536]{1,0:T(8,128)(2,1)S(1)}, bf16[96,1536]{1,0:T(8,128)(2,1)}, u32[]{:S(2)}, u32[]{:S(2)}) collective-permute-start(bf16[96,1536]{1,0:T(8,128)(2,1)S(1)} %collective-permute-done.5.rest_1_), channel_id=1, source_target_pairs={{0,1},{1,0},{2,3},{3,2},{4,5},{5,4},{6,7},{7,6},{8,9},{9,8},{10,11... | collective-permute-start | bytes 884744 | tf_op jit(solution)/shard_map/ppermute | solution.py:350
  79.8 4.1 %shard_map.130.action = f32[16,1536]{1,0:T(8,128)} custom-call(s32[16,7]{1,0:T(8,128)} %copy.14.actions, bf16[7,256,1536]{2,1,0:T(8,128)(2,1)} %table.1), custom_call_target="tpu_custom_call" | custom-call | tf_op jit(solution)/shard_map/pallas_call | solution.py:299
  86.0 0.7 collective-permute-done.16.rest_12_
  88.5 9.6 %shard_map.131 = (bf16[128,768]{1,0:T(8,128)(2,1)}, f32[128,1536]{1,0:T(8,128)}, bf16[128,1536]{1,0:T(8,128)(2,1)}, bf16[128,1536]{1,0:T(8,128)(2,1)}, bf16[1536,1536]{1,0:T(8,128)(2,1)}) custom-call(s32[1]{0:T(128)} %bitcast.me, s32[1]{0:T(128)} %bitcast.2.z, bf16[64,2304]{1,0:T(8,128)(2,1)} %get-tuple-element.63.q0, bf16[64,2304]{1,0:T(8,128)(2,1)} %copy-done.5, ...), custom_call_target="tpu_custom_call" | custom-call | tf_op jit(solution)/shard_map/pallas_call | solution.py:299
  98.2 5.3 %shard_map.134 = (bf16[16,3072]{1,0:T(8,128)(2,1)}, bf16[16,3072]{1,0:T(8,128)(2,1)}, bf16[16,3072]{1,0:T(8,128)(2,1)}, bf16[16,3072]{1,0:T(8,128)(2,1)}, bf16[1...) custom-call(s32[1]{0:T(128)} %bitcast.1.cam, ...), custom_call_target="tpu_custom_call" | custom-call | tf_op jit(solution)/shard_map/pallas_call | solution.py:299
  103.5 1.4 copy-done
  104.9 2.9 %shard_map.135 = bf16[16,12,768]{2,1,0:T(8,128)(2,1)} custom-call(bf16[8,192,768]{2,1,0:T(8,128)(2,1)} %copy-done), custom_call_target="tpu_custom_call" | custom-call | tf_op jit(solution)/shard_map/pallas_call | solution.py:299
  107.9 19.4 %all-to-all-start.2 = ((bf16[16,12,768]{2,1,0:T(8,128)(2,1)}), bf16[16,12,768]{2,1,0:T(8,128)(2,1)S(1)}, u32[]{:S(2)}, u32[]{:S(2)}) async-start(bf16[16,12,768]{2,1,0:T(8,128)(2,1)} %shard_map.135), calls=%async_computation.2 | async-start | bytes 786432 | tf_op jit(solution)/shard_map/all_to_all | solution.py:425
  127.3 1.3 collective-permute-start.22
  128.6 1.3 collective-permute-start.23
  130.5 1.2 collective-permute-start.25
  131.7 0.9 collective-permute-start.26
  132.7 1.8 %collective-permute-done.24.rest_1_ = bf16[16,3072]{1,0:T(8,128)(2,1)S(1)} collective-permute-done((bf16[16,3072]{1,0:T(8,128)(2,1)}, bf16[16,3072]{1,0:T(8,128)(2,1)S(1)}, u32[]{:S(2)}, u32[]{:S(2)}) %collective-permute-start.24) | collective-permute-done | bytes 98336 | tf_op jit(solution)/shard_map/ppermute | solution.py:427
  134.5 3.1 %collective-permute-done.26.rest_3_ = bf16[16,3072]{1,0:T(8,128)(2,1)S(1)} collective-permute-done((bf16[16,3072]{1,0:T(8,128)(2,1)}, bf16[16,3072]{1,0:T(8,128)(2,1)S(1)}, u32[]{:S(2)}, u32[]{:S(2)}) %collective-permute-start.26) | collective-permute-done | bytes 98336 | tf_op jit(solution)/shard_map/ppermute | solution.py:427
  137.7 9.0 %collective-permute-done.22.near = bf16[128,1536]{1,0:T(8,128)(2,1)S(1)} collective-permute-done((bf16[128,1536]{1,0:T(8,128)(2,1)S(1)}, bf16[128,1536]{1,0:T(8,128)(2,1)S(1)}, u32[]{:S(2)}, u32[]{:S(2)}) %collective-permute-start.22) | collective-permute-done | bytes 393248 | tf_op jit(solution)/shard_map/ppermute | solution.py:406
  146.7 9.1 %collective-permute-done.23.far = bf16[128,1536]{1,0:T(8,128)(2,1)S(1)} collective-permute-done((bf16[128,1536]{1,0:T(8,128)(2,1)S(1)}, bf16[128,1536]{1,0:T(8,128)(2,1)S(1)}, u32[]{:S(2)}, u32[]{:S(2)}) %collective-permute-start.23) | collective-permute-done | bytes 393248 | tf_op jit(solution)/shard_map/ppermute | solution.py:407
  155.9 1.5 collective-permute-start.32
  157.4 2.5 %collective-permute-start.28 = (bf16[16,3072]{1,0:T(8,128)(2,1)S(1)}, bf16[16,3072]{1,0:T(8,128)(2,1)S(1)}, u32[]{:S(2)}, u32[]{:S(2)}) collective-permute-start(bf16[16,3072]{1,0:T(8,128)(2,1)S(1)} %copy-done.32), channel_id=1, source_target_pairs={{0,128},{32,160},{64,192},{96,224},{128,0},{160,32},{192,64},{224,... | collective-permute-start | bytes 294920 | tf_op jit(solution)/shard_map/ppermute | solution.py:427
  159.9 0.7 collective-permute-start.29
  160.7 2.1 %collective-permute-start.30 = (bf16[16,3072]{1,0:T(8,128)(2,1)S(1)}, bf16[16,3072]{1,0:T(8,128)(2,1)S(1)}, u32[]{:S(2)}, u32[]{:S(2)}) collective-permute-start(bf16[16,3072]{1,0:T(8,128)(2,1)S(1)} %copy-done.30), channel_id=1, source_target_pairs={{0,192},{32,224},{64,128},{96,160},{128,64},{160,96},{192,0},{224,... | collective-permute-start | bytes 294920 | tf_op jit(solution)/shard_map/ppermute | solution.py:427
  162.7 1.2 collective-permute-start.31
  163.9 2.5 %shard_map.136 = (bf16[64,3072]{1,0:T(8,128)(2,1)}, bf16[64,3072]{1,0:T(8,128)(2,1)}) custom-call(bf16[128,1536]{1,0:T(8,128)(2,1)} %get-tuple-element.87.own_time.kept, bf16[128,768]{1,0:T(8,128)(2,1)} %get-tuple-element.88.dq, f32[128,1536]{1,0:T(8,128)} %get-tuple-element.89.own, bf16[128,1536]{1,0:T(8,128)(2,1)} %copy-done.7, bf16[128,1536]{1,0:T(8,128)(2,1)} %copy-done.8), custom_call_target="tpu_custom_call" | custom-call | tf_op jit(solution)/shard_map/pallas_call | solution.py:299
  166.5 1.3 collective-permute-start.27
  168.5 2.7 %collective-permute-done.31.rest_7_ = bf16[16,3072]{1,0:T(8,128)(2,1)S(1)} collective-permute-done((bf16[16,3072]{1,0:T(8,128)(2,1)S(1)}, bf16[16,3072]{1,0:T(8,128)(2,1)S(1)}, u32[]{:S(2)}, u32[]{:S(2)}) %collective-permute-start.31) | collective-permute-done | bytes 98336 | tf_op jit(solution)/shard_map/ppermute | solution.py:427
  172.0 4.9 %shard_map.137 = (bf16[128,1536]{1,0:T(8,128)(2,1)}, bf16[128,1536]{1,0:T(8,128)(2,1)}, bf16[128,1536]{1,0:T(8,128)(2,1)}, bf16[128,1536]{1,0:T(8,128)(2,1)}) custom-call(s32[1]{0:T(128)} %bitcast.me, s32[1]{0:T(128)} %bitcast.1.cam, bf16[1536,1536]{1,0:T(8,128)(2,1)} %get-tuple-element.85.w, f32[16,1536]{1,0:T(8,128)} %shard_map.130.action, ...), custom_call_target="tpu_custom_call" | custom-call | tf_op jit(solution)/shard_map/pallas_call | solution.py:299
  (107 shorter events, 7.5 us)
Async XLA Ops:
  0.6 8.4 %collective-permute-start.2 = (bf16[48,1536]{1,0:T(8,128)(2,1)}, bf16[48,1536]{1,0:T(8,128)(2,1)S(1)}, u32[]{:S(2)}, u32[]{:S(2)}) collective-permute-start(bf16[48,1536]{1,0:T(8,128)(2,1)} %param.16), channel_id=1, source_target_pairs={{0,34},{1,35},{2,32},{3,33},{4,38},{5,39},{6,36},{7,37},{8,42},{9,... | collective-permute-start | bytes 442376 | tf_op jit(solution)/shard_map/ppermute | solution.py:329
  8.0 5.1 %collective-permute-start.1 = (bf16[64,1536]{1,0:T(8,128)(2,1)}, bf16[64,1536]{1,0:T(8,128)(2,1)S(1)}, u32[]{:S(2)}, u32[]{:S(2)}) collective-permute-start(bf16[64,1536]{1,0:T(8,128)(2,1)} %get-tuple-element.66), channel_id=1, source_target_pairs={{0,1},{1,0},{2,3},{3,2},{4,5},{5,4},{6,7},{7,6},{8,9},{9,8},{10,11... | collective-permute-start | bytes 589832 | tf_op jit(solution)/shard_map/ppermute | solution.py:356
  9.1 40.7 %all-to-all-start = ((bf16[8,16,3968]{2,1,0:T(8,128)(2,1)}), bf16[8,16,3968]{2,1,0:T(8,128)(2,1)S(1)}, u32[]{:S(2)}, u32[]{:S(2)}) async-start(bf16[8,16,3968]{2,1,0:T(8,128)(2,1)} %bitcast.18), calls=%async_computation | async-start | bytes 2031616 | tf_op jit(solution)/shard_map/all_to_all | solution.py:341
  13.1 47.3 %copy-start.6 = (bf16[96,1536]{1,0:T(8,128)(2,1)}, bf16[96,1536]{1,0:T(8,128)(2,1)S(1)}, u32[]{:S(2)}) copy-start(bf16[96,1536]{1,0:T(8,128)(2,1)S(1)} %pad_maximum_fusion.1.rest_0_) | copy-start | bytes 884740
  13.2 30.0 %copy-start.2 = (bf16[128,1536]{1,0:T(8,128)(2,1)}, bf16[128,1536]{1,0:T(8,128)(2,1)S(1)}, u32[]{:S(2)}) copy-start(bf16[128,1536]{1,0:T(8,128)(2,1)S(1)} %pad_maximum_fusion.own) | copy-start | bytes 1179652
  13.2 20.4 %collective-permute-start.3 = (bf16[128,1536]{1,0:T(8,128)(2,1)S(1)}, bf16[128,1536]{1,0:T(8,128)(2,1)S(1)}, u32[]{:S(2)}, u32[]{:S(2)}) collective-permute-start(bf16[128,1536]{1,0:T(8,128)(2,1)S(1)} %pad_maximum_fusion.own), channel_id=1, source_target_pairs={{0,2},{1,3},{2,4},{3,5},{4,6},{5,7},{6,8},{7,9},{8,10},{9,11},{10,... | collective-permute-start | bytes 1179656 | tf_op jit(solution)/shard_map/ppermute | solution.py:360
  17.4 16.2 %collective-permute-start.4 = (bf16[128,1536]{1,0:T(8,128)(2,1)S(1)}, bf16[128,1536]{1,0:T(8,128)(2,1)S(1)}, u32[]{:S(2)}, u32[]{:S(2)}) collective-permute-start(bf16[128,1536]{1,0:T(8,128)(2,1)S(1)} %pad_maximum_fusion.own), channel_id=1, source_target_pairs={{0,4},{1,5},{2,6},{3,7},{4,8},{5,9},{6,10},{7,11},{8,12},{9,13},{1... | collective-permute-start | bytes 1179656 | tf_op jit(solution)/shard_map/ppermute | solution.py:361
  21.0 12.6 %collective-permute-start.5 = (bf16[96,1536]{1,0:T(8,128)(2,1)S(1)}, bf16[96,1536]{1,0:T(8,128)(2,1)S(1)}, u32[]{:S(2)}, u32[]{:S(2)}) collective-permute-start(bf16[96,1536]{1,0:T(8,128)(2,1)S(1)} %pad_maximum_fusion.1.rest_0_), channel_id=1, source_target_pairs={{0,4},{1,5},{2,6},{3,7},{4,8},{5,9},{6,10},{7,11},{8,12},{9,13},{1... | collective-permute-start | bytes 884744 | tf_op jit(solution)/shard_map/ppermute | solution.py:346
  22.6 10.9 %collective-permute-start.6 = (bf16[96,1536]{1,0:T(8,128)(2,1)S(1)}, bf16[96,1536]{1,0:T(8,128)(2,1)S(1)}, u32[]{:S(2)}, u32[]{:S(2)}) collective-permute-start(bf16[96,1536]{1,0:T(8,128)(2,1)S(1)} %pad_maximum_fusion.1.rest_0_), channel_id=1, source_target_pairs={{0,28},{1,29},{2,30},{3,31},{4,0},{5,1},{6,2},{7,3},{8,4},{9,5},{1... | collective-permute-start | bytes 884744 | tf_op jit(solution)/shard_map/ppermute | solution.py:346
  24.4 18.8 %collective-permute-start = (bf16[64,2304]{1,0:T(8,128)(2,1)}, bf16[64,2304]{1,0:T(8,128)(2,1)S(1)}, u32[]{:S(2)}, u32[]{:S(2)}) collective-permute-start(bf16[64,2304]{1,0:T(8,128)(2,1)} %get-tuple-element.64), channel_id=1, source_target_pairs={{0,1},{1,0},{2,3},{3,2},{4,5},{5,4},{6,7},{7,6},{8,9},{9,8},{10,11... | collective-permute-start | bytes 884744 | tf_op jit(solution)/shard_map/ppermute | solution.py:357
  33.5 50.4 %copy-start.12 = (bf16[96,1536]{1,0:T(8,128)(2,1)}, bf16[96,1536]{1,0:T(8,128)(2,1)S(1)}, u32[]{:S(2)}) copy-start(bf16[96,1536]{1,0:T(8,128)(2,1)S(1)} %collective-permute-done.5.rest_1_) | copy-start | bytes 884740
  33.5 50.4 %copy-start.13 = (bf16[96,1536]{1,0:T(8,128)(2,1)}, bf16[96,1536]{1,0:T(8,128)(2,1)S(1)}, u32[]{:S(2)}) copy-start(bf16[96,1536]{1,0:T(8,128)(2,1)S(1)} %collective-permute-done.6.rest_2_) | copy-start | bytes 884740
  33.6 16.2 %collective-permute-start.7 = (bf16[96,1536]{1,0:T(8,128)(2,1)S(1)}, bf16[96,1536]{1,0:T(8,128)(2,1)}, u32[]{:S(2)}, u32[]{:S(2)}) collective-permute-start(bf16[96,1536]{1,0:T(8,128)(2,1)S(1)} %collective-permute-done.5.rest_1_), channel_id=1, source_target_pairs={{0,4},{1,5},{2,6},{3,7},{4,8},{5,9},{6,10},{7,11},{8,12},{9,13},{1... | collective-permute-start | bytes 884744 | tf_op jit(solution)/shard_map/ppermute | solution.py:346
  35.9 13.9 %collective-permute-start.8 = (bf16[96,1536]{1,0:T(8,128)(2,1)S(1)}, bf16[96,1536]{1,0:T(8,128)(2,1)}, u32[]{:S(2)}, u32[]{:S(2)}) collective-permute-start(bf16[96,1536]{1,0:T(8,128)(2,1)S(1)} %collective-permute-done.6.rest_2_), channel_id=1, source_target_pairs={{0,28},{1,29},{2,30},{3,31},{4,0},{5,1},{6,2},{7,3},{8,4},{9,5},{1... | collective-permute-start | bytes 884744 | tf_op jit(solution)/shard_map/ppermute | solution.py:346
  39.9 9.9 %collective-permute-start.9 = (bf16[96,1536]{1,0:T(8,128)(2,1)S(1)}, bf16[96,1536]{1,0:T(8,128)(2,1)}, u32[]{:S(2)}, u32[]{:S(2)}) collective-permute-start(bf16[96,1536]{1,0:T(8,128)(2,1)S(1)} %pad_maximum_fusion.1.rest_0_), channel_id=1, source_target_pairs={{0,1},{1,0},{2,3},{3,2},{4,5},{5,4},{6,7},{7,6},{8,9},{9,8},{10,11... | collective-permute-start | bytes 884744 | tf_op jit(solution)/shard_map/ppermute | solution.py:350
  49.8 4.7 %collective-permute-start.21 = (bf16[128,1536]{1,0:T(8,128)(2,1)}, bf16[128,1536]{1,0:T(8,128)(2,1)S(1)}, u32[]{:S(2)}, u32[]{:S(2)}) collective-permute-start(bf16[128,1536]{1,0:T(8,128)(2,1)} %get-tuple-element.93), channel_id=1, source_target_pairs={{0,1},{1,0},{2,3},{3,2},{4,5},{5,4},{6,7},{7,6},{8,9},{9,8},{10,11... | collective-permute-start | bytes 1179656 | tf_op jit(solution)/shard_map/ppermute | solution.py:387
  54.0 2.1 %collective-permute-start.20 = (bf16[128,1536]{1,0:T(8,128)(2,1)}, bf16[128,1536]{1,0:T(8,128)(2,1)S(1)}, u32[]{:S(2)}, u32[]{:S(2)}) collective-permute-start(bf16[128,1536]{1,0:T(8,128)(2,1)} %get-tuple-element.92), channel_id=1, source_target_pairs={{0,1},{1,0},{2,3},{3,2},{4,5},{5,4},{6,7},{7,6},{8,9},{9,8},{10,11... | collective-permute-start | bytes 1179656 | tf_op jit(solution)/shard_map/ppermute | solution.py:386
  60.4 43.1 %all-to-all-start.1 = ((bf16[8,192,768]{2,1,0:T(8,128)(2,1)}), bf16[8,192,768]{2,1,0:T(8,128)(2,1)S(1)}, u32[]{:S(2)}, u32[]{:S(2)}) async-start(bf16[8,192,768]{2,1,0:T(8,128)(2,1)} %bitcast.15), calls=%async_computation.1 | async-start | bytes 4718592 | tf_op jit(solution)/shard_map/all_to_all | solution.py:395
  65.1 9.3 %collective-permute-start.10 = (bf16[96,1536]{1,0:T(8,128)(2,1)}, bf16[96,1536]{1,0:T(8,128)(2,1)S(1)}, u32[]{:S(2)}, u32[]{:S(2)}) collective-permute-start(bf16[96,1536]{1,0:T(8,128)(2,1)} %collective-permute-done.7.rest_3_), channel_id=1, source_target_pairs={{0,4},{1,5},{2,6},{3,7},{4,8},{5,9},{6,10},{7,11},{8,12},{9,13},{1... | collective-permute-start | bytes 884744 | tf_op jit(solution)/shard_map/ppermute | solution.py:346
  74.4 10.0 %collective-permute-start.12 = (bf16[96,1536]{1,0:T(8,128)(2,1)S(1)}, bf16[96,1536]{1,0:T(8,128)(2,1)}, u32[]{:S(2)}, u32[]{:S(2)}) collective-permute-start(bf16[96,1536]{1,0:T(8,128)(2,1)S(1)} %collective-permute-done.10.rest_5_), channel_id=1, source_target_pairs={{0,4},{1,5},{2,6},{3,7},{4,8},{5,9},{6,10},{7,11},{8,12},{9,13},{1... | collective-permute-start | bytes 884744 | tf_op jit(solution)/shard_map/ppermute | solution.py:346
  74.4 10.7 %collective-permute-start.11 = (bf16[96,1536]{1,0:T(8,128)(2,1)}, bf16[96,1536]{1,0:T(8,128)(2,1)}, u32[]{:S(2)}, u32[]{:S(2)}) collective-permute-start(bf16[96,1536]{1,0:T(8,128)(2,1)} %collective-permute-done.8.rest_4_), channel_id=1, source_target_pairs={{0,28},{1,29},{2,30},{3,31},{4,0},{5,1},{6,2},{7,3},{8,4},{9,5},{1... | collective-permute-start | bytes 884744 | tf_op jit(solution)/shard_map/ppermute | solution.py:346
  77.1 8.2 %collective-permute-start.13 = (bf16[96,1536]{1,0:T(8,128)(2,1)S(1)}, bf16[96,1536]{1,0:T(8,128)(2,1)}, u32[]{:S(2)}, u32[]{:S(2)}) collective-permute-start(bf16[96,1536]{1,0:T(8,128)(2,1)S(1)} %collective-permute-done.5.rest_1_), channel_id=1, source_target_pairs={{0,1},{1,0},{2,3},{3,2},{4,5},{5,4},{6,7},{7,6},{8,9},{9,8},{10,11... | collective-permute-start | bytes 884744 | tf_op jit(solution)/shard_map/ppermute | solution.py:350
  79.1 6.5 %collective-permute-start.14 = (bf16[96,1536]{1,0:T(8,128)(2,1)S(1)}, bf16[96,1536]{1,0:T(8,128)(2,1)}, u32[]{:S(2)}, u32[]{:S(2)}) collective-permute-start(bf16[96,1536]{1,0:T(8,128)(2,1)S(1)} %collective-permute-done.6.rest_2_), channel_id=1, source_target_pairs={{0,1},{1,0},{2,3},{3,2},{4,5},{5,4},{6,7},{7,6},{8,9},{9,8},{10,11... | collective-permute-start | bytes 884744 | tf_op jit(solution)/shard_map/ppermute | solution.py:350
  83.9 2.1 %collective-permute-start.15 = (bf16[96,1536]{1,0:T(8,128)(2,1)}, bf16[96,1536]{1,0:T(8,128)(2,1)}, u32[]{:S(2)}, u32[]{:S(2)}) collective-permute-start(bf16[96,1536]{1,0:T(8,128)(2,1)} %collective-permute-done.7.rest_3_), channel_id=1, source_target_pairs={{0,1},{1,0},{2,3},{3,2},{4,5},{5,4},{6,7},{7,6},{8,9},{9,8},{10,11... | collective-permute-start | bytes 884744 | tf_op jit(solution)/shard_map/ppermute | solution.py:350
  84.4 2.3 %collective-permute-start.16 = (bf16[96,1536]{1,0:T(8,128)(2,1)}, bf16[96,1536]{1,0:T(8,128)(2,1)}, u32[]{:S(2)}, u32[]{:S(2)}) collective-permute-start(bf16[96,1536]{1,0:T(8,128)(2,1)} %collective-permute-done.8.rest_4_), channel_id=1, source_target_pairs={{0,1},{1,0},{2,3},{3,2},{4,5},{5,4},{6,7},{7,6},{8,9},{9,8},{10,11... | collective-permute-start | bytes 884744 | tf_op jit(solution)/shard_map/ppermute | solution.py:350
  85.1 1.8 collective-permute-start.17
  85.2 2.2 %collective-permute-start.18 = (bf16[96,1536]{1,0:T(8,128)(2,1)}, bf16[96,1536]{1,0:T(8,128)(2,1)S(1)}, u32[]{:S(2)}, u32[]{:S(2)}) collective-permute-start(bf16[96,1536]{1,0:T(8,128)(2,1)} %collective-permute-done.11.rest_6_), channel_id=1, source_target_pairs={{0,1},{1,0},{2,3},{3,2},{4,5},{5,4},{6,7},{7,6},{8,9},{9,8},{10,11... | collective-permute-start | bytes 884744 | tf_op jit(solution)/shard_map/ppermute | solution.py:350
  85.6 2.2 %collective-permute-start.19 = (bf16[96,1536]{1,0:T(8,128)(2,1)}, bf16[96,1536]{1,0:T(8,128)(2,1)S(1)}, u32[]{:S(2)}, u32[]{:S(2)}) collective-permute-start(bf16[96,1536]{1,0:T(8,128)(2,1)} %collective-permute-done.12.rest_7_), channel_id=1, source_target_pairs={{0,1},{1,0},{2,3},{3,2},{4,5},{5,4},{6,7},{7,6},{8,9},{9,8},{10,11... | collective-permute-start | bytes 884744 | tf_op jit(solution)/shard_map/ppermute | solution.py:350
  103.5 25.1 %copy-start.27 = (bf16[128,1536]{1,0:T(8,128)(2,1)S(1)}, bf16[128,1536]{1,0:T(8,128)(2,1)}, u32[]{:S(2)}) copy-start(bf16[128,1536]{1,0:T(8,128)(2,1)} %get-tuple-element.100) | copy-start | bytes 1179652
  103.5 53.9 %copy-start.32 = (bf16[16,3072]{1,0:T(8,128)(2,1)S(1)}, bf16[16,3072]{1,0:T(8,128)(2,1)}, u32[]{:S(2)}) copy-start(bf16[16,3072]{1,0:T(8,128)(2,1)} %get-tuple-element.112) | copy-start | bytes 294916
  103.5 56.4 %copy-start.31 = (bf16[16,3072]{1,0:T(8,128)(2,1)S(1)}, bf16[16,3072]{1,0:T(8,128)(2,1)}, u32[]{:S(2)}) copy-start(bf16[16,3072]{1,0:T(8,128)(2,1)} %get-tuple-element.113) | copy-start | bytes 294916
  103.5 57.2 %copy-start.30 = (bf16[16,3072]{1,0:T(8,128)(2,1)S(1)}, bf16[16,3072]{1,0:T(8,128)(2,1)}, u32[]{:S(2)}) copy-start(bf16[16,3072]{1,0:T(8,128)(2,1)} %get-tuple-element.114) | copy-start | bytes 294916
  103.5 59.2 %copy-start.29 = (bf16[16,3072]{1,0:T(8,128)(2,1)S(1)}, bf16[16,3072]{1,0:T(8,128)(2,1)}, u32[]{:S(2)}) copy-start(bf16[16,3072]{1,0:T(8,128)(2,1)} %get-tuple-element.115) | copy-start | bytes 294916
  107.9 47.9 %all-to-all-start.2 = ((bf16[16,12,768]{2,1,0:T(8,128)(2,1)}), bf16[16,12,768]{2,1,0:T(8,128)(2,1)S(1)}, u32[]{:S(2)}, u32[]{:S(2)}) async-start(bf16[16,12,768]{2,1,0:T(8,128)(2,1)} %shard_map.135), calls=%async_computation.2 | async-start | bytes 786432 | tf_op jit(solution)/shard_map/all_to_all | solution.py:425
  127.3 19.4 %collective-permute-start.22 = (bf16[128,1536]{1,0:T(8,128)(2,1)S(1)}, bf16[128,1536]{1,0:T(8,128)(2,1)S(1)}, u32[]{:S(2)}, u32[]{:S(2)}) collective-permute-start(bf16[128,1536]{1,0:T(8,128)(2,1)S(1)} %copy-done.28), channel_id=1, source_target_pairs={{2,0},{3,1},{4,2},{5,3},{6,4},{7,5},{8,6},{9,7},{10,8},{11,9},{12,... | collective-permute-start | bytes 1179656 | tf_op jit(solution)/shard_map/ppermute | solution.py:406
  128.6 27.1 %collective-permute-start.23 = (bf16[128,1536]{1,0:T(8,128)(2,1)S(1)}, bf16[128,1536]{1,0:T(8,128)(2,1)S(1)}, u32[]{:S(2)}, u32[]{:S(2)}) collective-permute-start(bf16[128,1536]{1,0:T(8,128)(2,1)S(1)} %copy-done.27), channel_id=1, source_target_pairs={{4,0},{5,1},{6,2},{7,3},{8,4},{9,5},{10,6},{11,7},{12,8},{13,9},{1... | collective-permute-start | bytes 1179656 | tf_op jit(solution)/shard_map/ppermute | solution.py:407
  129.9 4.6 %collective-permute-start.24 = (bf16[16,3072]{1,0:T(8,128)(2,1)}, bf16[16,3072]{1,0:T(8,128)(2,1)S(1)}, u32[]{:S(2)}, u32[]{:S(2)}) collective-permute-start(bf16[16,3072]{1,0:T(8,128)(2,1)} %get-tuple-element.101), channel_id=1, source_target_pairs={{0,32},{32,0},{64,96},{96,64},{128,160},{160,128},{192,224},{224,1... | collective-permute-start | bytes 294920 | tf_op jit(solution)/shard_map/ppermute | solution.py:427
  130.5 4.0 %collective-permute-start.25 = (bf16[16,3072]{1,0:T(8,128)(2,1)}, bf16[16,3072]{1,0:T(8,128)(2,1)S(1)}, u32[]{:S(2)}, u32[]{:S(2)}) collective-permute-start(bf16[16,3072]{1,0:T(8,128)(2,1)} %get-tuple-element.102), channel_id=1, source_target_pairs={{0,64},{32,96},{64,0},{96,32},{128,192},{160,224},{192,128},{224,1... | collective-permute-start | bytes 294920 | tf_op jit(solution)/shard_map/ppermute | solution.py:427
  131.7 5.9 %collective-permute-start.26 = (bf16[16,3072]{1,0:T(8,128)(2,1)}, bf16[16,3072]{1,0:T(8,128)(2,1)S(1)}, u32[]{:S(2)}, u32[]{:S(2)}) collective-permute-start(bf16[16,3072]{1,0:T(8,128)(2,1)} %get-tuple-element.103), channel_id=1, source_target_pairs={{0,96},{32,64},{64,32},{96,0},{128,224},{160,192},{192,160},{224,1... | collective-permute-start | bytes 294920 | tf_op jit(solution)/shard_map/ppermute | solution.py:427
  134.5 36.8 %copy-start.19 = (bf16[16,3072]{1,0:T(8,128)(2,1)}, bf16[16,3072]{1,0:T(8,128)(2,1)S(1)}, u32[]{:S(2)}) copy-start(bf16[16,3072]{1,0:T(8,128)(2,1)S(1)} %collective-permute-done.24.rest_1_) | copy-start | bytes 294916
  134.5 36.8 %copy-start.20 = (bf16[16,3072]{1,0:T(8,128)(2,1)}, bf16[16,3072]{1,0:T(8,128)(2,1)S(1)}, u32[]{:S(2)}) copy-start(bf16[16,3072]{1,0:T(8,128)(2,1)S(1)} %collective-permute-done.25.rest_2_) | copy-start | bytes 294916
  137.7 33.6 %copy-start.21 = (bf16[16,3072]{1,0:T(8,128)(2,1)}, bf16[16,3072]{1,0:T(8,128)(2,1)S(1)}, u32[]{:S(2)}) copy-start(bf16[16,3072]{1,0:T(8,128)(2,1)S(1)} %collective-permute-done.26.rest_3_) | copy-start | bytes 294916
  155.9 10.6 %collective-permute-start.32 = (f32[6,768]{1,0:T(8,128)S(1)}, f32[6,768]{1,0:T(8,128)S(1)}, u32[]{:S(2)}, u32[]{:S(2)}) collective-permute-start(f32[6,768]{1,0:T(8,128)S(1)} %constant_dynamic-slice_fusion), channel_id=1, source_target_pairs={{0,1},{1,0},{2,3},{3,2},{4,5},{5,4},{6,7},{7,6},{8,9},{9,8},{10,11... | collective-permute-start | bytes 55304 | tf_op jit(solution)/shard_map/ppermute | solution.py:436
  157.4 11.0 %collective-permute-start.28 = (bf16[16,3072]{1,0:T(8,128)(2,1)S(1)}, bf16[16,3072]{1,0:T(8,128)(2,1)S(1)}, u32[]{:S(2)}, u32[]{:S(2)}) collective-permute-start(bf16[16,3072]{1,0:T(8,128)(2,1)S(1)} %copy-done.32), channel_id=1, source_target_pairs={{0,128},{32,160},{64,192},{96,224},{128,0},{160,32},{192,64},{224,... | collective-permute-start | bytes 294920 | tf_op jit(solution)/shard_map/ppermute | solution.py:427
  159.9 8.5 %collective-permute-start.29 = (bf16[16,3072]{1,0:T(8,128)(2,1)S(1)}, bf16[16,3072]{1,0:T(8,128)(2,1)S(1)}, u32[]{:S(2)}, u32[]{:S(2)}) collective-permute-start(bf16[16,3072]{1,0:T(8,128)(2,1)S(1)} %copy-done.31), channel_id=1, source_target_pairs={{0,160},{32,128},{64,224},{96,192},{128,32},{160,0},{192,96},{224,... | collective-permute-start | bytes 294920 | tf_op jit(solution)/shard_map/ppermute | solution.py:427
  160.7 7.8 %collective-permute-start.30 = (bf16[16,3072]{1,0:T(8,128)(2,1)S(1)}, bf16[16,3072]{1,0:T(8,128)(2,1)S(1)}, u32[]{:S(2)}, u32[]{:S(2)}) collective-permute-start(bf16[16,3072]{1,0:T(8,128)(2,1)S(1)} %copy-done.30), channel_id=1, source_target_pairs={{0,192},{32,224},{64,128},{96,160},{128,64},{160,96},{192,0},{224,... | collective-permute-start | bytes 294920 | tf_op jit(solution)/shard_map/ppermute | solution.py:427
  162.7 8.5 %collective-permute-start.31 = (bf16[16,3072]{1,0:T(8,128)(2,1)S(1)}, bf16[16,3072]{1,0:T(8,128)(2,1)S(1)}, u32[]{:S(2)}, u32[]{:S(2)}) collective-permute-start(bf16[16,3072]{1,0:T(8,128)(2,1)S(1)} %copy-done.29), channel_id=1, source_target_pairs={{0,224},{32,192},{64,160},{96,128},{128,96},{160,64},{192,32},{224... | collective-permute-start | bytes 294920 | tf_op jit(solution)/shard_map/ppermute | solution.py:427
  166.5 4.8 %collective-permute-start.27 = (bf16[64,3072]{1,0:T(8,128)(2,1)}, bf16[64,3072]{1,0:T(8,128)(2,1)S(1)}, u32[]{:S(2)}, u32[]{:S(2)}) collective-permute-start(bf16[64,3072]{1,0:T(8,128)(2,1)} %get-tuple-element.107), channel_id=1, source_target_pairs={{0,1},{1,0},{2,3},{3,2},{4,5},{5,4},{6,7},{7,6},{8,9},{9,8},{10,11... | collective-permute-start | bytes 1179656 | tf_op jit(solution)/shard_map/ppermute | solution.py:444
  (21 other events, 132.5 us)

commit v9 on v8

--- a/solution.py
+++ b/solution.py
@@ -380,6 +380,7 @@
         windows, me, pair, q0, q1, far, near, own,
     )
 
+    kept_view, w_own[5:7] = lax.optimization_barrier((kept_view, w_own[5:7]))
     pass_on(7, depth)
     w_own[-1], action_sum = lax.optimization_barrier((w_own[-1], action_sum))
     swap_blocks(depth)

time: 178 us -> 180 us (1.011)
  starting transfers between devices: 77.7 us -> 80.3 us
    all_to_all x1, waiting for transfers between devices: 0.01 us -> 5.36 us  [shards(): lax.all_to_all(part.reshape(cams, width // cams, CW), 'cam', 0, 0, tiled=...]
    ppermute x7, waiting for transfers between devices: 7.85 us -> 3.82 us  [shards(): lax.ppermute(view_out[d], 'cam', [(i, i ^ d) for i in range(cams)])]
  transfers between devices with their start and end apart: 36 -> 36, of which waited for: 14 -> 12; matrix products, arithmetic and copies ran while one was open for 1% -> 1% of each run, Pallas kernels for 19% -> 19%
where the time goes in v9:
time: 180 us; the launch traced here: 179 us
  starting transfers between devices  80.3 us (45%)
  Pallas kernels  45.7 us (25%)
  waiting for transfers between devices  44.8 us (25%)
  local copies, waits for them, and re-layouts  6.24 us (3%)
    pallas_call x10, Pallas kernels, call(): pl.pallas_call(kernel, out_shape=[jax.ShapeDtypeStruct(shape, kind) for s...  45.7 us
    all_to_all x1, starting transfers between devices, shards(): lax.all_to_all(part, 'tm', 0, 0, tiled=True, axis_index_groups=same_core)  19.3 us
    ppermute x7, waiting for transfers between devices, pass_on(): lax.ppermute(w_own[max(i - 2, 0)], 'tm', up if i % 2 else down)  14.5 us
    ppermute x7, starting transfers between devices, pass_on(): lax.ppermute(w_own[max(i - 2, 0)], 'tm', up if i % 2 else down)  14.1 us
    ppermute x1, waiting for transfers between devices, shards(): lax.ppermute(near_grad, 'tm', [(i + 2, i) for i in range(tm - 2)])  9.56 us
    ppermute x7, starting transfers between devices, shards(): lax.ppermute(view_out[d], 'cam', [(i, i ^ d) for i in range(cams)])  9.48 us
    ppermute x1, waiting for transfers between devices, shards(): far_grad = lax.ppermute(far_grad, 'tm', [(i + 4, i) for i in range(tm - 4)])  8.97 us
    ppermute x8, starting transfers between devices, swap_blocks(): w_other.append(lax.ppermute(block_rows, 'tm', swap))  7.77 us
  transfers between devices with their start and end apart: 36, of which 12 were waited for; matrix products, arithmetic and copies ran while one was open for 1% of the time, Pallas kernels for 19%

profile of v9, /device:TPU:1, one launch (start us, length us, event | category | flops | bytes accessed | tf_op | source)
XLA Modules:
  0.0 178.8 jit_solution(6169186051366303207)
XLA Ops:
  0.6 3.7 %collective-permute-start.2 = (bf16[48,1536]{1,0:T(8,128)(2,1)}, bf16[48,1536]{1,0:T(8,128)(2,1)S(1)}, u32[]{:S(2)}, u32[]{:S(2)}) collective-permute-start(bf16[48,1536]{1,0:T(8,128)(2,1)} %param.16), channel_id=1, source_target_pairs={{0,34},{1,35},{2,32},{3,33},{4,38},{5,39},{6,36},{7,37},{8,42},{9,... | collective-permute-start | bytes 442376 | tf_op jit(solution)/shard_map/ppermute | solution.py:329
  4.3 3.7 %shard_map.128 = (bf16[128,3968]{1,0:T(8,128)(2,1)}, bf16[64,1536]{1,0:T(8,128)(2,1)}, bf16[64,1536]{1,0:T(8,128)(2,1)}, bf16[64,2304]{1,0:T(8,128)(2,1)}, bf16[64,2304]{1,0:T(8,128)(2,1)}) custom-call(s32[1]{0:T(128)} %bitcast.me, s32[1,16]{1,0:T(1,128)} %valid.1, bf16[128,1536]{1,0:T(8,128)(2,1)} %bitcast.19, bf16[128,1536]{1,0:T(8,128)(2,1)} %bitcast.20, ...), custom_call_target="tpu_custom_call" | custom-call | tf_op jit(solution)/shard_map/pallas_call | solution.py:299
  8.0 1.0 collective-permute-start.1
  9.1 4.0 %all-to-all-start = ((bf16[8,16,3968]{2,1,0:T(8,128)(2,1)}), bf16[8,16,3968]{2,1,0:T(8,128)(2,1)S(1)}, u32[]{:S(2)}, u32[]{:S(2)}) async-start(bf16[8,16,3968]{2,1,0:T(8,128)(2,1)} %bitcast.18), calls=%async_computation | async-start | bytes 2031616 | tf_op jit(solution)/shard_map/all_to_all | solution.py:341
  13.2 4.2 %collective-permute-start.3 = (bf16[128,1536]{1,0:T(8,128)(2,1)S(1)}, bf16[128,1536]{1,0:T(8,128)(2,1)S(1)}, u32[]{:S(2)}, u32[]{:S(2)}) collective-permute-start(bf16[128,1536]{1,0:T(8,128)(2,1)S(1)} %pad_maximum_fusion.own), channel_id=1, source_target_pairs={{0,2},{1,3},{2,4},{3,5},{4,6},{5,7},{6,8},{7,9},{8,10},{9,11},{10,... | collective-permute-start | bytes 1179656 | tf_op jit(solution)/shard_map/ppermute | solution.py:360
  17.4 3.5 %collective-permute-start.4 = (bf16[128,1536]{1,0:T(8,128)(2,1)S(1)}, bf16[128,1536]{1,0:T(8,128)(2,1)S(1)}, u32[]{:S(2)}, u32[]{:S(2)}) collective-permute-start(bf16[128,1536]{1,0:T(8,128)(2,1)S(1)} %pad_maximum_fusion.own), channel_id=1, source_target_pairs={{0,4},{1,5},{2,6},{3,7},{4,8},{5,9},{6,10},{7,11},{8,12},{9,13},{1... | collective-permute-start | bytes 1179656 | tf_op jit(solution)/shard_map/ppermute | solution.py:361
  21.0 1.7 collective-permute-start.5
  22.6 1.8 collective-permute-start.6
  24.4 2.4 %collective-permute-start = (bf16[64,2304]{1,0:T(8,128)(2,1)}, bf16[64,2304]{1,0:T(8,128)(2,1)S(1)}, u32[]{:S(2)}, u32[]{:S(2)}) collective-permute-start(bf16[64,2304]{1,0:T(8,128)(2,1)} %get-tuple-element.67), channel_id=1, source_target_pairs={{0,1},{1,0},{2,3},{3,2},{4,5},{5,4},{6,7},{7,6},{8,9},{9,8},{10,11... | collective-permute-start | bytes 884744 | tf_op jit(solution)/shard_map/ppermute | solution.py:357
  26.8 6.7 %collective-permute-done.5.rest_1_ = bf16[96,1536]{1,0:T(8,128)(2,1)S(1)} collective-permute-done((bf16[96,1536]{1,0:T(8,128)(2,1)S(1)}, bf16[96,1536]{1,0:T(8,128)(2,1)S(1)}, u32[]{:S(2)}, u32[]{:S(2)}) %collective-permute-start.5) | collective-permute-done | bytes 294944 | tf_op jit(solution)/shard_map/ppermute | solution.py:346
  33.6 2.3 %collective-permute-start.7 = (bf16[96,1536]{1,0:T(8,128)(2,1)S(1)}, bf16[96,1536]{1,0:T(8,128)(2,1)}, u32[]{:S(2)}, u32[]{:S(2)}) collective-permute-start(bf16[96,1536]{1,0:T(8,128)(2,1)S(1)} %collective-permute-done.5.rest_1_), channel_id=1, source_target_pairs={{0,4},{1,5},{2,6},{3,7},{4,8},{5,9},{6,10},{7,11},{8,12},{9,13},{1... | collective-permute-start | bytes 884744 | tf_op jit(solution)/shard_map/ppermute | solution.py:346
  35.9 4.0 %collective-permute-start.8 = (bf16[96,1536]{1,0:T(8,128)(2,1)S(1)}, bf16[96,1536]{1,0:T(8,128)(2,1)}, u32[]{:S(2)}, u32[]{:S(2)}) collective-permute-start(bf16[96,1536]{1,0:T(8,128)(2,1)S(1)} %collective-permute-done.6.rest_2_), channel_id=1, source_target_pairs={{0,28},{1,29},{2,30},{3,31},{4,0},{5,1},{6,2},{7,3},{8,4},{9,5},{1... | collective-permute-start | bytes 884744 | tf_op jit(solution)/shard_map/ppermute | solution.py:346
  39.9 3.3 %collective-permute-start.9 = (bf16[96,1536]{1,0:T(8,128)(2,1)S(1)}, bf16[96,1536]{1,0:T(8,128)(2,1)}, u32[]{:S(2)}, u32[]{:S(2)}) collective-permute-start(bf16[96,1536]{1,0:T(8,128)(2,1)S(1)} %pad_maximum_fusion.1.rest_0_), channel_id=1, source_target_pairs={{0,1},{1,0},{2,3},{3,2},{4,5},{5,4},{6,7},{7,6},{8,9},{9,8},{10,11... | collective-permute-start | bytes 884744 | tf_op jit(solution)/shard_map/ppermute | solution.py:350
  43.2 0.7 copy-done.5
  43.9 5.8 %shard_map.129 = (bf16[128,1536]{1,0:T(8,128)(2,1)}, bf16[128,1536]{1,0:T(8,128)(2,1)}, f32[6,256,384]{2,1,0:T(8,128)}) custom-call(s32[12]{0:T(128)} %windows.1, s32[1]{0:T(128)} %bitcast.me, s32[1]{0:T(128)} %bitcast.7.pair, bf16[64,2304]{1,0:T(8,128)(2,1)} %get-tuple-element.66.q0, bf16[64,2304]{1,0:T(8,128)(2,1)} %copy-done.5, ...), custom_call_target="tpu_custom_call" | custom-call | tf_op jit(solution)/shard_map/pallas_call | solution.py:299
  49.8 1.0 copy-done.1
  50.8 3.2 %shard_map.130 = (bf16[128,1536]{1,0:T(8,128)(2,1)}, bf16[128,1536]{1,0:T(8,128)(2,1)}, f32[6,256,128]{2,1,0:T(8,128)}) custom-call(s32[1]{0:T(128)} %bitcast.me, bf16[128,3968]{1,0:T(8,128)(2,1)} %bitcast.16), custom_call_target="tpu_custom_call" | custom-call | tf_op jit(solution)/shard_map/pallas_call | solution.py:299
  54.5 2.7 %collective-permute-start.11 = (bf16[96,1536]{1,0:T(8,128)(2,1)}, bf16[96,1536]{1,0:T(8,128)(2,1)}, u32[]{:S(2)}, u32[]{:S(2)}) collective-permute-start(bf16[96,1536]{1,0:T(8,128)(2,1)} %collective-permute-done.8.rest_4_), channel_id=1, source_target_pairs={{0,28},{1,29},{2,30},{3,31},{4,0},{5,1},{6,2},{7,3},{8,4},{9,5},{1... | collective-permute-start | bytes 884744 | tf_op jit(solution)/shard_map/ppermute | solution.py:346
  57.2 7.4 %collective-permute-done.10.rest_5_ = bf16[96,1536]{1,0:T(8,128)(2,1)S(1)} collective-permute-done((bf16[96,1536]{1,0:T(8,128)(2,1)}, bf16[96,1536]{1,0:T(8,128)(2,1)S(1)}, u32[]{:S(2)}, u32[]{:S(2)}) %collective-permute-start.10) | collective-permute-done | bytes 294944 | tf_op jit(solution)/shard_map/ppermute | solution.py:346
  64.6 0.8 copy-done.10
  65.5 3.6 %shard_map.133 = bf16[1536,768]{1,0:T(8,128)(2,1)} custom-call(bf16[128,1536]{1,0:T(8,128)(2,1)} %get-tuple-element.97.own_view.kept, bf16[128,1536]{1,0:T(8,128)(2,1)} %copy-done.11, bf16[128,1536]{1,0:T(8,128)(2,1)} %get-tuple-element.94.own_time.kept, bf16[128,1536]{1,0:T(8,128)(2,1)} %copy-done.10), custom_call_target="tpu_custom_call" | custom-call | tf_op jit(solution)/shard_map/pallas_call | solution.py:299
  69.1 4.7 %all-to-all-start.1 = ((bf16[8,192,768]{2,1,0:T(8,128)(2,1)}), bf16[8,192,768]{2,1,0:T(8,128)(2,1)S(1)}, u32[]{:S(2)}, u32[]{:S(2)}) async-start(bf16[8,192,768]{2,1,0:T(8,128)(2,1)} %bitcast.15), calls=%async_computation.1 | async-start | bytes 4718592 | tf_op jit(solution)/shard_map/all_to_all | solution.py:396
  73.7 1.7 collective-permute-start.12
  75.4 1.3 collective-permute-start.13
  77.4 4.1 %shard_map.131.action = f32[16,1536]{1,0:T(8,128)} custom-call(s32[16,7]{1,0:T(8,128)} %copy.14.actions, bf16[7,256,1536]{2,1,0:T(8,128)(2,1)} %table.1), custom_call_target="tpu_custom_call" | custom-call | tf_op jit(solution)/shard_map/pallas_call | solution.py:299
  82.5 2.0 %collective-permute-start.17 = (bf16[96,1536]{1,0:T(8,128)(2,1)S(1)}, bf16[96,1536]{1,0:T(8,128)(2,1)}, u32[]{:S(2)}, u32[]{:S(2)}) collective-permute-start(bf16[96,1536]{1,0:T(8,128)(2,1)S(1)} %collective-permute-done.10.rest_5_), channel_id=1, source_target_pairs={{0,1},{1,0},{2,3},{3,2},{4,5},{5,4},{6,7},{7,6},{8,9},{9,8},{10,11... | collective-permute-start | bytes 884744 | tf_op jit(solution)/shard_map/ppermute | solution.py:350
  85.0 0.8 collective-permute-done.17.rest_13_
  87.5 9.6 %shard_map.132 = (bf16[128,768]{1,0:T(8,128)(2,1)}, f32[128,1536]{1,0:T(8,128)}, bf16[128,1536]{1,0:T(8,128)(2,1)}, bf16[128,1536]{1,0:T(8,128)(2,1)}, bf16[1536,1536]{1,0:T(8,128)(2,1)}) custom-call(s32[1]{0:T(128)} %bitcast.me, s32[1]{0:T(128)} %bitcast.2.z, bf16[64,2304]{1,0:T(8,128)(2,1)} %get-tuple-element.66.q0, bf16[64,2304]{1,0:T(8,128)(2,1)} %copy-done.5, ...), custom_call_target="tpu_custom_call" | custom-call | tf_op jit(solution)/shard_map/pallas_call | solution.py:299
  97.1 5.3 %shard_map.134 = (bf16[16,3072]{1,0:T(8,128)(2,1)}, bf16[16,3072]{1,0:T(8,128)(2,1)}, bf16[16,3072]{1,0:T(8,128)(2,1)}, bf16[16,3072]{1,0:T(8,128)(2,1)}, bf16[1...) custom-call(s32[1]{0:T(128)} %bitcast.1.cam, ...), custom_call_target="tpu_custom_call" | custom-call | tf_op jit(solution)/shard_map/pallas_call | solution.py:299
  102.5 5.4 %all-to-all-done.1.parts = bf16[8,192,768]{2,1,0:T(8,128)(2,1)S(1)} async-done(((bf16[8,192,768]{2,1,0:T(8,128)(2,1)}), bf16[8,192,768]{2,1,0:T(8,128)(2,1)S(1)}, u32[]{:S(2)}, u32[]{:S(2)}) %all-to-all-start.1) | async-done | bytes 2359328 | tf_op jit(solution)/shard_map/all_to_all | solution.py:396
  107.8 1.4 copy-done
  109.2 2.9 %shard_map.135 = bf16[16,12,768]{2,1,0:T(8,128)(2,1)} custom-call(bf16[8,192,768]{2,1,0:T(8,128)(2,1)} %copy-done), custom_call_target="tpu_custom_call" | custom-call | tf_op jit(solution)/shard_map/pallas_call | solution.py:299
  112.2 19.3 %all-to-all-start.2 = ((bf16[16,12,768]{2,1,0:T(8,128)(2,1)}), bf16[16,12,768]{2,1,0:T(8,128)(2,1)S(1)}, u32[]{:S(2)}, u32[]{:S(2)}) async-start(bf16[16,12,768]{2,1,0:T(8,128)(2,1)} %shard_map.135), calls=%async_computation.2 | async-start | bytes 786432 | tf_op jit(solution)/shard_map/all_to_all | solution.py:426
  131.5 1.3 collective-permute-start.22
  132.8 1.3 collective-permute-start.23
  134.6 2.5 %collective-permute-start.26 = (bf16[16,3072]{1,0:T(8,128)(2,1)}, bf16[16,3072]{1,0:T(8,128)(2,1)S(1)}, u32[]{:S(2)}, u32[]{:S(2)}) collective-permute-start(bf16[16,3072]{1,0:T(8,128)(2,1)} %get-tuple-element.109), channel_id=1, source_target_pairs={{0,96},{32,64},{64,32},{96,0},{128,224},{160,192},{192,160},{224,1... | collective-permute-start | bytes 294920 | tf_op jit(solution)/shard_map/ppermute | solution.py:428
  137.1 2.2 %collective-permute-done.24.rest_1_ = bf16[16,3072]{1,0:T(8,128)(2,1)S(1)} collective-permute-done((bf16[16,3072]{1,0:T(8,128)(2,1)}, bf16[16,3072]{1,0:T(8,128)(2,1)S(1)}, u32[]{:S(2)}, u32[]{:S(2)}) %collective-permute-start.24) | collective-permute-done | bytes 98336 | tf_op jit(solution)/shard_map/ppermute | solution.py:428
  139.3 1.6 collective-permute-done.26.rest_3_
  140.9 9.6 %collective-permute-done.22.near = bf16[128,1536]{1,0:T(8,128)(2,1)S(1)} collective-permute-done((bf16[128,1536]{1,0:T(8,128)(2,1)S(1)}, bf16[128,1536]{1,0:T(8,128)(2,1)S(1)}, u32[]{:S(2)}, u32[]{:S(2)}) %collective-permute-start.22) | collective-permute-done | bytes 393248 | tf_op jit(solution)/shard_map/ppermute | solution.py:407
  150.5 9.0 %collective-permute-done.23.far = bf16[128,1536]{1,0:T(8,128)(2,1)S(1)} collective-permute-done((bf16[128,1536]{1,0:T(8,128)(2,1)S(1)}, bf16[128,1536]{1,0:T(8,128)(2,1)S(1)}, u32[]{:S(2)}, u32[]{:S(2)}) %collective-permute-start.23) | collective-permute-done | bytes 393248 | tf_op jit(solution)/shard_map/ppermute | solution.py:408
  159.5 1.7 collective-permute-start.32
  161.3 2.2 %collective-permute-start.29 = (bf16[16,3072]{1,0:T(8,128)(2,1)S(1)}, bf16[16,3072]{1,0:T(8,128)(2,1)S(1)}, u32[]{:S(2)}, u32[]{:S(2)}) collective-permute-start(bf16[16,3072]{1,0:T(8,128)(2,1)S(1)} %copy-done.31), channel_id=1, source_target_pairs={{0,160},{32,128},{64,224},{96,192},{128,32},{160,0},{192,96},{224,... | collective-permute-start | bytes 294920 | tf_op jit(solution)/shard_map/ppermute | solution.py:428
  163.5 4.3 %collective-permute-start.31 = (bf16[16,3072]{1,0:T(8,128)(2,1)S(1)}, bf16[16,3072]{1,0:T(8,128)(2,1)S(1)}, u32[]{:S(2)}, u32[]{:S(2)}) collective-permute-start(bf16[16,3072]{1,0:T(8,128)(2,1)S(1)} %copy-done.29), channel_id=1, source_target_pairs={{0,224},{32,192},{64,160},{96,128},{128,96},{160,64},{192,32},{224... | collective-permute-start | bytes 294920 | tf_op jit(solution)/shard_map/ppermute | solution.py:428
  167.8 2.5 %shard_map.136 = (bf16[64,3072]{1,0:T(8,128)(2,1)}, bf16[64,3072]{1,0:T(8,128)(2,1)}) custom-call(bf16[128,1536]{1,0:T(8,128)(2,1)} %get-tuple-element.94.own_time.kept, bf16[128,768]{1,0:T(8,128)(2,1)} %get-tuple-element.95.dq, f32[128,1536]{1,0:T(8,128)} %get-tuple-element.96.own, bf16[128,1536]{1,0:T(8,128)(2,1)} %copy-done.7, bf16[128,1536]{1,0:T(8,128)(2,1)} %copy-done.8), custom_call_target="tpu_custom_call" | custom-call | tf_op jit(solution)/shard_map/pallas_call | solution.py:299
  170.4 1.3 collective-permute-start.27
  172.3 0.9 collective-permute-done.27.t1
  173.2 0.7 copy-done.9
  173.9 4.9 %shard_map.137 = (bf16[128,1536]{1,0:T(8,128)(2,1)}, bf16[128,1536]{1,0:T(8,128)(2,1)}, bf16[128,1536]{1,0:T(8,128)(2,1)}, bf16[128,1536]{1,0:T(8,128)(2,1)}) custom-call(s32[1]{0:T(128)} %bitcast.me, s32[1]{0:T(128)} %bitcast.1.cam, bf16[1536,1536]{1,0:T(8,128)(2,1)} %get-tuple-element.92.w, f32[16,1536]{1,0:T(8,128)} %shard_map.131.action, ...), custom_call_target="tpu_custom_call" | custom-call | tf_op jit(solution)/shard_map/pallas_call | solution.py:299
  (107 shorter events, 5.9 us)
Async XLA Ops:
  0.6 8.4 %collective-permute-start.2 = (bf16[48,1536]{1,0:T(8,128)(2,1)}, bf16[48,1536]{1,0:T(8,128)(2,1)S(1)}, u32[]{:S(2)}, u32[]{:S(2)}) collective-permute-start(bf16[48,1536]{1,0:T(8,128)(2,1)} %param.16), channel_id=1, source_target_pairs={{0,34},{1,35},{2,32},{3,33},{4,38},{5,39},{6,36},{7,37},{8,42},{9,... | collective-permute-start | bytes 442376 | tf_op jit(solution)/shard_map/ppermute | solution.py:329
  8.0 5.1 %collective-permute-start.1 = (bf16[64,1536]{1,0:T(8,128)(2,1)}, bf16[64,1536]{1,0:T(8,128)(2,1)S(1)}, u32[]{:S(2)}, u32[]{:S(2)}) collective-permute-start(bf16[64,1536]{1,0:T(8,128)(2,1)} %get-tuple-element.69), channel_id=1, source_target_pairs={{0,1},{1,0},{2,3},{3,2},{4,5},{5,4},{6,7},{7,6},{8,9},{9,8},{10,11... | collective-permute-start | bytes 589832 | tf_op jit(solution)/shard_map/ppermute | solution.py:356
  9.1 40.7 %all-to-all-start = ((bf16[8,16,3968]{2,1,0:T(8,128)(2,1)}), bf16[8,16,3968]{2,1,0:T(8,128)(2,1)S(1)}, u32[]{:S(2)}, u32[]{:S(2)}) async-start(bf16[8,16,3968]{2,1,0:T(8,128)(2,1)} %bitcast.18), calls=%async_computation | async-start | bytes 2031616 | tf_op jit(solution)/shard_map/all_to_all | solution.py:341
  13.1 56.0 %copy-start.6 = (bf16[96,1536]{1,0:T(8,128)(2,1)}, bf16[96,1536]{1,0:T(8,128)(2,1)S(1)}, u32[]{:S(2)}) copy-start(bf16[96,1536]{1,0:T(8,128)(2,1)S(1)} %pad_maximum_fusion.1.rest_0_) | copy-start | bytes 884740
  13.2 30.0 %copy-start.2 = (bf16[128,1536]{1,0:T(8,128)(2,1)}, bf16[128,1536]{1,0:T(8,128)(2,1)S(1)}, u32[]{:S(2)}) copy-start(bf16[128,1536]{1,0:T(8,128)(2,1)S(1)} %pad_maximum_fusion.own) | copy-start | bytes 1179652
  13.2 20.4 %collective-permute-start.3 = (bf16[128,1536]{1,0:T(8,128)(2,1)S(1)}, bf16[128,1536]{1,0:T(8,128)(2,1)S(1)}, u32[]{:S(2)}, u32[]{:S(2)}) collective-permute-start(bf16[128,1536]{1,0:T(8,128)(2,1)S(1)} %pad_maximum_fusion.own), channel_id=1, source_target_pairs={{0,2},{1,3},{2,4},{3,5},{4,6},{5,7},{6,8},{7,9},{8,10},{9,11},{10,... | collective-permute-start | bytes 1179656 | tf_op jit(solution)/shard_map/ppermute | solution.py:360
  17.4 16.2 %collective-permute-start.4 = (bf16[128,1536]{1,0:T(8,128)(2,1)S(1)}, bf16[128,1536]{1,0:T(8,128)(2,1)S(1)}, u32[]{:S(2)}, u32[]{:S(2)}) collective-permute-start(bf16[128,1536]{1,0:T(8,128)(2,1)S(1)} %pad_maximum_fusion.own), channel_id=1, source_target_pairs={{0,4},{1,5},{2,6},{3,7},{4,8},{5,9},{6,10},{7,11},{8,12},{9,13},{1... | collective-permute-start | bytes 1179656 | tf_op jit(solution)/shard_map/ppermute | solution.py:361
  21.0 12.6 %collective-permute-start.5 = (bf16[96,1536]{1,0:T(8,128)(2,1)S(1)}, bf16[96,1536]{1,0:T(8,128)(2,1)S(1)}, u32[]{:S(2)}, u32[]{:S(2)}) collective-permute-start(bf16[96,1536]{1,0:T(8,128)(2,1)S(1)} %pad_maximum_fusion.1.rest_0_), channel_id=1, source_target_pairs={{0,4},{1,5},{2,6},{3,7},{4,8},{5,9},{6,10},{7,11},{8,12},{9,13},{1... | collective-permute-start | bytes 884744 | tf_op jit(solution)/shard_map/ppermute | solution.py:346
  22.6 10.9 %collective-permute-start.6 = (bf16[96,1536]{1,0:T(8,128)(2,1)S(1)}, bf16[96,1536]{1,0:T(8,128)(2,1)S(1)}, u32[]{:S(2)}, u32[]{:S(2)}) collective-permute-start(bf16[96,1536]{1,0:T(8,128)(2,1)S(1)} %pad_maximum_fusion.1.rest_0_), channel_id=1, source_target_pairs={{0,28},{1,29},{2,30},{3,31},{4,0},{5,1},{6,2},{7,3},{8,4},{9,5},{1... | collective-permute-start | bytes 884744 | tf_op jit(solution)/shard_map/ppermute | solution.py:346
  24.4 18.8 %collective-permute-start = (bf16[64,2304]{1,0:T(8,128)(2,1)}, bf16[64,2304]{1,0:T(8,128)(2,1)S(1)}, u32[]{:S(2)}, u32[]{:S(2)}) collective-permute-start(bf16[64,2304]{1,0:T(8,128)(2,1)} %get-tuple-element.67), channel_id=1, source_target_pairs={{0,1},{1,0},{2,3},{3,2},{4,5},{5,4},{6,7},{7,6},{8,9},{9,8},{10,11... | collective-permute-start | bytes 884744 | tf_op jit(solution)/shard_map/ppermute | solution.py:357
  33.5 48.0 %copy-start.12 = (bf16[96,1536]{1,0:T(8,128)(2,1)}, bf16[96,1536]{1,0:T(8,128)(2,1)S(1)}, u32[]{:S(2)}) copy-start(bf16[96,1536]{1,0:T(8,128)(2,1)S(1)} %collective-permute-done.5.rest_1_) | copy-start | bytes 884740
  33.5 48.0 %copy-start.13 = (bf16[96,1536]{1,0:T(8,128)(2,1)}, bf16[96,1536]{1,0:T(8,128)(2,1)S(1)}, u32[]{:S(2)}) copy-start(bf16[96,1536]{1,0:T(8,128)(2,1)S(1)} %collective-permute-done.6.rest_2_) | copy-start | bytes 884740
  33.6 16.2 %collective-permute-start.7 = (bf16[96,1536]{1,0:T(8,128)(2,1)S(1)}, bf16[96,1536]{1,0:T(8,128)(2,1)}, u32[]{:S(2)}, u32[]{:S(2)}) collective-permute-start(bf16[96,1536]{1,0:T(8,128)(2,1)S(1)} %collective-permute-done.5.rest_1_), channel_id=1, source_target_pairs={{0,4},{1,5},{2,6},{3,7},{4,8},{5,9},{6,10},{7,11},{8,12},{9,13},{1... | collective-permute-start | bytes 884744 | tf_op jit(solution)/shard_map/ppermute | solution.py:346
  35.9 13.9 %collective-permute-start.8 = (bf16[96,1536]{1,0:T(8,128)(2,1)S(1)}, bf16[96,1536]{1,0:T(8,128)(2,1)}, u32[]{:S(2)}, u32[]{:S(2)}) collective-permute-start(bf16[96,1536]{1,0:T(8,128)(2,1)S(1)} %collective-permute-done.6.rest_2_), channel_id=1, source_target_pairs={{0,28},{1,29},{2,30},{3,31},{4,0},{5,1},{6,2},{7,3},{8,4},{9,5},{1... | collective-permute-start | bytes 884744 | tf_op jit(solution)/shard_map/ppermute | solution.py:346
  39.9 9.9 %collective-permute-start.9 = (bf16[96,1536]{1,0:T(8,128)(2,1)S(1)}, bf16[96,1536]{1,0:T(8,128)(2,1)}, u32[]{:S(2)}, u32[]{:S(2)}) collective-permute-start(bf16[96,1536]{1,0:T(8,128)(2,1)S(1)} %pad_maximum_fusion.1.rest_0_), channel_id=1, source_target_pairs={{0,1},{1,0},{2,3},{3,2},{4,5},{5,4},{6,7},{7,6},{8,9},{9,8},{10,11... | collective-permute-start | bytes 884744 | tf_op jit(solution)/shard_map/ppermute | solution.py:350
  49.8 14.8 %collective-permute-start.21 = (bf16[128,1536]{1,0:T(8,128)(2,1)}, bf16[128,1536]{1,0:T(8,128)(2,1)S(1)}, u32[]{:S(2)}, u32[]{:S(2)}) collective-permute-start(bf16[128,1536]{1,0:T(8,128)(2,1)} %get-tuple-element.99), channel_id=1, source_target_pairs={{0,1},{1,0},{2,3},{3,2},{4,5},{5,4},{6,7},{7,6},{8,9},{9,8},{10,11... | collective-permute-start | bytes 1179656 | tf_op jit(solution)/shard_map/ppermute | solution.py:388
  54.0 10.6 %collective-permute-start.20 = (bf16[128,1536]{1,0:T(8,128)(2,1)}, bf16[128,1536]{1,0:T(8,128)(2,1)S(1)}, u32[]{:S(2)}, u32[]{:S(2)}) collective-permute-start(bf16[128,1536]{1,0:T(8,128)(2,1)} %get-tuple-element.98), channel_id=1, source_target_pairs={{0,1},{1,0},{2,3},{3,2},{4,5},{5,4},{6,7},{7,6},{8,9},{9,8},{10,11... | collective-permute-start | bytes 1179656 | tf_op jit(solution)/shard_map/ppermute | solution.py:387
  54.5 10.0 %collective-permute-start.10 = (bf16[96,1536]{1,0:T(8,128)(2,1)}, bf16[96,1536]{1,0:T(8,128)(2,1)S(1)}, u32[]{:S(2)}, u32[]{:S(2)}) collective-permute-start(bf16[96,1536]{1,0:T(8,128)(2,1)} %collective-permute-done.7.rest_3_), channel_id=1, source_target_pairs={{0,4},{1,5},{2,6},{3,7},{4,8},{5,9},{6,10},{7,11},{8,12},{9,13},{1... | collective-permute-start | bytes 884744 | tf_op jit(solution)/shard_map/ppermute | solution.py:346
  54.5 10.0 %collective-permute-start.11 = (bf16[96,1536]{1,0:T(8,128)(2,1)}, bf16[96,1536]{1,0:T(8,128)(2,1)}, u32[]{:S(2)}, u32[]{:S(2)}) collective-permute-start(bf16[96,1536]{1,0:T(8,128)(2,1)} %collective-permute-done.8.rest_4_), channel_id=1, source_target_pairs={{0,28},{1,29},{2,30},{3,31},{4,0},{5,1},{6,2},{7,3},{8,4},{9,5},{1... | collective-permute-start | bytes 884744 | tf_op jit(solution)/shard_map/ppermute | solution.py:346
  69.1 38.7 %all-to-all-start.1 = ((bf16[8,192,768]{2,1,0:T(8,128)(2,1)}), bf16[8,192,768]{2,1,0:T(8,128)(2,1)S(1)}, u32[]{:S(2)}, u32[]{:S(2)}) async-start(bf16[8,192,768]{2,1,0:T(8,128)(2,1)} %bitcast.15), calls=%async_computation.1 | async-start | bytes 4718592 | tf_op jit(solution)/shard_map/all_to_all | solution.py:396
  73.7 8.7 %collective-permute-start.12 = (bf16[96,1536]{1,0:T(8,128)(2,1)S(1)}, bf16[96,1536]{1,0:T(8,128)(2,1)}, u32[]{:S(2)}, u32[]{:S(2)}) collective-permute-start(bf16[96,1536]{1,0:T(8,128)(2,1)S(1)} %collective-permute-done.10.rest_5_), channel_id=1, source_target_pairs={{0,4},{1,5},{2,6},{3,7},{4,8},{5,9},{6,10},{7,11},{8,12},{9,13},{1... | collective-permute-start | bytes 884744 | tf_op jit(solution)/shard_map/ppermute | solution.py:346
  75.4 9.1 %collective-permute-start.13 = (bf16[96,1536]{1,0:T(8,128)(2,1)S(1)}, bf16[96,1536]{1,0:T(8,128)(2,1)}, u32[]{:S(2)}, u32[]{:S(2)}) collective-permute-start(bf16[96,1536]{1,0:T(8,128)(2,1)S(1)} %collective-permute-done.5.rest_1_), channel_id=1, source_target_pairs={{0,1},{1,0},{2,3},{3,2},{4,5},{5,4},{6,7},{7,6},{8,9},{9,8},{10,11... | collective-permute-start | bytes 884744 | tf_op jit(solution)/shard_map/ppermute | solution.py:350
  76.7 7.8 %collective-permute-start.14 = (bf16[96,1536]{1,0:T(8,128)(2,1)S(1)}, bf16[96,1536]{1,0:T(8,128)(2,1)}, u32[]{:S(2)}, u32[]{:S(2)}) collective-permute-start(bf16[96,1536]{1,0:T(8,128)(2,1)S(1)} %collective-permute-done.6.rest_2_), channel_id=1, source_target_pairs={{0,1},{1,0},{2,3},{3,2},{4,5},{5,4},{6,7},{7,6},{8,9},{9,8},{10,11... | collective-permute-start | bytes 884744 | tf_op jit(solution)/shard_map/ppermute | solution.py:350
  81.5 3.5 %collective-permute-start.15 = (bf16[96,1536]{1,0:T(8,128)(2,1)}, bf16[96,1536]{1,0:T(8,128)(2,1)}, u32[]{:S(2)}, u32[]{:S(2)}) collective-permute-start(bf16[96,1536]{1,0:T(8,128)(2,1)} %collective-permute-done.7.rest_3_), channel_id=1, source_target_pairs={{0,1},{1,0},{2,3},{3,2},{4,5},{5,4},{6,7},{7,6},{8,9},{9,8},{10,11... | collective-permute-start | bytes 884744 | tf_op jit(solution)/shard_map/ppermute | solution.py:350
  82.0 3.0 %collective-permute-start.16 = (bf16[96,1536]{1,0:T(8,128)(2,1)}, bf16[96,1536]{1,0:T(8,128)(2,1)}, u32[]{:S(2)}, u32[]{:S(2)}) collective-permute-start(bf16[96,1536]{1,0:T(8,128)(2,1)} %collective-permute-done.8.rest_4_), channel_id=1, source_target_pairs={{0,1},{1,0},{2,3},{3,2},{4,5},{5,4},{6,7},{7,6},{8,9},{9,8},{10,11... | collective-permute-start | bytes 884744 | tf_op jit(solution)/shard_map/ppermute | solution.py:350
  82.5 3.3 %collective-permute-start.17 = (bf16[96,1536]{1,0:T(8,128)(2,1)S(1)}, bf16[96,1536]{1,0:T(8,128)(2,1)}, u32[]{:S(2)}, u32[]{:S(2)}) collective-permute-start(bf16[96,1536]{1,0:T(8,128)(2,1)S(1)} %collective-permute-done.10.rest_5_), channel_id=1, source_target_pairs={{0,1},{1,0},{2,3},{3,2},{4,5},{5,4},{6,7},{7,6},{8,9},{9,8},{10,11... | collective-permute-start | bytes 884744 | tf_op jit(solution)/shard_map/ppermute | solution.py:350
  84.5 1.8 %collective-permute-start.18 = (bf16[96,1536]{1,0:T(8,128)(2,1)}, bf16[96,1536]{1,0:T(8,128)(2,1)S(1)}, u32[]{:S(2)}, u32[]{:S(2)}) collective-permute-start(bf16[96,1536]{1,0:T(8,128)(2,1)} %collective-permute-done.11.rest_6_), channel_id=1, source_target_pairs={{0,1},{1,0},{2,3},{3,2},{4,5},{5,4},{6,7},{7,6},{8,9},{9,8},{10,11... | collective-permute-start | bytes 884744 | tf_op jit(solution)/shard_map/ppermute | solution.py:350
  84.6 2.2 %collective-permute-start.19 = (bf16[96,1536]{1,0:T(8,128)(2,1)}, bf16[96,1536]{1,0:T(8,128)(2,1)S(1)}, u32[]{:S(2)}, u32[]{:S(2)}) collective-permute-start(bf16[96,1536]{1,0:T(8,128)(2,1)} %collective-permute-done.12.rest_7_), channel_id=1, source_target_pairs={{0,1},{1,0},{2,3},{3,2},{4,5},{5,4},{6,7},{7,6},{8,9},{9,8},{10,11... | collective-permute-start | bytes 884744 | tf_op jit(solution)/shard_map/ppermute | solution.py:350
  102.4 30.4 %copy-start.27 = (bf16[128,1536]{1,0:T(8,128)(2,1)S(1)}, bf16[128,1536]{1,0:T(8,128)(2,1)}, u32[]{:S(2)}) copy-start(bf16[128,1536]{1,0:T(8,128)(2,1)} %get-tuple-element.106) | copy-start | bytes 1179652
  102.4 58.8 %copy-start.32 = (bf16[16,3072]{1,0:T(8,128)(2,1)S(1)}, bf16[16,3072]{1,0:T(8,128)(2,1)}, u32[]{:S(2)}) copy-start(bf16[16,3072]{1,0:T(8,128)(2,1)} %get-tuple-element.118) | copy-start | bytes 294916
  102.4 58.8 %copy-start.31 = (bf16[16,3072]{1,0:T(8,128)(2,1)S(1)}, bf16[16,3072]{1,0:T(8,128)(2,1)}, u32[]{:S(2)}) copy-start(bf16[16,3072]{1,0:T(8,128)(2,1)} %get-tuple-element.119) | copy-start | bytes 294916
  102.4 61.0 %copy-start.30 = (bf16[16,3072]{1,0:T(8,128)(2,1)S(1)}, bf16[16,3072]{1,0:T(8,128)(2,1)}, u32[]{:S(2)}) copy-start(bf16[16,3072]{1,0:T(8,128)(2,1)} %get-tuple-element.120) | copy-start | bytes 294916
  102.4 61.1 %copy-start.29 = (bf16[16,3072]{1,0:T(8,128)(2,1)S(1)}, bf16[16,3072]{1,0:T(8,128)(2,1)}, u32[]{:S(2)}) copy-start(bf16[16,3072]{1,0:T(8,128)(2,1)} %get-tuple-element.121) | copy-start | bytes 294916
  112.2 47.3 %all-to-all-start.2 = ((bf16[16,12,768]{2,1,0:T(8,128)(2,1)}), bf16[16,12,768]{2,1,0:T(8,128)(2,1)S(1)}, u32[]{:S(2)}, u32[]{:S(2)}) async-start(bf16[16,12,768]{2,1,0:T(8,128)(2,1)} %shard_map.135), calls=%async_computation.2 | async-start | bytes 786432 | tf_op jit(solution)/shard_map/all_to_all | solution.py:426
  131.5 18.9 %collective-permute-start.22 = (bf16[128,1536]{1,0:T(8,128)(2,1)S(1)}, bf16[128,1536]{1,0:T(8,128)(2,1)S(1)}, u32[]{:S(2)}, u32[]{:S(2)}) collective-permute-start(bf16[128,1536]{1,0:T(8,128)(2,1)S(1)} %copy-done.28), channel_id=1, source_target_pairs={{2,0},{3,1},{4,2},{5,3},{6,4},{7,5},{8,6},{9,7},{10,8},{11,9},{12,... | collective-permute-start | bytes 1179656 | tf_op jit(solution)/shard_map/ppermute | solution.py:407
  132.8 26.6 %collective-permute-start.23 = (bf16[128,1536]{1,0:T(8,128)(2,1)S(1)}, bf16[128,1536]{1,0:T(8,128)(2,1)S(1)}, u32[]{:S(2)}, u32[]{:S(2)}) collective-permute-start(bf16[128,1536]{1,0:T(8,128)(2,1)S(1)} %copy-done.27), channel_id=1, source_target_pairs={{4,0},{5,1},{6,2},{7,3},{8,4},{9,5},{10,6},{11,7},{12,8},{13,9},{1... | collective-permute-start | bytes 1179656 | tf_op jit(solution)/shard_map/ppermute | solution.py:408
  134.1 5.2 %collective-permute-start.24 = (bf16[16,3072]{1,0:T(8,128)(2,1)}, bf16[16,3072]{1,0:T(8,128)(2,1)S(1)}, u32[]{:S(2)}, u32[]{:S(2)}) collective-permute-start(bf16[16,3072]{1,0:T(8,128)(2,1)} %get-tuple-element.107), channel_id=1, source_target_pairs={{0,32},{32,0},{64,96},{96,64},{128,160},{160,128},{192,224},{224,1... | collective-permute-start | bytes 294920 | tf_op jit(solution)/shard_map/ppermute | solution.py:428
  134.5 4.9 %collective-permute-start.25 = (bf16[16,3072]{1,0:T(8,128)(2,1)}, bf16[16,3072]{1,0:T(8,128)(2,1)S(1)}, u32[]{:S(2)}, u32[]{:S(2)}) collective-permute-start(bf16[16,3072]{1,0:T(8,128)(2,1)} %get-tuple-element.108), channel_id=1, source_target_pairs={{0,64},{32,96},{64,0},{96,32},{128,192},{160,224},{192,128},{224,1... | collective-permute-start | bytes 294920 | tf_op jit(solution)/shard_map/ppermute | solution.py:428
  134.6 6.3 %collective-permute-start.26 = (bf16[16,3072]{1,0:T(8,128)(2,1)}, bf16[16,3072]{1,0:T(8,128)(2,1)S(1)}, u32[]{:S(2)}, u32[]{:S(2)}) collective-permute-start(bf16[16,3072]{1,0:T(8,128)(2,1)} %get-tuple-element.109), channel_id=1, source_target_pairs={{0,96},{32,64},{64,32},{96,0},{128,224},{160,192},{192,160},{224,1... | collective-permute-start | bytes 294920 | tf_op jit(solution)/shard_map/ppermute | solution.py:428
  139.3 33.9 %copy-start.19 = (bf16[16,3072]{1,0:T(8,128)(2,1)}, bf16[16,3072]{1,0:T(8,128)(2,1)S(1)}, u32[]{:S(2)}) copy-start(bf16[16,3072]{1,0:T(8,128)(2,1)S(1)} %collective-permute-done.24.rest_1_) | copy-start | bytes 294916
  139.3 33.9 %copy-start.20 = (bf16[16,3072]{1,0:T(8,128)(2,1)}, bf16[16,3072]{1,0:T(8,128)(2,1)S(1)}, u32[]{:S(2)}) copy-start(bf16[16,3072]{1,0:T(8,128)(2,1)S(1)} %collective-permute-done.25.rest_2_) | copy-start | bytes 294916
  140.9 32.3 %copy-start.21 = (bf16[16,3072]{1,0:T(8,128)(2,1)}, bf16[16,3072]{1,0:T(8,128)(2,1)S(1)}, u32[]{:S(2)}) copy-start(bf16[16,3072]{1,0:T(8,128)(2,1)S(1)} %collective-permute-done.26.rest_3_) | copy-start | bytes 294916
  159.5 10.8 %collective-permute-start.32 = (f32[6,768]{1,0:T(8,128)S(1)}, f32[6,768]{1,0:T(8,128)S(1)}, u32[]{:S(2)}, u32[]{:S(2)}) collective-permute-start(f32[6,768]{1,0:T(8,128)S(1)} %constant_dynamic-slice_fusion), channel_id=1, source_target_pairs={{0,1},{1,0},{2,3},{3,2},{4,5},{5,4},{6,7},{7,6},{8,9},{9,8},{10,11... | collective-permute-start | bytes 55304 | tf_op jit(solution)/shard_map/ppermute | solution.py:437
  161.3 11.0 %collective-permute-start.28 = (bf16[16,3072]{1,0:T(8,128)(2,1)S(1)}, bf16[16,3072]{1,0:T(8,128)(2,1)S(1)}, u32[]{:S(2)}, u32[]{:S(2)}) collective-permute-start(bf16[16,3072]{1,0:T(8,128)(2,1)S(1)} %copy-done.32), channel_id=1, source_target_pairs={{0,128},{32,160},{64,192},{96,224},{128,0},{160,32},{192,64},{224,... | collective-permute-start | bytes 294920 | tf_op jit(solution)/shard_map/ppermute | solution.py:428
  161.3 11.0 %collective-permute-start.29 = (bf16[16,3072]{1,0:T(8,128)(2,1)S(1)}, bf16[16,3072]{1,0:T(8,128)(2,1)S(1)}, u32[]{:S(2)}, u32[]{:S(2)}) collective-permute-start(bf16[16,3072]{1,0:T(8,128)(2,1)S(1)} %copy-done.31), channel_id=1, source_target_pairs={{0,160},{32,128},{64,224},{96,192},{128,32},{160,0},{192,96},{224,... | collective-permute-start | bytes 294920 | tf_op jit(solution)/shard_map/ppermute | solution.py:428
  163.5 8.8 %collective-permute-start.30 = (bf16[16,3072]{1,0:T(8,128)(2,1)S(1)}, bf16[16,3072]{1,0:T(8,128)(2,1)S(1)}, u32[]{:S(2)}, u32[]{:S(2)}) collective-permute-start(bf16[16,3072]{1,0:T(8,128)(2,1)S(1)} %copy-done.30), channel_id=1, source_target_pairs={{0,192},{32,224},{64,128},{96,160},{128,64},{160,96},{192,0},{224,... | collective-permute-start | bytes 294920 | tf_op jit(solution)/shard_map/ppermute | solution.py:428
  163.5 8.8 %collective-permute-start.31 = (bf16[16,3072]{1,0:T(8,128)(2,1)S(1)}, bf16[16,3072]{1,0:T(8,128)(2,1)S(1)}, u32[]{:S(2)}, u32[]{:S(2)}) collective-permute-start(bf16[16,3072]{1,0:T(8,128)(2,1)S(1)} %copy-done.29), channel_id=1, source_target_pairs={{0,224},{32,192},{64,160},{96,128},{128,96},{160,64},{192,32},{224... | collective-permute-start | bytes 294920 | tf_op jit(solution)/shard_map/ppermute | solution.py:428
  170.4 2.8 %collective-permute-start.27 = (bf16[64,3072]{1,0:T(8,128)(2,1)}, bf16[64,3072]{1,0:T(8,128)(2,1)S(1)}, u32[]{:S(2)}, u32[]{:S(2)}) collective-permute-start(bf16[64,3072]{1,0:T(8,128)(2,1)} %get-tuple-element.113), channel_id=1, source_target_pairs={{0,1},{1,0},{2,3},{3,2},{4,5},{5,4},{6,7},{7,6},{8,9},{9,8},{10,11... | collective-permute-start | bytes 1179656 | tf_op jit(solution)/shard_map/ppermute | solution.py:445
  (21 other events, 128.1 us)
